TPU v7x, 256 devices: a whole 4x4x8 slice. The times are simulated.
256 devices in a mesh: blocks: 8 (over z), views: 4 (over y), rows: 8 (over x, core).
Axes of the slice: x: 4, y: 4, z: 8, core: 2. Of those that a mesh axis runs over, the one named last changes fastest.
Arguments:
- estimate: float32 [64, 1024, 256], P('rows', 'blocks'), may hold values from 0.5 to 2
- views_data: float32 [4, 64, 1024, 256], P('views', 'rows', 'blocks'), may hold values from 0.2 to 5
- target: int32 [4, 64, 1024, 2], P('views', 'rows', 'blocks'), may hold values from 0 to 131071, as said below
- psf_taps: float32 [4, 3, 7], P('views'), may hold values from 0.2 to 1
- shifts: int32 [4], P('views'), may hold values from 0 to 127
Outputs:
- restored: float32 [64, 1024, 256], P('rows', 'blocks')
Inputs may be any that keep to these rules, and one draw needn't show every extreme that they name: `target`: for each view every output brick is named exactly once. The bricks of one view held by one device name at most 64 = 64 output bricks held by any one device, and exactly 64 of some device.
All inputs are finite; a program needn't handle non-finite values.
Results may differ from a plain program's by a relative error of at most 0.00002.
Values sent between devices are 32-bit elements; how exact they have to be, the bound alone decides.
No kernel may reach another device: no remote copies, remote signals or barrier semaphores. Data moves between devices by JAX's collectives and lax.ppermute only.
A program may use at most 64 MiB of HBM per device.

v0:
```python
import jax
import jax.numpy as jnp
from jax import lax
from jax.sharding import PartitionSpec as P

BRICK = 128
HALO = 3
ITERS = 2


def with_halo(value, sides, width):
    for axis, dim in sides:
        count, length = (lax.axis_size(axis), value.shape[dim])
        up = [(i, (i + 1) % count) for i in range(count - 1)]
        down = [(j, i) for i, j in up]
        last = lax.slice_in_dim(value, length - width, length, axis=dim)
        leading = lax.slice_in_dim(value, 0, width, axis=dim)
        before = lax.ppermute(last, axis, up)
        after = lax.ppermute(leading, axis, down)
        value = jnp.concatenate([before, value, after], axis=dim)
    return value


def axis_blur(volume, weights, dim_index, length_along):
    result = jnp.zeros(
        volume.shape[:dim_index] + (length_along,) + volume.shape[dim_index + 1 :], jnp.float32
    )
    for offset in range(2 * HALO + 1):
        result = result + weights[offset] * lax.slice_in_dim(
            volume, offset, offset + length_along, axis=dim_index
        )
    return result


def blur_local(volume, weights):
    x_cells, y_cells, z_cells = volume.shape
    extended = with_halo(volume, (("rows", 0),), HALO)
    result = axis_blur(extended, weights[0], 0, x_cells)
    widened = with_halo(result, (("blocks", 1),), HALO)
    result = axis_blur(widened, weights[1], 1, y_cells)
    padded = jnp.pad(result, ((0, 0), (0, 0), (HALO, HALO)))
    return axis_blur(padded, weights[2], 2, z_cells)


def rotate_bricks(bricks, start_at):
    doubled = jnp.concatenate([bricks, bricks], axis=1)
    return lax.dynamic_slice_in_dim(doubled, start_at, BRICK, 1)


def send_to_views(buffer):
    result = lax.all_to_all(buffer, ("blocks", "rows"), split_axis=0, concat_axis=0, tiled=True)
    return result


def send_to_blocks(buffer):
    result = lax.all_to_all(buffer, ("blocks", "rows"), split_axis=0, concat_axis=0, tiled=True)
    return result


def per_device(estimate, views_data, target, psf_taps, shifts):
    x_cells, y_cells, z_cells = estimate.shape
    block_count = lax.axis_size("blocks")
    row_count = lax.axis_size("rows")
    peer_count = block_count * row_count
    view_count = lax.axis_size("views")
    brick_cols = z_cells // BRICK
    brick_count = x_cells * y_cells * brick_cols
    capacity = 2 * brick_count // peer_count
    all_cols = y_cells * block_count
    targets = target.reshape(brick_count)
    brick_z = targets % brick_cols
    column = targets // brick_cols % all_cols
    row_line = targets // (brick_cols * all_cols)
    dest_dev = column // y_cells * row_count + row_line // x_cells
    dest_slot = (row_line % x_cells * y_cells + column % y_cells) * brick_cols + brick_z
    one_hot = (dest_dev[:, None] == jnp.arange(peer_count, dtype=jnp.int32)[None, :]).astype(
        jnp.int32
    )
    before = jnp.cumsum(one_hot, axis=0) - one_hot
    rank_in = jnp.sum(before * one_hot, axis=1)
    position = dest_dev * capacity + rank_in
    request_list = (
        jnp.full((peer_count * capacity,), brick_count, jnp.int32).at[position].set(dest_slot)
    )
    wanted = lax.all_to_all(
        request_list.reshape(peer_count, capacity),
        ("blocks", "rows"),
        split_axis=0,
        concat_axis=0,
        tiled=True,
    ).reshape(-1)
    present = (wanted < brick_count).astype(jnp.float32)[:, None]
    safe_wanted = jnp.minimum(wanted, brick_count - 1)
    weights = psf_taps[0] / jnp.sum(psf_taps[0], axis=1, keepdims=True)
    flipped = weights[:, ::-1]
    shift_by = shifts[0]
    observed = views_data.reshape(brick_count, BRICK)
    for iteration in range(ITERS):
        blurred = blur_local(estimate, weights).reshape(brick_count, BRICK)
        outgoing = (jnp.take(blurred, safe_wanted, axis=0) * present).reshape(
            peer_count, capacity, BRICK
        )
        incoming = send_to_views(outgoing).reshape(peer_count * capacity, BRICK)
        forward = jnp.take(incoming, position, axis=0)
        predicted = rotate_bricks(forward, shift_by)
        returned_ratio = rotate_bricks(observed / predicted, BRICK - shift_by)
        back_buffer = (
            jnp.zeros((peer_count * capacity, BRICK), jnp.float32).at[position].set(returned_ratio)
        )
        arrived = send_to_blocks(back_buffer.reshape(peer_count, capacity, BRICK))
        placed = (
            jnp.zeros((brick_count, BRICK), jnp.float32)
            .at[wanted]
            .set(arrived.reshape(peer_count * capacity, BRICK), mode="drop")
        )
        projected = blur_local(placed.reshape(x_cells, y_cells, z_cells), flipped)
        combined = lax.psum(projected, "views")
        estimate = estimate * combined / view_count
    return estimate


def solution(mesh):
    placed = (
        P("rows", "blocks", None),
        P("views", "rows", "blocks", None),
        P("views", "rows", "blocks", None),
        P("views", None, None),
        P("views"),
    )
    return jax.shard_map(
        per_device, mesh=mesh, in_specs=placed, out_specs=P("rows", "blocks", None), check_vma=False
    )
```

profile of v0, /device:TPU:34, one launch (start us, length us, event | category | flops | bytes accessed | tf_op | source)
XLA Modules:
  0.0 632.5 jit_solution(7560720862158683624)
XLA Ops:
  14.5 18.1 %reduce-window.6 = s32[64,16,128]{2,1,0:T(8,128)S(1)} reduce-window(s32[64,16,128]{2,1,0:T(8,128)S(1)} %fusion.165, s32[]{:T(128)} %constant.122.clone.1), window={size=1x1x128 pad=0_0x0_0x127_0}, to_apply=%region_1.2 | reduce-window | flops 16646144 | bytes 1048580 | tf_op jit(solution)/shard_map/reduce-window
  34.2 8.1 %scatter_custom_fusion = s32[4096]{0:T(1024)S(1)} fusion(s32[2048]{0:T(1024)S(1)} %bitcast.81, s32[2048]{0:T(1024)S(1)} %get-tuple-element.31, s32[]{:T(128)} %constant.120.clone.1), kind=kCustom, calls=%fused_computation.383 | custom fusion | bytes 16388 | tf_op jit(solution)/shard_map/scatter | solution.py:83
  42.9 11.6 %all-to-all-start = ((s32[64,1,64]{2,1,0:T(1,128)}), s32[64,1,64]{2,1,0:T(1,128)S(1)}, u32[]{:S(2)}, u32[]{:S(2)}) async-start(s32[64,1,64]{2,1,0:T(1,128)} %all_to_all.18), calls=%async_computation | async-start | bytes 65536 | tf_op jit(solution)/shard_map/all_to_all | solution.py:85
  56.1 6.1 all-to-all-done
  63.9 4.6 fusion.150
  77.0 5.3 fusion.45
  82.2 6.2 fusion.86
  88.5 14.2 %gather_fusion = f32[4096,128]{1,0:T(8,128)} fusion(f32[2048,128]{1,0:T(8,128)S(1)} %reshape.478, s32[4096]{0:T(1024)S(1)} %fusion.167), kind=kCustom, calls=%fused_computation.clone | custom fusion | bytes 4210688 | tf_op jit(solution)/shard_map/jit(_take)/gather | solution.py:100
  107.1 6.7 %all-to-all-start.1 = ((f32[64,64,128]{2,1,0:T(8,128)}), f32[64,64,128]{2,1,0:T(8,128)S(1)}, u32[]{:S(2)}, u32[]{:S(2)}) async-start(f32[64,64,128]{2,1,0:T(8,128)} %bitcast.70), calls=%async_computation.1 | async-start | bytes 4194304 | tf_op jit(solution)/shard_map/all_to_all | solution.py:51
  116.8 47.5 %all-to-all-done.1 = f32[64,64,128]{2,1,0:T(8,128)S(1)} async-done(((f32[64,64,128]{2,1,0:T(8,128)}), f32[64,64,128]{2,1,0:T(8,128)S(1)}, u32[]{:S(2)}, u32[]{:S(2)}) %all-to-all-start.1) | async-done | bytes 2097184 | tf_op jit(solution)/shard_map/all_to_all | solution.py:51
  164.3 7.6 %gather_fusion.1 = f32[2048,128]{1,0:T(8,128)} fusion(f32[4096,128]{1,0:T(8,128)S(1)} %bitcast.68, s32[2048]{0:T(1024)S(1)} %broadcast_clamp_fusion), kind=kCustom, calls=%fused_computation.1.clone | custom fusion | bytes 2105344 | tf_op jit(solution)/shard_map/jit(_take)/gather | solution.py:104
  174.2 7.8 %scatter_custom_fusion.1 = f32[4096,128]{1,0:T(8,128)} fusion(s32[2048]{0:T(1024)S(1)} %bitcast.82, s32[]{:T(128)} %constant.122.clone.1, s32[]{:T(128)S(6)} %select_n.173, f32[2048,128]{1,0:T(8,128)S(1)} %fusion.79, f32[]{:T(128)} %constant.157, f32[]{:T(128)} %constant.119.clone.1), kind=kCustom, calls=%fused_computation.158 | custom fusion | flops 262144 | bytes 3145744 | tf_op jit(solution)/shard_map/scatter | solution.py:108
  182.0 6.3 all-to-all-start.2
  188.4 50.2 %all-to-all-done.2 = f32[64,64,128]{2,1,0:T(8,128)S(1)} async-done(((f32[64,64,128]{2,1,0:T(8,128)}), f32[64,64,128]{2,1,0:T(8,128)S(1)}, u32[]{:S(2)}, u32[]{:S(2)}) %all-to-all-start.2) | async-done | bytes 2097184 | tf_op jit(solution)/shard_map/all_to_all | solution.py:56
  240.0 11.2 %scatter_custom_fusion.2 = f32[2048,128]{1,0:T(8,128)S(1)} fusion(s32[4096]{0:T(1024)S(1)} %bitcast.79, f32[4096,128]{1,0:T(8,128)} %bitcast.73, f32[]{:T(128)} %constant.119.clone.1), kind=kCustom, calls=%fused_computation.279 | custom fusion | bytes 1049088 | tf_op jit(solution)/shard_map/scatter | solution.py:114
  264.0 4.6 fusion.142
  276.4 5.3 fusion.31
  281.7 7.2 %fusion.98 = f32[8,128,256]{2,1,0:T(8,128)} fusion(f32[8,128,256]{2,1,0:T(8,128)S(1)} %fusion.31, f32[]{:T(128)} %bitcast.26, f32[]{:T(128)} %bitcast.25, f32[]{:T(128)} %bitcast.24, f32[]{:T(128)} %bitcast.23, f32[]{:T(128)} %bitcast.22, f32[]{:T(128)} %bitcast.9, f32[]{:T(128)} %bitcast), kind=kLoop, calls=%fused_computation.179 | loop fusion | flops 3407872 | bytes 2097180 | tf_op jit(solution)/shard_map/add | solution.py:29
  289.0 49.7 %all-reduce.7.cloned.1.call-done = f32[8,128,256]{2,1,0:T(8,128)} async-done(((f32[8,128,256]{2,1,0:T(8,128)}), f32[8,128,256]{2,1,0:T(8,128)}) %all-reduce.7.cloned.1.call-update) | async-done | bytes 1048592 | tf_op jit(solution)/shard_map/psum | solution.py:117
  351.8 5.4 fusion.59
  366.6 5.3 fusion.17
  371.9 6.2 fusion.110
  378.8 10.8 %gather_fusion.2 = f32[4096,128]{1,0:T(8,128)S(1)} fusion(f32[2048,128]{1,0:T(8,128)S(1)} %reshape.484, s32[4096]{0:T(1024)S(1)} %copy-done.8), kind=kCustom, calls=%fused_computation.2.clone | custom fusion | bytes 4210688 | tf_op jit(solution)/shard_map/jit(_take)/gather | solution.py:100
  391.0 60.9 %all_to_all.29 = f32[64,64,128]{2,1,0:T(8,128)S(1)} all-to-all(f32[64,64,128]{2,1,0:T(8,128)S(1)} %bitcast.71), channel_id=1, replica_groups=mesh['blocks'=8,'views'=4,'rows'=8] {'blocks','rows'}, dimensions={0} | all-to-all | bytes 4194304 | tf_op jit(solution)/shard_map/all_to_all | solution.py:51
  451.9 7.6 %gather_fusion.3 = f32[2048,128]{1,0:T(8,128)} fusion(f32[4096,128]{1,0:T(8,128)S(1)} %bitcast.69, s32[2048]{0:T(1024)S(1)} %copy-done.10), kind=kCustom, calls=%fused_computation.3.clone | custom fusion | bytes 2105344 | tf_op jit(solution)/shard_map/jit(_take)/gather | solution.py:104
  462.9 7.4 %scatter_custom_fusion.3 = f32[4096,128]{1,0:T(8,128)S(1)} fusion(s32[2048]{0:T(1024)} %bitcast.83, s32[]{:T(128)} %constant.122.clone.1, s32[]{:T(128)S(6)} %select_n.173, f32[2048,128]{1,0:T(8,128)} %fusion.74, f32[]{:T(128)} %constant.157, f32[]{:T(128)} %constant.119.clone.1), kind=kCustom, calls=%fused_computation.154 | custom fusion | flops 262144 | bytes 3147268 | tf_op jit(solution)/shard_map/scatter | solution.py:108
  470.2 56.6 %all_to_all.30 = f32[64,64,128]{2,1,0:T(8,128)} all-to-all(f32[64,64,128]{2,1,0:T(8,128)S(1)} %bitcast.72), channel_id=1, replica_groups=mesh['blocks'=8,'views'=4,'rows'=8] {'blocks','rows'}, dimensions={0} | all-to-all | bytes 4194304 | tf_op jit(solution)/shard_map/all_to_all | solution.py:56
  526.8 11.2 %scatter_custom_fusion.4 = f32[2048,128]{1,0:T(8,128)S(1)} fusion(s32[4096]{0:T(1024)} %bitcast.80, f32[4096,128]{1,0:T(8,128)} %bitcast.74, f32[]{:T(128)} %constant.119.clone.1), kind=kCustom, calls=%fused_computation.277 | custom fusion | bytes 1049088 | tf_op jit(solution)/shard_map/scatter | solution.py:114
  549.2 4.6 fusion.130
  561.6 5.3 fusion.3
  566.9 7.3 %fusion.122 = f32[8,128,256]{2,1,0:T(8,128)} fusion(f32[8,128,256]{2,1,0:T(8,128)S(1)} %fusion.3, f32[]{:T(128)} %bitcast.26, f32[]{:T(128)} %bitcast.25, f32[]{:T(128)} %bitcast.24, f32[]{:T(128)} %bitcast.23, f32[]{:T(128)} %bitcast.22, f32[]{:T(128)} %bitcast.9, f32[]{:T(128)} %bitcast), kind=kLoop, calls=%fused_computation.203 | loop fusion | flops 3407872 | bytes 2097180 | tf_op jit(solution)/shard_map/add | solution.py:29
  574.2 49.1 %all-reduce.9.cloned.1.call-done = f32[8,128,256]{2,1,0:T(8,128)} async-done(((f32[8,128,256]{2,1,0:T(8,128)}), f32[8,128,256]{2,1,0:T(8,128)}) %all-reduce.9.cloned.1.call-update) | async-done | bytes 1048592 | tf_op jit(solution)/shard_map/psum | solution.py:117
  (137 shorter events, 101.2 us)
Async XLA Ops:
  7.7 55.9 %collective-permute-start = (f32[3,128,256]{2,1,0:T(8,128)S(1)}, f32[3,128,256]{2,1,0:T(8,128)S(1)}, u32[]{:S(2)}, u32[]{:S(2)}) collective-permute-start(f32[3,128,256]{2,1,0:T(8,128)S(1)} %get-tuple-element.29), channel_id=1, source_target_pairs={{0,1},{1,2},{2,3},{3,4},{4,5},{5,6},{6,7},{8,9},{9,10},{10,11},{11... | collective-permute-start | bytes 1179656 | tf_op jit(solution)/shard_map/ppermute | solution.py:18
  9.6 54.2 %collective-permute-start.1 = (f32[3,128,256]{2,1,0:T(8,128)S(1)}, f32[3,128,256]{2,1,0:T(8,128)S(1)}, u32[]{:S(2)}, u32[]{:S(2)}) collective-permute-start(f32[3,128,256]{2,1,0:T(8,128)S(1)} %get-tuple-element.30), channel_id=1, source_target_pairs={{1,0},{2,1},{3,2},{4,3},{5,4},{6,5},{7,6},{9,8},{10,9},{11,10},{12... | collective-permute-start | bytes 1179656 | tf_op jit(solution)/shard_map/ppermute | solution.py:19
  32.8 21.7 %copy-start.18 = (f32[1,3,7]{2,0,1:T(1,128)S(1)}, f32[1,3,7]{2,0,1:T(1,128)}, u32[]{:S(2)}) copy-start(f32[1,3,7]{2,0,1:T(1,128)} %param.12) | copy-start | bytes 256
  33.3 30.4 %copy-start = (f32[8,128,256]{2,1,0:T(8,128)S(1)}, f32[8,128,256]{2,1,0:T(8,128)}, u32[]{:S(2)}) copy-start(f32[8,128,256]{2,1,0:T(8,128)} %param.9) | copy-start | bytes 3145732
  34.2 140.0 %copy-start.17 = (s32[2048,1]{0,1:T(1,128)}, s32[2048,1]{0,1:T(1,128)S(1)}, u32[]{:S(2)}) copy-start(s32[2048,1]{0,1:T(1,128)S(1)} %compare_select_fusion.1) | copy-start | bytes 24580
  42.9 19.2 %all-to-all-start = ((s32[64,1,64]{2,1,0:T(1,128)}), s32[64,1,64]{2,1,0:T(1,128)S(1)}, u32[]{:S(2)}, u32[]{:S(2)}) async-start(s32[64,1,64]{2,1,0:T(1,128)} %all_to_all.18), calls=%async_computation | async-start | bytes 65536 | tf_op jit(solution)/shard_map/all_to_all | solution.py:85
  63.6 25.0 %copy-start.7 = (s32[4096]{0:T(1024)}, s32[4096]{0:T(1024)S(1)}, u32[]{:S(2)}) copy-start(s32[4096]{0:T(1024)S(1)} %fusion.167) | copy-start | bytes 49156
  63.6 39.1 %copy-start.11 = (pred[4096]{0:T(1024)(128)(4,1)}, pred[4096]{0:T(1024)(128)(4,1)S(1)}, u32[]{:S(2)}) copy-start(pred[4096]{0:T(1024)(128)(4,1)S(1)} %compare_and_fusion) | copy-start | bytes 12292
  68.6 6.0 collective-permute-start.2
  71.1 5.8 collective-permute-start.3
  107.1 57.1 %all-to-all-start.1 = ((f32[64,64,128]{2,1,0:T(8,128)}), f32[64,64,128]{2,1,0:T(8,128)S(1)}, u32[]{:S(2)}, u32[]{:S(2)}) async-start(f32[64,64,128]{2,1,0:T(8,128)} %bitcast.70), calls=%async_computation.1 | async-start | bytes 4194304 | tf_op jit(solution)/shard_map/all_to_all | solution.py:51
  116.8 55.1 %copy-start.13 = (pred[2048]{0:T(1024)(128)(4,1)}, pred[2048]{0:T(1024)(128)(4,1)S(1)}, u32[]{:S(2)}) copy-start(pred[2048]{0:T(1024)(128)(4,1)S(1)} %compare_and_fusion.1) | copy-start | bytes 6148
  116.8 55.0 %copy-start.9 = (s32[2048]{0:T(1024)}, s32[2048]{0:T(1024)S(1)}, u32[]{:S(2)}) copy-start(s32[2048]{0:T(1024)S(1)} %broadcast_clamp_fusion) | copy-start | bytes 24580
  182.0 56.7 %all-to-all-start.2 = ((f32[64,64,128]{2,1,0:T(8,128)}), f32[64,64,128]{2,1,0:T(8,128)S(1)}, u32[]{:S(2)}, u32[]{:S(2)}) async-start(f32[64,64,128]{2,1,0:T(8,128)} %bitcast.30), calls=%async_computation.2 | async-start | bytes 4194304 | tf_op jit(solution)/shard_map/all_to_all | solution.py:56
  188.3 150.5 %all-reduce.7.cloned.1.call-start = ((), (), s32[]{:S(2)}) async-start(), calls=%async_computation.5 | async-start | bytes 2097152 | tf_op jit(solution)/shard_map/psum | solution.py:117
  188.4 65.6 %copy-start.15 = (s32[4096,1]{0,1:T(1,128)}, s32[4096,1]{0,1:T(1,128)S(1)}, u32[]{:S(2)}) copy-start(s32[4096,1]{0,1:T(1,128)S(1)} %compare_select_fusion) | copy-start | bytes 49156
  252.1 9.4 %collective-permute-start.4 = (f32[3,128,256]{2,1,0:T(8,128)}, f32[3,128,256]{2,1,0:T(8,128)}, u32[]{:S(2)}, u32[]{:S(2)}) collective-permute-start(f32[3,128,256]{2,1,0:T(8,128)} %slice.626), channel_id=1, source_target_pairs={{0,1},{1,2},{2,3},{3,4},{4,5},{5,6},{6,7},{8,9},{9,10},{10,11},{11... | collective-permute-start | bytes 1179656 | tf_op jit(solution)/shard_map/ppermute | solution.py:18
  254.1 8.9 %collective-permute-start.5 = (f32[3,128,256]{2,1,0:T(8,128)S(1)}, f32[3,128,256]{2,1,0:T(8,128)}, u32[]{:S(2)}, u32[]{:S(2)}) collective-permute-start(f32[3,128,256]{2,1,0:T(8,128)S(1)} %slice.631), channel_id=1, source_target_pairs={{1,0},{2,1},{3,2},{4,3},{5,4},{6,5},{7,6},{9,8},{10,9},{11,10},{12... | collective-permute-start | bytes 1179656 | tf_op jit(solution)/shard_map/ppermute | solution.py:19
  268.7 5.9 collective-permute-start.6
  270.6 5.8 collective-permute-start.7
  289.0 334.3 %all-reduce.9.cloned.1.call-start = ((), (), s32[]{:S(2)}) async-start(), calls=%async_computation.6 | async-start | bytes 2097152 | tf_op jit(solution)/shard_map/psum | solution.py:117
  340.1 17.1 %copy-start.1 = (f32[8,128,256]{2,1,0:T(8,128)}, f32[8,128,256]{2,1,0:T(8,128)S(1)}, u32[]{:S(2)}) copy-start(f32[8,128,256]{2,1,0:T(8,128)S(1)} %broadcast_multiply_fusion) | copy-start | bytes 3145732
  341.0 9.4 %collective-permute-start.8 = (f32[3,128,256]{2,1,0:T(8,128)}, f32[3,128,256]{2,1,0:T(8,128)}, u32[]{:S(2)}, u32[]{:S(2)}) collective-permute-start(f32[3,128,256]{2,1,0:T(8,128)} %get-tuple-element.17), channel_id=1, source_target_pairs={{0,1},{1,2},{2,3},{3,4},{4,5},{5,6},{6,7},{8,9},{9,10},{10,11},{11... | collective-permute-start | bytes 1179656 | tf_op jit(solution)/shard_map/ppermute | solution.py:18
  342.9 8.9 %collective-permute-start.9 = (f32[3,128,256]{2,1,0:T(8,128)S(1)}, f32[3,128,256]{2,1,0:T(8,128)}, u32[]{:S(2)}, u32[]{:S(2)}) collective-permute-start(f32[3,128,256]{2,1,0:T(8,128)S(1)} %get-tuple-element.18), channel_id=1, source_target_pairs={{1,0},{2,1},{3,2},{4,3},{5,4},{6,5},{7,6},{9,8},{10,9},{11,10},{12... | collective-permute-start | bytes 1179656 | tf_op jit(solution)/shard_map/ppermute | solution.py:19
  357.3 6.1 collective-permute-start.10
  360.8 5.8 collective-permute-start.11
  391.0 60.9 %copy-start.10 = (s32[2048]{0:T(1024)S(1)}, s32[2048]{0:T(1024)}, u32[]{:S(2)}) copy-start(s32[2048]{0:T(1024)} %copy-done.9) | copy-start | bytes 24580
  538.2 9.2 %collective-permute-start.12 = (f32[3,128,256]{2,1,0:T(8,128)S(1)}, f32[3,128,256]{2,1,0:T(8,128)}, u32[]{:S(2)}, u32[]{:S(2)}) collective-permute-start(f32[3,128,256]{2,1,0:T(8,128)S(1)} %slice.672), channel_id=1, source_target_pairs={{0,1},{1,2},{2,3},{3,4},{4,5},{5,6},{6,7},{8,9},{9,10},{10,11},{11... | collective-permute-start | bytes 1179656 | tf_op jit(solution)/shard_map/ppermute | solution.py:18
  540.2 8.9 %collective-permute-start.13 = (f32[3,128,256]{2,1,0:T(8,128)S(1)}, f32[3,128,256]{2,1,0:T(8,128)S(1)}, u32[]{:S(2)}, u32[]{:S(2)}) collective-permute-start(f32[3,128,256]{2,1,0:T(8,128)S(1)} %slice.677), channel_id=1, source_target_pairs={{1,0},{2,1},{3,2},{4,3},{5,4},{6,5},{7,6},{9,8},{10,9},{11,10},{12... | collective-permute-start | bytes 1179656 | tf_op jit(solution)/shard_map/ppermute | solution.py:19
  553.8 6.1 collective-permute-start.14
  555.8 5.8 collective-permute-start.15
  566.9 56.5 %copy-start.2 = (f32[8,128,256]{2,1,0:T(8,128)S(1)}, f32[8,128,256]{2,1,0:T(8,128)}, u32[]{:S(2)}) copy-start(f32[8,128,256]{2,1,0:T(8,128)} %copy-done.1) | copy-start | bytes 3145732
  (8 other events, 42.1 us)
Sparse Core Ops, SparseCore 0:
  289.1 49.5 all-reduce.6
  574.3 48.9 all-reduce.8
where the time goes:
time: 635 us; the launch traced here: 633 us
  waiting for transfers between devices  224 us (35%)
  other arithmetic  118 us (19%)
  blocking collectives  118 us (19%)
  local copies, waits for them, and re-layouts  87.1 us (14%)
  starting transfers between devices  70.7 us (11%)
  between operations  15.4 us (2%)
    psum x2, waiting for transfers between devices, per_device(): combined = lax.psum(projected, 'views')  98.9 us
    add x12, other arithmetic, axis_blur(): result + weights[offset] * lax.slice_in_dim(volume, offset, offset + leng...  67.4 us
    all_to_all x1, blocking collectives, send_to_views(): lax.all_to_all(buffer, ('blocks', 'rows'), split_axis=0, concat_axis=0, t...  60.9 us
    all_to_all x1, blocking collectives, send_to_blocks(): lax.all_to_all(buffer, ('blocks', 'rows'), split_axis=0, concat_axis=0, t...  56.6 us
    all_to_all x1, waiting for transfers between devices, send_to_blocks(): lax.all_to_all(buffer, ('blocks', 'rows'), split_axis=0, concat_axis=0, t...  50.2 us
    all_to_all x1, waiting for transfers between devices, send_to_views(): lax.all_to_all(buffer, ('blocks', 'rows'), split_axis=0, concat_axis=0, t...  47.5 us
    ppermute x8, starting transfers between devices, with_halo(): after = lax.ppermute(leading, axis, down)  28.6 us
    gather x2, local copies, waits for them, and re-layouts, per_device(): jnp.take(blurred, safe_wanted, axis=0) * present  25 us
  transfers between devices with their start and end apart: 21, of which 15 were waited for; matrix products, arithmetic and copies ran while one was open for 6% of the time, Pallas kernels for 0%

commit v1 on v0

--- a/solution.py
+++ b/solution.py
@@ -47,11 +47,6 @@
     return lax.dynamic_slice_in_dim(doubled, start_at, BRICK, 1)
 
 
-def send_to_views(buffer):
-    result = lax.all_to_all(buffer, ("blocks", "rows"), split_axis=0, concat_axis=0, tiled=True)
-    return result
-
-
 def send_to_blocks(buffer):
     result = lax.all_to_all(buffer, ("blocks", "rows"), split_axis=0, concat_axis=0, tiled=True)
     return result
@@ -89,31 +84,22 @@
         concat_axis=0,
         tiled=True,
     ).reshape(-1)
-    present = (wanted < brick_count).astype(jnp.float32)[:, None]
-    safe_wanted = jnp.minimum(wanted, brick_count - 1)
     weights = psf_taps[0] / jnp.sum(psf_taps[0], axis=1, keepdims=True)
     flipped = weights[:, ::-1]
     shift_by = shifts[0]
-    observed = views_data.reshape(brick_count, BRICK)
+    observed = rotate_bricks(views_data.reshape(brick_count, BRICK), BRICK - shift_by)
+    outgoing = (
+        jnp.zeros((peer_count * capacity, BRICK), jnp.float32).at[position].set(observed)
+    )
+    arrived = send_to_blocks(outgoing.reshape(peer_count, capacity, BRICK))
+    moved = (
+        jnp.zeros((brick_count, BRICK), jnp.float32)
+        .at[wanted]
+        .set(arrived.reshape(peer_count * capacity, BRICK), mode="drop")
+    ).reshape(x_cells, y_cells, z_cells)
     for iteration in range(ITERS):
-        blurred = blur_local(estimate, weights).reshape(brick_count, BRICK)
-        outgoing = (jnp.take(blurred, safe_wanted, axis=0) * present).reshape(
-            peer_count, capacity, BRICK
-        )
-        incoming = send_to_views(outgoing).reshape(peer_count * capacity, BRICK)
-        forward = jnp.take(incoming, position, axis=0)
-        predicted = rotate_bricks(forward, shift_by)
-        returned_ratio = rotate_bricks(observed / predicted, BRICK - shift_by)
-        back_buffer = (
-            jnp.zeros((peer_count * capacity, BRICK), jnp.float32).at[position].set(returned_ratio)
-        )
-        arrived = send_to_blocks(back_buffer.reshape(peer_count, capacity, BRICK))
-        placed = (
-            jnp.zeros((brick_count, BRICK), jnp.float32)
-            .at[wanted]
-            .set(arrived.reshape(peer_count * capacity, BRICK), mode="drop")
-        )
-        projected = blur_local(placed.reshape(x_cells, y_cells, z_cells), flipped)
+        placed = moved / blur_local(estimate, weights)
+        projected = blur_local(placed, flipped)
         combined = lax.psum(projected, "views")
         estimate = estimate * combined / view_count
     return estimate

time: 635 us -> 369 us (0.58)
  blocking collectives: 118 us -> 0 us
  waiting for transfers between devices: 224 us -> 157 us
  local copies, waits for them, and re-layouts: 87.1 us -> 28 us
  other arithmetic: 118 us -> 98.9 us
    all_to_all x2 -> x0, blocking collectives: 118 us -> none  [the longest x1 60.9 us: send_to_views(): lax.all_to_all(buffer, ('blocks', 'rows'), split_axis=0, concat_axis=0, t...]
    all_to_all x1, waiting for transfers between devices: 50.2 us -> 0.01 us  [send_to_blocks(): lax.all_to_all(buffer, ('blocks', 'rows'), split_axis=0, concat_axis=0, t...]
    all_to_all x1 -> x0, waiting for transfers between devices: 47.5 us -> none  [send_to_views(): lax.all_to_all(buffer, ('blocks', 'rows'), split_axis=0, concat_axis=0, t...]
    gather x4 -> x0, local copies, waits for them, and re-layouts: 40.1 us -> none  [the longest x2 25 us: per_device(): jnp.take(blurred, safe_wanted, axis=0) * present]
    ppermute x8, waiting for transfers between devices: 9.83 us -> 36.8 us  [with_halo(): before = lax.ppermute(last, axis, up)]
    add x12 -> x10, other arithmetic: 67.4 us -> 55.4 us  [axis_blur(): result + weights[offset] * lax.slice_in_dim(volume, offset, offset + leng...]
    scatter x2 -> x1, local copies, waits for them, and re-layouts: 22.3 us -> 11.9 us  [per_device(): moved = jnp.zeros((brick_count, BRICK), jnp.float32).at[wanted].set(arriv...]
    div x2, other arithmetic: 2.33 us -> 12 us  [per_device(): placed = moved / blur_local(estimate, weights)]
  transfers between devices with their start and end apart: 21 -> 20, of which waited for: 15 -> 14; matrix products, arithmetic and copies ran while one was open for 6% -> 6% of each run, Pallas kernels for 0% -> 0%
where the time goes in v1:
time: 369 us; the launch traced here: 367 us
  waiting for transfers between devices  157 us (43%)
  other arithmetic  98.9 us (27%)
  starting transfers between devices  68.4 us (19%)
  local copies, waits for them, and re-layouts  28 us (8%)
  between operations  15.2 us (4%)
    psum x2, waiting for transfers between devices, per_device(): combined = lax.psum(projected, 'views')  101 us
    add x10, other arithmetic, axis_blur(): result + weights[offset] * lax.slice_in_dim(volume, offset, offset + leng...  55.4 us
    ppermute x8, waiting for transfers between devices, with_halo(): before = lax.ppermute(last, axis, up)  36.8 us
    ppermute x8, starting transfers between devices, with_halo(): before = lax.ppermute(last, axis, up)  23.6 us
    ppermute x8, starting transfers between devices, with_halo(): after = lax.ppermute(leading, axis, down)  22.5 us
    ppermute x8, waiting for transfers between devices, with_halo(): after = lax.ppermute(leading, axis, down)  19 us
    another operation x3, other arithmetic  18.5 us
    div x2, other arithmetic, per_device(): placed = moved / blur_local(estimate, weights)  12 us
  transfers between devices with their start and end apart: 20, of which 14 were waited for; matrix products, arithmetic and copies ran while one was open for 6% of the time, Pallas kernels for 0%

profile of v1, /device:TPU:34, one launch (start us, length us, event | category | flops | bytes accessed | tf_op | source)
XLA Modules:
  0.0 367.4 jit_solution(6227605222141121556)
XLA Ops:
  8.4 18.1 %reduce-window.6 = s32[64,16,128]{2,1,0:T(8,128)S(1)} reduce-window(s32[64,16,128]{2,1,0:T(8,128)S(1)} %fusion.177, s32[]{:T(128)} %constant.103.clone.1), window={size=1x1x128 pad=0_0x0_0x127_0}, to_apply=%region_1.2 | reduce-window | flops 16646144 | bytes 1048580 | tf_op jit(solution)/shard_map/reduce-window
  28.1 8.1 %scatter_custom_fusion = s32[4096]{0:T(1024)S(1)} fusion(s32[2048]{0:T(1024)S(1)} %bitcast.63, s32[2048]{0:T(1024)S(1)} %get-tuple-element.23, s32[]{:T(128)} %constant.101.clone.1), kind=kCustom, calls=%fused_computation.373 | custom fusion | bytes 16388 | tf_op jit(solution)/shard_map/scatter | solution.py:78
  36.8 11.6 %all-to-all-start = ((s32[64,1,64]{2,1,0:T(1,128)}), s32[64,1,64]{2,1,0:T(1,128)S(1)}, u32[]{:S(2)}, u32[]{:S(2)}) async-start(s32[64,1,64]{2,1,0:T(1,128)} %all_to_all.9), calls=%async_computation | async-start | bytes 65536 | tf_op jit(solution)/shard_map/all_to_all | solution.py:80
  49.2 7.8 %scatter_custom_fusion.1 = f32[4096,128]{1,0:T(8,128)} fusion(s32[2048]{0:T(1024)S(1)} %bitcast.64, s32[]{:T(128)} %constant.103.clone.1, s32[]{:T(128)S(6)} %select_n.152, f32[2048,128]{1,0:T(8,128)S(1)} %reshape.426, f32[]{:T(128)} %constant.134, f32[]{:T(128)} %constant.100.clone.1), kind=kCustom, calls=%fused_computation.184 | custom fusion | flops 262144 | bytes 3145744 | tf_op jit(solution)/shard_map/scatter | solution.py:92
  57.0 10.6 %all-to-all-start.1 = ((f32[64,64,128]{2,1,0:T(8,128)}), f32[64,64,128]{2,1,0:T(8,128)}, u32[]{:S(2)}, u32[]{:S(2)}) async-start(f32[64,64,128]{2,1,0:T(8,128)} %bitcast.11), calls=%async_computation.1 | async-start | bytes 4194304 | tf_op jit(solution)/shard_map/all_to_all | solution.py:51
  69.8 3.5 collective-permute-start.1
  76.2 5.9 %collective-permute-done = f32[3,128,256]{2,1,0:T(8,128)S(1)} collective-permute-done((f32[3,128,256]{2,1,0:T(8,128)S(1)}, f32[3,128,256]{2,1,0:T(8,128)S(1)}, u32[]{:S(2)}, u32[]{:S(2)}) %collective-permute-start) | collective-permute-done | bytes 393248 | tf_op jit(solution)/shard_map/ppermute | solution.py:18
  82.4 4.7 %fusion.165 = f32[8,128,256]{2,1,0:T(8,128)S(1)} fusion(f32[11,128,256]{2,1,0:T(8,128)S(1)} %constant_dynamic-update-slice_fusion.2, f32[11,128,256]{2,1,0:T(8,128)S(1)} %get-tuple-element.19, f32[8,128,256]{2,1,0:T(8,128)S(1)} %copy-done, f32[]{:T(128)} %bitcast.20, f32[]{:T(128)} %bitcast.19, f32[]{:T(128)} %bitcast.18, f32[]{:T(128)} %bitcast.17, ...), kind=kLoop, calls=%fused_computation.264 | loop fusion | flops 3407872 | bytes 8388636 | tf_op jit(solution)/shard_map/add | solution.py:29
  87.2 3.9 %collective-permute-start.2 = (f32[8,3,256]{2,1,0:T(4,128)S(1)}, f32[8,3,256]{2,1,0:T(4,128)S(1)}, u32[]{:S(2)}, u32[]{:S(2)}) collective-permute-start(f32[8,3,256]{2,1,0:T(4,128)S(1)} %get-tuple-element.17), channel_id=1, source_target_pairs={{0,32},{32,64},{64,96},{96,128},{128,160},{160,192},{192,224},{1,3... | collective-permute-start | bytes 73736 | tf_op jit(solution)/shard_map/ppermute | solution.py:18
  93.1 20.6 %collective-permute-done.2 = f32[8,3,256]{2,1,0:T(4,128)S(1)} collective-permute-done((f32[8,3,256]{2,1,0:T(4,128)S(1)}, f32[8,3,256]{2,1,0:T(4,128)S(1)}, u32[]{:S(2)}, u32[]{:S(2)}) %collective-permute-start.2) | collective-permute-done | bytes 24608 | tf_op jit(solution)/shard_map/ppermute | solution.py:18
  114.1 5.4 %fusion.45 = f32[8,128,256]{2,1,0:T(8,128)S(1)} fusion(f32[8,128,256]{2,1,0:T(8,128)S(1)} %fusion.165, f32[8,3,256]{2,1,0:T(4,128)S(1)} %collective-permute-done.3, f32[8,3,256]{2,1,0:T(4,128)S(1)} %collective-permute-done.2, f32[]{:T(128)} %bitcast.25, f32[]{:T(128)} %bitcast.24, f32[]{:T(128)} %bitcast.23, f32[]{:T(128)} %bitcast.22, f32[]{:T(128)} %bitcast.21, ...), kind=kLoop, calls=%fused_computation.130 | loop fusion | flops 4980736 | bytes 2146332 | tf_op jit(solution)/shard_map/add | solution.py:29
  119.5 11.9 %scatter_custom_fusion.2 = f32[2048,128]{1,0:T(8,128)} fusion(s32[4096]{0:T(1024)S(1)} %bitcast.62, f32[4096,128]{1,0:T(8,128)} %bitcast.12, f32[]{:T(128)} %constant.100.clone.1), kind=kCustom, calls=%fused_computation.284 | custom fusion | bytes 1049088 | tf_op jit(solution)/shard_map/scatter | solution.py:98
  132.9 6.0 %fusion.108 = f32[8,128,256]{2,1,0:T(8,128)S(1)} fusion(f32[8,128,256]{2,1,0:T(8,128)S(1)} %reshape.429, f32[8,128,256]{2,1,0:T(8,128)S(1)} %fusion.45, f32[]{:T(128)} %bitcast.30, f32[]{:T(128)} %bitcast.29, f32[]{:T(128)} %bitcast.28, f32[]{:T(128)} %bitcast.27, f32[]{:T(128)} %bitcast.26, f32[]{:T(128)} %bitcast.13, f32[]{:T(128)} %bitcast), kind=kLoop, calls=%fused_computation.192 | loop fusion | flops 3670016 | bytes 3145756 | tf_op jit(solution)/shard_map/div | solution.py:101
  141.0 3.6 collective-permute-start.5
  144.6 3.5 collective-permute-done.4
  149.9 4.7 %fusion.87 = f32[8,128,256]{2,1,0:T(8,128)S(1)} fusion(f32[8,128,256]{2,1,0:T(8,128)S(1)} %fusion.108, f32[3,128,256]{2,1,0:T(8,128)S(1)} %collective-permute-done.5, f32[3,128,256]{2,1,0:T(8,128)S(1)} %collective-permute-done.4, f32[]{:T(128)} %bitcast.20, f32[]{:T(128)} %bitcast.19, f32[]{:T(128)} %bitcast.18, f32[]{:T(128)} %bitcast.17, f32[]{:T(128)} %bitcast.16, ...), kind=kLoop, calls=%fused_computation.172 | loop fusion | flops 4980736 | bytes 2883612 | tf_op jit(solution)/shard_map/add | solution.py:29
  154.6 3.8 %collective-permute-start.6 = (f32[8,3,256]{2,1,0:T(4,128)S(1)}, f32[8,3,256]{2,1,0:T(4,128)S(1)}, u32[]{:S(2)}, u32[]{:S(2)}) collective-permute-start(f32[8,3,256]{2,1,0:T(4,128)S(1)} %get-tuple-element.13), channel_id=1, source_target_pairs={{0,32},{32,64},{64,96},{96,128},{128,160},{160,192},{192,224},{1,3... | collective-permute-start | bytes 73736 | tf_op jit(solution)/shard_map/ppermute | solution.py:18
  160.5 5.4 %collective-permute-done.7 = f32[8,3,256]{2,1,0:T(4,128)S(1)} collective-permute-done((f32[8,3,256]{2,1,0:T(4,128)S(1)}, f32[8,3,256]{2,1,0:T(4,128)S(1)}, u32[]{:S(2)}, u32[]{:S(2)}) %collective-permute-start.7) | collective-permute-done | bytes 24608 | tf_op jit(solution)/shard_map/ppermute | solution.py:19
  165.8 5.4 %fusion.31 = f32[8,128,256]{2,1,0:T(8,128)S(1)} fusion(f32[8,128,256]{2,1,0:T(8,128)S(1)} %fusion.87, f32[8,3,256]{2,1,0:T(4,128)S(1)} %collective-permute-done.7, f32[8,3,256]{2,1,0:T(4,128)S(1)} %collective-permute-done.6, f32[]{:T(128)} %bitcast.25, f32[]{:T(128)} %bitcast.24, f32[]{:T(128)} %bitcast.23, f32[]{:T(128)} %bitcast.22, f32[]{:T(128)} %bitcast.21, ...), kind=kLoop, calls=%fused_computation.116 | loop fusion | flops 4980736 | bytes 2146332 | tf_op jit(solution)/shard_map/add | solution.py:29
  171.2 7.0 %fusion.120 = f32[8,128,256]{2,1,0:T(8,128)} fusion(f32[8,128,256]{2,1,0:T(8,128)S(1)} %fusion.31, f32[]{:T(128)} %bitcast.30, f32[]{:T(128)} %bitcast.29, f32[]{:T(128)} %bitcast.28, f32[]{:T(128)} %bitcast.27, f32[]{:T(128)} %bitcast.26, f32[]{:T(128)} %bitcast.13, f32[]{:T(128)} %bitcast), kind=kLoop, calls=%fused_computation.204 | loop fusion | flops 3407872 | bytes 2097180 | tf_op jit(solution)/shard_map/add | solution.py:29
  178.3 51.2 %all-reduce.7.cloned.1.call-done = f32[8,128,256]{2,1,0:T(8,128)} async-done(((f32[8,128,256]{2,1,0:T(8,128)}), f32[8,128,256]{2,1,0:T(8,128)}) %all-reduce.7.cloned.1.call-update) | async-done | bytes 1048592 | tf_op jit(solution)/shard_map/psum | solution.py:103
  233.6 3.6 collective-permute-start.9
  242.5 5.8 %fusion.73 = f32[8,128,256]{2,1,0:T(8,128)S(1)} fusion(f32[8,128,256]{2,1,0:T(8,128)S(1)} %broadcast_multiply_fusion, f32[3,128,256]{2,1,0:T(8,128)} %collective-permute-done.9, f32[3,128,256]{2,1,0:T(8,128)} %collective-permute-done.8, f32[]{:T(128)S(6)} %mul.515, f32[]{:T(128)} %bitcast.20, f32[]{:T(128)} %bitcast.19, f32[]{:T(128)} %bitcast.17, ...), kind=kLoop, calls=%fused_computation.158 | loop fusion | flops 5242880 | bytes 4980764 | tf_op jit(solution)/shard_map/add | solution.py:29
  257.6 5.4 %fusion.17 = f32[8,128,256]{2,1,0:T(8,128)S(1)} fusion(f32[8,128,256]{2,1,0:T(8,128)S(1)} %fusion.73, f32[8,3,256]{2,1,0:T(4,128)S(1)} %collective-permute-done.11, f32[8,3,256]{2,1,0:T(4,128)S(1)} %collective-permute-done.10, f32[]{:T(128)} %bitcast.25, f32[]{:T(128)} %bitcast.24, f32[]{:T(128)} %bitcast.23, f32[]{:T(128)} %bitcast.22, f32[]{:T(128)} %bitcast.21, ...), kind=kLoop, calls=%fused_computation.102 | loop fusion | flops 4980736 | bytes 2146332 | tf_op jit(solution)/shard_map/add | solution.py:29
  263.0 6.0 %fusion.133 = f32[8,128,256]{2,1,0:T(8,128)S(1)} fusion(f32[8,128,256]{2,1,0:T(8,128)S(1)} %reshape.429, f32[8,128,256]{2,1,0:T(8,128)S(1)} %fusion.17, f32[]{:T(128)} %bitcast.30, f32[]{:T(128)} %bitcast.29, f32[]{:T(128)} %bitcast.28, f32[]{:T(128)} %bitcast.27, f32[]{:T(128)} %bitcast.26, f32[]{:T(128)} %bitcast.13, f32[]{:T(128)} %bitcast), kind=kLoop, calls=%fused_computation.217 | loop fusion | flops 3670016 | bytes 3145756 | tf_op jit(solution)/shard_map/div | solution.py:101
  274.7 3.5 collective-permute-done.12
  280.0 4.7 %fusion.59 = f32[8,128,256]{2,1,0:T(8,128)S(1)} fusion(f32[8,128,256]{2,1,0:T(8,128)S(1)} %fusion.133, f32[3,128,256]{2,1,0:T(8,128)S(1)} %collective-permute-done.13, f32[3,128,256]{2,1,0:T(8,128)S(1)} %collective-permute-done.12, f32[]{:T(128)} %bitcast.20, f32[]{:T(128)} %bitcast.19, f32[]{:T(128)} %bitcast.18, f32[]{:T(128)} %bitcast.17, f32[]{:T(128)} %bitcast.16, ...), kind=kLoop, calls=%fused_computation.144 | loop fusion | flops 4980736 | bytes 2883612 | tf_op jit(solution)/shard_map/add | solution.py:29
  284.7 4.2 %collective-permute-start.14 = (f32[8,3,256]{2,1,0:T(4,128)S(1)}, f32[8,3,256]{2,1,0:T(4,128)S(1)}, u32[]{:S(2)}, u32[]{:S(2)}) collective-permute-start(f32[8,3,256]{2,1,0:T(4,128)S(1)} %get-tuple-element.5), channel_id=1, source_target_pairs={{0,32},{32,64},{64,96},{96,128},{128,160},{160,192},{192,224},{1,3... | collective-permute-start | bytes 73736 | tf_op jit(solution)/shard_map/ppermute | solution.py:18
  291.1 4.9 %collective-permute-done.15 = f32[8,3,256]{2,1,0:T(4,128)S(1)} collective-permute-done((f32[8,3,256]{2,1,0:T(4,128)S(1)}, f32[8,3,256]{2,1,0:T(4,128)S(1)}, u32[]{:S(2)}, u32[]{:S(2)}) %collective-permute-start.15) | collective-permute-done | bytes 24608 | tf_op jit(solution)/shard_map/ppermute | solution.py:19
  295.9 5.4 %fusion.3 = f32[8,128,256]{2,1,0:T(8,128)S(1)} fusion(f32[8,128,256]{2,1,0:T(8,128)S(1)} %fusion.59, f32[8,3,256]{2,1,0:T(4,128)S(1)} %collective-permute-done.15, f32[8,3,256]{2,1,0:T(4,128)S(1)} %collective-permute-done.14, f32[]{:T(128)} %bitcast.25, f32[]{:T(128)} %bitcast.24, f32[]{:T(128)} %bitcast.23, f32[]{:T(128)} %bitcast.22, f32[]{:T(128)} %bitcast.21, ...), kind=kLoop, calls=%fused_computation.88 | loop fusion | flops 4980736 | bytes 2146332 | tf_op jit(solution)/shard_map/add | solution.py:29
  301.3 7.0 %fusion.145 = f32[8,128,256]{2,1,0:T(8,128)} fusion(f32[8,128,256]{2,1,0:T(8,128)S(1)} %fusion.3, f32[]{:T(128)} %bitcast.30, f32[]{:T(128)} %bitcast.29, f32[]{:T(128)} %bitcast.28, f32[]{:T(128)} %bitcast.27, f32[]{:T(128)} %bitcast.26, f32[]{:T(128)} %bitcast.13, f32[]{:T(128)} %bitcast), kind=kLoop, calls=%fused_computation.229 | loop fusion | flops 3407872 | bytes 2097180 | tf_op jit(solution)/shard_map/add | solution.py:29
  308.3 49.9 %all-reduce.9.cloned.1.call-done = f32[8,128,256]{2,1,0:T(8,128)} async-done(((f32[8,128,256]{2,1,0:T(8,128)}), f32[8,128,256]{2,1,0:T(8,128)}) %all-reduce.9.cloned.1.call-update) | async-done | bytes 1048592 | tf_op jit(solution)/shard_map/psum | solution.py:103
  (69 shorter events, 49.0 us)
Async XLA Ops:
  26.7 22.3 %copy-start.1 = (f32[1,8,128,256]{3,2,1,0:T(8,128)S(1)}, f32[1,8,128,256]{3,2,1,0:T(8,128)}, u32[]{:S(2)}) copy-start(f32[1,8,128,256]{3,2,1,0:T(8,128)} %param.6) | copy-start | bytes 3145732
  36.8 20.1 %all-to-all-start = ((s32[64,1,64]{2,1,0:T(1,128)}), s32[64,1,64]{2,1,0:T(1,128)S(1)}, u32[]{:S(2)}, u32[]{:S(2)}) async-start(s32[64,1,64]{2,1,0:T(1,128)} %all_to_all.9), calls=%async_computation | async-start | bytes 65536 | tf_op jit(solution)/shard_map/all_to_all | solution.py:80
  57.0 10.7 %copy-start = (f32[8,128,256]{2,1,0:T(8,128)S(1)}, f32[8,128,256]{2,1,0:T(8,128)}, u32[]{:S(2)}) copy-start(f32[8,128,256]{2,1,0:T(8,128)} %param.5) | copy-start | bytes 3145732
  57.0 62.5 %all-to-all-start.1 = ((f32[64,64,128]{2,1,0:T(8,128)}), f32[64,64,128]{2,1,0:T(8,128)}, u32[]{:S(2)}, u32[]{:S(2)}) async-start(f32[64,64,128]{2,1,0:T(8,128)} %bitcast.11), calls=%async_computation.1 | async-start | bytes 4194304 | tf_op jit(solution)/shard_map/all_to_all | solution.py:51
  67.6 5.7 %copy-start.2 = (f32[1,3,7]{2,0,1:T(1,128)S(1)}, f32[1,3,7]{2,0,1:T(1,128)}, u32[]{:S(2)}) copy-start(f32[1,3,7]{2,0,1:T(1,128)} %param.8) | copy-start | bytes 256
  67.6 161.9 %all-reduce.7.cloned.1.call-start = ((), (), s32[]{:S(2)}) async-start(), calls=%async_computation.2 | async-start | bytes 2097152 | tf_op jit(solution)/shard_map/psum | solution.py:103
  67.8 14.4 %collective-permute-start = (f32[3,128,256]{2,1,0:T(8,128)S(1)}, f32[3,128,256]{2,1,0:T(8,128)S(1)}, u32[]{:S(2)}, u32[]{:S(2)}) collective-permute-start(f32[3,128,256]{2,1,0:T(8,128)S(1)} %get-tuple-element.21), channel_id=1, source_target_pairs={{0,1},{1,2},{2,3},{3,4},{4,5},{5,6},{6,7},{8,9},{9,10},{10,11},{11... | collective-permute-start | bytes 1179656 | tf_op jit(solution)/shard_map/ppermute | solution.py:18
  69.8 12.6 %collective-permute-start.1 = (f32[3,128,256]{2,1,0:T(8,128)S(1)}, f32[3,128,256]{2,1,0:T(8,128)S(1)}, u32[]{:S(2)}, u32[]{:S(2)}) collective-permute-start(f32[3,128,256]{2,1,0:T(8,128)S(1)} %get-tuple-element.22), channel_id=1, source_target_pairs={{1,0},{2,1},{3,2},{4,3},{5,4},{6,5},{7,6},{9,8},{10,9},{11,10},{12... | collective-permute-start | bytes 1179656 | tf_op jit(solution)/shard_map/ppermute | solution.py:19
  87.2 26.5 %collective-permute-start.2 = (f32[8,3,256]{2,1,0:T(4,128)S(1)}, f32[8,3,256]{2,1,0:T(4,128)S(1)}, u32[]{:S(2)}, u32[]{:S(2)}) collective-permute-start(f32[8,3,256]{2,1,0:T(4,128)S(1)} %get-tuple-element.17), channel_id=1, source_target_pairs={{0,32},{32,64},{64,96},{96,128},{128,160},{160,192},{192,224},{1,3... | collective-permute-start | bytes 73736 | tf_op jit(solution)/shard_map/ppermute | solution.py:18
  91.1 23.0 %collective-permute-start.3 = (f32[8,3,256]{2,1,0:T(4,128)S(1)}, f32[8,3,256]{2,1,0:T(4,128)S(1)}, u32[]{:S(2)}, u32[]{:S(2)}) collective-permute-start(f32[8,3,256]{2,1,0:T(4,128)S(1)} %get-tuple-element.18), channel_id=1, source_target_pairs={{32,0},{64,32},{96,64},{128,96},{160,128},{192,160},{224,192},{33,... | collective-permute-start | bytes 73736 | tf_op jit(solution)/shard_map/ppermute | solution.py:19
  139.0 9.1 %collective-permute-start.4 = (f32[3,128,256]{2,1,0:T(8,128)S(1)}, f32[3,128,256]{2,1,0:T(8,128)S(1)}, u32[]{:S(2)}, u32[]{:S(2)}) collective-permute-start(f32[3,128,256]{2,1,0:T(8,128)S(1)} %get-tuple-element.15), channel_id=1, source_target_pairs={{0,1},{1,2},{2,3},{3,4},{4,5},{5,6},{6,7},{8,9},{9,10},{10,11},{11... | collective-permute-start | bytes 1179656 | tf_op jit(solution)/shard_map/ppermute | solution.py:18
  141.0 8.9 %collective-permute-start.5 = (f32[3,128,256]{2,1,0:T(8,128)S(1)}, f32[3,128,256]{2,1,0:T(8,128)S(1)}, u32[]{:S(2)}, u32[]{:S(2)}) collective-permute-start(f32[3,128,256]{2,1,0:T(8,128)S(1)} %get-tuple-element.16), channel_id=1, source_target_pairs={{1,0},{2,1},{3,2},{4,3},{5,4},{6,5},{7,6},{9,8},{10,9},{11,10},{12... | collective-permute-start | bytes 1179656 | tf_op jit(solution)/shard_map/ppermute | solution.py:19
  154.6 5.9 %collective-permute-start.6 = (f32[8,3,256]{2,1,0:T(4,128)S(1)}, f32[8,3,256]{2,1,0:T(4,128)S(1)}, u32[]{:S(2)}, u32[]{:S(2)}) collective-permute-start(f32[8,3,256]{2,1,0:T(4,128)S(1)} %get-tuple-element.13), channel_id=1, source_target_pairs={{0,32},{32,64},{64,96},{96,128},{128,160},{160,192},{192,224},{1,3... | collective-permute-start | bytes 73736 | tf_op jit(solution)/shard_map/ppermute | solution.py:18
  158.4 7.5 %collective-permute-start.7 = (f32[8,3,256]{2,1,0:T(4,128)S(1)}, f32[8,3,256]{2,1,0:T(4,128)S(1)}, u32[]{:S(2)}, u32[]{:S(2)}) collective-permute-start(f32[8,3,256]{2,1,0:T(4,128)S(1)} %get-tuple-element.14), channel_id=1, source_target_pairs={{32,0},{64,32},{96,64},{128,96},{160,128},{192,160},{224,192},{33,... | collective-permute-start | bytes 73736 | tf_op jit(solution)/shard_map/ppermute | solution.py:19
  178.2 180.0 %all-reduce.9.cloned.1.call-start = ((), (), s32[]{:S(2)}) async-start(), calls=%async_computation.3 | async-start | bytes 2097152 | tf_op jit(solution)/shard_map/psum | solution.py:103
  231.7 9.4 %collective-permute-start.8 = (f32[3,128,256]{2,1,0:T(8,128)}, f32[3,128,256]{2,1,0:T(8,128)}, u32[]{:S(2)}, u32[]{:S(2)}) collective-permute-start(f32[3,128,256]{2,1,0:T(8,128)} %get-tuple-element.11), channel_id=1, source_target_pairs={{0,1},{1,2},{2,3},{3,4},{4,5},{5,6},{6,7},{8,9},{9,10},{10,11},{11... | collective-permute-start | bytes 1179656 | tf_op jit(solution)/shard_map/ppermute | solution.py:18
  233.6 8.9 %collective-permute-start.9 = (f32[3,128,256]{2,1,0:T(8,128)S(1)}, f32[3,128,256]{2,1,0:T(8,128)}, u32[]{:S(2)}, u32[]{:S(2)}) collective-permute-start(f32[3,128,256]{2,1,0:T(8,128)S(1)} %get-tuple-element.12), channel_id=1, source_target_pairs={{1,0},{2,1},{3,2},{4,3},{5,4},{6,5},{7,6},{9,8},{10,9},{11,10},{12... | collective-permute-start | bytes 1179656 | tf_op jit(solution)/shard_map/ppermute | solution.py:19
  248.3 5.9 %collective-permute-start.10 = (f32[8,3,256]{2,1,0:T(4,128)S(1)}, f32[8,3,256]{2,1,0:T(4,128)S(1)}, u32[]{:S(2)}, u32[]{:S(2)}) collective-permute-start(f32[8,3,256]{2,1,0:T(4,128)S(1)} %get-tuple-element.9), channel_id=1, source_target_pairs={{0,32},{32,64},{64,96},{96,128},{128,160},{160,192},{192,224},{1,3... | collective-permute-start | bytes 73736 | tf_op jit(solution)/shard_map/ppermute | solution.py:18
  251.8 5.8 %collective-permute-start.11 = (f32[8,3,256]{2,1,0:T(4,128)S(1)}, f32[8,3,256]{2,1,0:T(4,128)S(1)}, u32[]{:S(2)}, u32[]{:S(2)}) collective-permute-start(f32[8,3,256]{2,1,0:T(4,128)S(1)} %get-tuple-element.10), channel_id=1, source_target_pairs={{32,0},{64,32},{96,64},{128,96},{160,128},{192,160},{224,192},{33,... | collective-permute-start | bytes 73736 | tf_op jit(solution)/shard_map/ppermute | solution.py:19
  269.1 9.1 %collective-permute-start.12 = (f32[3,128,256]{2,1,0:T(8,128)S(1)}, f32[3,128,256]{2,1,0:T(8,128)S(1)}, u32[]{:S(2)}, u32[]{:S(2)}) collective-permute-start(f32[3,128,256]{2,1,0:T(8,128)S(1)} %get-tuple-element.7), channel_id=1, source_target_pairs={{0,1},{1,2},{2,3},{3,4},{4,5},{5,6},{6,7},{8,9},{9,10},{10,11},{11... | collective-permute-start | bytes 1179656 | tf_op jit(solution)/shard_map/ppermute | solution.py:18
  271.4 8.5 %collective-permute-start.13 = (f32[3,128,256]{2,1,0:T(8,128)S(1)}, f32[3,128,256]{2,1,0:T(8,128)S(1)}, u32[]{:S(2)}, u32[]{:S(2)}) collective-permute-start(f32[3,128,256]{2,1,0:T(8,128)S(1)} %get-tuple-element.8), channel_id=1, source_target_pairs={{1,0},{2,1},{3,2},{4,3},{5,4},{6,5},{7,6},{9,8},{10,9},{11,10},{12... | collective-permute-start | bytes 1179656 | tf_op jit(solution)/shard_map/ppermute | solution.py:19
  284.7 6.4 %collective-permute-start.14 = (f32[8,3,256]{2,1,0:T(4,128)S(1)}, f32[8,3,256]{2,1,0:T(4,128)S(1)}, u32[]{:S(2)}, u32[]{:S(2)}) collective-permute-start(f32[8,3,256]{2,1,0:T(4,128)S(1)} %get-tuple-element.5), channel_id=1, source_target_pairs={{0,32},{32,64},{64,96},{96,128},{128,160},{160,192},{192,224},{1,3... | collective-permute-start | bytes 73736 | tf_op jit(solution)/shard_map/ppermute | solution.py:18
  288.9 7.0 %collective-permute-start.15 = (f32[8,3,256]{2,1,0:T(4,128)S(1)}, f32[8,3,256]{2,1,0:T(4,128)S(1)}, u32[]{:S(2)}, u32[]{:S(2)}) collective-permute-start(f32[8,3,256]{2,1,0:T(4,128)S(1)} %get-tuple-element.6), channel_id=1, source_target_pairs={{32,0},{64,32},{96,64},{128,96},{160,128},{192,160},{224,192},{33,... | collective-permute-start | bytes 73736 | tf_op jit(solution)/shard_map/ppermute | solution.py:19
Sparse Core Ops, SparseCore 0:
  178.4 51.0 all-reduce.6
  308.4 49.7 all-reduce.8

commit v2 on v1

v2 whole, which is shorter than its diff:
```python
import functools
import jax
import jax.numpy as jnp
from jax import lax
from jax.experimental import pallas as pl
from jax.experimental.pallas import tpu as pltpu
from jax.sharding import PartitionSpec as P

VMEM = pltpu.VMEM
BRICK = 128
HALO = 3
ITERS = 2
UNROLL = 8


def with_halo(value, sides, width):
    for axis, dim in sides:
        count, length = (lax.axis_size(axis), value.shape[dim])
        up = [(i, (i + 1) % count) for i in range(count - 1)]
        down = [(j, i) for i, j in up]
        last = lax.slice_in_dim(value, length - width, length, axis=dim)
        leading = lax.slice_in_dim(value, 0, width, axis=dim)
        before = lax.ppermute(last, axis, up)
        after = lax.ppermute(leading, axis, down)
        value = jnp.concatenate([before, value, after], axis=dim)
    return value


def axis_blur(volume, weights, dim_index, length_along):
    result = jnp.zeros(
        volume.shape[:dim_index] + (length_along,) + volume.shape[dim_index + 1 :], jnp.float32
    )
    for offset in range(2 * HALO + 1):
        result = result + weights[offset] * lax.slice_in_dim(
            volume, offset, offset + length_along, axis=dim_index
        )
    return result


def blur_local(volume, weights):
    x_cells, y_cells, z_cells = volume.shape
    extended = with_halo(volume, (("rows", 0),), HALO)
    result = axis_blur(extended, weights[0], 0, x_cells)
    widened = with_halo(result, (("blocks", 1),), HALO)
    result = axis_blur(widened, weights[1], 1, y_cells)
    padded = jnp.pad(result, ((0, 0), (0, 0), (HALO, HALO)))
    return axis_blur(padded, weights[2], 2, z_cells)


def lane_sum(x):
    return jnp.sum(x, axis=1, keepdims=True)


def pack_kernel(geo, shift_ref, target_ref, views_ref, out_ref, rolled, pos_v, pos_s, sem):
    peers, cap, x_cells, y_cells, brick_cols, row_count, all_cols = geo
    groups = brick_cols * x_cells
    rows_per = cap + 1
    t = target_ref[...]
    bz = t % brick_cols
    column = t // brick_cols % all_cols
    line = t // (brick_cols * all_cols)
    dest = column // y_cells * row_count + line // x_cells
    slot = (bz * x_cells + line % x_cells) * y_cells + column % y_cells + 1
    high, low = slot // 64, slot % 64
    peer_id = lax.broadcasted_iota(jnp.int32, (peers, y_cells), 0)
    before = (
        lax.broadcasted_iota(jnp.int32, (y_cells, y_cells), 0)
        < lax.broadcasted_iota(jnp.int32, (y_cells, y_cells), 1)
    ).astype(jnp.bfloat16)
    kid = lax.broadcasted_iota(jnp.int32, (BRICK, y_cells), 0)
    carry = jnp.zeros((peers, 1), jnp.float32)
    listed = jnp.zeros((2 * peers, BRICK), jnp.float32)
    for g in range(groups):
        d = dest[g : g + 1, :]
        hot = d == peer_id
        hot_f = hot.astype(jnp.float32)
        ahead = jnp.dot(hot_f.astype(jnp.bfloat16), before, preferred_element_type=jnp.float32)
        ranks = jnp.sum(hot_f * (ahead + carry), axis=0, keepdims=True)
        carry = carry + lane_sum(hot_f)
        rank_i = ranks.astype(jnp.int32)
        pos_v[g : g + 1, :] = d * rows_per + rank_i
        h = hot_f * high[g : g + 1, :].astype(jnp.float32)
        l = hot_f * low[g : g + 1, :].astype(jnp.float32)
        both = jnp.concatenate([h, l], axis=0).astype(jnp.bfloat16)
        at = (rank_i == kid).astype(jnp.float32).astype(jnp.bfloat16)
        listed = listed + lax.dot_general(
            both, at, (((1,), (1,)), ((), ())), preferred_element_type=jnp.float32
        )
    copy = pltpu.make_async_copy(pos_v, pos_s, sem)
    copy.start()
    entries = 64.0 * listed[:peers] + listed[peers:]
    for p in range(peers):
        out_ref[p * rows_per + cap] = entries[p : p + 1, :]
    shift = shift_ref[0]
    for bz_i in range(brick_cols):
        for x in range(x_cells):
            rolled[bz_i * x_cells + x] = pltpu.roll(
                views_ref[x, :, bz_i * BRICK : (bz_i + 1) * BRICK], shift, 1
            )
    copy.wait()

    def body(i, c):
        g = i // (y_cells // UNROLL)
        base = i % (y_cells // UNROLL) * UNROLL
        for s in range(UNROLL):
            out_ref[pos_s[g, base + s]] = rolled[g, pl.ds(base + s, 1), :]
        return c

    lax.fori_loop(0, groups * y_cells // UNROLL, body, 0)


def pack(shift, target, views, geo):
    peers, cap, x_cells, y_cells, brick_cols, row_count, all_cols = geo
    groups = brick_cols * x_cells
    return pl.pallas_call(
        functools.partial(pack_kernel, geo),
        out_shape=jax.ShapeDtypeStruct((peers * (cap + 1), 1, BRICK), jnp.float32),
        in_specs=[
            pl.BlockSpec(memory_space=pltpu.SMEM),
            pl.BlockSpec(memory_space=pltpu.VMEM),
            pl.BlockSpec(memory_space=pltpu.VMEM),
        ],
        out_specs=pl.BlockSpec(memory_space=pltpu.VMEM),
        scratch_shapes=[
            pltpu.VMEM((groups, y_cells, BRICK), jnp.float32),
            pltpu.VMEM((groups, y_cells), jnp.int32),
            pltpu.SMEM((groups, y_cells), jnp.int32),
            pltpu.SemaphoreType.DMA,
        ],
        name="pack",
    )(shift, target, views)


def unpack_kernel(peers, cap, slots, in_ref, out_ref, list_v, idx_v, idx_s, sem):
    rows_per = cap + 1
    for p in range(peers):
        list_v[p : p + 1, :] = in_ref[p * rows_per + cap]
    e = list_v[...].astype(jnp.int32)
    count = jnp.sum((e > 0).astype(jnp.int32), axis=1, keepdims=True)
    idx_v[...] = jnp.where(
        lax.broadcasted_iota(jnp.int32, (peers, BRICK), 1) == cap,
        count,
        jnp.where(e > 0, e - 1, slots),
    )
    copy = pltpu.make_async_copy(idx_v, idx_s, sem)
    copy.start()
    copy.wait()

    def per_peer(p, c):
        def body(i, c):
            for s in range(UNROLL):
                k = i * UNROLL + s
                out_ref[pl.ds(idx_s[p, k], 1), :] = in_ref[p * rows_per + k]
            return c

        lax.fori_loop(0, (idx_s[p, cap] + UNROLL - 1) // UNROLL, body, 0)
        return c

    lax.fori_loop(0, peers, per_peer, 0)


def unpack(arrived, peers, cap, slots):
    return pl.pallas_call(
        functools.partial(unpack_kernel, peers, cap, slots),
        out_shape=jax.ShapeDtypeStruct((slots + UNROLL, BRICK), jnp.float32),
        in_specs=[pl.BlockSpec(memory_space=pltpu.VMEM)],
        out_specs=pl.BlockSpec(memory_space=pltpu.VMEM),
        scratch_shapes=[
            pltpu.VMEM((peers, BRICK), jnp.float32),
            pltpu.VMEM((peers, BRICK), jnp.int32),
            pltpu.SMEM((peers, BRICK), jnp.int32),
            pltpu.SemaphoreType.DMA,
        ],
        name="unpack",
    )(arrived)


def per_device(estimate, views_data, target, psf_taps, shifts):
    x_cells, y_cells, z_cells = estimate.shape
    row_count = lax.axis_size("rows")
    block_count = lax.axis_size("blocks")
    peer_count = block_count * row_count
    view_count = lax.axis_size("views")
    brick_cols = z_cells // BRICK
    brick_count = x_cells * y_cells * brick_cols
    capacity = 2 * brick_count // peer_count
    geo = (peer_count, capacity, x_cells, y_cells, brick_cols, row_count, y_cells * block_count)
    targets = target[0].transpose(2, 0, 1).reshape(brick_cols * x_cells, y_cells)
    outgoing = pack(shifts, targets, views_data[0], geo)
    arrived = lax.all_to_all(
        outgoing.reshape(peer_count, capacity + 1, 1, BRICK),
        ("blocks", "rows"), split_axis=0, concat_axis=0, tiled=True,
    ).reshape(peer_count * (capacity + 1), 1, BRICK)
    moved = unpack(arrived, peer_count, capacity, brick_count)[:brick_count]
    moved = (
        moved.reshape(brick_cols, x_cells, y_cells, BRICK)
        .transpose(1, 2, 0, 3)
        .reshape(x_cells, y_cells, z_cells)
    )
    weights = psf_taps[0] / jnp.sum(psf_taps[0], axis=1, keepdims=True)
    flipped = weights[:, ::-1]
    for iteration in range(ITERS):
        placed = moved / blur_local(estimate, weights)
        projected = blur_local(placed, flipped)
        combined = lax.psum(projected, "views")
        estimate = estimate * combined / view_count
    return estimate


def solution(mesh):
    placed = (
        P("rows", "blocks", None),
        P("views", "rows", "blocks", None),
        P("views", "rows", "blocks", None),
        P("views", None, None),
        P("views"),
    )
    return jax.shard_map(
        per_device, mesh=mesh, in_specs=placed, out_specs=P("rows", "blocks", None), check_vma=False
    )
```

time: 369 us -> 336 us (0.911)
  other arithmetic: 98.9 us -> 72.4 us
  Pallas kernels: 0 us -> 22.3 us
  local copies, waits for them, and re-layouts: 28 us -> 9.94 us
  starting transfers between devices: 68.4 us -> 57.9 us
    pallas_call x0 -> x2, Pallas kernels: none -> 22.3 us  [the longest x1 11.3 us: pack(): pl.pallas_call(functools.partial(pack_kernel, geo), out_shape=jax.ShapeDt...]
    scatter x2 -> x0, local copies, waits for them, and re-layouts: 20 us -> none  [the longest x1 11.9 us: per_device(): moved = jnp.zeros((brick_count, BRICK), jnp.float32).at[wanted].set(arriv...]
    another operation x3 -> x0, other arithmetic: 18.5 us -> none
    all_to_all x2 -> x1, starting transfers between devices: 22.2 us -> 11.7 us  [per_device(): lax.all_to_all(outgoing.reshape(peer_count, capacity + 1, 1, BRICK), ('bl...]
    scatter x1 -> x0, other arithmetic: 7.82 us -> none  [per_device(): jnp.zeros((peer_count * capacity, BRICK), jnp.float32).at[position]]
  transfers between devices with their start and end apart: 20 -> 19, of which waited for: 14 -> 14; matrix products, arithmetic and copies ran while one was open for 6% -> 5% of each run, Pallas kernels for 0% -> 0%
where the time goes in v2:
time: 336 us; the launch traced here: 334 us
  waiting for transfers between devices  157 us (47%)
  other arithmetic  72.4 us (22%)
  starting transfers between devices  57.9 us (17%)
  Pallas kernels  22.3 us (7%)
  between operations  15 us (4%)
  local copies, waits for them, and re-layouts  9.94 us (3%)
    psum x2, waiting for transfers between devices, per_device(): combined = lax.psum(projected, 'views')  101 us
    add x10, other arithmetic, axis_blur(): result + weights[offset] * lax.slice_in_dim(volume, offset, offset + leng...  56.4 us
    ppermute x8, waiting for transfers between devices, with_halo(): before = lax.ppermute(last, axis, up)  36 us
    ppermute x8, starting transfers between devices, with_halo(): before = lax.ppermute(last, axis, up)  23.3 us
    ppermute x8, starting transfers between devices, with_halo(): after = lax.ppermute(leading, axis, down)  22.7 us
    ppermute x8, waiting for transfers between devices, with_halo(): after = lax.ppermute(leading, axis, down)  19.4 us
    div x2, other arithmetic, per_device(): placed = moved / blur_local(estimate, weights)  12.1 us
    all_to_all x1, starting transfers between devices, per_device(): lax.all_to_all(outgoing.reshape(peer_count, capacity + 1, 1, BRICK), ('bl...  11.7 us
  transfers between devices with their start and end apart: 19, of which 14 were waited for; matrix products, arithmetic and copies ran while one was open for 5% of the time, Pallas kernels for 0%

profile of v2, /device:TPU:34, one launch (start us, length us, event | category | flops | bytes accessed | tf_op | source)
XLA Modules:
  0.0 334.2 jit_solution(2469238417231528388)
XLA Ops:
  8.5 11.3 %pack.1 = f32[4160,1,128]{2,1,0:T(1,128)} custom-call(s32[1]{0:T(128)S(6)} %copy.19.shift_ref, s32[16,128]{1,0:T(8,128)} %bitcast.44, f32[8,128,256]{2,1,0:T(8,128)} %bitcast.43), custom_call_target="tpu_custom_call" | custom-call | tf_op jit(solution)/shard_map/pack/pallas_call | solution.py:115
  19.8 11.7 %all-to-all-start = ((f32[64,65,1,128]{3,2,1,0:T(1,128)}), f32[64,65,1,128]{3,2,1,0:T(1,128)S(1)}, u32[]{:S(2)}, u32[]{:S(2)}) async-start(f32[64,65,1,128]{3,2,1,0:T(1,128)} %bitcast.42), calls=%async_computation | async-start | bytes 4259840 | tf_op jit(solution)/shard_map/all_to_all | solution.py:190
  34.6 3.5 %collective-permute-start.1 = (f32[3,128,256]{2,1,0:T(8,128)}, f32[3,128,256]{2,1,0:T(8,128)}, u32[]{:S(2)}, u32[]{:S(2)}) collective-permute-start(f32[3,128,256]{2,1,0:T(8,128)} %get-tuple-element.22), channel_id=1, source_target_pairs={{1,0},{2,1},{3,2},{4,3},{5,4},{6,5},{7,6},{9,8},{10,9},{11,10},{12... | collective-permute-start | bytes 1179656 | tf_op jit(solution)/shard_map/ppermute | solution.py:24
  39.7 6.6 %collective-permute-done = f32[3,128,256]{2,1,0:T(8,128)} collective-permute-done((f32[3,128,256]{2,1,0:T(8,128)}, f32[3,128,256]{2,1,0:T(8,128)}, u32[]{:S(2)}, u32[]{:S(2)}) %collective-permute-start) | collective-permute-done | bytes 393248 | tf_op jit(solution)/shard_map/ppermute | solution.py:23
  48.6 4.9 %fusion.162 = f32[8,128,256]{2,1,0:T(8,128)S(1)} fusion(f32[11,128,256]{2,1,0:T(8,128)S(1)} %constant_dynamic-update-slice_fusion.2, f32[11,128,256]{2,1,0:T(8,128)S(1)} %get-tuple-element.19, f32[8,128,256]{2,1,0:T(8,128)S(1)} %copy-done, f32[]{:T(128)} %bitcast.18, f32[]{:T(128)} %bitcast.17, f32[]{:T(128)} %bitcast.16, f32[]{:T(128)} %bitcast.15, ...), kind=kLoop, calls=%fused_computation.257 | loop fusion | flops 3407872 | bytes 8388636 | tf_op jit(solution)/shard_map/add | solution.py:34
  53.5 3.8 %collective-permute-start.2 = (f32[8,3,256]{2,1,0:T(4,128)S(1)}, f32[8,3,256]{2,1,0:T(4,128)S(1)}, u32[]{:S(2)}, u32[]{:S(2)}) collective-permute-start(f32[8,3,256]{2,1,0:T(4,128)S(1)} %get-tuple-element.17), channel_id=1, source_target_pairs={{0,32},{32,64},{64,96},{96,128},{128,160},{160,192},{192,224},{1,3... | collective-permute-start | bytes 73736 | tf_op jit(solution)/shard_map/ppermute | solution.py:23
  59.4 19.1 %collective-permute-done.2 = f32[8,3,256]{2,1,0:T(4,128)S(1)} collective-permute-done((f32[8,3,256]{2,1,0:T(4,128)S(1)}, f32[8,3,256]{2,1,0:T(4,128)S(1)}, u32[]{:S(2)}, u32[]{:S(2)}) %collective-permute-start.2) | collective-permute-done | bytes 24608 | tf_op jit(solution)/shard_map/ppermute | solution.py:23
  78.9 6.1 %fusion.45 = f32[8,128,256]{2,1,0:T(8,128)} fusion(f32[8,128,256]{2,1,0:T(8,128)S(1)} %fusion.162, f32[8,3,256]{2,1,0:T(4,128)S(1)} %collective-permute-done.3, f32[8,3,256]{2,1,0:T(4,128)S(1)} %collective-permute-done.2, f32[]{:T(128)} %bitcast.23, f32[]{:T(128)} %bitcast.22, f32[]{:T(128)} %bitcast.21, f32[]{:T(128)} %bitcast.20, f32[]{:T(128)} %bitcast.19, ...), kind=kLoop, calls=%fused_computation.125 | loop fusion | flops 4980736 | bytes 2146332 | tf_op jit(solution)/shard_map/add | solution.py:34
  86.4 11.0 %unpack.1 = f32[2056,128]{1,0:T(8,128)} custom-call(f32[4160,1,128]{2,1,0:T(1,128)} %bitcast.41), custom_call_target="tpu_custom_call" | custom-call | tf_op jit(solution)/shard_map/unpack/pallas_call | solution.py:163
  99.0 6.0 %fusion.105 = f32[8,128,256]{2,1,0:T(8,128)S(1)} fusion(f32[8,128,256]{2,1,0:T(8,128)S(1)} %copy-done.2, f32[2,8,16,8,128]{4,3,2,1,0:T(8,128)S(1)} %bitcast.39, f32[]{:T(128)} %bitcast.28, f32[]{:T(128)} %bitcast.27, f32[]{:T(128)} %bitcast.26, f32[]{:T(128)} %bitcast.25, f32[]{:T(128)} %bitcast.24, f32[]{:T(128)} %bitcast.11, f32[]{:T(128)} %bitcast), kind=kLoop, calls=%fused_computation.185 | loop fusion | flops 3670016 | bytes 3145756 | tf_op jit(solution)/shard_map/div | solution.py:203
  107.0 3.6 %collective-permute-start.5 = (f32[3,128,256]{2,1,0:T(8,128)S(1)}, f32[3,128,256]{2,1,0:T(8,128)S(1)}, u32[]{:S(2)}, u32[]{:S(2)}) collective-permute-start(f32[3,128,256]{2,1,0:T(8,128)S(1)} %get-tuple-element.16), channel_id=1, source_target_pairs={{1,0},{2,1},{3,2},{4,3},{5,4},{6,5},{7,6},{9,8},{10,9},{11,10},{12... | collective-permute-start | bytes 1179656 | tf_op jit(solution)/shard_map/ppermute | solution.py:24
  110.6 3.5 %collective-permute-done.4 = f32[3,128,256]{2,1,0:T(8,128)S(1)} collective-permute-done((f32[3,128,256]{2,1,0:T(8,128)S(1)}, f32[3,128,256]{2,1,0:T(8,128)S(1)}, u32[]{:S(2)}, u32[]{:S(2)}) %collective-permute-start.4) | collective-permute-done | bytes 393248 | tf_op jit(solution)/shard_map/ppermute | solution.py:23
  115.9 4.9 %fusion.87 = f32[8,128,256]{2,1,0:T(8,128)S(1)} fusion(f32[8,128,256]{2,1,0:T(8,128)S(1)} %fusion.105, f32[3,128,256]{2,1,0:T(8,128)S(1)} %collective-permute-done.5, f32[3,128,256]{2,1,0:T(8,128)S(1)} %collective-permute-done.4, f32[]{:T(128)} %bitcast.18, f32[]{:T(128)} %bitcast.17, f32[]{:T(128)} %bitcast.16, f32[]{:T(128)} %bitcast.15, f32[]{:T(128)} %bitcast.14, ...), kind=kLoop, calls=%fused_computation.167 | loop fusion | flops 4980736 | bytes 2883612 | tf_op jit(solution)/shard_map/add | solution.py:34
  120.8 3.8 %collective-permute-start.6 = (f32[8,3,256]{2,1,0:T(4,128)S(1)}, f32[8,3,256]{2,1,0:T(4,128)S(1)}, u32[]{:S(2)}, u32[]{:S(2)}) collective-permute-start(f32[8,3,256]{2,1,0:T(4,128)S(1)} %get-tuple-element.13), channel_id=1, source_target_pairs={{0,32},{32,64},{64,96},{96,128},{128,160},{160,192},{192,224},{1,3... | collective-permute-start | bytes 73736 | tf_op jit(solution)/shard_map/ppermute | solution.py:23
  126.7 5.4 %collective-permute-done.7 = f32[8,3,256]{2,1,0:T(4,128)S(1)} collective-permute-done((f32[8,3,256]{2,1,0:T(4,128)S(1)}, f32[8,3,256]{2,1,0:T(4,128)S(1)}, u32[]{:S(2)}, u32[]{:S(2)}) %collective-permute-start.7) | collective-permute-done | bytes 24608 | tf_op jit(solution)/shard_map/ppermute | solution.py:24
  132.1 5.2 %fusion.31 = f32[8,128,256]{2,1,0:T(8,128)S(1)} fusion(f32[8,128,256]{2,1,0:T(8,128)S(1)} %fusion.87, f32[8,3,256]{2,1,0:T(4,128)S(1)} %collective-permute-done.7, f32[8,3,256]{2,1,0:T(4,128)S(1)} %collective-permute-done.6, f32[]{:T(128)} %bitcast.23, f32[]{:T(128)} %bitcast.22, f32[]{:T(128)} %bitcast.21, f32[]{:T(128)} %bitcast.20, f32[]{:T(128)} %bitcast.19, ...), kind=kLoop, calls=%fused_computation.111 | loop fusion | flops 4980736 | bytes 2146332 | tf_op jit(solution)/shard_map/add | solution.py:34
  137.3 7.0 %fusion.117 = f32[8,128,256]{2,1,0:T(8,128)} fusion(f32[8,128,256]{2,1,0:T(8,128)S(1)} %fusion.31, f32[]{:T(128)} %bitcast.28, f32[]{:T(128)} %bitcast.27, f32[]{:T(128)} %bitcast.26, f32[]{:T(128)} %bitcast.25, f32[]{:T(128)} %bitcast.24, f32[]{:T(128)} %bitcast.11, f32[]{:T(128)} %bitcast), kind=kLoop, calls=%fused_computation.197 | loop fusion | flops 3407872 | bytes 2097180 | tf_op jit(solution)/shard_map/add | solution.py:34
  144.3 51.3 %all-reduce.7.cloned.1.call-done = f32[8,128,256]{2,1,0:T(8,128)} async-done(((f32[8,128,256]{2,1,0:T(8,128)}), f32[8,128,256]{2,1,0:T(8,128)}) %all-reduce.7.cloned.1.call-update) | async-done | bytes 1048592 | tf_op jit(solution)/shard_map/psum | solution.py:205
  199.9 3.6 %collective-permute-start.9 = (f32[3,128,256]{2,1,0:T(8,128)}, f32[3,128,256]{2,1,0:T(8,128)}, u32[]{:S(2)}, u32[]{:S(2)}) collective-permute-start(f32[3,128,256]{2,1,0:T(8,128)} %get-tuple-element.12), channel_id=1, source_target_pairs={{1,0},{2,1},{3,2},{4,3},{5,4},{6,5},{7,6},{9,8},{10,9},{11,10},{12... | collective-permute-start | bytes 1179656 | tf_op jit(solution)/shard_map/ppermute | solution.py:24
  209.1 6.1 %fusion.73 = f32[8,128,256]{2,1,0:T(8,128)S(1)} fusion(f32[8,128,256]{2,1,0:T(8,128)S(1)} %broadcast_multiply_fusion, f32[3,128,256]{2,1,0:T(8,128)} %collective-permute-done.9, f32[3,128,256]{2,1,0:T(8,128)} %collective-permute-done.8, f32[]{:T(128)S(6)} %mul.455, f32[]{:T(128)} %bitcast.18, f32[]{:T(128)} %bitcast.17, f32[]{:T(128)} %bitcast.15, ...), kind=kLoop, calls=%fused_computation.153 | loop fusion | flops 5242880 | bytes 4980764 | tf_op jit(solution)/shard_map/add | solution.py:34
  215.2 3.5 %collective-permute-start.10 = (f32[8,3,256]{2,1,0:T(4,128)S(1)}, f32[8,3,256]{2,1,0:T(4,128)S(1)}, u32[]{:S(2)}, u32[]{:S(2)}) collective-permute-start(f32[8,3,256]{2,1,0:T(4,128)S(1)} %get-tuple-element.9), channel_id=1, source_target_pairs={{0,32},{32,64},{64,96},{96,128},{128,160},{160,192},{192,224},{1,3... | collective-permute-start | bytes 73736 | tf_op jit(solution)/shard_map/ppermute | solution.py:23
  221.2 3.2 collective-permute-done.11
  224.5 5.2 %fusion.17 = f32[8,128,256]{2,1,0:T(8,128)S(1)} fusion(f32[8,128,256]{2,1,0:T(8,128)S(1)} %fusion.73, f32[8,3,256]{2,1,0:T(4,128)S(1)} %collective-permute-done.11, f32[8,3,256]{2,1,0:T(4,128)S(1)} %collective-permute-done.10, f32[]{:T(128)} %bitcast.23, f32[]{:T(128)} %bitcast.22, f32[]{:T(128)} %bitcast.21, f32[]{:T(128)} %bitcast.20, f32[]{:T(128)} %bitcast.19, ...), kind=kLoop, calls=%fused_computation.97 | loop fusion | flops 4980736 | bytes 2146332 | tf_op jit(solution)/shard_map/add | solution.py:34
  229.6 6.0 %fusion.130 = f32[8,128,256]{2,1,0:T(8,128)S(1)} fusion(f32[8,128,256]{2,1,0:T(8,128)S(1)} %fusion.17, f32[2,8,16,8,128]{4,3,2,1,0:T(8,128)S(1)} %bitcast.40, f32[]{:T(128)} %bitcast.28, f32[]{:T(128)} %bitcast.27, f32[]{:T(128)} %bitcast.26, f32[]{:T(128)} %bitcast.25, f32[]{:T(128)} %bitcast.24, f32[]{:T(128)} %bitcast.11, f32[]{:T(128)} %bitcast), kind=kLoop, calls=%fused_computation.210 | loop fusion | flops 3670016 | bytes 3145756 | tf_op jit(solution)/shard_map/div | solution.py:203
  238.0 3.3 collective-permute-start.13
  241.3 3.5 %collective-permute-done.12 = f32[3,128,256]{2,1,0:T(8,128)S(1)} collective-permute-done((f32[3,128,256]{2,1,0:T(8,128)S(1)}, f32[3,128,256]{2,1,0:T(8,128)S(1)}, u32[]{:S(2)}, u32[]{:S(2)}) %collective-permute-start.12) | collective-permute-done | bytes 393248 | tf_op jit(solution)/shard_map/ppermute | solution.py:23
  246.6 4.9 %fusion.59 = f32[8,128,256]{2,1,0:T(8,128)S(1)} fusion(f32[8,128,256]{2,1,0:T(8,128)S(1)} %fusion.130, f32[3,128,256]{2,1,0:T(8,128)S(1)} %collective-permute-done.13, f32[3,128,256]{2,1,0:T(8,128)S(1)} %collective-permute-done.12, f32[]{:T(128)} %bitcast.18, f32[]{:T(128)} %bitcast.17, f32[]{:T(128)} %bitcast.16, f32[]{:T(128)} %bitcast.15, f32[]{:T(128)} %bitcast.14, ...), kind=kLoop, calls=%fused_computation.139 | loop fusion | flops 4980736 | bytes 2883612 | tf_op jit(solution)/shard_map/add | solution.py:34
  251.6 4.2 %collective-permute-start.14 = (f32[8,3,256]{2,1,0:T(4,128)S(1)}, f32[8,3,256]{2,1,0:T(4,128)S(1)}, u32[]{:S(2)}, u32[]{:S(2)}) collective-permute-start(f32[8,3,256]{2,1,0:T(4,128)S(1)} %get-tuple-element.5), channel_id=1, source_target_pairs={{0,32},{32,64},{64,96},{96,128},{128,160},{160,192},{192,224},{1,3... | collective-permute-start | bytes 73736 | tf_op jit(solution)/shard_map/ppermute | solution.py:23
  257.7 5.1 %collective-permute-done.15 = f32[8,3,256]{2,1,0:T(4,128)S(1)} collective-permute-done((f32[8,3,256]{2,1,0:T(4,128)S(1)}, f32[8,3,256]{2,1,0:T(4,128)S(1)}, u32[]{:S(2)}, u32[]{:S(2)}) %collective-permute-start.15) | collective-permute-done | bytes 24608 | tf_op jit(solution)/shard_map/ppermute | solution.py:24
  262.8 5.2 %fusion.3 = f32[8,128,256]{2,1,0:T(8,128)S(1)} fusion(f32[8,128,256]{2,1,0:T(8,128)S(1)} %fusion.59, f32[8,3,256]{2,1,0:T(4,128)S(1)} %collective-permute-done.15, f32[8,3,256]{2,1,0:T(4,128)S(1)} %collective-permute-done.14, f32[]{:T(128)} %bitcast.23, f32[]{:T(128)} %bitcast.22, f32[]{:T(128)} %bitcast.21, f32[]{:T(128)} %bitcast.20, f32[]{:T(128)} %bitcast.19, ...), kind=kLoop, calls=%fused_computation.83 | loop fusion | flops 4980736 | bytes 2146332 | tf_op jit(solution)/shard_map/add | solution.py:34
  268.0 7.0 %fusion.142 = f32[8,128,256]{2,1,0:T(8,128)} fusion(f32[8,128,256]{2,1,0:T(8,128)S(1)} %fusion.3, f32[]{:T(128)} %bitcast.28, f32[]{:T(128)} %bitcast.27, f32[]{:T(128)} %bitcast.26, f32[]{:T(128)} %bitcast.25, f32[]{:T(128)} %bitcast.24, f32[]{:T(128)} %bitcast.11, f32[]{:T(128)} %bitcast), kind=kLoop, calls=%fused_computation.222 | loop fusion | flops 3407872 | bytes 2097180 | tf_op jit(solution)/shard_map/add | solution.py:34
  275.0 50.1 %all-reduce.9.cloned.1.call-done = f32[8,128,256]{2,1,0:T(8,128)} async-done(((f32[8,128,256]{2,1,0:T(8,128)}), f32[8,128,256]{2,1,0:T(8,128)}) %all-reduce.9.cloned.1.call-update) | async-done | bytes 1048592 | tf_op jit(solution)/shard_map/psum | solution.py:205
  (49 shorter events, 39.5 us)
Async XLA Ops:
  19.8 11.8 %copy-start = (f32[8,128,256]{2,1,0:T(8,128)S(1)}, f32[8,128,256]{2,1,0:T(8,128)}, u32[]{:S(2)}) copy-start(f32[8,128,256]{2,1,0:T(8,128)} %param.5) | copy-start | bytes 3145732
  19.8 65.2 %all-to-all-start = ((f32[64,65,1,128]{3,2,1,0:T(1,128)}), f32[64,65,1,128]{3,2,1,0:T(1,128)S(1)}, u32[]{:S(2)}, u32[]{:S(2)}) async-start(f32[64,65,1,128]{3,2,1,0:T(1,128)} %bitcast.42), calls=%async_computation | async-start | bytes 4259840 | tf_op jit(solution)/shard_map/all_to_all | solution.py:190
  31.5 6.6 %copy-start.3 = (f32[1,3,7]{2,0,1:T(1,128)S(1)}, f32[1,3,7]{2,0,1:T(1,128)}, u32[]{:S(2)}) copy-start(f32[1,3,7]{2,0,1:T(1,128)} %param.8) | copy-start | bytes 256
  31.5 164.1 %all-reduce.7.cloned.1.call-start = ((), (), s32[]{:S(2)}) async-start(), calls=%async_computation.1 | async-start | bytes 2097152 | tf_op jit(solution)/shard_map/psum | solution.py:205
  32.5 13.8 %collective-permute-start = (f32[3,128,256]{2,1,0:T(8,128)}, f32[3,128,256]{2,1,0:T(8,128)}, u32[]{:S(2)}, u32[]{:S(2)}) collective-permute-start(f32[3,128,256]{2,1,0:T(8,128)} %get-tuple-element.21), channel_id=1, source_target_pairs={{0,1},{1,2},{2,3},{3,4},{4,5},{5,6},{6,7},{8,9},{9,10},{10,11},{11... | collective-permute-start | bytes 1179656 | tf_op jit(solution)/shard_map/ppermute | solution.py:23
  34.6 13.0 %collective-permute-start.1 = (f32[3,128,256]{2,1,0:T(8,128)}, f32[3,128,256]{2,1,0:T(8,128)}, u32[]{:S(2)}, u32[]{:S(2)}) collective-permute-start(f32[3,128,256]{2,1,0:T(8,128)} %get-tuple-element.22), channel_id=1, source_target_pairs={{1,0},{2,1},{3,2},{4,3},{5,4},{6,5},{7,6},{9,8},{10,9},{11,10},{12... | collective-permute-start | bytes 1179656 | tf_op jit(solution)/shard_map/ppermute | solution.py:24
  53.5 24.9 %collective-permute-start.2 = (f32[8,3,256]{2,1,0:T(4,128)S(1)}, f32[8,3,256]{2,1,0:T(4,128)S(1)}, u32[]{:S(2)}, u32[]{:S(2)}) collective-permute-start(f32[8,3,256]{2,1,0:T(4,128)S(1)} %get-tuple-element.17), channel_id=1, source_target_pairs={{0,32},{32,64},{64,96},{96,128},{128,160},{160,192},{192,224},{1,3... | collective-permute-start | bytes 73736 | tf_op jit(solution)/shard_map/ppermute | solution.py:23
  57.3 21.5 %collective-permute-start.3 = (f32[8,3,256]{2,1,0:T(4,128)S(1)}, f32[8,3,256]{2,1,0:T(4,128)S(1)}, u32[]{:S(2)}, u32[]{:S(2)}) collective-permute-start(f32[8,3,256]{2,1,0:T(4,128)S(1)} %get-tuple-element.18), channel_id=1, source_target_pairs={{32,0},{64,32},{96,64},{128,96},{160,128},{192,160},{224,192},{33,... | collective-permute-start | bytes 73736 | tf_op jit(solution)/shard_map/ppermute | solution.py:24
  85.0 1.4 copy-start.1
  97.4 1.5 copy-start.2
  105.1 9.1 %collective-permute-start.4 = (f32[3,128,256]{2,1,0:T(8,128)S(1)}, f32[3,128,256]{2,1,0:T(8,128)S(1)}, u32[]{:S(2)}, u32[]{:S(2)}) collective-permute-start(f32[3,128,256]{2,1,0:T(8,128)S(1)} %get-tuple-element.15), channel_id=1, source_target_pairs={{0,1},{1,2},{2,3},{3,4},{4,5},{5,6},{6,7},{8,9},{9,10},{10,11},{11... | collective-permute-start | bytes 1179656 | tf_op jit(solution)/shard_map/ppermute | solution.py:23
  107.0 8.9 %collective-permute-start.5 = (f32[3,128,256]{2,1,0:T(8,128)S(1)}, f32[3,128,256]{2,1,0:T(8,128)S(1)}, u32[]{:S(2)}, u32[]{:S(2)}) collective-permute-start(f32[3,128,256]{2,1,0:T(8,128)S(1)} %get-tuple-element.16), channel_id=1, source_target_pairs={{1,0},{2,1},{3,2},{4,3},{5,4},{6,5},{7,6},{9,8},{10,9},{11,10},{12... | collective-permute-start | bytes 1179656 | tf_op jit(solution)/shard_map/ppermute | solution.py:24
  120.8 5.9 %collective-permute-start.6 = (f32[8,3,256]{2,1,0:T(4,128)S(1)}, f32[8,3,256]{2,1,0:T(4,128)S(1)}, u32[]{:S(2)}, u32[]{:S(2)}) collective-permute-start(f32[8,3,256]{2,1,0:T(4,128)S(1)} %get-tuple-element.13), channel_id=1, source_target_pairs={{0,32},{32,64},{64,96},{96,128},{128,160},{160,192},{192,224},{1,3... | collective-permute-start | bytes 73736 | tf_op jit(solution)/shard_map/ppermute | solution.py:23
  124.6 7.5 %collective-permute-start.7 = (f32[8,3,256]{2,1,0:T(4,128)S(1)}, f32[8,3,256]{2,1,0:T(4,128)S(1)}, u32[]{:S(2)}, u32[]{:S(2)}) collective-permute-start(f32[8,3,256]{2,1,0:T(4,128)S(1)} %get-tuple-element.14), channel_id=1, source_target_pairs={{32,0},{64,32},{96,64},{128,96},{160,128},{192,160},{224,192},{33,... | collective-permute-start | bytes 73736 | tf_op jit(solution)/shard_map/ppermute | solution.py:24
  144.3 180.8 %all-reduce.9.cloned.1.call-start = ((), (), s32[]{:S(2)}) async-start(), calls=%async_computation.2 | async-start | bytes 2097152 | tf_op jit(solution)/shard_map/psum | solution.py:205
  197.9 9.4 %collective-permute-start.8 = (f32[3,128,256]{2,1,0:T(8,128)}, f32[3,128,256]{2,1,0:T(8,128)}, u32[]{:S(2)}, u32[]{:S(2)}) collective-permute-start(f32[3,128,256]{2,1,0:T(8,128)} %get-tuple-element.11), channel_id=1, source_target_pairs={{0,1},{1,2},{2,3},{3,4},{4,5},{5,6},{6,7},{8,9},{9,10},{10,11},{11... | collective-permute-start | bytes 1179656 | tf_op jit(solution)/shard_map/ppermute | solution.py:23
  199.9 9.2 %collective-permute-start.9 = (f32[3,128,256]{2,1,0:T(8,128)}, f32[3,128,256]{2,1,0:T(8,128)}, u32[]{:S(2)}, u32[]{:S(2)}) collective-permute-start(f32[3,128,256]{2,1,0:T(8,128)} %get-tuple-element.12), channel_id=1, source_target_pairs={{1,0},{2,1},{3,2},{4,3},{5,4},{6,5},{7,6},{9,8},{10,9},{11,10},{12... | collective-permute-start | bytes 1179656 | tf_op jit(solution)/shard_map/ppermute | solution.py:24
  215.2 6.0 %collective-permute-start.10 = (f32[8,3,256]{2,1,0:T(4,128)S(1)}, f32[8,3,256]{2,1,0:T(4,128)S(1)}, u32[]{:S(2)}, u32[]{:S(2)}) collective-permute-start(f32[8,3,256]{2,1,0:T(4,128)S(1)} %get-tuple-element.9), channel_id=1, source_target_pairs={{0,32},{32,64},{64,96},{96,128},{128,160},{160,192},{192,224},{1,3... | collective-permute-start | bytes 73736 | tf_op jit(solution)/shard_map/ppermute | solution.py:23
  218.6 5.8 %collective-permute-start.11 = (f32[8,3,256]{2,1,0:T(4,128)S(1)}, f32[8,3,256]{2,1,0:T(4,128)S(1)}, u32[]{:S(2)}, u32[]{:S(2)}) collective-permute-start(f32[8,3,256]{2,1,0:T(4,128)S(1)} %get-tuple-element.10), channel_id=1, source_target_pairs={{32,0},{64,32},{96,64},{128,96},{160,128},{192,160},{224,192},{33,... | collective-permute-start | bytes 73736 | tf_op jit(solution)/shard_map/ppermute | solution.py:24
  235.7 9.1 %collective-permute-start.12 = (f32[3,128,256]{2,1,0:T(8,128)S(1)}, f32[3,128,256]{2,1,0:T(8,128)S(1)}, u32[]{:S(2)}, u32[]{:S(2)}) collective-permute-start(f32[3,128,256]{2,1,0:T(8,128)S(1)} %get-tuple-element.7), channel_id=1, source_target_pairs={{0,1},{1,2},{2,3},{3,4},{4,5},{5,6},{6,7},{8,9},{9,10},{10,11},{11... | collective-permute-start | bytes 1179656 | tf_op jit(solution)/shard_map/ppermute | solution.py:23
  238.0 8.6 %collective-permute-start.13 = (f32[3,128,256]{2,1,0:T(8,128)S(1)}, f32[3,128,256]{2,1,0:T(8,128)S(1)}, u32[]{:S(2)}, u32[]{:S(2)}) collective-permute-start(f32[3,128,256]{2,1,0:T(8,128)S(1)} %get-tuple-element.8), channel_id=1, source_target_pairs={{1,0},{2,1},{3,2},{4,3},{5,4},{6,5},{7,6},{9,8},{10,9},{11,10},{12... | collective-permute-start | bytes 1179656 | tf_op jit(solution)/shard_map/ppermute | solution.py:24
  251.6 6.2 %collective-permute-start.14 = (f32[8,3,256]{2,1,0:T(4,128)S(1)}, f32[8,3,256]{2,1,0:T(4,128)S(1)}, u32[]{:S(2)}, u32[]{:S(2)}) collective-permute-start(f32[8,3,256]{2,1,0:T(4,128)S(1)} %get-tuple-element.5), channel_id=1, source_target_pairs={{0,32},{32,64},{64,96},{96,128},{128,160},{160,192},{192,224},{1,3... | collective-permute-start | bytes 73736 | tf_op jit(solution)/shard_map/ppermute | solution.py:23
  255.8 7.0 %collective-permute-start.15 = (f32[8,3,256]{2,1,0:T(4,128)S(1)}, f32[8,3,256]{2,1,0:T(4,128)S(1)}, u32[]{:S(2)}, u32[]{:S(2)}) collective-permute-start(f32[8,3,256]{2,1,0:T(4,128)S(1)} %get-tuple-element.6), channel_id=1, source_target_pairs={{32,0},{64,32},{96,64},{128,96},{160,128},{192,160},{224,192},{33,... | collective-permute-start | bytes 73736 | tf_op jit(solution)/shard_map/ppermute | solution.py:24
Sparse Core Ops, SparseCore 0:
  144.4 51.1 all-reduce.6
  275.1 49.8 all-reduce.8

commit v3 on v2

--- a/solution.py
+++ b/solution.py
@@ -11,40 +11,9 @@
 HALO = 3
 ITERS = 2
 UNROLL = 8
-
-
-def with_halo(value, sides, width):
-    for axis, dim in sides:
-        count, length = (lax.axis_size(axis), value.shape[dim])
-        up = [(i, (i + 1) % count) for i in range(count - 1)]
-        down = [(j, i) for i, j in up]
-        last = lax.slice_in_dim(value, length - width, length, axis=dim)
-        leading = lax.slice_in_dim(value, 0, width, axis=dim)
-        before = lax.ppermute(last, axis, up)
-        after = lax.ppermute(leading, axis, down)
-        value = jnp.concatenate([before, value, after], axis=dim)
-    return value
-
-
-def axis_blur(volume, weights, dim_index, length_along):
-    result = jnp.zeros(
-        volume.shape[:dim_index] + (length_along,) + volume.shape[dim_index + 1 :], jnp.float32
-    )
-    for offset in range(2 * HALO + 1):
-        result = result + weights[offset] * lax.slice_in_dim(
-            volume, offset, offset + length_along, axis=dim_index
-        )
-    return result
-
-
-def blur_local(volume, weights):
-    x_cells, y_cells, z_cells = volume.shape
-    extended = with_halo(volume, (("rows", 0),), HALO)
-    result = axis_blur(extended, weights[0], 0, x_cells)
-    widened = with_halo(result, (("blocks", 1),), HALO)
-    result = axis_blur(widened, weights[1], 1, y_cells)
-    padded = jnp.pad(result, ((0, 0), (0, 0), (HALO, HALO)))
-    return axis_blur(padded, weights[2], 2, z_cells)
+TAPS = 2 * HALO + 1
+EDGE = 8
+ROWS = 32
 
 
 def lane_sum(x):
@@ -175,6 +144,260 @@
     )(arrived)
 
 
+def vmem():
+    return pl.BlockSpec(memory_space=pltpu.VMEM)
+
+
+def smem():
+    return pl.BlockSpec(memory_space=pltpu.SMEM)
+
+
+def f32(*shape):
+    return jax.ShapeDtypeStruct(shape, jnp.float32)
+
+
+def call(kernel, name, outs, args, scalars=1, scratch=(), work=4_000_000):
+    return pl.pallas_call(
+        kernel,
+        out_shape=outs,
+        in_specs=[smem()] * scalars + [vmem()] * (len(args) - scalars),
+        out_specs=[vmem()] * len(outs),
+        scratch_shapes=list(scratch),
+        cost_estimate=pl.CostEstimate(flops=work, bytes_accessed=work, transcendentals=0),
+        compiler_params=pltpu.CompilerParams(vmem_limit_bytes=32 * 1024 * 1024),
+        name=name,
+    )(*args)
+
+
+def taps_of(w_ref, dim, flip):
+    return [w_ref[dim * TAPS + (TAPS - 1 - k if flip else k)] for k in range(TAPS)]
+
+
+def blur_z(a, b, w):
+    lane = lax.broadcasted_iota(jnp.int32, a.shape, 1)
+    out_a, out_b = w[HALO] * a, w[HALO] * b
+    for s in range(1, HALO + 1):
+        keep = lane < BRICK - s
+        ra, rb = pltpu.roll(a, BRICK - s, 1), pltpu.roll(b, BRICK - s, 1)
+        out_a += w[HALO + s] * jnp.where(keep, ra, rb)
+        out_b += w[HALO + s] * jnp.where(keep, rb, 0.0)
+        fresh = lane < s
+        la, lb = pltpu.roll(a, s, 1), pltpu.roll(b, s, 1)
+        out_a += w[HALO - s] * jnp.where(fresh, 0.0, la)
+        out_b += w[HALO - s] * jnp.where(fresh, la, lb)
+    return out_a, out_b
+
+
+def put_edges(field, first, last, x, y_cells):
+    for c in range(2):
+        first[c, x] = field[c, x, 0:EDGE, :]
+        last[c, x] = field[c, x, y_cells - EDGE : y_cells, :]
+
+
+def z_first_kernel(w_ref, est_ref, out_ref, first, last):
+    x_cells, y_cells, _ = est_ref.shape
+    w = taps_of(w_ref, 2, False)
+
+    def body(x, carry):
+        for y in range(0, y_cells, ROWS):
+            at = pl.ds(y, ROWS)
+            a, b = blur_z(est_ref[x, at, 0:BRICK], est_ref[x, at, BRICK : 2 * BRICK], w)
+            out_ref[0, x, at, :] = a
+            out_ref[1, x, at, :] = b
+        put_edges(out_ref, first, last, x, y_cells)
+        return carry
+
+    lax.fori_loop(0, x_cells, body, 0)
+
+
+def z_first(w, estimate):
+    x, y, _ = estimate.shape
+    outs = [f32(2, x, y, BRICK), f32(2, x, EDGE, BRICK), f32(2, x, EDGE, BRICK)]
+    return call(z_first_kernel, "z_blur", outs, (w, estimate))
+
+
+def z_pieces_kernel(views, w_ref, v_ref, *refs):
+    pieces, (out_ref, first, last) = refs[: 2 * views], refs[2 * views :]
+    depth, y_cells, _ = pieces[0].shape
+    w = taps_of(w_ref, 2, False)
+    for d in range(views):
+        base = lax.rem(v_ref[0] + d, views) * depth
+
+        def body(i, carry, d=d, base=base):
+            for y in range(0, y_cells, ROWS):
+                at = pl.ds(y, ROWS)
+                a, b = blur_z(pieces[2 * d][i, at, :], pieces[2 * d + 1][i, at, :], w)
+                out_ref[0, base + i, at, :] = a
+                out_ref[1, base + i, at, :] = b
+            put_edges(out_ref, first, last, base + i, y_cells)
+            return carry
+
+        lax.fori_loop(0, depth, body, 0)
+
+
+def z_pieces(w, v, pieces):
+    views = len(pieces) // 2
+    depth, y, _ = pieces[0].shape
+    x = views * depth
+    outs = [f32(2, x, y, BRICK), f32(2, x, EDGE, BRICK), f32(2, x, EDGE, BRICK)]
+    return call(
+        functools.partial(z_pieces_kernel, views), "z_blur_pieces", outs, (w, v, *pieces), 2
+    )
+
+
+def y_kernel(flip, w_ref, in_ref, lo, hi, out_ref, first, last, wide):
+    _, x_cells, y_cells, _ = in_ref.shape
+    w = taps_of(w_ref, 1, flip)
+
+    def body(x, carry):
+        for c in range(2):
+            wide[c, 0:EDGE, :] = lo[c, x]
+            wide[c, pl.ds(EDGE, y_cells), :] = in_ref[c, x]
+            wide[c, EDGE + y_cells : 2 * EDGE + y_cells, :] = hi[c, x]
+            for y in range(0, y_cells, ROWS):
+                total = w[0] * wide[c, pl.ds(EDGE - HALO + y, ROWS), :]
+                for k in range(1, TAPS):
+                    total += w[k] * wide[c, pl.ds(EDGE - HALO + k + y, ROWS), :]
+                out_ref[c, x, pl.ds(y, ROWS), :] = total
+        return carry
+
+    lax.fori_loop(0, x_cells, body, 0)
+    for c in range(2):
+        for i in range(HALO):
+            first[c, i] = out_ref[c, i]
+            last[c, i] = out_ref[c, x_cells - HALO + i]
+
+
+def y_blur(w, field, lo, hi, flip):
+    _, x, y, _ = field.shape
+    outs = [f32(2, x, y, BRICK), f32(2, HALO, y, BRICK), f32(2, HALO, y, BRICK)]
+    return call(
+        functools.partial(y_kernel, flip), "y_blur", outs, (w, field, lo, hi),
+        scratch=[pltpu.VMEM((2, y + 2 * EDGE, BRICK), jnp.float32)],
+    )
+
+
+def x_layers(lo, field, hi, c, at):
+    x_cells = field.shape[1]
+    return (
+        [lo[c, i, at, :] for i in range(HALO)]
+        + [field[c, i, at, :] for i in range(x_cells)]
+        + [hi[c, i, at, :] for i in range(HALO)]
+    )
+
+
+def weigh(layers, w):
+    total = w[0] * layers[0]
+    for k in range(1, TAPS):
+        total += w[k] * layers[k]
+    return total
+
+
+def ratio_kernel(w_ref, field, lo, hi, obs, out_ref, first, last):
+    _, x_cells, y_cells, _ = field.shape
+    w = taps_of(w_ref, 0, False)
+    u = taps_of(w_ref, 2, True)
+
+    def body(t, carry):
+        at = pl.ds(pl.multiple_of(t * EDGE, EDGE), EDGE)
+        la, lb = x_layers(lo, field, hi, 0, at), x_layers(lo, field, hi, 1, at)
+        for x in range(x_cells):
+            rows = [
+                obs[pl.ds(pl.multiple_of((c * x_cells + x) * y_cells + t * EDGE, EDGE), EDGE), :]
+                for c in range(2)
+            ]
+            a, b = blur_z(
+                rows[0] / weigh(la[x : x + TAPS], w), rows[1] / weigh(lb[x : x + TAPS], w), u
+            )
+            out_ref[0, x, at, :] = a
+            out_ref[1, x, at, :] = b
+        return carry
+
+    lax.fori_loop(0, y_cells // EDGE, body, 0)
+    for x in range(x_cells):
+        put_edges(out_ref, first, last, x, y_cells)
+
+
+def ratio(w, field, lo, hi, obs):
+    _, x, y, _ = field.shape
+    outs = [f32(2, x, y, BRICK), f32(2, x, EDGE, BRICK), f32(2, x, EDGE, BRICK)]
+    return call(ratio_kernel, "ratio", outs, (w, field, lo, hi, obs), work=8_000_000)
+
+
+def split_kernel(views, w_ref, v_ref, field, lo, hi, a2, b2, a1, b1, a3, b3, a0, b0, wide):
+    _, x_cells, y_cells, _ = field.shape
+    depth = x_cells // views
+    w = taps_of(w_ref, 0, True)
+    for c in range(2):
+        for i in range(HALO):
+            wide[c, i] = lo[c, i]
+            wide[c, HALO + x_cells + i] = hi[c, i]
+        for i in range(x_cells):
+            wide[c, HALO + i] = field[c, i]
+    outs = ((0, a0, b0), (1, a1, b1), (2, a2, b2), (3, a3, b3))
+    for r, out_a, out_b in outs:
+        base = lax.rem(v_ref[0] + r, views) * depth
+
+        def body(t, carry, base=base, pair=(out_a, out_b)):
+            at = pl.ds(pl.multiple_of(t * EDGE, EDGE), EDGE)
+            for c in range(2):
+                layers = [wide[c, base + i, at, :] for i in range(depth + 2 * HALO)]
+                for i in range(depth):
+                    pair[c][i, at, :] = weigh(layers[i : i + TAPS], w)
+            return carry
+
+        lax.fori_loop(0, y_cells // EDGE, body, 0, unroll=2)
+
+
+def split(w, v, views, field, lo, hi):
+    _, x, y, _ = field.shape
+    outs = [f32(x // views, y, BRICK)] * 8
+    return call(
+        functools.partial(split_kernel, views), "x_blur_split", outs, (w, v, field, lo, hi), 2,
+        scratch=[pltpu.VMEM((2, x + 2 * HALO, y, BRICK), jnp.float32)],
+    )
+
+
+def add_kernel(a, ra, b, rb, out_a, out_b):
+    out_a[...] = a[...] + ra[...]
+    out_b[...] = b[...] + rb[...]
+
+
+def update_first_kernel(views, v_ref, est, a, a1, a2, b, b1, b2, out_a, out_b):
+    depth = a.shape[0]
+    base = v_ref[0] * depth
+    for i in range(depth):
+        row = est[base + i]
+        out_a[i] = row[:, 0:BRICK] * (a[i] + a1[i] + a2[i]) / views
+        out_b[i] = row[:, BRICK : 2 * BRICK] * (b[i] + b1[i] + b2[i]) / views
+
+
+def update_kernel(views, est_a, est_b, a, a1, a2, b, b1, b2, out_a, out_b):
+    out_a[...] = est_a[...] * (a[...] + a1[...] + a2[...]) / views
+    out_b[...] = est_b[...] * (b[...] + b1[...] + b2[...]) / views
+
+
+def join_kernel(views, v_ref, *refs):
+    pieces, out_ref = refs[: 2 * views], refs[2 * views]
+    depth = pieces[0].shape[0]
+    for d in range(views):
+        base = lax.rem(v_ref[0] + d, views) * depth
+        for i in range(depth):
+            out_ref[base + i, :, 0:BRICK] = pieces[2 * d][i]
+            out_ref[base + i, :, BRICK : 2 * BRICK] = pieces[2 * d + 1][i]
+
+
+def exchange(first, last, axis):
+    count = lax.axis_size(axis)
+    up = [(i, i + 1) for i in range(count - 1)]
+    down = [(i + 1, i) for i in range(count - 1)]
+    return lax.ppermute(last, axis, up), lax.ppermute(first, axis, down)
+
+
+def turn(value, step, count):
+    return lax.ppermute(value, "views", [(i, (i + step) % count) for i in range(count)])
+
+
 def per_device(estimate, views_data, target, psf_taps, shifts):
     x_cells, y_cells, z_cells = estimate.shape
     row_count = lax.axis_size("rows")
@@ -191,20 +414,47 @@
         outgoing.reshape(peer_count, capacity + 1, 1, BRICK),
         ("blocks", "rows"), split_axis=0, concat_axis=0, tiled=True,
     ).reshape(peer_count * (capacity + 1), 1, BRICK)
-    moved = unpack(arrived, peer_count, capacity, brick_count)[:brick_count]
-    moved = (
-        moved.reshape(brick_cols, x_cells, y_cells, BRICK)
-        .transpose(1, 2, 0, 3)
-        .reshape(x_cells, y_cells, z_cells)
-    )
-    weights = psf_taps[0] / jnp.sum(psf_taps[0], axis=1, keepdims=True)
-    flipped = weights[:, ::-1]
+    w = (psf_taps[0] / jnp.sum(psf_taps[0], axis=1, keepdims=True)).reshape(-1)
+    v = lax.axis_index("views").astype(jnp.int32).reshape(1)
+    depth = x_cells // view_count
+    pair = [f32(depth, y_cells, BRICK)] * 2
+    pieces = None
     for iteration in range(ITERS):
-        placed = moved / blur_local(estimate, weights)
-        projected = blur_local(placed, flipped)
-        combined = lax.psum(projected, "views")
-        estimate = estimate * combined / view_count
-    return estimate
+        if pieces is None:
+            field, first, last = z_first(w, estimate)
+        else:
+            field, first, last = z_pieces(w, v, pieces)
+        field, first, last = y_blur(w, field, *exchange(first, last, "blocks"), False)
+        lo, hi = exchange(first, last, "rows")
+        if pieces is None:
+            moved = unpack(arrived, peer_count, capacity, brick_count)
+        field, first, last = ratio(w, field, lo, hi, moved)
+        field, first, last = y_blur(w, field, *exchange(first, last, "blocks"), True)
+        lo, hi = exchange(first, last, "rows")
+        a2, b2, a1, b1, a3, b3, a0, b0 = split(w, v, view_count, field, lo, hi)
+        ra, rb = turn(a2, 1, view_count), turn(b2, -1, view_count)
+        near_b, near_a = turn(b1, 1, view_count), turn(a3, -1, view_count)
+        a1, b3 = call(add_kernel, "add", pair, (a1, ra, b3, rb), 0)
+        far_a, far_b = turn(a1, 1, view_count), turn(b3, -1, view_count)
+        sums = (a0, near_a, far_a, b0, near_b, far_b)
+        if pieces is None:
+            own = call(
+                functools.partial(update_first_kernel, view_count), "update", pair,
+                (v, estimate, *sums),
+            )
+        else:
+            own = call(
+                functools.partial(update_kernel, view_count), "update", pair,
+                (*pieces[:2], *sums), 0,
+            )
+        prev_a, next_b = turn(own[0], 1, view_count), turn(own[1], -1, view_count)
+        prev_b, next_a = turn(own[1], 1, view_count), turn(own[0], -1, view_count)
+        far_a, far_b = turn(prev_a, 1, view_count), turn(next_b, -1, view_count)
+        pieces = (*own, next_a, next_b, far_a, far_b, prev_a, prev_b)
+    return call(
+        functools.partial(join_kernel, view_count), "join", [f32(x_cells, y_cells, z_cells)],
+        (v, *pieces),
+    )[0]
 
 
 def solution(mesh):

time: 336 us -> 237 us (0.71)
  other arithmetic: 72.4 us -> 0.12 us
  waiting for transfers between devices: 157 us -> 92.8 us
  starting transfers between devices: 57.9 us -> 93.8 us
  Pallas kernels: 22.3 us -> 44.8 us
  between operations: 15 us -> 1.01 us
  local copies, waits for them, and re-layouts: 9.94 us -> 2.77 us
    psum x2 -> x0, waiting for transfers between devices: 101 us -> none  [per_device(): combined = lax.psum(projected, 'views')]
    add x10 -> x0, other arithmetic: 56.4 us -> none  [axis_blur(): result + weights[offset] * lax.slice_in_dim(volume, offset, offset + leng...]
    ppermute x16 -> x40, waiting for transfers between devices: 55.3 us -> 92.8 us  [the longest x16 69.1 us: exchange(): return (lax.ppermute(last, axis, up), lax.ppermute(first, axis, down))]
    ppermute x16 -> x40, starting transfers between devices: 46.1 us -> 81.9 us  [the longest x16 45.6 us: exchange(): return (lax.ppermute(last, axis, up), lax.ppermute(first, axis, down))]
    pallas_call x0 -> x15, Pallas kernels: none -> 22.4 us  [call(): pl.pallas_call(kernel, out_shape=outs, in_specs=[smem()] * scalars + [vme...]
    div x5 -> x1, other arithmetic: 15.8 us -> 0.01 us  [per_device(): w = (psf_taps[0] / jnp.sum(psf_taps[0], axis=1, keepdims=True)).reshape(-1)]
    slice x11 -> x0, local copies, waits for them, and re-layouts: 4.87 us -> none  [the longest x8 2.11 us: with_halo(): last = lax.slice_in_dim(value, length - width, length, axis=dim)]
  transfers between devices with their start and end apart: 19 -> 41, of which waited for: 14 -> 28; matrix products, arithmetic and copies ran while one was open for 5% -> 0% of each run, Pallas kernels for 0% -> 7%
where the time goes in v3:
time: 237 us; the launch traced here: 235 us
  starting transfers between devices  93.8 us (40%)
  waiting for transfers between devices  92.8 us (39%)
  Pallas kernels  44.8 us (19%)
  local copies, waits for them, and re-layouts  2.77 us (1%)
    ppermute x16, waiting for transfers between devices, exchange(): return (lax.ppermute(last, axis, up), lax.ppermute(first, axis, down))  69.1 us
    ppermute x16, starting transfers between devices, exchange(): return (lax.ppermute(last, axis, up), lax.ppermute(first, axis, down))  45.6 us
    ppermute x24, starting transfers between devices, turn(): lax.ppermute(value, 'views', [(i, (i + step) % count) for i in range(coun...  36.3 us
    ppermute x24, waiting for transfers between devices, turn(): lax.ppermute(value, 'views', [(i, (i + step) % count) for i in range(coun...  23.8 us
    pallas_call x15, Pallas kernels, call(): pl.pallas_call(kernel, out_shape=outs, in_specs=[smem()] * scalars + [vme...  22.4 us
    all_to_all x1, starting transfers between devices, per_device(): lax.all_to_all(outgoing.reshape(peer_count, capacity + 1, 1, BRICK), ('bl...  11.9 us
    pallas_call x1, Pallas kernels, pack(): pl.pallas_call(functools.partial(pack_kernel, geo), out_shape=jax.ShapeDt...  11.3 us
    pallas_call x1, Pallas kernels, unpack(): pl.pallas_call(functools.partial(unpack_kernel, peers, cap, slots), out_s...  11.1 us
  transfers between devices with their start and end apart: 41, of which 28 were waited for; matrix products, arithmetic and copies ran while one was open for 0% of the time, Pallas kernels for 7%

profile of v3, /device:TPU:34, one launch (start us, length us, event | category | flops | bytes accessed | tf_op | source)
XLA Modules:
  0.0 235.2 jit_solution(13548826508302358647)
XLA Ops:
  1.9 11.3 %pack.1 = f32[4160,1,128]{2,1,0:T(1,128)} custom-call(s32[1]{0:T(128)S(6)} %copy.9.shift_ref, s32[16,128]{1,0:T(8,128)} %bitcast.12, f32[8,128,256]{2,1,0:T(8,128)} %bitcast.11), custom_call_target="tpu_custom_call" | custom-call | tf_op jit(solution)/shard_map/pack/pallas_call | solution.py:84
  13.2 11.9 %all-to-all-start = ((f32[64,65,1,128]{3,2,1,0:T(1,128)}), f32[64,65,1,128]{3,2,1,0:T(1,128)}, u32[]{:S(2)}, u32[]{:S(2)}) async-start(f32[64,65,1,128]{3,2,1,0:T(1,128)} %bitcast.10), calls=%async_computation | async-start | bytes 4259840 | tf_op jit(solution)/shard_map/all_to_all | solution.py:413
  25.5 2.7 %z_blur.1 = (f32[2,8,128,128]{3,2,1,0:T(8,128)S(1)}, f32[2,8,8,128]{3,2,1,0:T(8,128)S(1)}, f32[2,8,8,128]{3,2,1,0:T(8,128)S(1)}) custom-call(f32[21]{0:T(128)S(1)} %div.13.w_ref, f32[8,128,256]{2,1,0:T(8,128)S(1)} %copy-done.2), custom_call_target="tpu_custom_call" | custom-call | flops 4000000 | bytes 4000000 | tf_op jit(solution)/shard_map/z_blur/pallas_call | solution.py:160
  28.2 3.4 %collective-permute-start = (f32[2,8,8,128]{3,2,1,0:T(8,128)S(1)}, f32[2,8,8,128]{3,2,1,0:T(8,128)S(1)}, u32[]{:S(2)}, u32[]{:S(2)}) collective-permute-start(f32[2,8,8,128]{3,2,1,0:T(8,128)S(1)} %get-tuple-element.54), channel_id=1, source_target_pairs={{0,32},{32,64},{64,96},{96,128},{128,160},{160,192},{192,224},{1,3... | collective-permute-start | bytes 196616 | tf_op jit(solution)/shard_map/ppermute | solution.py:394
  34.1 38.6 %collective-permute-done.lo = f32[2,8,8,128]{3,2,1,0:T(8,128)S(1)} collective-permute-done((f32[2,8,8,128]{3,2,1,0:T(8,128)S(1)}, f32[2,8,8,128]{3,2,1,0:T(8,128)S(1)}, u32[]{:S(2)}, u32[]{:S(2)}) %collective-permute-start) | collective-permute-done | bytes 65568 | tf_op jit(solution)/shard_map/ppermute | solution.py:394
  77.3 3.6 %collective-permute-start.3 = (f32[2,3,128,128]{3,2,1,0:T(8,128)S(1)}, f32[2,3,128,128]{3,2,1,0:T(8,128)S(1)}, u32[]{:S(2)}, u32[]{:S(2)}) collective-permute-start(f32[2,3,128,128]{3,2,1,0:T(8,128)S(1)} %get-tuple-element.58), channel_id=1, source_target_pairs={{1,0},{2,1},{3,2},{4,3},{5,4},{6,5},{7,6},{9,8},{10,9},{11,10},{12... | collective-permute-start | bytes 1179656 | tf_op jit(solution)/shard_map/ppermute | solution.py:394
  81.0 11.1 %unpack.1.obs = f32[2056,128]{1,0:T(8,128)} custom-call(f32[4160,1,128]{2,1,0:T(1,128)} %bitcast.6.in_ref), custom_call_target="tpu_custom_call" | custom-call | tf_op jit(solution)/shard_map/unpack/pallas_call | solution.py:132
  93.3 3.5 %ratio.2 = (f32[2,8,128,128]{3,2,1,0:T(8,128)S(1)}, f32[2,8,8,128]{3,2,1,0:T(8,128)S(1)}, f32[2,8,8,128]{3,2,1,0:T(8,128)S(1)}) custom-call(f32[21]{0:T(128)S(1)} %div.13.w_ref, f32[2,8,128,128]{3,2,1,0:T(8,128)S(1)} %get-tuple-element.56.field, f32[2,3,128,128]{3,2,1,0:T(8,128)S(1)} %collective-permute-done.2.lo, ...), custom_call_target="tpu_custom_call" | custom-call | flops 8000000 | bytes 8000000 | tf_op jit(solution)/shard_map/ratio/pallas_call | solution.py:160
  96.9 3.5 %collective-permute-start.4 = (f32[2,8,8,128]{3,2,1,0:T(8,128)S(1)}, f32[2,8,8,128]{3,2,1,0:T(8,128)S(1)}, u32[]{:S(2)}, u32[]{:S(2)}) collective-permute-start(f32[2,8,8,128]{3,2,1,0:T(8,128)S(1)} %get-tuple-element.60), channel_id=1, source_target_pairs={{0,32},{32,64},{64,96},{96,128},{128,160},{160,192},{192,224},{1,3... | collective-permute-start | bytes 196616 | tf_op jit(solution)/shard_map/ppermute | solution.py:394
  103.0 4.9 %collective-permute-done.5.hi = f32[2,8,8,128]{3,2,1,0:T(8,128)S(1)} collective-permute-done((f32[2,8,8,128]{3,2,1,0:T(8,128)S(1)}, f32[2,8,8,128]{3,2,1,0:T(8,128)S(1)}, u32[]{:S(2)}, u32[]{:S(2)}) %collective-permute-start.5) | collective-permute-done | bytes 65568 | tf_op jit(solution)/shard_map/ppermute | solution.py:394
  111.7 3.6 %collective-permute-start.7 = (f32[2,3,128,128]{3,2,1,0:T(8,128)S(1)}, f32[2,3,128,128]{3,2,1,0:T(8,128)S(1)}, u32[]{:S(2)}, u32[]{:S(2)}) collective-permute-start(f32[2,3,128,128]{3,2,1,0:T(8,128)S(1)} %get-tuple-element.64), channel_id=1, source_target_pairs={{1,0},{2,1},{3,2},{4,3},{5,4},{6,5},{7,6},{9,8},{10,9},{11,10},{12... | collective-permute-start | bytes 1179656 | tf_op jit(solution)/shard_map/ppermute | solution.py:394
  115.4 3.7 %collective-permute-done.6.lo = f32[2,3,128,128]{3,2,1,0:T(8,128)S(1)} collective-permute-done((f32[2,3,128,128]{3,2,1,0:T(8,128)}, f32[2,3,128,128]{3,2,1,0:T(8,128)S(1)}, u32[]{:S(2)}, u32[]{:S(2)}) %collective-permute-start.6) | collective-permute-done | bytes 393248 | tf_op jit(solution)/shard_map/ppermute | solution.py:394
  122.0 3.2 %collective-permute-start.10 = (f32[2,128,128]{2,1,0:T(8,128)S(1)}, f32[2,128,128]{2,1,0:T(8,128)S(1)}, u32[]{:S(2)}, u32[]{:S(2)}) collective-permute-start(f32[2,128,128]{2,1,0:T(8,128)S(1)} %get-tuple-element.70), channel_id=1, source_target_pairs={{0,24},{8,0},{16,8},{24,16},{1,25},{9,1},{17,9},{25,17},{2,26},{10... | collective-permute-start | bytes 393224 | tf_op jit(solution)/shard_map/ppermute | solution.py:398
  125.7 2.7 %collective-permute-start.8 = (f32[2,128,128]{2,1,0:T(8,128)S(1)}, f32[2,128,128]{2,1,0:T(8,128)S(1)}, u32[]{:S(2)}, u32[]{:S(2)}) collective-permute-start(f32[2,128,128]{2,1,0:T(8,128)S(1)} %get-tuple-element.66), channel_id=1, source_target_pairs={{0,24},{8,0},{16,8},{24,16},{1,25},{9,1},{17,9},{25,17},{2,26},{10... | collective-permute-start | bytes 393224 | tf_op jit(solution)/shard_map/ppermute | solution.py:398
  128.5 3.9 %collective-permute-done.9.ra = f32[2,128,128]{2,1,0:T(8,128)S(1)} collective-permute-done((f32[2,128,128]{2,1,0:T(8,128)S(1)}, f32[2,128,128]{2,1,0:T(8,128)S(1)}, u32[]{:S(2)}, u32[]{:S(2)}) %collective-permute-start.9) | collective-permute-done | bytes 131104 | tf_op jit(solution)/shard_map/ppermute | solution.py:398
  132.5 3.2 %collective-permute-start.13 = (f32[2,128,128]{2,1,0:T(8,128)S(1)}, f32[2,128,128]{2,1,0:T(8,128)S(1)}, u32[]{:S(2)}, u32[]{:S(2)}) collective-permute-start(f32[2,128,128]{2,1,0:T(8,128)S(1)} %get-tuple-element.74), channel_id=1, source_target_pairs={{0,24},{8,0},{16,8},{24,16},{1,25},{9,1},{17,9},{25,17},{2,26},{10... | collective-permute-start | bytes 393224 | tf_op jit(solution)/shard_map/ppermute | solution.py:398
  135.7 4.3 %collective-permute-done.11.a2 = f32[2,128,128]{2,1,0:T(8,128)S(1)} collective-permute-done((f32[2,128,128]{2,1,0:T(8,128)S(1)}, f32[2,128,128]{2,1,0:T(8,128)S(1)}, u32[]{:S(2)}, u32[]{:S(2)}) %collective-permute-start.11) | collective-permute-done | bytes 131104 | tf_op jit(solution)/shard_map/ppermute | solution.py:398
  140.2 3.2 %collective-permute-start.15 = (f32[2,128,128]{2,1,0:T(8,128)S(1)}, f32[2,128,128]{2,1,0:T(8,128)S(1)}, u32[]{:S(2)}, u32[]{:S(2)}) collective-permute-start(f32[2,128,128]{2,1,0:T(8,128)S(1)} %get-tuple-element.76.refs_1_.est_b), channel_id=1, source_target_pairs={{0,24},{8,0},{16,8},{24,16},{1,25},{9,1},{17,9},{25,17},{2,26},{10... | collective-permute-start | bytes 393224 | tf_op jit(solution)/shard_map/ppermute | solution.py:398
  147.3 3.7 %collective-permute-start.18 = (f32[2,128,128]{2,1,0:T(8,128)S(1)}, f32[2,128,128]{2,1,0:T(8,128)S(1)}, u32[]{:S(2)}, u32[]{:S(2)}) collective-permute-start(f32[2,128,128]{2,1,0:T(8,128)S(1)} %collective-permute-done.15.refs_3_), channel_id=1, source_target_pairs={{0,24},{8,0},{16,8},{24,16},{1,25},{9,1},{17,9},{25,17},{2,26},{10... | collective-permute-start | bytes 393224 | tf_op jit(solution)/shard_map/ppermute | solution.py:398
  154.2 2.7 %z_blur_pieces.1 = (f32[2,8,128,128]{3,2,1,0:T(8,128)S(1)}, f32[2,8,8,128]{3,2,1,0:T(8,128)S(1)}, f32[2,8,8,128]{3,2,1,0:T(8,128)S(1)}) custom-call(f32[21]{0:T(128)S(1)} %div.13.w_ref, s32[1]{0:T(128)} %bitcast.v_ref, f32[2,128,128]{2,1,0:T(8,128)S(1)} %get-tuple-element.75.refs_0_.est_a, f32[2,128,128]{2,1,0:T(8,128)S(1)} %get-tuple-element.76.refs_1_.est_b, ...), custom_call_target="tpu_custom_call" | custom-call | flops 4000000 | bytes 4000000 | tf_op jit(solution)/shard_map/z_blur_pieces/pallas_call | solution.py:160
  156.9 3.9 %collective-permute-start.20 = (f32[2,8,8,128]{3,2,1,0:T(8,128)S(1)}, f32[2,8,8,128]{3,2,1,0:T(8,128)S(1)}, u32[]{:S(2)}, u32[]{:S(2)}) collective-permute-start(f32[2,8,8,128]{3,2,1,0:T(8,128)S(1)} %get-tuple-element.78), channel_id=1, source_target_pairs={{0,32},{32,64},{64,96},{96,128},{128,160},{160,192},{192,224},{1,3... | collective-permute-start | bytes 196616 | tf_op jit(solution)/shard_map/ppermute | solution.py:394
  163.0 3.9 %collective-permute-done.21.hi = f32[2,8,8,128]{3,2,1,0:T(8,128)S(1)} collective-permute-done((f32[2,8,8,128]{3,2,1,0:T(8,128)S(1)}, f32[2,8,8,128]{3,2,1,0:T(8,128)S(1)}, u32[]{:S(2)}, u32[]{:S(2)}) %collective-permute-start.21) | collective-permute-done | bytes 65568 | tf_op jit(solution)/shard_map/ppermute | solution.py:394
  170.0 3.6 %collective-permute-start.23 = (f32[2,3,128,128]{3,2,1,0:T(8,128)S(1)}, f32[2,3,128,128]{3,2,1,0:T(8,128)S(1)}, u32[]{:S(2)}, u32[]{:S(2)}) collective-permute-start(f32[2,3,128,128]{3,2,1,0:T(8,128)S(1)} %get-tuple-element.82), channel_id=1, source_target_pairs={{1,0},{2,1},{3,2},{4,3},{5,4},{6,5},{7,6},{9,8},{10,9},{11,10},{12... | collective-permute-start | bytes 1179656 | tf_op jit(solution)/shard_map/ppermute | solution.py:394
  173.7 3.5 %collective-permute-done.22.lo = f32[2,3,128,128]{3,2,1,0:T(8,128)S(1)} collective-permute-done((f32[2,3,128,128]{3,2,1,0:T(8,128)S(1)}, f32[2,3,128,128]{3,2,1,0:T(8,128)S(1)}, u32[]{:S(2)}, u32[]{:S(2)}) %collective-permute-start.22) | collective-permute-done | bytes 393248 | tf_op jit(solution)/shard_map/ppermute | solution.py:394
  178.9 3.5 %ratio.3 = (f32[2,8,128,128]{3,2,1,0:T(8,128)S(1)}, f32[2,8,8,128]{3,2,1,0:T(8,128)S(1)}, f32[2,8,8,128]{3,2,1,0:T(8,128)S(1)}) custom-call(f32[21]{0:T(128)S(1)} %div.13.w_ref, f32[2,8,128,128]{3,2,1,0:T(8,128)S(1)} %get-tuple-element.80.field, f32[2,3,128,128]{3,2,1,0:T(8,128)S(1)} %collective-permute-done.22.lo, ...), custom_call_target="tpu_custom_call" | custom-call | flops 8000000 | bytes 8000000 | tf_op jit(solution)/shard_map/ratio/pallas_call | solution.py:160
  182.5 3.7 %collective-permute-start.24 = (f32[2,8,8,128]{3,2,1,0:T(8,128)S(1)}, f32[2,8,8,128]{3,2,1,0:T(8,128)S(1)}, u32[]{:S(2)}, u32[]{:S(2)}) collective-permute-start(f32[2,8,8,128]{3,2,1,0:T(8,128)S(1)} %get-tuple-element.84), channel_id=1, source_target_pairs={{0,32},{32,64},{64,96},{96,128},{128,160},{160,192},{192,224},{1,3... | collective-permute-start | bytes 196616 | tf_op jit(solution)/shard_map/ppermute | solution.py:394
  189.2 3.5 %collective-permute-done.25.hi = f32[2,8,8,128]{3,2,1,0:T(8,128)S(1)} collective-permute-done((f32[2,8,8,128]{3,2,1,0:T(8,128)S(1)}, f32[2,8,8,128]{3,2,1,0:T(8,128)S(1)}, u32[]{:S(2)}, u32[]{:S(2)}) %collective-permute-start.25) | collective-permute-done | bytes 65568 | tf_op jit(solution)/shard_map/ppermute | solution.py:394
  195.7 3.6 %collective-permute-start.27 = (f32[2,3,128,128]{3,2,1,0:T(8,128)S(1)}, f32[2,3,128,128]{3,2,1,0:T(8,128)S(1)}, u32[]{:S(2)}, u32[]{:S(2)}) collective-permute-start(f32[2,3,128,128]{3,2,1,0:T(8,128)S(1)} %get-tuple-element.88), channel_id=1, source_target_pairs={{1,0},{2,1},{3,2},{4,3},{5,4},{6,5},{7,6},{9,8},{10,9},{11,10},{12... | collective-permute-start | bytes 1179656 | tf_op jit(solution)/shard_map/ppermute | solution.py:394
  199.4 3.5 %collective-permute-done.26.lo = f32[2,3,128,128]{3,2,1,0:T(8,128)S(1)} collective-permute-done((f32[2,3,128,128]{3,2,1,0:T(8,128)S(1)}, f32[2,3,128,128]{3,2,1,0:T(8,128)S(1)}, u32[]{:S(2)}, u32[]{:S(2)}) %collective-permute-start.26) | collective-permute-done | bytes 393248 | tf_op jit(solution)/shard_map/ppermute | solution.py:394
  206.1 3.3 %collective-permute-start.30 = (f32[2,128,128]{2,1,0:T(8,128)S(1)}, f32[2,128,128]{2,1,0:T(8,128)S(1)}, u32[]{:S(2)}, u32[]{:S(2)}) collective-permute-start(f32[2,128,128]{2,1,0:T(8,128)S(1)} %get-tuple-element.94), channel_id=1, source_target_pairs={{0,24},{8,0},{16,8},{24,16},{1,25},{9,1},{17,9},{25,17},{2,26},{10... | collective-permute-start | bytes 393224 | tf_op jit(solution)/shard_map/ppermute | solution.py:398
  218.1 2.8 %collective-permute-done.31.a2 = f32[2,128,128]{2,1,0:T(8,128)S(1)} collective-permute-done((f32[2,128,128]{2,1,0:T(8,128)S(1)}, f32[2,128,128]{2,1,0:T(8,128)S(1)}, u32[]{:S(2)}, u32[]{:S(2)}) %collective-permute-start.31) | collective-permute-done | bytes 131104 | tf_op jit(solution)/shard_map/ppermute | solution.py:398
  228.6 3.0 %collective-permute-start.38 = (f32[2,128,128]{2,1,0:T(8,128)S(1)}, f32[2,128,128]{2,1,0:T(8,128)S(1)}, u32[]{:S(2)}, u32[]{:S(2)}) collective-permute-start(f32[2,128,128]{2,1,0:T(8,128)S(1)} %collective-permute-done.35.refs_3_), channel_id=1, source_target_pairs={{0,24},{8,0},{16,8},{24,16},{1,25},{9,1},{17,9},{25,17},{2,26},{10... | collective-permute-start | bytes 393224 | tf_op jit(solution)/shard_map/ppermute | solution.py:398
  (81 shorter events, 63.3 us)
Async XLA Ops:
  13.2 67.7 %all-to-all-start = ((f32[64,65,1,128]{3,2,1,0:T(1,128)}), f32[64,65,1,128]{3,2,1,0:T(1,128)}, u32[]{:S(2)}, u32[]{:S(2)}) async-start(f32[64,65,1,128]{3,2,1,0:T(1,128)} %bitcast.10), calls=%async_computation | async-start | bytes 4259840 | tf_op jit(solution)/shard_map/all_to_all | solution.py:413
  28.2 44.5 %collective-permute-start = (f32[2,8,8,128]{3,2,1,0:T(8,128)S(1)}, f32[2,8,8,128]{3,2,1,0:T(8,128)S(1)}, u32[]{:S(2)}, u32[]{:S(2)}) collective-permute-start(f32[2,8,8,128]{3,2,1,0:T(8,128)S(1)} %get-tuple-element.54), channel_id=1, source_target_pairs={{0,32},{32,64},{64,96},{96,128},{128,160},{160,192},{192,224},{1,3... | collective-permute-start | bytes 196616 | tf_op jit(solution)/shard_map/ppermute | solution.py:394
  31.6 41.9 %collective-permute-start.1 = (f32[2,8,8,128]{3,2,1,0:T(8,128)S(1)}, f32[2,8,8,128]{3,2,1,0:T(8,128)S(1)}, u32[]{:S(2)}, u32[]{:S(2)}) collective-permute-start(f32[2,8,8,128]{3,2,1,0:T(8,128)S(1)} %get-tuple-element.55), channel_id=1, source_target_pairs={{32,0},{64,32},{96,64},{128,96},{160,128},{192,160},{224,192},{33,... | collective-permute-start | bytes 196616 | tf_op jit(solution)/shard_map/ppermute | solution.py:394
  75.4 16.7 %collective-permute-start.2 = (f32[2,3,128,128]{3,2,1,0:T(8,128)}, f32[2,3,128,128]{3,2,1,0:T(8,128)S(1)}, u32[]{:S(2)}, u32[]{:S(2)}) collective-permute-start(f32[2,3,128,128]{3,2,1,0:T(8,128)} %get-tuple-element.57), channel_id=1, source_target_pairs={{0,1},{1,2},{2,3},{3,4},{4,5},{5,6},{6,7},{8,9},{9,10},{10,11},{11... | collective-permute-start | bytes 1179656 | tf_op jit(solution)/shard_map/ppermute | solution.py:394
  77.3 14.8 %collective-permute-start.3 = (f32[2,3,128,128]{3,2,1,0:T(8,128)S(1)}, f32[2,3,128,128]{3,2,1,0:T(8,128)S(1)}, u32[]{:S(2)}, u32[]{:S(2)}) collective-permute-start(f32[2,3,128,128]{3,2,1,0:T(8,128)S(1)} %get-tuple-element.58), channel_id=1, source_target_pairs={{1,0},{2,1},{3,2},{4,3},{5,4},{6,5},{7,6},{9,8},{10,9},{11,10},{12... | collective-permute-start | bytes 1179656 | tf_op jit(solution)/shard_map/ppermute | solution.py:394
  100.4 7.6 %collective-permute-start.5 = (f32[2,8,8,128]{3,2,1,0:T(8,128)S(1)}, f32[2,8,8,128]{3,2,1,0:T(8,128)S(1)}, u32[]{:S(2)}, u32[]{:S(2)}) collective-permute-start(f32[2,8,8,128]{3,2,1,0:T(8,128)S(1)} %get-tuple-element.61), channel_id=1, source_target_pairs={{32,0},{64,32},{96,64},{128,96},{160,128},{192,160},{224,192},{33,... | collective-permute-start | bytes 196616 | tf_op jit(solution)/shard_map/ppermute | solution.py:394
  109.8 9.3 %collective-permute-start.6 = (f32[2,3,128,128]{3,2,1,0:T(8,128)}, f32[2,3,128,128]{3,2,1,0:T(8,128)S(1)}, u32[]{:S(2)}, u32[]{:S(2)}) collective-permute-start(f32[2,3,128,128]{3,2,1,0:T(8,128)} %get-tuple-element.63), channel_id=1, source_target_pairs={{0,1},{1,2},{2,3},{3,4},{4,5},{5,6},{6,7},{8,9},{9,10},{10,11},{11... | collective-permute-start | bytes 1179656 | tf_op jit(solution)/shard_map/ppermute | solution.py:394
  111.7 8.9 %collective-permute-start.7 = (f32[2,3,128,128]{3,2,1,0:T(8,128)S(1)}, f32[2,3,128,128]{3,2,1,0:T(8,128)S(1)}, u32[]{:S(2)}, u32[]{:S(2)}) collective-permute-start(f32[2,3,128,128]{3,2,1,0:T(8,128)S(1)} %get-tuple-element.64), channel_id=1, source_target_pairs={{1,0},{2,1},{3,2},{4,3},{5,4},{6,5},{7,6},{9,8},{10,9},{11,10},{12... | collective-permute-start | bytes 1179656 | tf_op jit(solution)/shard_map/ppermute | solution.py:394
  125.2 7.1 %collective-permute-start.9 = (f32[2,128,128]{2,1,0:T(8,128)S(1)}, f32[2,128,128]{2,1,0:T(8,128)S(1)}, u32[]{:S(2)}, u32[]{:S(2)}) collective-permute-start(f32[2,128,128]{2,1,0:T(8,128)S(1)} %get-tuple-element.68), channel_id=1, source_target_pairs={{0,8},{8,16},{16,24},{24,0},{1,9},{9,17},{17,25},{25,1},{2,10},{10... | collective-permute-start | bytes 393224 | tf_op jit(solution)/shard_map/ppermute | solution.py:398
  125.2 10.5 %collective-permute-start.12 = (f32[2,128,128]{2,1,0:T(8,128)S(1)}, f32[2,128,128]{2,1,0:T(8,128)S(1)}, u32[]{:S(2)}, u32[]{:S(2)}) collective-permute-start(f32[2,128,128]{2,1,0:T(8,128)S(1)} %get-tuple-element.73), channel_id=1, source_target_pairs={{0,8},{8,16},{16,24},{24,0},{1,9},{9,17},{17,25},{25,1},{2,10},{10... | collective-permute-start | bytes 393224 | tf_op jit(solution)/shard_map/ppermute | solution.py:398
  125.7 10.0 %collective-permute-start.8 = (f32[2,128,128]{2,1,0:T(8,128)S(1)}, f32[2,128,128]{2,1,0:T(8,128)S(1)}, u32[]{:S(2)}, u32[]{:S(2)}) collective-permute-start(f32[2,128,128]{2,1,0:T(8,128)S(1)} %get-tuple-element.66), channel_id=1, source_target_pairs={{0,24},{8,0},{16,8},{24,16},{1,25},{9,1},{17,9},{25,17},{2,26},{10... | collective-permute-start | bytes 393224 | tf_op jit(solution)/shard_map/ppermute | solution.py:398
  132.4 7.6 %collective-permute-start.11 = (f32[2,128,128]{2,1,0:T(8,128)S(1)}, f32[2,128,128]{2,1,0:T(8,128)S(1)}, u32[]{:S(2)}, u32[]{:S(2)}) collective-permute-start(f32[2,128,128]{2,1,0:T(8,128)S(1)} %get-tuple-element.71), channel_id=1, source_target_pairs={{0,8},{8,16},{16,24},{24,0},{1,9},{9,17},{17,25},{25,1},{2,10},{10... | collective-permute-start | bytes 393224 | tf_op jit(solution)/shard_map/ppermute | solution.py:398
  132.5 7.6 %collective-permute-start.13 = (f32[2,128,128]{2,1,0:T(8,128)S(1)}, f32[2,128,128]{2,1,0:T(8,128)S(1)}, u32[]{:S(2)}, u32[]{:S(2)}) collective-permute-start(f32[2,128,128]{2,1,0:T(8,128)S(1)} %get-tuple-element.74), channel_id=1, source_target_pairs={{0,24},{8,0},{16,8},{24,16},{1,25},{9,1},{17,9},{25,17},{2,26},{10... | collective-permute-start | bytes 393224 | tf_op jit(solution)/shard_map/ppermute | solution.py:398
  140.1 6.8 %collective-permute-start.16 = (f32[2,128,128]{2,1,0:T(8,128)S(1)}, f32[2,128,128]{2,1,0:T(8,128)S(1)}, u32[]{:S(2)}, u32[]{:S(2)}) collective-permute-start(f32[2,128,128]{2,1,0:T(8,128)S(1)} %get-tuple-element.75.refs_0_.est_a), channel_id=1, source_target_pairs={{0,8},{8,16},{16,24},{24,0},{1,9},{9,17},{17,25},{25,1},{2,10},{10... | collective-permute-start | bytes 393224 | tf_op jit(solution)/shard_map/ppermute | solution.py:398
  140.2 7.1 %collective-permute-start.15 = (f32[2,128,128]{2,1,0:T(8,128)S(1)}, f32[2,128,128]{2,1,0:T(8,128)S(1)}, u32[]{:S(2)}, u32[]{:S(2)}) collective-permute-start(f32[2,128,128]{2,1,0:T(8,128)S(1)} %get-tuple-element.76.refs_1_.est_b), channel_id=1, source_target_pairs={{0,24},{8,0},{16,8},{24,16},{1,25},{9,1},{17,9},{25,17},{2,26},{10... | collective-permute-start | bytes 393224 | tf_op jit(solution)/shard_map/ppermute | solution.py:398
  143.4 7.6 %collective-permute-start.14 = (f32[2,128,128]{2,1,0:T(8,128)S(1)}, f32[2,128,128]{2,1,0:T(8,128)S(1)}, u32[]{:S(2)}, u32[]{:S(2)}) collective-permute-start(f32[2,128,128]{2,1,0:T(8,128)S(1)} %get-tuple-element.75.refs_0_.est_a), channel_id=1, source_target_pairs={{0,24},{8,0},{16,8},{24,16},{1,25},{9,1},{17,9},{25,17},{2,26},{10... | collective-permute-start | bytes 393224 | tf_op jit(solution)/shard_map/ppermute | solution.py:398
  145.2 7.5 %collective-permute-start.19 = (f32[2,128,128]{2,1,0:T(8,128)S(1)}, f32[2,128,128]{2,1,0:T(8,128)S(1)}, u32[]{:S(2)}, u32[]{:S(2)}) collective-permute-start(f32[2,128,128]{2,1,0:T(8,128)S(1)} %get-tuple-element.76.refs_1_.est_b), channel_id=1, source_target_pairs={{0,8},{8,16},{16,24},{24,0},{1,9},{9,17},{17,25},{25,1},{2,10},{10... | collective-permute-start | bytes 393224 | tf_op jit(solution)/shard_map/ppermute | solution.py:398
  146.9 7.3 %collective-permute-start.17 = (f32[2,128,128]{2,1,0:T(8,128)S(1)}, f32[2,128,128]{2,1,0:T(8,128)S(1)}, u32[]{:S(2)}, u32[]{:S(2)}) collective-permute-start(f32[2,128,128]{2,1,0:T(8,128)S(1)} %collective-permute-done.16.refs_6_), channel_id=1, source_target_pairs={{0,8},{8,16},{16,24},{24,0},{1,9},{9,17},{17,25},{25,1},{2,10},{10... | collective-permute-start | bytes 393224 | tf_op jit(solution)/shard_map/ppermute | solution.py:398
  147.3 6.8 %collective-permute-start.18 = (f32[2,128,128]{2,1,0:T(8,128)S(1)}, f32[2,128,128]{2,1,0:T(8,128)S(1)}, u32[]{:S(2)}, u32[]{:S(2)}) collective-permute-start(f32[2,128,128]{2,1,0:T(8,128)S(1)} %collective-permute-done.15.refs_3_), channel_id=1, source_target_pairs={{0,24},{8,0},{16,8},{24,16},{1,25},{9,1},{17,9},{25,17},{2,26},{10... | collective-permute-start | bytes 393224 | tf_op jit(solution)/shard_map/ppermute | solution.py:398
  168.1 9.1 %collective-permute-start.22 = (f32[2,3,128,128]{3,2,1,0:T(8,128)S(1)}, f32[2,3,128,128]{3,2,1,0:T(8,128)S(1)}, u32[]{:S(2)}, u32[]{:S(2)}) collective-permute-start(f32[2,3,128,128]{3,2,1,0:T(8,128)S(1)} %get-tuple-element.81), channel_id=1, source_target_pairs={{0,1},{1,2},{2,3},{3,4},{4,5},{5,6},{6,7},{8,9},{9,10},{10,11},{11... | collective-permute-start | bytes 1179656 | tf_op jit(solution)/shard_map/ppermute | solution.py:394
  170.0 8.9 %collective-permute-start.23 = (f32[2,3,128,128]{3,2,1,0:T(8,128)S(1)}, f32[2,3,128,128]{3,2,1,0:T(8,128)S(1)}, u32[]{:S(2)}, u32[]{:S(2)}) collective-permute-start(f32[2,3,128,128]{3,2,1,0:T(8,128)S(1)} %get-tuple-element.82), channel_id=1, source_target_pairs={{1,0},{2,1},{3,2},{4,3},{5,4},{6,5},{7,6},{9,8},{10,9},{11,10},{12... | collective-permute-start | bytes 1179656 | tf_op jit(solution)/shard_map/ppermute | solution.py:394
  182.5 6.7 %collective-permute-start.24 = (f32[2,8,8,128]{3,2,1,0:T(8,128)S(1)}, f32[2,8,8,128]{3,2,1,0:T(8,128)S(1)}, u32[]{:S(2)}, u32[]{:S(2)}) collective-permute-start(f32[2,8,8,128]{3,2,1,0:T(8,128)S(1)} %get-tuple-element.84), channel_id=1, source_target_pairs={{0,32},{32,64},{64,96},{96,128},{128,160},{160,192},{192,224},{1,3... | collective-permute-start | bytes 196616 | tf_op jit(solution)/shard_map/ppermute | solution.py:394
  193.8 9.1 %collective-permute-start.26 = (f32[2,3,128,128]{3,2,1,0:T(8,128)S(1)}, f32[2,3,128,128]{3,2,1,0:T(8,128)S(1)}, u32[]{:S(2)}, u32[]{:S(2)}) collective-permute-start(f32[2,3,128,128]{3,2,1,0:T(8,128)S(1)} %get-tuple-element.87), channel_id=1, source_target_pairs={{0,1},{1,2},{2,3},{3,4},{4,5},{5,6},{6,7},{8,9},{9,10},{10,11},{11... | collective-permute-start | bytes 1179656 | tf_op jit(solution)/shard_map/ppermute | solution.py:394
  195.7 8.9 %collective-permute-start.27 = (f32[2,3,128,128]{3,2,1,0:T(8,128)S(1)}, f32[2,3,128,128]{3,2,1,0:T(8,128)S(1)}, u32[]{:S(2)}, u32[]{:S(2)}) collective-permute-start(f32[2,3,128,128]{3,2,1,0:T(8,128)S(1)} %get-tuple-element.88), channel_id=1, source_target_pairs={{1,0},{2,1},{3,2},{4,3},{5,4},{6,5},{7,6},{9,8},{10,9},{11,10},{12... | collective-permute-start | bytes 1179656 | tf_op jit(solution)/shard_map/ppermute | solution.py:394
  206.0 7.4 %collective-permute-start.29 = (f32[2,128,128]{2,1,0:T(8,128)S(1)}, f32[2,128,128]{2,1,0:T(8,128)S(1)}, u32[]{:S(2)}, u32[]{:S(2)}) collective-permute-start(f32[2,128,128]{2,1,0:T(8,128)S(1)} %get-tuple-element.92), channel_id=1, source_target_pairs={{0,8},{8,16},{16,24},{24,0},{1,9},{9,17},{17,25},{25,1},{2,10},{10... | collective-permute-start | bytes 393224 | tf_op jit(solution)/shard_map/ppermute | solution.py:398
  206.1 7.3 %collective-permute-start.30 = (f32[2,128,128]{2,1,0:T(8,128)S(1)}, f32[2,128,128]{2,1,0:T(8,128)S(1)}, u32[]{:S(2)}, u32[]{:S(2)}) collective-permute-start(f32[2,128,128]{2,1,0:T(8,128)S(1)} %get-tuple-element.94), channel_id=1, source_target_pairs={{0,24},{8,0},{16,8},{24,16},{1,25},{9,1},{17,9},{25,17},{2,26},{10... | collective-permute-start | bytes 393224 | tf_op jit(solution)/shard_map/ppermute | solution.py:398
  209.4 7.8 %collective-permute-start.28 = (f32[2,128,128]{2,1,0:T(8,128)S(1)}, f32[2,128,128]{2,1,0:T(8,128)S(1)}, u32[]{:S(2)}, u32[]{:S(2)}) collective-permute-start(f32[2,128,128]{2,1,0:T(8,128)S(1)} %get-tuple-element.90), channel_id=1, source_target_pairs={{0,24},{8,0},{16,8},{24,16},{1,25},{9,1},{17,9},{25,17},{2,26},{10... | collective-permute-start | bytes 393224 | tf_op jit(solution)/shard_map/ppermute | solution.py:398
  211.3 6.8 %collective-permute-start.32 = (f32[2,128,128]{2,1,0:T(8,128)S(1)}, f32[2,128,128]{2,1,0:T(8,128)S(1)}, u32[]{:S(2)}, u32[]{:S(2)}) collective-permute-start(f32[2,128,128]{2,1,0:T(8,128)S(1)} %get-tuple-element.97), channel_id=1, source_target_pairs={{0,8},{8,16},{16,24},{24,0},{1,9},{9,17},{17,25},{25,1},{2,10},{10... | collective-permute-start | bytes 393224 | tf_op jit(solution)/shard_map/ppermute | solution.py:398
  213.5 7.5 %collective-permute-start.31 = (f32[2,128,128]{2,1,0:T(8,128)S(1)}, f32[2,128,128]{2,1,0:T(8,128)S(1)}, u32[]{:S(2)}, u32[]{:S(2)}) collective-permute-start(f32[2,128,128]{2,1,0:T(8,128)S(1)} %get-tuple-element.95), channel_id=1, source_target_pairs={{0,8},{8,16},{16,24},{24,0},{1,9},{9,17},{17,25},{25,1},{2,10},{10... | collective-permute-start | bytes 393224 | tf_op jit(solution)/shard_map/ppermute | solution.py:398
  224.3 7.4 %collective-permute-start.34 = (f32[2,128,128]{2,1,0:T(8,128)S(1)}, f32[2,128,128]{2,1,0:T(8,128)S(1)}, u32[]{:S(2)}, u32[]{:S(2)}) collective-permute-start(f32[2,128,128]{2,1,0:T(8,128)S(1)} %get-tuple-element.99.refs_0_), channel_id=1, source_target_pairs={{0,24},{8,0},{16,8},{24,16},{1,25},{9,1},{17,9},{25,17},{2,26},{10... | collective-permute-start | bytes 393224 | tf_op jit(solution)/shard_map/ppermute | solution.py:398
  226.1 6.6 %collective-permute-start.39 = (f32[2,128,128]{2,1,0:T(8,128)S(1)}, f32[2,128,128]{2,1,0:T(8,128)S(1)}, u32[]{:S(2)}, u32[]{:S(2)}) collective-permute-start(f32[2,128,128]{2,1,0:T(8,128)S(1)} %get-tuple-element.100.refs_1_), channel_id=1, source_target_pairs={{0,8},{8,16},{16,24},{24,0},{1,9},{9,17},{17,25},{25,1},{2,10},{10... | collective-permute-start | bytes 393224 | tf_op jit(solution)/shard_map/ppermute | solution.py:398
  227.3 6.8 %collective-permute-start.37 = (f32[2,128,128]{2,1,0:T(8,128)S(1)}, f32[2,128,128]{2,1,0:T(8,128)S(1)}, u32[]{:S(2)}, u32[]{:S(2)}) collective-permute-start(f32[2,128,128]{2,1,0:T(8,128)S(1)} %collective-permute-done.36.refs_6_), channel_id=1, source_target_pairs={{0,8},{8,16},{16,24},{24,0},{1,9},{9,17},{17,25},{25,1},{2,10},{10... | collective-permute-start | bytes 393224 | tf_op jit(solution)/shard_map/ppermute | solution.py:398
  (13 other events, 127.3 us)

commit v4 on v3

--- a/solution.py
+++ b/solution.py
@@ -10,9 +10,12 @@
 BRICK = 128
 HALO = 3
 ITERS = 2
-UNROLL = 8
+GROUP = 16
+SPARE = 8
 TAPS = 2 * HALO + 1
-EDGE = 8
+TILE = 8
+TRIM = 4
+DEEP = 16
 ROWS = 32
 
 
@@ -68,14 +71,15 @@
             )
     copy.wait()
 
-    def body(i, c):
-        g = i // (y_cells // UNROLL)
-        base = i % (y_cells // UNROLL) * UNROLL
-        for s in range(UNROLL):
-            out_ref[pos_s[g, base + s]] = rolled[g, pl.ds(base + s, 1), :]
+    def body(g, c):
+        for base in range(0, y_cells, GROUP):
+            places = [pos_s[g, base + i] for i in range(GROUP)]
+            rows = [rolled[g, base + i : base + i + 1, :] for i in range(GROUP)]
+            for place, row in zip(places, rows):
+                out_ref[place] = row
         return c
 
-    lax.fori_loop(0, groups * y_cells // UNROLL, body, 0)
+    lax.fori_loop(0, groups, body, 0)
 
 
 def pack(shift, target, views, geo):
@@ -105,24 +109,17 @@
     for p in range(peers):
         list_v[p : p + 1, :] = in_ref[p * rows_per + cap]
     e = list_v[...].astype(jnp.int32)
-    count = jnp.sum((e > 0).astype(jnp.int32), axis=1, keepdims=True)
-    idx_v[...] = jnp.where(
-        lax.broadcasted_iota(jnp.int32, (peers, BRICK), 1) == cap,
-        count,
-        jnp.where(e > 0, e - 1, slots),
-    )
+    idx_v[...] = jnp.where(e > 0, e - 1, slots)
     copy = pltpu.make_async_copy(idx_v, idx_s, sem)
     copy.start()
     copy.wait()
 
     def per_peer(p, c):
-        def body(i, c):
-            for s in range(UNROLL):
-                k = i * UNROLL + s
-                out_ref[pl.ds(idx_s[p, k], 1), :] = in_ref[p * rows_per + k]
-            return c
-
-        lax.fori_loop(0, (idx_s[p, cap] + UNROLL - 1) // UNROLL, body, 0)
+        for base in range(0, cap, GROUP):
+            places = [idx_s[p, base + i] for i in range(GROUP)]
+            rows = [in_ref[p * rows_per + base + i] for i in range(GROUP)]
+            for place, row in zip(places, rows):
+                out_ref[pl.ds(place, 1), :] = row
         return c
 
     lax.fori_loop(0, peers, per_peer, 0)
@@ -131,7 +128,7 @@
 def unpack(arrived, peers, cap, slots):
     return pl.pallas_call(
         functools.partial(unpack_kernel, peers, cap, slots),
-        out_shape=jax.ShapeDtypeStruct((slots + UNROLL, BRICK), jnp.float32),
+        out_shape=jax.ShapeDtypeStruct((slots + SPARE, BRICK), jnp.float32),
         in_specs=[pl.BlockSpec(memory_space=pltpu.VMEM)],
         out_specs=pl.BlockSpec(memory_space=pltpu.VMEM),
         scratch_shapes=[
@@ -188,101 +185,112 @@
     return out_a, out_b
 
 
-def put_edges(field, first, last, x, y_cells):
-    for c in range(2):
-        first[c, x] = field[c, x, 0:EDGE, :]
-        last[c, x] = field[c, x, y_cells - EDGE : y_cells, :]
-
-
-def z_first_kernel(w_ref, est_ref, out_ref, first, last):
+def row_parts(rows):
+    return [(y, min(ROWS, rows - y)) for y in range(0, rows, ROWS)]
+
+
+def z_first_kernel(w_ref, est_ref, lo, hi, out_ref):
     x_cells, y_cells, _ = est_ref.shape
     w = taps_of(w_ref, 2, False)
+    spans = [(lo, 0, 0, DEEP), (hi, 0, DEEP + y_cells, DEEP)]
+    spans += [(est_ref, y, DEEP + y, n) for y, n in row_parts(y_cells)]
 
     def body(x, carry):
-        for y in range(0, y_cells, ROWS):
-            at = pl.ds(y, ROWS)
-            a, b = blur_z(est_ref[x, at, 0:BRICK], est_ref[x, at, BRICK : 2 * BRICK], w)
-            out_ref[0, x, at, :] = a
-            out_ref[1, x, at, :] = b
-        put_edges(out_ref, first, last, x, y_cells)
+        for ref, y, to, n in spans:
+            a, b = blur_z(ref[x, y : y + n, 0:BRICK], ref[x, y : y + n, BRICK : 2 * BRICK], w)
+            out_ref[0, x, to : to + n, :] = a
+            out_ref[1, x, to : to + n, :] = b
         return carry
 
     lax.fori_loop(0, x_cells, body, 0)
 
 
-def z_first(w, estimate):
+def z_first(w, estimate, lo, hi):
     x, y, _ = estimate.shape
-    outs = [f32(2, x, y, BRICK), f32(2, x, EDGE, BRICK), f32(2, x, EDGE, BRICK)]
-    return call(z_first_kernel, "z_blur", outs, (w, estimate))
-
-
-def z_pieces_kernel(views, w_ref, v_ref, *refs):
-    pieces, (out_ref, first, last) = refs[: 2 * views], refs[2 * views :]
+    return call(z_first_kernel, "z_blur", [f32(2, x, y + 2 * DEEP, BRICK)], (w, estimate, lo, hi))[0]
+
+
+def z_pieces_kernel(views, w_ref, id_ref, *refs):
+    pieces, out_ref = refs[: 2 * views], refs[2 * views]
     depth, y_cells, _ = pieces[0].shape
     w = taps_of(w_ref, 2, False)
     for d in range(views):
-        base = lax.rem(v_ref[0] + d, views) * depth
+        base = lax.rem(id_ref[0] + d, views) * depth
 
         def body(i, carry, d=d, base=base):
-            for y in range(0, y_cells, ROWS):
-                at = pl.ds(y, ROWS)
+            for y, n in row_parts(y_cells):
+                at = pl.ds(y, n)
                 a, b = blur_z(pieces[2 * d][i, at, :], pieces[2 * d + 1][i, at, :], w)
                 out_ref[0, base + i, at, :] = a
                 out_ref[1, base + i, at, :] = b
-            put_edges(out_ref, first, last, base + i, y_cells)
             return carry
 
         lax.fori_loop(0, depth, body, 0)
 
 
-def z_pieces(w, v, pieces):
+def z_pieces(w, ids, pieces):
     views = len(pieces) // 2
     depth, y, _ = pieces[0].shape
-    x = views * depth
-    outs = [f32(2, x, y, BRICK), f32(2, x, EDGE, BRICK), f32(2, x, EDGE, BRICK)]
     return call(
-        functools.partial(z_pieces_kernel, views), "z_blur_pieces", outs, (w, v, *pieces), 2
-    )
-
-
-def y_kernel(flip, w_ref, in_ref, lo, hi, out_ref, first, last, wide):
-    _, x_cells, y_cells, _ = in_ref.shape
+        functools.partial(z_pieces_kernel, views), "z_blur_pieces",
+        [f32(2, views * depth, y, BRICK)], (w, ids, *pieces), 2,
+    )[0]
+
+
+def y_kernel(flip, w_ref, id_ref, in_ref, out_ref, inner, outer):
+    _, x_cells, y_cells, _ = out_ref.shape
     w = taps_of(w_ref, 1, flip)
 
     def body(x, carry):
         for c in range(2):
-            wide[c, 0:EDGE, :] = lo[c, x]
-            wide[c, pl.ds(EDGE, y_cells), :] = in_ref[c, x]
-            wide[c, EDGE + y_cells : 2 * EDGE + y_cells, :] = hi[c, x]
-            for y in range(0, y_cells, ROWS):
-                total = w[0] * wide[c, pl.ds(EDGE - HALO + y, ROWS), :]
+            for y, n in row_parts(y_cells):
+                total = w[0] * in_ref[c, x, pl.ds(TRIM - HALO + y, n), :]
                 for k in range(1, TAPS):
-                    total += w[k] * wide[c, pl.ds(EDGE - HALO + k + y, ROWS), :]
-                out_ref[c, x, pl.ds(y, ROWS), :] = total
+                    total += w[k] * in_ref[c, x, pl.ds(TRIM - HALO + k + y, n), :]
+                out_ref[c, x, pl.ds(y, n), :] = total
         return carry
 
     lax.fori_loop(0, x_cells, body, 0)
+    odd = id_ref[1]
     for c in range(2):
         for i in range(HALO):
-            first[c, i] = out_ref[c, i]
-            last[c, i] = out_ref[c, x_cells - HALO + i]
-
-
-def y_blur(w, field, lo, hi, flip):
+            inner[c, i] = out_ref[c, (1 - odd) * (x_cells - HALO) + i]
+            outer[c, i] = out_ref[c, odd * (x_cells - HALO) + i]
+
+
+def y_blur(w, ids, field, flip):
     _, x, y, _ = field.shape
+    y -= 2 * TRIM
     outs = [f32(2, x, y, BRICK), f32(2, HALO, y, BRICK), f32(2, HALO, y, BRICK)]
-    return call(
-        functools.partial(y_kernel, flip), "y_blur", outs, (w, field, lo, hi),
-        scratch=[pltpu.VMEM((2, y + 2 * EDGE, BRICK), jnp.float32)],
+    field, inner, outer = call(
+        functools.partial(y_kernel, flip), "y_blur", outs, (w, ids, field), 2
     )
-
-
-def x_layers(lo, field, hi, c, at):
+    count = lax.axis_size("rows")
+    links = [(i, i + 1) for i in range(1, count - 1, 2)]
+    outer = lax.ppermute(outer, "rows", links + [(j, i) for i, j in links])
+    inner = lax.ppermute(inner, "rows", [(i, i ^ 1) for i in range(count)])
+    return field, inner, outer
+
+
+def set_sides(id_ref, inner, outer, side):
+    odd = id_ref[1]
+    for c in range(2):
+        for i in range(HALO):
+            side[1 - odd, c, i] = inner[c, i]
+            side[odd, c, i] = outer[c, i]
+
+
+def sides(field):
+    _, _, y, _ = field.shape
+    return pltpu.VMEM((2, 2, HALO, y, BRICK), jnp.float32)
+
+
+def x_layers(field, side, c, at):
     x_cells = field.shape[1]
     return (
-        [lo[c, i, at, :] for i in range(HALO)]
+        [side[0, c, i, at, :] for i in range(HALO)]
         + [field[c, i, at, :] for i in range(x_cells)]
-        + [hi[c, i, at, :] for i in range(HALO)]
+        + [side[1, c, i, at, :] for i in range(HALO)]
     )
 
 
@@ -293,67 +301,129 @@
     return total
 
 
-def ratio_kernel(w_ref, field, lo, hi, obs, out_ref, first, last):
+def x_kernel(w_ref, id_ref, field, inner, outer, out_ref, side):
     _, x_cells, y_cells, _ = field.shape
     w = taps_of(w_ref, 0, False)
+    set_sides(id_ref, inner, outer, side)
+
+    def body(t, carry):
+        at = pl.ds(pl.multiple_of(t * TILE, TILE), TILE)
+        for c in range(2):
+            layers = x_layers(field, side, c, at)
+            for x in range(x_cells):
+                out_ref[c, x, at, :] = weigh(layers[x : x + TAPS], w)
+        return carry
+
+    lax.fori_loop(0, y_cells // TILE, body, 0)
+
+
+def x_blur(w, ids, field, inner, outer):
+    return call(
+        x_kernel, "x_blur", [f32(*field.shape)], (w, ids, field, inner, outer), 2,
+        scratch=[sides(field)],
+    )[0]
+
+
+def inside(id_ref, y, shape):
+    row = lax.broadcasted_iota(jnp.int32, shape, 0) + y
+    return (row >= id_ref[2]) & (row < id_ref[3])
+
+
+def edges_kernel(moved, first, last):
+    _, x_cells, deep, _ = first.shape
+    y_cells = (moved.shape[0] - SPARE) // (2 * x_cells)
+    for c in range(2):
+        for x in range(x_cells):
+            at = (c * x_cells + x) * y_cells
+            first[c, x] = moved[at : at + deep, :]
+            last[c, x] = moved[at + y_cells - deep : at + y_cells, :]
+
+
+def ratio_first_kernel(w_ref, id_ref, below, moved, lo, hi, out_ref, obs):
+    _, x_cells, y_cells, _ = below.shape
+    own = obs.shape[2] - 2 * DEEP
     u = taps_of(w_ref, 2, True)
+    base = (own - y_cells) // 2
+
+    def body(x, carry):
+        for c in range(2):
+            at = pl.multiple_of((c * x_cells + x) * own, own)
+            obs[c, x, 0:DEEP, :] = lo[c, x]
+            obs[c, x, DEEP : DEEP + own, :] = moved[pl.ds(at, own), :]
+            obs[c, x, DEEP + own : 2 * DEEP + own, :] = hi[c, x]
+        for y, n in row_parts(y_cells):
+            ok = inside(id_ref, base + y, (n, BRICK))
+            rows = [
+                jnp.where(
+                    ok, obs[c, x, DEEP + base + y : DEEP + base + y + n, :] / below[c, x, y : y + n, :], 0.0
+                )
+                for c in range(2)
+            ]
+            a, b = blur_z(*rows, u)
+            out_ref[0, x, y : y + n, :] = a
+            out_ref[1, x, y : y + n, :] = b
+        return carry
+
+    lax.fori_loop(0, x_cells, body, 0)
+
+
+def ratio_kernel(w_ref, id_ref, field, inner, outer, obs, out_ref, side):
+    _, x_cells, y_cells, _ = field.shape
+    skip = (obs.shape[2] - y_cells) // 2
+    w = taps_of(w_ref, 0, False)
+    u = taps_of(w_ref, 2, True)
+    set_sides(id_ref, inner, outer, side)
 
     def body(t, carry):
-        at = pl.ds(pl.multiple_of(t * EDGE, EDGE), EDGE)
-        la, lb = x_layers(lo, field, hi, 0, at), x_layers(lo, field, hi, 1, at)
+        start = pl.multiple_of(t * TILE, TILE)
+        at = pl.ds(start, TILE)
+        ok = inside(id_ref, start + skip - DEEP, (TILE, BRICK))
+        la, lb = x_layers(field, side, 0, at), x_layers(field, side, 1, at)
         for x in range(x_cells):
             rows = [
-                obs[pl.ds(pl.multiple_of((c * x_cells + x) * y_cells + t * EDGE, EDGE), EDGE), :]
-                for c in range(2)
+                jnp.where(ok, obs[c, x, pl.ds(start + skip, TILE), :] / weigh(l[x : x + TAPS], w), 0.0)
+                for c, l in ((0, la), (1, lb))
             ]
-            a, b = blur_z(
-                rows[0] / weigh(la[x : x + TAPS], w), rows[1] / weigh(lb[x : x + TAPS], w), u
-            )
+            a, b = blur_z(*rows, u)
             out_ref[0, x, at, :] = a
             out_ref[1, x, at, :] = b
         return carry
 
-    lax.fori_loop(0, y_cells // EDGE, body, 0)
-    for x in range(x_cells):
-        put_edges(out_ref, first, last, x, y_cells)
-
-
-def ratio(w, field, lo, hi, obs):
-    _, x, y, _ = field.shape
-    outs = [f32(2, x, y, BRICK), f32(2, x, EDGE, BRICK), f32(2, x, EDGE, BRICK)]
-    return call(ratio_kernel, "ratio", outs, (w, field, lo, hi, obs), work=8_000_000)
-
-
-def split_kernel(views, w_ref, v_ref, field, lo, hi, a2, b2, a1, b1, a3, b3, a0, b0, wide):
+    lax.fori_loop(0, y_cells // TILE, body, 0)
+
+
+def split_kernel(views, w_ref, id_ref, field, inner, outer, a2, b2, a1, b1, a3, b3, a0, b0, wide):
     _, x_cells, y_cells, _ = field.shape
     depth = x_cells // views
     w = taps_of(w_ref, 0, True)
+    odd = id_ref[1]
     for c in range(2):
         for i in range(HALO):
-            wide[c, i] = lo[c, i]
-            wide[c, HALO + x_cells + i] = hi[c, i]
+            wide[c, (1 - odd) * (HALO + x_cells) + i] = inner[c, i]
+            wide[c, odd * (HALO + x_cells) + i] = outer[c, i]
         for i in range(x_cells):
             wide[c, HALO + i] = field[c, i]
     outs = ((0, a0, b0), (1, a1, b1), (2, a2, b2), (3, a3, b3))
     for r, out_a, out_b in outs:
-        base = lax.rem(v_ref[0] + r, views) * depth
+        base = lax.rem(id_ref[0] + r, views) * depth
 
         def body(t, carry, base=base, pair=(out_a, out_b)):
-            at = pl.ds(pl.multiple_of(t * EDGE, EDGE), EDGE)
+            at = pl.ds(pl.multiple_of(t * TILE, TILE), TILE)
             for c in range(2):
                 layers = [wide[c, base + i, at, :] for i in range(depth + 2 * HALO)]
                 for i in range(depth):
                     pair[c][i, at, :] = weigh(layers[i : i + TAPS], w)
             return carry
 
-        lax.fori_loop(0, y_cells // EDGE, body, 0, unroll=2)
-
-
-def split(w, v, views, field, lo, hi):
+        lax.fori_loop(0, y_cells // TILE, body, 0, unroll=2)
+
+
+def split(w, ids, views, field, inner, outer):
     _, x, y, _ = field.shape
     outs = [f32(x // views, y, BRICK)] * 8
     return call(
-        functools.partial(split_kernel, views), "x_blur_split", outs, (w, v, field, lo, hi), 2,
+        functools.partial(split_kernel, views), "x_blur_split", outs,
+        (w, ids, field, inner, outer), 2,
         scratch=[pltpu.VMEM((2, x + 2 * HALO, y, BRICK), jnp.float32)],
     )
 
@@ -363,25 +433,34 @@
     out_b[...] = b[...] + rb[...]
 
 
-def update_first_kernel(views, v_ref, est, a, a1, a2, b, b1, b2, out_a, out_b):
-    depth = a.shape[0]
-    base = v_ref[0] * depth
+def update_first_kernel(views, id_ref, est, lo, hi, a, a1, a2, b, b1, b2, out_a, out_b):
+    depth, y_cells, _ = a.shape
+    own = est.shape[1]
+    side = (y_cells - own) // 2
+    base = id_ref[0] * depth
+    spans = ((lo, DEEP - side, 0, side), (est, 0, side, own), (hi, 0, side + own, side))
     for i in range(depth):
-        row = est[base + i]
-        out_a[i] = row[:, 0:BRICK] * (a[i] + a1[i] + a2[i]) / views
-        out_b[i] = row[:, BRICK : 2 * BRICK] * (b[i] + b1[i] + b2[i]) / views
+        for ref, y, to, n in spans:
+            at = slice(to, to + n)
+            row = ref[base + i, y : y + n, :]
+            out_a[i, at, :] = row[:, 0:BRICK] * (a[i, at, :] + a1[i, at, :] + a2[i, at, :]) / views
+            out_b[i, at, :] = (
+                row[:, BRICK : 2 * BRICK] * (b[i, at, :] + b1[i, at, :] + b2[i, at, :]) / views
+            )
 
 
 def update_kernel(views, est_a, est_b, a, a1, a2, b, b1, b2, out_a, out_b):
-    out_a[...] = est_a[...] * (a[...] + a1[...] + a2[...]) / views
-    out_b[...] = est_b[...] * (b[...] + b1[...] + b2[...]) / views
-
-
-def join_kernel(views, v_ref, *refs):
+    side = (est_a.shape[1] - a.shape[1]) // 2
+    at = slice(side, side + a.shape[1])
+    out_a[...] = est_a[:, at, :] * (a[...] + a1[...] + a2[...]) / views
+    out_b[...] = est_b[:, at, :] * (b[...] + b1[...] + b2[...]) / views
+
+
+def join_kernel(views, id_ref, *refs):
     pieces, out_ref = refs[: 2 * views], refs[2 * views]
     depth = pieces[0].shape[0]
     for d in range(views):
-        base = lax.rem(v_ref[0] + d, views) * depth
+        base = lax.rem(id_ref[0] + d, views) * depth
         for i in range(depth):
             out_ref[base + i, :, 0:BRICK] = pieces[2 * d][i]
             out_ref[base + i, :, BRICK : 2 * BRICK] = pieces[2 * d + 1][i]
@@ -408,30 +487,43 @@
     brick_count = x_cells * y_cells * brick_cols
     capacity = 2 * brick_count // peer_count
     geo = (peer_count, capacity, x_cells, y_cells, brick_cols, row_count, y_cells * block_count)
+    est_lo, est_hi = exchange(estimate[:, :DEEP], estimate[:, y_cells - DEEP :], "blocks")
     targets = target[0].transpose(2, 0, 1).reshape(brick_cols * x_cells, y_cells)
     outgoing = pack(shifts, targets, views_data[0], geo)
+    outgoing, est_lo, est_hi = lax.optimization_barrier((outgoing, est_lo, est_hi))
     arrived = lax.all_to_all(
         outgoing.reshape(peer_count, capacity + 1, 1, BRICK),
         ("blocks", "rows"), split_axis=0, concat_axis=0, tiled=True,
     ).reshape(peer_count * (capacity + 1), 1, BRICK)
     w = (psf_taps[0] / jnp.sum(psf_taps[0], axis=1, keepdims=True)).reshape(-1)
-    v = lax.axis_index("views").astype(jnp.int32).reshape(1)
-    depth = x_cells // view_count
-    pair = [f32(depth, y_cells, BRICK)] * 2
+    block = lax.axis_index("blocks")
+    ids = jnp.stack([
+        lax.axis_index("views"),
+        lax.axis_index("rows") % 2,
+        jnp.where(block == 0, 0, -DEEP),
+        jnp.where(block == block_count - 1, y_cells, y_cells + DEEP),
+    ]).astype(jnp.int32)
     pieces = None
     for iteration in range(ITERS):
         if pieces is None:
-            field, first, last = z_first(w, estimate)
+            field = z_first(w, estimate, est_lo, est_hi)
+            below = x_blur(w, ids, *y_blur(w, ids, field, False))
+            moved = unpack(arrived, peer_count, capacity, brick_count)
+            edge = f32(2, x_cells, DEEP, BRICK)
+            lo, hi = exchange(*call(edges_kernel, "edges", [edge, edge], (moved,), 0), "blocks")
+            field, obs = call(
+                ratio_first_kernel, "ratio_first",
+                [f32(*below.shape), f32(2, x_cells, y_cells + 2 * DEEP, BRICK)],
+                (w, ids, below, moved, lo, hi), 2,
+            )
         else:
-            field, first, last = z_pieces(w, v, pieces)
-        field, first, last = y_blur(w, field, *exchange(first, last, "blocks"), False)
-        lo, hi = exchange(first, last, "rows")
-        if pieces is None:
-            moved = unpack(arrived, peer_count, capacity, brick_count)
-        field, first, last = ratio(w, field, lo, hi, moved)
-        field, first, last = y_blur(w, field, *exchange(first, last, "blocks"), True)
-        lo, hi = exchange(first, last, "rows")
-        a2, b2, a1, b1, a3, b3, a0, b0 = split(w, v, view_count, field, lo, hi)
+            field, inner, outer = y_blur(w, ids, z_pieces(w, ids, pieces), False)
+            field = call(
+                ratio_kernel, "ratio", [f32(*field.shape)], (w, ids, field, inner, outer, obs), 2,
+                scratch=[sides(field)],
+            )[0]
+        a2, b2, a1, b1, a3, b3, a0, b0 = split(w, ids, view_count, *y_blur(w, ids, field, True))
+        pair = [f32(*a0.shape)] * 2
         ra, rb = turn(a2, 1, view_count), turn(b2, -1, view_count)
         near_b, near_a = turn(b1, 1, view_count), turn(a3, -1, view_count)
         a1, b3 = call(add_kernel, "add", pair, (a1, ra, b3, rb), 0)
@@ -439,8 +531,8 @@
         sums = (a0, near_a, far_a, b0, near_b, far_b)
         if pieces is None:
             own = call(
-                functools.partial(update_first_kernel, view_count), "update", pair,
-                (v, estimate, *sums),
+                functools.partial(update_first_kernel, view_count), "update_first", pair,
+                (ids, estimate, est_lo, est_hi, *sums),
             )
         else:
             own = call(
@@ -453,7 +545,7 @@
         pieces = (*own, next_a, next_b, far_a, far_b, prev_a, prev_b)
     return call(
         functools.partial(join_kernel, view_count), "join", [f32(x_cells, y_cells, z_cells)],
-        (v, *pieces),
+        (ids, *pieces),
     )[0]
 
 

time: 237 us -> 201 us (0.85)
  starting transfers between devices: 93.8 us -> 69.1 us
  Pallas kernels: 44.8 us -> 38.1 us
  waiting for transfers between devices: 92.8 us -> 86.9 us
    ppermute x16 -> x4, waiting for transfers between devices: 69.1 us -> 1.98 us  [exchange(): return (lax.ppermute(last, axis, up), lax.ppermute(first, axis, down))]
    all_to_all x1, waiting for transfers between devices: 0.01 us -> 42.7 us  [per_device(): lax.all_to_all(outgoing.reshape(peer_count, capacity + 1, 1, BRICK), ('bl...]
    ppermute x16 -> x4, starting transfers between devices: 45.6 us -> 11.7 us  [exchange(): return (lax.ppermute(last, axis, up), lax.ppermute(first, axis, down))]
    ppermute x0 -> x8, waiting for transfers between devices: none -> 20.9 us  [the longest x4 20.9 us: y_blur(): outer = lax.ppermute(outer, 'rows', links + [(j, i) for i, j in links])]
    ppermute x0 -> x8, starting transfers between devices: none -> 10.4 us  [the longest x4 9.5 us: y_blur(): outer = lax.ppermute(outer, 'rows', links + [(j, i) for i, j in links])]
    pallas_call x1, Pallas kernels: 11.3 us -> 5.95 us  [pack(): pl.pallas_call(functools.partial(pack_kernel, geo), out_shape=jax.ShapeDt...]
    pallas_call x1, Pallas kernels: 11.1 us -> 7.25 us  [unpack(): pl.pallas_call(functools.partial(unpack_kernel, peers, cap, slots), out_s...]
    pallas_call x15 -> x17, Pallas kernels: 22.4 us -> 24.9 us  [call(): pl.pallas_call(kernel, out_shape=outs, in_specs=[smem()] * scalars + [vme...]
  transfers between devices with their start and end apart: 41 -> 37, of which waited for: 28 -> 20; matrix products, arithmetic and copies ran while one was open for 0% -> 1% of each run, Pallas kernels for 7% -> 10%
where the time goes in v4:
time: 201 us; the launch traced here: 199 us
  waiting for transfers between devices  86.9 us (43%)
  starting transfers between devices  69.1 us (34%)
  Pallas kernels  38.1 us (19%)
  local copies, waits for them, and re-layouts  3.76 us (2%)
    all_to_all x1, waiting for transfers between devices, per_device(): lax.all_to_all(outgoing.reshape(peer_count, capacity + 1, 1, BRICK), ('bl...  42.7 us
    ppermute x24, starting transfers between devices, turn(): lax.ppermute(value, 'views', [(i, (i + step) % count) for i in range(coun...  35.1 us
    pallas_call x17, Pallas kernels, call(): pl.pallas_call(kernel, out_shape=outs, in_specs=[smem()] * scalars + [vme...  24.9 us
    ppermute x24, waiting for transfers between devices, turn(): lax.ppermute(value, 'views', [(i, (i + step) % count) for i in range(coun...  21.3 us
    ppermute x4, waiting for transfers between devices, y_blur(): outer = lax.ppermute(outer, 'rows', links + [(j, i) for i, j in links])  20.9 us
    all_to_all x1, starting transfers between devices, per_device(): lax.all_to_all(outgoing.reshape(peer_count, capacity + 1, 1, BRICK), ('bl...  11.9 us
    ppermute x4, starting transfers between devices, exchange(): return (lax.ppermute(last, axis, up), lax.ppermute(first, axis, down))  11.7 us
    ppermute x4, starting transfers between devices, y_blur(): outer = lax.ppermute(outer, 'rows', links + [(j, i) for i, j in links])  9.5 us
  transfers between devices with their start and end apart: 37, of which 20 were waited for; matrix products, arithmetic and copies ran while one was open for 1% of the time, Pallas kernels for 10%

profile of v4, /device:TPU:34, one launch (start us, length us, event | category | flops | bytes accessed | tf_op | source)
XLA Modules:
  0.0 199.1 jit_solution(3297437034051623648)
XLA Ops:
  1.0 2.0 %collective-permute-start.1 = (f32[8,16,256]{2,1,0:T(8,128)S(1)}, f32[8,16,256]{2,1,0:T(8,128)S(1)}, u32[]{:S(2)}, u32[]{:S(2)}) collective-permute-start(f32[8,16,256]{2,1,0:T(8,128)S(1)} %get-tuple-element.93), channel_id=1, source_target_pairs={{32,0},{64,32},{96,64},{128,96},{160,128},{192,160},{224,192},{33,... | collective-permute-start | bytes 393224 | tf_op jit(solution)/shard_map/ppermute | solution.py:473
  3.0 3.8 %collective-permute-start = (f32[8,16,256]{2,1,0:T(8,128)S(1)}, f32[8,16,256]{2,1,0:T(8,128)S(1)}, u32[]{:S(2)}, u32[]{:S(2)}) collective-permute-start(f32[8,16,256]{2,1,0:T(8,128)S(1)} %get-tuple-element.94), channel_id=1, source_target_pairs={{0,32},{32,64},{64,96},{96,128},{128,160},{160,192},{192,224},{1,3... | collective-permute-start | bytes 393224 | tf_op jit(solution)/shard_map/ppermute | solution.py:473
  8.8 6.0 %pack.1 = f32[4160,1,128]{2,1,0:T(1,128)} custom-call(s32[1]{0:T(128)S(6)} %copy.9.shift_ref, s32[16,128]{1,0:T(8,128)} %bitcast.15, f32[8,128,256]{2,1,0:T(8,128)} %bitcast.14), custom_call_target="tpu_custom_call" | custom-call | tf_op jit(solution)/shard_map/pack/pallas_call | solution.py:88
  14.8 11.9 %all-to-all-start = ((f32[64,65,1,128]{3,2,1,0:T(1,128)}), f32[64,65,1,128]{3,2,1,0:T(1,128)}, u32[]{:S(2)}, u32[]{:S(2)}) async-start(f32[64,65,1,128]{3,2,1,0:T(1,128)} %bitcast.13), calls=%async_computation | async-start | bytes 4259840 | tf_op jit(solution)/shard_map/all_to_all | solution.py:494
  27.1 3.1 %z_blur.1.in_ref = f32[2,8,160,128]{3,2,1,0:T(8,128)S(1)} custom-call(f32[21]{0:T(128)S(1)} %div.13.w_ref, f32[8,128,256]{2,1,0:T(8,128)S(1)} %copy-done.2, f32[8,16,256]{2,1,0:T(8,128)S(1)} %collective-permute-done.lo, f32[8,16,256]{2,1,0:T(8,128)S(1)} %collective-permute-done.1.hi), custom_call_target="tpu_custom_call" | custom-call | flops 4000000 | bytes 4000000 | tf_op jit(solution)/shard_map/z_blur/pallas_call | solution.py:157
  30.3 2.1 %y_blur.4 = (f32[2,8,152,128]{3,2,1,0:T(8,128)S(1)}, f32[2,3,152,128]{3,2,1,0:T(8,128)}, f32[2,3,152,128]{3,2,1,0:T(8,128)}) custom-call(f32[21]{0:T(128)S(1)} %div.13.w_ref, s32[4]{0:T(128)S(1)} %pad_add_fusion.id_ref, f32[2,8,160,128]{3,2,1,0:T(8,128)S(1)} %z_blur.1.in_ref), custom_call_target="tpu_custom_call" | custom-call | flops 4000000 | bytes 4000000 | tf_op jit(solution)/shard_map/y_blur/pallas_call | solution.py:157
  32.6 2.4 %collective-permute-start.3 = (f32[2,3,152,128]{3,2,1,0:T(8,128)}, f32[2,3,152,128]{3,2,1,0:T(8,128)S(1)}, u32[]{:S(2)}, u32[]{:S(2)}) collective-permute-start(f32[2,3,152,128]{3,2,1,0:T(8,128)} %get-tuple-element.52), channel_id=1, source_target_pairs={{1,2},{3,4},{5,6},{2,1},{4,3},{6,5},{9,10},{11,12},{13,14},{10,9},... | collective-permute-start | bytes 1400840 | tf_op jit(solution)/shard_map/ppermute | solution.py:270
  35.0 42.7 %all-to-all-done = f32[64,65,1,128]{3,2,1,0:T(1,128)} async-done(((f32[64,65,1,128]{3,2,1,0:T(1,128)}), f32[64,65,1,128]{3,2,1,0:T(1,128)}, u32[]{:S(2)}, u32[]{:S(2)}) %all-to-all-start) | async-done | bytes 2129952 | tf_op jit(solution)/shard_map/all_to_all | solution.py:494
  77.7 7.3 %unpack.1.moved = f32[2056,128]{1,0:T(8,128)} custom-call(f32[4160,1,128]{2,1,0:T(1,128)} %bitcast.9.in_ref), custom_call_target="tpu_custom_call" | custom-call | tf_op jit(solution)/shard_map/unpack/pallas_call | solution.py:129
  86.2 1.9 collective-permute-start.4
  88.2 3.9 %collective-permute-start.5 = (f32[2,8,16,128]{3,2,1,0:T(8,128)S(1)}, f32[2,8,16,128]{3,2,1,0:T(8,128)S(1)}, u32[]{:S(2)}, u32[]{:S(2)}) collective-permute-start(f32[2,8,16,128]{3,2,1,0:T(8,128)S(1)} %get-tuple-element.55), channel_id=1, source_target_pairs={{32,0},{64,32},{96,64},{128,96},{160,128},{192,160},{224,192},{33,... | collective-permute-start | bytes 393224 | tf_op jit(solution)/shard_map/ppermute | solution.py:473
  93.4 2.0 collective-permute-done.5.hi
  95.4 3.1 %ratio_first.1 = (f32[2,8,152,128]{3,2,1,0:T(8,128)S(1)}, f32[2,8,160,128]{3,2,1,0:T(8,128)S(1)}) custom-call(f32[21]{0:T(128)S(1)} %div.13.w_ref, s32[4]{0:T(128)S(1)} %pad_add_fusion.id_ref, f32[2,8,152,128]{3,2,1,0:T(8,128)S(1)} %x_blur.1.below, f32[2056,128]{1,0:T(8,128)S(1)} %copy-done.1, f32[2,8,16,128]{3,2,1,0:T(8,128)S(1)} %collective-permute-done.4.lo, ...), custom_call_target="tpu_custom_call" | custom-call | flops 4000000 | bytes 4000000 | tf_op jit(solution)/shard_map/ratio_first/pallas_call | solution.py:157
  99.8 3.3 %collective-permute-start.7 = (f32[2,3,144,128]{3,2,1,0:T(8,128)S(1)}, f32[2,3,144,128]{3,2,1,0:T(8,128)S(1)}, u32[]{:S(2)}, u32[]{:S(2)}) collective-permute-start(f32[2,3,144,128]{3,2,1,0:T(8,128)S(1)} %get-tuple-element.59), channel_id=1, source_target_pairs={{1,2},{3,4},{5,6},{2,1},{4,3},{6,5},{9,10},{11,12},{13,14},{10,9},... | collective-permute-start | bytes 1327112 | tf_op jit(solution)/shard_map/ppermute | solution.py:270
  103.1 6.4 %collective-permute-done.7.outer = f32[2,3,144,128]{3,2,1,0:T(8,128)S(1)} collective-permute-done((f32[2,3,144,128]{3,2,1,0:T(8,128)S(1)}, f32[2,3,144,128]{3,2,1,0:T(8,128)S(1)}, u32[]{:S(2)}, u32[]{:S(2)}) %collective-permute-start.7) | collective-permute-done | bytes 442400 | tf_op jit(solution)/shard_map/ppermute | solution.py:270
  116.2 2.2 %collective-permute-done.9.ra = f32[2,144,128]{2,1,0:T(8,128)S(1)} collective-permute-done((f32[2,144,128]{2,1,0:T(8,128)S(1)}, f32[2,144,128]{2,1,0:T(8,128)S(1)}, u32[]{:S(2)}, u32[]{:S(2)}) %collective-permute-start.9) | collective-permute-done | bytes 147488 | tf_op jit(solution)/shard_map/ppermute | solution.py:477
  123.0 2.8 %collective-permute-done.11.a2 = f32[2,144,128]{2,1,0:T(8,128)S(1)} collective-permute-done((f32[2,144,128]{2,1,0:T(8,128)S(1)}, f32[2,144,128]{2,1,0:T(8,128)S(1)}, u32[]{:S(2)}, u32[]{:S(2)}) %collective-permute-start.11) | collective-permute-done | bytes 147488 | tf_op jit(solution)/shard_map/ppermute | solution.py:477
  128.0 2.0 collective-permute-start.15
  132.0 2.0 %collective-permute-done.16.refs_6_ = f32[2,144,128]{2,1,0:T(8,128)S(1)} collective-permute-done((f32[2,144,128]{2,1,0:T(8,128)S(1)}, f32[2,144,128]{2,1,0:T(8,128)S(1)}, u32[]{:S(2)}, u32[]{:S(2)}) %collective-permute-start.16) | collective-permute-done | bytes 147488 | tf_op jit(solution)/shard_map/ppermute | solution.py:477
  134.4 2.9 %collective-permute-start.18 = (f32[2,144,128]{2,1,0:T(8,128)S(1)}, f32[2,144,128]{2,1,0:T(8,128)S(1)}, u32[]{:S(2)}, u32[]{:S(2)}) collective-permute-start(f32[2,144,128]{2,1,0:T(8,128)S(1)} %collective-permute-done.15.refs_3_), channel_id=1, source_target_pairs={{0,24},{8,0},{16,8},{24,16},{1,25},{9,1},{17,9},{25,17},{2,26},{10... | collective-permute-start | bytes 442376 | tf_op jit(solution)/shard_map/ppermute | solution.py:477
  138.0 2.4 %collective-permute-done.17.refs_4_ = f32[2,144,128]{2,1,0:T(8,128)S(1)} collective-permute-done((f32[2,144,128]{2,1,0:T(8,128)S(1)}, f32[2,144,128]{2,1,0:T(8,128)S(1)}, u32[]{:S(2)}, u32[]{:S(2)}) %collective-permute-start.17) | collective-permute-done | bytes 147488 | tf_op jit(solution)/shard_map/ppermute | solution.py:477
  140.4 2.9 %z_blur_pieces.1.in_ref = f32[2,8,144,128]{3,2,1,0:T(8,128)S(1)} custom-call(f32[21]{0:T(128)S(1)} %div.13.w_ref, s32[4]{0:T(128)S(1)} %pad_add_fusion.id_ref, f32[2,144,128]{2,1,0:T(8,128)S(1)} %get-tuple-element.70.refs_0_.est_a, f32[2,144,128]{2,1,0:T(8,128)S(1)} %get-tuple-element.71.refs_1_.est_b, f32[2,144,128]{2,1,0:T(8,128)S(1)} %collective-permute-done.14.refs_2_, ...), custom_call_target="tpu_custom_call" | custom-call | flops 4000000 | bytes 4000000 | tf_op jit(solution)/shard_map/z_blur_pieces/pallas_call | solution.py:157
  144.6 1.9 collective-permute-start.21
  146.5 7.4 %collective-permute-done.21.outer = f32[2,3,136,128]{3,2,1,0:T(8,128)S(1)} collective-permute-done((f32[2,3,136,128]{3,2,1,0:T(8,128)S(1)}, f32[2,3,136,128]{3,2,1,0:T(8,128)S(1)}, u32[]{:S(2)}, u32[]{:S(2)}) %collective-permute-start.21) | collective-permute-done | bytes 417824 | tf_op jit(solution)/shard_map/ppermute | solution.py:270
  154.0 3.8 %ratio.1.in_ref = f32[2,8,136,128]{3,2,1,0:T(8,128)S(1)} custom-call(f32[21]{0:T(128)S(1)} %div.13.w_ref, s32[4]{0:T(128)S(1)} %pad_add_fusion.id_ref, f32[2,8,136,128]{3,2,1,0:T(8,128)S(1)} %get-tuple-element.72.field, f32[2,3,136,128]{3,2,1,0:T(8,128)S(1)} %collective-permute-done.20.inner, f32[2,3,136,128]{3,2,1,0:T(8,128)S(1)} %collective-permute-done.21.outer, ...), custom_call_target="tpu_custom_call" | custom-call | flops 4000000 | bytes 4000000 | tf_op jit(solution)/shard_map/ratio/pallas_call | solution.py:157
  159.4 1.9 collective-permute-start.23
  161.4 7.2 %collective-permute-done.23.outer = f32[2,3,128,128]{3,2,1,0:T(8,128)S(1)} collective-permute-done((f32[2,3,128,128]{3,2,1,0:T(8,128)S(1)}, f32[2,3,128,128]{3,2,1,0:T(8,128)S(1)}, u32[]{:S(2)}, u32[]{:S(2)}) %collective-permute-start.23) | collective-permute-done | bytes 393248 | tf_op jit(solution)/shard_map/ppermute | solution.py:270
  170.8 2.5 %collective-permute-start.26 = (f32[2,128,128]{2,1,0:T(8,128)S(1)}, f32[2,128,128]{2,1,0:T(8,128)S(1)}, u32[]{:S(2)}, u32[]{:S(2)}) collective-permute-start(f32[2,128,128]{2,1,0:T(8,128)S(1)} %get-tuple-element.84), channel_id=1, source_target_pairs={{0,24},{8,0},{16,8},{24,16},{1,25},{9,1},{17,9},{25,17},{2,26},{10... | collective-permute-start | bytes 393224 | tf_op jit(solution)/shard_map/ppermute | solution.py:477
  173.3 1.9 collective-permute-start.24
  179.1 2.0 %collective-permute-start.29 = (f32[2,128,128]{2,1,0:T(8,128)S(1)}, f32[2,128,128]{2,1,0:T(8,128)S(1)}, u32[]{:S(2)}, u32[]{:S(2)}) collective-permute-start(f32[2,128,128]{2,1,0:T(8,128)S(1)} %get-tuple-element.88), channel_id=1, source_target_pairs={{0,24},{8,0},{16,8},{24,16},{1,25},{9,1},{17,9},{25,17},{2,26},{10... | collective-permute-start | bytes 393224 | tf_op jit(solution)/shard_map/ppermute | solution.py:477
  184.3 1.9 collective-permute-start.32
  192.1 2.4 %collective-permute-start.34 = (f32[2,128,128]{2,1,0:T(8,128)S(1)}, f32[2,128,128]{2,1,0:T(8,128)S(1)}, u32[]{:S(2)}, u32[]{:S(2)}) collective-permute-start(f32[2,128,128]{2,1,0:T(8,128)S(1)} %collective-permute-done.31.refs_3_), channel_id=1, source_target_pairs={{0,24},{8,0},{16,8},{24,16},{1,25},{9,1},{17,9},{25,17},{2,26},{10... | collective-permute-start | bytes 393224 | tf_op jit(solution)/shard_map/ppermute | solution.py:477
  (77 shorter events, 45.9 us)
Async XLA Ops:
  1.0 13.8 %collective-permute-start.1 = (f32[8,16,256]{2,1,0:T(8,128)S(1)}, f32[8,16,256]{2,1,0:T(8,128)S(1)}, u32[]{:S(2)}, u32[]{:S(2)}) collective-permute-start(f32[8,16,256]{2,1,0:T(8,128)S(1)} %get-tuple-element.93), channel_id=1, source_target_pairs={{32,0},{64,32},{96,64},{128,96},{160,128},{192,160},{224,192},{33,... | collective-permute-start | bytes 393224 | tf_op jit(solution)/shard_map/ppermute | solution.py:473
  3.0 11.8 %collective-permute-start = (f32[8,16,256]{2,1,0:T(8,128)S(1)}, f32[8,16,256]{2,1,0:T(8,128)S(1)}, u32[]{:S(2)}, u32[]{:S(2)}) collective-permute-start(f32[8,16,256]{2,1,0:T(8,128)S(1)} %get-tuple-element.94), channel_id=1, source_target_pairs={{0,32},{32,64},{64,96},{96,128},{128,160},{160,192},{192,224},{1,3... | collective-permute-start | bytes 393224 | tf_op jit(solution)/shard_map/ppermute | solution.py:473
  14.8 62.9 %all-to-all-start = ((f32[64,65,1,128]{3,2,1,0:T(1,128)}), f32[64,65,1,128]{3,2,1,0:T(1,128)}, u32[]{:S(2)}, u32[]{:S(2)}) async-start(f32[64,65,1,128]{3,2,1,0:T(1,128)} %bitcast.13), calls=%async_computation | async-start | bytes 4259840 | tf_op jit(solution)/shard_map/all_to_all | solution.py:494
  32.4 59.7 %collective-permute-start.2 = (f32[2,3,152,128]{3,2,1,0:T(8,128)}, f32[2,3,152,128]{3,2,1,0:T(8,128)S(1)}, u32[]{:S(2)}, u32[]{:S(2)}) collective-permute-start(f32[2,3,152,128]{3,2,1,0:T(8,128)} %get-tuple-element.51), channel_id=1, source_target_pairs={{0,1},{1,0},{2,3},{3,2},{4,5},{5,4},{6,7},{7,6},{8,9},{9,8},{10,11... | collective-permute-start | bytes 1400840 | tf_op jit(solution)/shard_map/ppermute | solution.py:271
  32.6 59.6 %collective-permute-start.3 = (f32[2,3,152,128]{3,2,1,0:T(8,128)}, f32[2,3,152,128]{3,2,1,0:T(8,128)S(1)}, u32[]{:S(2)}, u32[]{:S(2)}) collective-permute-start(f32[2,3,152,128]{3,2,1,0:T(8,128)} %get-tuple-element.52), channel_id=1, source_target_pairs={{1,2},{3,4},{5,6},{2,1},{4,3},{6,5},{9,10},{11,12},{13,14},{10,9},... | collective-permute-start | bytes 1400840 | tf_op jit(solution)/shard_map/ppermute | solution.py:270
  86.2 7.1 %collective-permute-start.4 = (f32[2,8,16,128]{3,2,1,0:T(8,128)S(1)}, f32[2,8,16,128]{3,2,1,0:T(8,128)S(1)}, u32[]{:S(2)}, u32[]{:S(2)}) collective-permute-start(f32[2,8,16,128]{3,2,1,0:T(8,128)S(1)} %get-tuple-element.54), channel_id=1, source_target_pairs={{0,32},{32,64},{64,96},{96,128},{128,160},{160,192},{192,224},{1,3... | collective-permute-start | bytes 393224 | tf_op jit(solution)/shard_map/ppermute | solution.py:473
  88.2 7.2 %collective-permute-start.5 = (f32[2,8,16,128]{3,2,1,0:T(8,128)S(1)}, f32[2,8,16,128]{3,2,1,0:T(8,128)S(1)}, u32[]{:S(2)}, u32[]{:S(2)}) collective-permute-start(f32[2,8,16,128]{3,2,1,0:T(8,128)S(1)} %get-tuple-element.55), channel_id=1, source_target_pairs={{32,0},{64,32},{96,64},{128,96},{160,128},{192,160},{224,192},{33,... | collective-permute-start | bytes 393224 | tf_op jit(solution)/shard_map/ppermute | solution.py:473
  99.8 9.6 %collective-permute-start.7 = (f32[2,3,144,128]{3,2,1,0:T(8,128)S(1)}, f32[2,3,144,128]{3,2,1,0:T(8,128)S(1)}, u32[]{:S(2)}, u32[]{:S(2)}) collective-permute-start(f32[2,3,144,128]{3,2,1,0:T(8,128)S(1)} %get-tuple-element.59), channel_id=1, source_target_pairs={{1,2},{3,4},{5,6},{2,1},{4,3},{6,5},{9,10},{11,12},{13,14},{10,9},... | collective-permute-start | bytes 1327112 | tf_op jit(solution)/shard_map/ppermute | solution.py:270
  110.9 7.6 %collective-permute-start.9 = (f32[2,144,128]{2,1,0:T(8,128)S(1)}, f32[2,144,128]{2,1,0:T(8,128)S(1)}, u32[]{:S(2)}, u32[]{:S(2)}) collective-permute-start(f32[2,144,128]{2,1,0:T(8,128)S(1)} %get-tuple-element.63), channel_id=1, source_target_pairs={{0,8},{8,16},{16,24},{24,0},{1,9},{9,17},{17,25},{25,1},{2,10},{10... | collective-permute-start | bytes 442376 | tf_op jit(solution)/shard_map/ppermute | solution.py:477
  112.5 6.7 %collective-permute-start.10 = (f32[2,144,128]{2,1,0:T(8,128)S(1)}, f32[2,144,128]{2,1,0:T(8,128)S(1)}, u32[]{:S(2)}, u32[]{:S(2)}) collective-permute-start(f32[2,144,128]{2,1,0:T(8,128)S(1)} %get-tuple-element.65), channel_id=1, source_target_pairs={{0,24},{8,0},{16,8},{24,16},{1,25},{9,1},{17,9},{25,17},{2,26},{10... | collective-permute-start | bytes 442376 | tf_op jit(solution)/shard_map/ppermute | solution.py:477
  114.2 8.4 %collective-permute-start.8 = (f32[2,144,128]{2,1,0:T(8,128)S(1)}, f32[2,144,128]{2,1,0:T(8,128)S(1)}, u32[]{:S(2)}, u32[]{:S(2)}) collective-permute-start(f32[2,144,128]{2,1,0:T(8,128)S(1)} %get-tuple-element.61), channel_id=1, source_target_pairs={{0,24},{8,0},{16,8},{24,16},{1,25},{9,1},{17,9},{25,17},{2,26},{10... | collective-permute-start | bytes 442376 | tf_op jit(solution)/shard_map/ppermute | solution.py:477
  116.0 7.0 %collective-permute-start.12 = (f32[2,144,128]{2,1,0:T(8,128)S(1)}, f32[2,144,128]{2,1,0:T(8,128)S(1)}, u32[]{:S(2)}, u32[]{:S(2)}) collective-permute-start(f32[2,144,128]{2,1,0:T(8,128)S(1)} %get-tuple-element.68), channel_id=1, source_target_pairs={{0,8},{8,16},{16,24},{24,0},{1,9},{9,17},{17,25},{25,1},{2,10},{10... | collective-permute-start | bytes 442376 | tf_op jit(solution)/shard_map/ppermute | solution.py:477
  119.2 6.5 %collective-permute-start.11 = (f32[2,144,128]{2,1,0:T(8,128)S(1)}, f32[2,144,128]{2,1,0:T(8,128)S(1)}, u32[]{:S(2)}, u32[]{:S(2)}) collective-permute-start(f32[2,144,128]{2,1,0:T(8,128)S(1)} %get-tuple-element.66), channel_id=1, source_target_pairs={{0,8},{8,16},{16,24},{24,0},{1,9},{9,17},{17,25},{25,1},{2,10},{10... | collective-permute-start | bytes 442376 | tf_op jit(solution)/shard_map/ppermute | solution.py:477
  126.7 7.4 %collective-permute-start.16 = (f32[2,144,128]{2,1,0:T(8,128)S(1)}, f32[2,144,128]{2,1,0:T(8,128)S(1)}, u32[]{:S(2)}, u32[]{:S(2)}) collective-permute-start(f32[2,144,128]{2,1,0:T(8,128)S(1)} %get-tuple-element.70.refs_0_.est_a), channel_id=1, source_target_pairs={{0,8},{8,16},{16,24},{24,0},{1,9},{9,17},{17,25},{25,1},{2,10},{10... | collective-permute-start | bytes 442376 | tf_op jit(solution)/shard_map/ppermute | solution.py:477
  128.0 6.4 %collective-permute-start.15 = (f32[2,144,128]{2,1,0:T(8,128)S(1)}, f32[2,144,128]{2,1,0:T(8,128)S(1)}, u32[]{:S(2)}, u32[]{:S(2)}) collective-permute-start(f32[2,144,128]{2,1,0:T(8,128)S(1)} %get-tuple-element.71.refs_1_.est_b), channel_id=1, source_target_pairs={{0,24},{8,0},{16,8},{24,16},{1,25},{9,1},{17,9},{25,17},{2,26},{10... | collective-permute-start | bytes 442376 | tf_op jit(solution)/shard_map/ppermute | solution.py:477
  130.0 7.3 %collective-permute-start.14 = (f32[2,144,128]{2,1,0:T(8,128)S(1)}, f32[2,144,128]{2,1,0:T(8,128)S(1)}, u32[]{:S(2)}, u32[]{:S(2)}) collective-permute-start(f32[2,144,128]{2,1,0:T(8,128)S(1)} %get-tuple-element.70.refs_0_.est_a), channel_id=1, source_target_pairs={{0,24},{8,0},{16,8},{24,16},{1,25},{9,1},{17,9},{25,17},{2,26},{10... | collective-permute-start | bytes 442376 | tf_op jit(solution)/shard_map/ppermute | solution.py:477
  131.6 6.4 %collective-permute-start.19 = (f32[2,144,128]{2,1,0:T(8,128)S(1)}, f32[2,144,128]{2,1,0:T(8,128)S(1)}, u32[]{:S(2)}, u32[]{:S(2)}) collective-permute-start(f32[2,144,128]{2,1,0:T(8,128)S(1)} %get-tuple-element.71.refs_1_.est_b), channel_id=1, source_target_pairs={{0,8},{8,16},{16,24},{24,0},{1,9},{9,17},{17,25},{25,1},{2,10},{10... | collective-permute-start | bytes 442376 | tf_op jit(solution)/shard_map/ppermute | solution.py:477
  134.1 6.4 %collective-permute-start.17 = (f32[2,144,128]{2,1,0:T(8,128)S(1)}, f32[2,144,128]{2,1,0:T(8,128)S(1)}, u32[]{:S(2)}, u32[]{:S(2)}) collective-permute-start(f32[2,144,128]{2,1,0:T(8,128)S(1)} %collective-permute-done.16.refs_6_), channel_id=1, source_target_pairs={{0,8},{8,16},{16,24},{24,0},{1,9},{9,17},{17,25},{25,1},{2,10},{10... | collective-permute-start | bytes 442376 | tf_op jit(solution)/shard_map/ppermute | solution.py:477
  134.4 6.0 %collective-permute-start.18 = (f32[2,144,128]{2,1,0:T(8,128)S(1)}, f32[2,144,128]{2,1,0:T(8,128)S(1)}, u32[]{:S(2)}, u32[]{:S(2)}) collective-permute-start(f32[2,144,128]{2,1,0:T(8,128)S(1)} %collective-permute-done.15.refs_3_), channel_id=1, source_target_pairs={{0,24},{8,0},{16,8},{24,16},{1,25},{9,1},{17,9},{25,17},{2,26},{10... | collective-permute-start | bytes 442376 | tf_op jit(solution)/shard_map/ppermute | solution.py:477
  144.6 9.4 %collective-permute-start.21 = (f32[2,3,136,128]{3,2,1,0:T(8,128)S(1)}, f32[2,3,136,128]{3,2,1,0:T(8,128)S(1)}, u32[]{:S(2)}, u32[]{:S(2)}) collective-permute-start(f32[2,3,136,128]{3,2,1,0:T(8,128)S(1)} %get-tuple-element.74), channel_id=1, source_target_pairs={{1,2},{3,4},{5,6},{2,1},{4,3},{6,5},{9,10},{11,12},{13,14},{10,9},... | collective-permute-start | bytes 1253384 | tf_op jit(solution)/shard_map/ppermute | solution.py:270
  159.4 9.1 %collective-permute-start.23 = (f32[2,3,128,128]{3,2,1,0:T(8,128)S(1)}, f32[2,3,128,128]{3,2,1,0:T(8,128)S(1)}, u32[]{:S(2)}, u32[]{:S(2)}) collective-permute-start(f32[2,3,128,128]{3,2,1,0:T(8,128)S(1)} %get-tuple-element.78), channel_id=1, source_target_pairs={{1,2},{3,4},{5,6},{2,1},{4,3},{6,5},{9,10},{11,12},{13,14},{10,9},... | collective-permute-start | bytes 1179656 | tf_op jit(solution)/shard_map/ppermute | solution.py:270
  169.9 7.1 %collective-permute-start.25 = (f32[2,128,128]{2,1,0:T(8,128)S(1)}, f32[2,128,128]{2,1,0:T(8,128)S(1)}, u32[]{:S(2)}, u32[]{:S(2)}) collective-permute-start(f32[2,128,128]{2,1,0:T(8,128)S(1)} %get-tuple-element.82), channel_id=1, source_target_pairs={{0,8},{8,16},{16,24},{24,0},{1,9},{9,17},{17,25},{25,1},{2,10},{10... | collective-permute-start | bytes 393224 | tf_op jit(solution)/shard_map/ppermute | solution.py:477
  170.8 6.4 %collective-permute-start.26 = (f32[2,128,128]{2,1,0:T(8,128)S(1)}, f32[2,128,128]{2,1,0:T(8,128)S(1)}, u32[]{:S(2)}, u32[]{:S(2)}) collective-permute-start(f32[2,128,128]{2,1,0:T(8,128)S(1)} %get-tuple-element.84), channel_id=1, source_target_pairs={{0,24},{8,0},{16,8},{24,16},{1,25},{9,1},{17,9},{25,17},{2,26},{10... | collective-permute-start | bytes 393224 | tf_op jit(solution)/shard_map/ppermute | solution.py:477
  173.3 7.8 %collective-permute-start.24 = (f32[2,128,128]{2,1,0:T(8,128)S(1)}, f32[2,128,128]{2,1,0:T(8,128)S(1)}, u32[]{:S(2)}, u32[]{:S(2)}) collective-permute-start(f32[2,128,128]{2,1,0:T(8,128)S(1)} %get-tuple-element.80), channel_id=1, source_target_pairs={{0,24},{8,0},{16,8},{24,16},{1,25},{9,1},{17,9},{25,17},{2,26},{10... | collective-permute-start | bytes 393224 | tf_op jit(solution)/shard_map/ppermute | solution.py:477
  175.2 7.2 %collective-permute-start.28 = (f32[2,128,128]{2,1,0:T(8,128)S(1)}, f32[2,128,128]{2,1,0:T(8,128)S(1)}, u32[]{:S(2)}, u32[]{:S(2)}) collective-permute-start(f32[2,128,128]{2,1,0:T(8,128)S(1)} %get-tuple-element.87), channel_id=1, source_target_pairs={{0,8},{8,16},{16,24},{24,0},{1,9},{9,17},{17,25},{25,1},{2,10},{10... | collective-permute-start | bytes 393224 | tf_op jit(solution)/shard_map/ppermute | solution.py:477
  177.2 7.0 %collective-permute-start.27 = (f32[2,128,128]{2,1,0:T(8,128)S(1)}, f32[2,128,128]{2,1,0:T(8,128)S(1)}, u32[]{:S(2)}, u32[]{:S(2)}) collective-permute-start(f32[2,128,128]{2,1,0:T(8,128)S(1)} %get-tuple-element.85), channel_id=1, source_target_pairs={{0,8},{8,16},{16,24},{24,0},{1,9},{9,17},{17,25},{25,1},{2,10},{10... | collective-permute-start | bytes 393224 | tf_op jit(solution)/shard_map/ppermute | solution.py:477
  184.3 7.0 %collective-permute-start.32 = (f32[2,128,128]{2,1,0:T(8,128)S(1)}, f32[2,128,128]{2,1,0:T(8,128)S(1)}, u32[]{:S(2)}, u32[]{:S(2)}) collective-permute-start(f32[2,128,128]{2,1,0:T(8,128)S(1)} %get-tuple-element.89.refs_0_), channel_id=1, source_target_pairs={{0,8},{8,16},{16,24},{24,0},{1,9},{9,17},{17,25},{25,1},{2,10},{10... | collective-permute-start | bytes 393224 | tf_op jit(solution)/shard_map/ppermute | solution.py:477
  186.2 5.9 %collective-permute-start.31 = (f32[2,128,128]{2,1,0:T(8,128)S(1)}, f32[2,128,128]{2,1,0:T(8,128)S(1)}, u32[]{:S(2)}, u32[]{:S(2)}) collective-permute-start(f32[2,128,128]{2,1,0:T(8,128)S(1)} %get-tuple-element.90.refs_1_), channel_id=1, source_target_pairs={{0,24},{8,0},{16,8},{24,16},{1,25},{9,1},{17,9},{25,17},{2,26},{10... | collective-permute-start | bytes 393224 | tf_op jit(solution)/shard_map/ppermute | solution.py:477
  187.6 6.9 %collective-permute-start.30 = (f32[2,128,128]{2,1,0:T(8,128)S(1)}, f32[2,128,128]{2,1,0:T(8,128)S(1)}, u32[]{:S(2)}, u32[]{:S(2)}) collective-permute-start(f32[2,128,128]{2,1,0:T(8,128)S(1)} %get-tuple-element.89.refs_0_), channel_id=1, source_target_pairs={{0,24},{8,0},{16,8},{24,16},{1,25},{9,1},{17,9},{25,17},{2,26},{10... | collective-permute-start | bytes 393224 | tf_op jit(solution)/shard_map/ppermute | solution.py:477
  189.4 6.2 %collective-permute-start.35 = (f32[2,128,128]{2,1,0:T(8,128)S(1)}, f32[2,128,128]{2,1,0:T(8,128)S(1)}, u32[]{:S(2)}, u32[]{:S(2)}) collective-permute-start(f32[2,128,128]{2,1,0:T(8,128)S(1)} %get-tuple-element.90.refs_1_), channel_id=1, source_target_pairs={{0,8},{8,16},{16,24},{24,0},{1,9},{9,17},{17,25},{25,1},{2,10},{10... | collective-permute-start | bytes 393224 | tf_op jit(solution)/shard_map/ppermute | solution.py:477
  191.3 6.2 %collective-permute-start.33 = (f32[2,128,128]{2,1,0:T(8,128)S(1)}, f32[2,128,128]{2,1,0:T(8,128)S(1)}, u32[]{:S(2)}, u32[]{:S(2)}) collective-permute-start(f32[2,128,128]{2,1,0:T(8,128)S(1)} %collective-permute-done.32.refs_6_), channel_id=1, source_target_pairs={{0,8},{8,16},{16,24},{24,0},{1,9},{9,17},{17,25},{25,1},{2,10},{10... | collective-permute-start | bytes 393224 | tf_op jit(solution)/shard_map/ppermute | solution.py:477
  192.1 5.3 %collective-permute-start.34 = (f32[2,128,128]{2,1,0:T(8,128)S(1)}, f32[2,128,128]{2,1,0:T(8,128)S(1)}, u32[]{:S(2)}, u32[]{:S(2)}) collective-permute-start(f32[2,128,128]{2,1,0:T(8,128)S(1)} %collective-permute-done.31.refs_3_), channel_id=1, source_target_pairs={{0,24},{8,0},{16,8},{24,16},{1,25},{9,1},{17,9},{25,17},{2,26},{10... | collective-permute-start | bytes 393224 | tf_op jit(solution)/shard_map/ppermute | solution.py:477
  (9 other events, 46.9 us)

commit v5 on v4

--- a/solution.py
+++ b/solution.py
@@ -43,7 +43,8 @@
     carry = jnp.zeros((peers, 1), jnp.float32)
     listed = jnp.zeros((2 * peers, BRICK), jnp.float32)
     for g in range(groups):
-        d = dest[g : g + 1, :]
+        here = (g % x_cells, slice(g // x_cells, g // x_cells + 1))
+        d = dest[here]
         hot = d == peer_id
         hot_f = hot.astype(jnp.float32)
         ahead = jnp.dot(hot_f.astype(jnp.bfloat16), before, preferred_element_type=jnp.float32)
@@ -51,8 +52,8 @@
         carry = carry + lane_sum(hot_f)
         rank_i = ranks.astype(jnp.int32)
         pos_v[g : g + 1, :] = d * rows_per + rank_i
-        h = hot_f * high[g : g + 1, :].astype(jnp.float32)
-        l = hot_f * low[g : g + 1, :].astype(jnp.float32)
+        h = hot_f * high[here].astype(jnp.float32)
+        l = hot_f * low[here].astype(jnp.float32)
         both = jnp.concatenate([h, l], axis=0).astype(jnp.bfloat16)
         at = (rank_i == kid).astype(jnp.float32).astype(jnp.bfloat16)
         listed = listed + lax.dot_general(
@@ -104,7 +105,7 @@
     )(shift, target, views)
 
 
-def unpack_kernel(peers, cap, slots, in_ref, out_ref, list_v, idx_v, idx_s, sem):
+def unpack_kernel(peers, cap, slots, id_ref, in_ref, out_ref, inner, outer, list_v, idx_v, idx_s, sem):
     rows_per = cap + 1
     for p in range(peers):
         list_v[p : p + 1, :] = in_ref[p * rows_per + cap]
@@ -123,22 +124,31 @@
         return c
 
     lax.fori_loop(0, peers, per_peer, 0)
-
-
-def unpack(arrived, peers, cap, slots):
-    return pl.pallas_call(
-        functools.partial(unpack_kernel, peers, cap, slots),
-        out_shape=jax.ShapeDtypeStruct((slots + SPARE, BRICK), jnp.float32),
-        in_specs=[pl.BlockSpec(memory_space=pltpu.VMEM)],
-        out_specs=pl.BlockSpec(memory_space=pltpu.VMEM),
-        scratch_shapes=[
+    _, x_cells, deep, _ = inner.shape
+    y_cells = slots // (2 * x_cells)
+    odd = id_ref[4]
+    for c in range(2):
+        for x in range(x_cells):
+            at = (c * x_cells + x) * y_cells
+            near = pl.multiple_of(at + odd * (y_cells - deep), deep)
+            far = pl.multiple_of(at + (1 - odd) * (y_cells - deep), deep)
+            inner[c, x] = out_ref[pl.ds(far, deep), :]
+            outer[c, x] = out_ref[pl.ds(near, deep), :]
+
+
+def unpack(ids, arrived, peers, cap, x_cells, y_cells):
+    slots = 2 * x_cells * y_cells
+    edge = f32(2, x_cells, DEEP, BRICK)
+    return call(
+        functools.partial(unpack_kernel, peers, cap, slots), "unpack",
+        [f32(slots + SPARE, BRICK), edge, edge], (ids, arrived),
+        scratch=[
             pltpu.VMEM((peers, BRICK), jnp.float32),
             pltpu.VMEM((peers, BRICK), jnp.int32),
             pltpu.SMEM((peers, BRICK), jnp.int32),
             pltpu.SemaphoreType.DMA,
         ],
-        name="unpack",
-    )(arrived)
+    )
 
 
 def vmem():
@@ -153,7 +163,7 @@
     return jax.ShapeDtypeStruct(shape, jnp.float32)
 
 
-def call(kernel, name, outs, args, scalars=1, scratch=(), work=4_000_000):
+def call(kernel, name, outs, args, scalars=1, scratch=(), work=1000):
     return pl.pallas_call(
         kernel,
         out_shape=outs,
@@ -210,66 +220,92 @@
     return call(z_first_kernel, "z_blur", [f32(2, x, y + 2 * DEEP, BRICK)], (w, estimate, lo, hi))[0]
 
 
-def z_pieces_kernel(views, w_ref, id_ref, *refs):
-    pieces, out_ref = refs[: 2 * views], refs[2 * views]
-    depth, y_cells, _ = pieces[0].shape
+def z_piece_kernel(w_ref, in_a, in_b, out_a, out_b):
+    depth, y_cells, _ = in_a.shape
     w = taps_of(w_ref, 2, False)
-    for d in range(views):
-        base = lax.rem(id_ref[0] + d, views) * depth
-
-        def body(i, carry, d=d, base=base):
-            for y, n in row_parts(y_cells):
-                at = pl.ds(y, n)
-                a, b = blur_z(pieces[2 * d][i, at, :], pieces[2 * d + 1][i, at, :], w)
-                out_ref[0, base + i, at, :] = a
-                out_ref[1, base + i, at, :] = b
-            return carry
-
-        lax.fori_loop(0, depth, body, 0)
-
-
-def z_pieces(w, ids, pieces):
-    views = len(pieces) // 2
-    depth, y, _ = pieces[0].shape
-    return call(
-        functools.partial(z_pieces_kernel, views), "z_blur_pieces",
-        [f32(2, views * depth, y, BRICK)], (w, ids, *pieces), 2,
-    )[0]
-
-
-def y_kernel(flip, w_ref, id_ref, in_ref, out_ref, inner, outer):
+
+    def body(i, carry):
+        for y, n in row_parts(y_cells):
+            at = pl.ds(y, n)
+            out_a[i, at, :], out_b[i, at, :] = blur_z(in_a[i, at, :], in_b[i, at, :], w)
+        return carry
+
+    lax.fori_loop(0, depth, body, 0)
+
+
+def z_piece(w, a, b):
+    return call(z_piece_kernel, "z_piece", [f32(*a.shape)] * 2, (w, a, b))
+
+
+def y_rows(ref, at, trim, w, y, n):
+    total = w[0] * ref[(*at, pl.ds(trim - HALO + y, n))]
+    for k in range(1, TAPS):
+        total += w[k] * ref[(*at, pl.ds(trim - HALO + k + y, n))]
+    return total
+
+
+def put_layers(id_ref, field, inner, outer):
+    x_cells = field.shape[1]
+    odd = id_ref[1]
+    for c in range(2):
+        for i in range(HALO):
+            inner[c, i] = field[c, (1 - odd) * (x_cells - HALO) + i]
+            outer[c, i] = field[c, odd * (x_cells - HALO) + i]
+
+
+def y_kernel(flip, trim, w_ref, id_ref, in_ref, out_ref, inner, outer):
     _, x_cells, y_cells, _ = out_ref.shape
     w = taps_of(w_ref, 1, flip)
 
     def body(x, carry):
         for c in range(2):
             for y, n in row_parts(y_cells):
-                total = w[0] * in_ref[c, x, pl.ds(TRIM - HALO + y, n), :]
-                for k in range(1, TAPS):
-                    total += w[k] * in_ref[c, x, pl.ds(TRIM - HALO + k + y, n), :]
-                out_ref[c, x, pl.ds(y, n), :] = total
+                out_ref[c, x, pl.ds(y, n), :] = y_rows(in_ref, (c, x), trim, w, y, n)
         return carry
 
     lax.fori_loop(0, x_cells, body, 0)
-    odd = id_ref[1]
-    for c in range(2):
-        for i in range(HALO):
-            inner[c, i] = out_ref[c, (1 - odd) * (x_cells - HALO) + i]
-            outer[c, i] = out_ref[c, odd * (x_cells - HALO) + i]
-
-
-def y_blur(w, ids, field, flip):
-    _, x, y, _ = field.shape
-    y -= 2 * TRIM
-    outs = [f32(2, x, y, BRICK), f32(2, HALO, y, BRICK), f32(2, HALO, y, BRICK)]
-    field, inner, outer = call(
-        functools.partial(y_kernel, flip), "y_blur", outs, (w, ids, field), 2
-    )
+    put_layers(id_ref, out_ref, inner, outer)
+
+
+def y_pieces_kernel(views, w_ref, id_ref, *refs):
+    pieces, (out_ref, inner, outer) = refs[: 2 * views], refs[2 * views :]
+    depth = pieces[0].shape[0]
+    w = taps_of(w_ref, 1, False)
+    for d in range(views):
+        base = lax.rem(id_ref[0] + d, views) * depth
+        for c in range(2):
+            for i in range(depth):
+                for y, n in row_parts(out_ref.shape[2]):
+                    out_ref[c, base + i, pl.ds(y, n), :] = y_rows(pieces[2 * d + c], (i,), TRIM, w, y, n)
+    put_layers(id_ref, out_ref, inner, outer)
+
+
+def swap_layers(field, inner, outer):
     count = lax.axis_size("rows")
     links = [(i, i + 1) for i in range(1, count - 1, 2)]
     outer = lax.ppermute(outer, "rows", links + [(j, i) for i, j in links])
     inner = lax.ppermute(inner, "rows", [(i, i ^ 1) for i in range(count)])
     return field, inner, outer
+
+
+def swap_rows(inner, outer):
+    count = lax.axis_size("blocks")
+    links = [(i, i + 1) for i in range(1, count - 1, 2)]
+    outer = lax.ppermute(outer, "blocks", links + [(j, i) for i, j in links])
+    inner = lax.ppermute(inner, "blocks", [(i, i ^ 1) for i in range(count)])
+    return inner, outer
+
+
+def field_and_layers(x, y):
+    return [f32(2, x, y, BRICK), f32(2, HALO, y, BRICK), f32(2, HALO, y, BRICK)]
+
+
+def y_blur(w, ids, field, flip, trim):
+    _, x, y, _ = field.shape
+    return swap_layers(*call(
+        functools.partial(y_kernel, flip, trim), "y_blur", field_and_layers(x, y - 2 * trim),
+        (w, ids, field), 2,
+    ))
 
 
 def set_sides(id_ref, inner, outer, side):
@@ -329,42 +365,87 @@
     return (row >= id_ref[2]) & (row < id_ref[3])
 
 
-def edges_kernel(moved, first, last):
-    _, x_cells, deep, _ = first.shape
-    y_cells = (moved.shape[0] - SPARE) // (2 * x_cells)
+def ratio_own_kernel(w_ref, below, moved, out_ref):
+    _, x_cells, own, _ = out_ref.shape
+    u = taps_of(w_ref, 2, True)
+    skip = (below.shape[2] - own) // 2
+
+    def body(x, carry):
+        for y, n in row_parts(own):
+            rows = [
+                moved[pl.ds(pl.multiple_of((c * x_cells + x) * own + y, TILE), n), :]
+                / below[c, x, pl.ds(skip + y, n), :]
+                for c in range(2)
+            ]
+            a, b = blur_z(*rows, u)
+            out_ref[0, x, pl.ds(y, n), :] = a
+            out_ref[1, x, pl.ds(y, n), :] = b
+        return carry
+
+    lax.fori_loop(0, x_cells, body, 0)
+
+
+def rim_kernel(w_ref, id_ref, below, own_ref, inner, outer, out_ref, layers_in, layers_out, halo, strip):
+    _, x_cells, own, _ = own_ref.shape
+    u = taps_of(w_ref, 2, True)
+    w = taps_of(w_ref, 1, True)
+    skip = (below.shape[2] - own) // 2
+    span = DEEP + 2 * TRIM
+    odd = id_ref[4]
     for c in range(2):
-        for x in range(x_cells):
-            at = (c * x_cells + x) * y_cells
-            first[c, x] = moved[at : at + deep, :]
-            last[c, x] = moved[at + y_cells - deep : at + y_cells, :]
-
-
-def ratio_first_kernel(w_ref, id_ref, below, moved, lo, hi, out_ref, obs):
-    _, x_cells, y_cells, _ = below.shape
-    own = obs.shape[2] - 2 * DEEP
-    u = taps_of(w_ref, 2, True)
-    base = (own - y_cells) // 2
+        halo[1 - odd, c] = inner[c]
+        halo[odd, c] = outer[c]
+    sides = (
+        (0, DEEP - skip, 0, -skip, 0, skip, 0),
+        (1, 0, skip + own, own, skip, 0, own - skip),
+    )
 
     def body(x, carry):
-        for c in range(2):
-            at = pl.multiple_of((c * x_cells + x) * own, own)
-            obs[c, x, 0:DEEP, :] = lo[c, x]
-            obs[c, x, DEEP : DEEP + own, :] = moved[pl.ds(at, own), :]
-            obs[c, x, DEEP + own : 2 * DEEP + own, :] = hi[c, x]
-        for y, n in row_parts(y_cells):
-            ok = inside(id_ref, base + y, (n, BRICK))
+        for side, obs_at, below_at, row, here, there, rest in sides:
+            ok = inside(id_ref, row, (skip, BRICK))
             rows = [
                 jnp.where(
-                    ok, obs[c, x, DEEP + base + y : DEEP + base + y + n, :] / below[c, x, y : y + n, :], 0.0
+                    ok,
+                    halo[side, c, x, obs_at : obs_at + skip, :]
+                    / below[c, x, below_at : below_at + skip, :],
+                    0.0,
                 )
                 for c in range(2)
             ]
-            a, b = blur_z(*rows, u)
-            out_ref[0, x, y : y + n, :] = a
-            out_ref[1, x, y : y + n, :] = b
+            for c, value in enumerate(blur_z(*rows, u)):
+                strip[c, here : here + skip, :] = value
+                strip[c, there : there + skip, :] = own_ref[c, x, rest : rest + skip, :]
+                out_ref[c, x, side * DEEP : (side + 1) * DEEP, :] = y_rows(strip, (c,), TRIM, w, 0, DEEP)
         return carry
 
     lax.fori_loop(0, x_cells, body, 0)
+    put_layers(id_ref, out_ref, layers_in, layers_out)
+
+
+def rim(w, ids, below, own, inner, outer):
+    _, x, y, _ = own.shape
+    skip = (below.shape[2] - y) // 2
+    return swap_layers(*call(
+        rim_kernel, "rim", field_and_layers(x, 2 * DEEP), (w, ids, below, own, inner, outer), 2,
+        scratch=[
+            pltpu.VMEM((2, 2, x, DEEP, BRICK), jnp.float32),
+            pltpu.VMEM((2, 2 * skip, BRICK), jnp.float32),
+        ],
+    ))
+
+
+def widen_kernel(id_ref, moved, inner, outer, obs):
+    _, x_cells, rows, _ = obs.shape
+    own = rows - 2 * DEEP
+    odd = id_ref[4]
+    for c in range(2):
+        for x in range(x_cells):
+            at = (c * x_cells + x) * own
+            obs[c, x, DEEP : DEEP + own, :] = moved[at : at + own, :]
+            low = pl.multiple_of((1 - odd) * (DEEP + own), DEEP)
+            high = pl.multiple_of(odd * (DEEP + own), DEEP)
+            obs[c, x, pl.ds(low, DEEP), :] = inner[c, x]
+            obs[c, x, pl.ds(high, DEEP), :] = outer[c, x]
 
 
 def ratio_kernel(w_ref, id_ref, field, inner, outer, obs, out_ref, side):
@@ -392,22 +473,26 @@
     lax.fori_loop(0, y_cells // TILE, body, 0)
 
 
-def split_kernel(views, w_ref, id_ref, field, inner, outer, a2, b2, a1, b1, a3, b3, a0, b0, wide):
-    _, x_cells, y_cells, _ = field.shape
+def split_kernel(views, parts, w_ref, id_ref, *refs):
+    fields, outs, wide = refs[: 3 * len(parts)], refs[3 * len(parts) : -1], refs[-1]
+    x_cells = fields[0].shape[1]
+    y_cells = wide.shape[2]
     depth = x_cells // views
     w = taps_of(w_ref, 0, True)
     odd = id_ref[1]
-    for c in range(2):
-        for i in range(HALO):
-            wide[c, (1 - odd) * (HALO + x_cells) + i] = inner[c, i]
-            wide[c, odd * (HALO + x_cells) + i] = outer[c, i]
-        for i in range(x_cells):
-            wide[c, HALO + i] = field[c, i]
-    outs = ((0, a0, b0), (1, a1, b1), (2, a2, b2), (3, a3, b3))
-    for r, out_a, out_b in outs:
+    for p, spans in enumerate(parts):
+        field, inner, outer = fields[3 * p : 3 * p + 3]
+        for y, to, n in spans:
+            for c in range(2):
+                for i in range(HALO):
+                    wide[c, (1 - odd) * (HALO + x_cells) + i, to : to + n, :] = inner[c, i, y : y + n, :]
+                    wide[c, odd * (HALO + x_cells) + i, to : to + n, :] = outer[c, i, y : y + n, :]
+                for i in range(x_cells):
+                    wide[c, HALO + i, to : to + n, :] = field[c, i, y : y + n, :]
+    for r in range(views):
         base = lax.rem(id_ref[0] + r, views) * depth
 
-        def body(t, carry, base=base, pair=(out_a, out_b)):
+        def body(t, carry, base=base, pair=outs[2 * r : 2 * r + 2]):
             at = pl.ds(pl.multiple_of(t * TILE, TILE), TILE)
             for c in range(2):
                 layers = [wide[c, base + i, at, :] for i in range(depth + 2 * HALO)]
@@ -418,12 +503,12 @@
         lax.fori_loop(0, y_cells // TILE, body, 0, unroll=2)
 
 
-def split(w, ids, views, field, inner, outer):
-    _, x, y, _ = field.shape
-    outs = [f32(x // views, y, BRICK)] * 8
+def split(w, ids, views, fields, parts):
+    x = fields[0].shape[1]
+    y = sum(n for spans in parts for _, _, n in spans)
+    outs = [f32(x // views, y, BRICK)] * (2 * views)
     return call(
-        functools.partial(split_kernel, views), "x_blur_split", outs,
-        (w, ids, field, inner, outer), 2,
+        functools.partial(split_kernel, views, parts), "x_blur_split", outs, (w, ids, *fields), 2,
         scratch=[pltpu.VMEM((2, x + 2 * HALO, y, BRICK), jnp.float32)],
     )
 
@@ -457,20 +542,29 @@
 
 
 def join_kernel(views, id_ref, *refs):
-    pieces, out_ref = refs[: 2 * views], refs[2 * views]
+    pieces, out_ref, sems = refs[: 2 * views], refs[2 * views], refs[2 * views + 1]
     depth = pieces[0].shape[0]
+    copies = []
     for d in range(views):
         base = lax.rem(id_ref[0] + d, views) * depth
-        for i in range(depth):
-            out_ref[base + i, :, 0:BRICK] = pieces[2 * d][i]
-            out_ref[base + i, :, BRICK : 2 * BRICK] = pieces[2 * d + 1][i]
-
-
-def exchange(first, last, axis):
-    count = lax.axis_size(axis)
-    up = [(i, i + 1) for i in range(count - 1)]
-    down = [(i + 1, i) for i in range(count - 1)]
-    return lax.ppermute(last, axis, up), lax.ppermute(first, axis, down)
+        for c in range(2):
+            part = out_ref.at[pl.ds(base, depth), :, pl.ds(c * BRICK, BRICK)]
+            copies.append(pltpu.make_async_copy(pieces[2 * d + c], part, sems.at[2 * d + c]))
+    for copy in copies:
+        copy.start()
+    for copy in copies:
+        copy.wait()
+
+
+def join(views, shape, ids, pieces):
+    return pl.pallas_call(
+        functools.partial(join_kernel, views),
+        out_shape=f32(*shape),
+        in_specs=[smem()] + [pl.BlockSpec(memory_space=pl.ANY)] * len(pieces),
+        out_specs=pl.BlockSpec(memory_space=pl.ANY),
+        scratch_shapes=[pltpu.SemaphoreType.DMA((len(pieces),))],
+        name="join",
+    )(ids, *pieces)
 
 
 def turn(value, step, count):
@@ -487,42 +581,63 @@
     brick_count = x_cells * y_cells * brick_cols
     capacity = 2 * brick_count // peer_count
     geo = (peer_count, capacity, x_cells, y_cells, brick_cols, row_count, y_cells * block_count)
-    est_lo, est_hi = exchange(estimate[:, :DEEP], estimate[:, y_cells - DEEP :], "blocks")
-    targets = target[0].transpose(2, 0, 1).reshape(brick_cols * x_cells, y_cells)
+    block, row = lax.axis_index("blocks"), lax.axis_index("rows")
+    odd = block % 2
+    sent = [
+        lax.dynamic_slice_in_dim(estimate, at * (y_cells - DEEP), DEEP, 1) for at in (1 - odd, odd)
+    ]
+    est_in, est_out = swap_rows(*sent)
+    targets = target[0].transpose(0, 2, 1)
     outgoing = pack(shifts, targets, views_data[0], geo)
-    outgoing, est_lo, est_hi = lax.optimization_barrier((outgoing, est_lo, est_hi))
+    outgoing, est_in, est_out = lax.optimization_barrier((outgoing, est_in, est_out))
+    est_lo = jnp.where(odd == 1, est_in, est_out)
+    est_hi = jnp.where(odd == 1, est_out, est_in)
     arrived = lax.all_to_all(
         outgoing.reshape(peer_count, capacity + 1, 1, BRICK),
         ("blocks", "rows"), split_axis=0, concat_axis=0, tiled=True,
     ).reshape(peer_count * (capacity + 1), 1, BRICK)
     w = (psf_taps[0] / jnp.sum(psf_taps[0], axis=1, keepdims=True)).reshape(-1)
-    block = lax.axis_index("blocks")
     ids = jnp.stack([
         lax.axis_index("views"),
-        lax.axis_index("rows") % 2,
+        row % 2,
         jnp.where(block == 0, 0, -DEEP),
         jnp.where(block == block_count - 1, y_cells, y_cells + DEEP),
+        odd,
     ]).astype(jnp.int32)
     pieces = None
     for iteration in range(ITERS):
         if pieces is None:
             field = z_first(w, estimate, est_lo, est_hi)
-            below = x_blur(w, ids, *y_blur(w, ids, field, False))
-            moved = unpack(arrived, peer_count, capacity, brick_count)
-            edge = f32(2, x_cells, DEEP, BRICK)
-            lo, hi = exchange(*call(edges_kernel, "edges", [edge, edge], (moved,), 0), "blocks")
-            field, obs = call(
-                ratio_first_kernel, "ratio_first",
-                [f32(*below.shape), f32(2, x_cells, y_cells + 2 * DEEP, BRICK)],
-                (w, ids, below, moved, lo, hi), 2,
-            )
+            below = x_blur(w, ids, *y_blur(w, ids, field, False, TRIM))
+            arrived, below = lax.optimization_barrier((arrived, below))
+            moved, inner, outer = unpack(ids, arrived, peer_count, capacity, x_cells, y_cells)
+            inner, outer = swap_rows(inner, outer)
+            own = call(
+                ratio_own_kernel, "ratio_own", [f32(2, x_cells, y_cells, BRICK)], (w, below, moved)
+            )[0]
+            middle = y_blur(w, ids, own, True, TILE)
+            ends = rim(w, ids, below, own, inner, outer)
+            obs = call(
+                widen_kernel, "widen", [f32(2, x_cells, y_cells + 2 * DEEP, BRICK)],
+                (ids, moved, inner, outer),
+            )[0]
+            wider = y_cells + 2 * TILE
+            parts = (((0, DEEP, wider - 2 * DEEP),), ((0, 0, DEEP), (DEEP, wider - DEEP, DEEP)))
+            sent = split(w, ids, view_count, (*middle, *ends), parts)
         else:
-            field, inner, outer = y_blur(w, ids, z_pieces(w, ids, pieces), False)
+            y = pieces[0].shape[1] - 2 * TRIM
+            field, inner, outer = swap_layers(*call(
+                functools.partial(y_pieces_kernel, view_count), "y_blur_pieces",
+                field_and_layers(x_cells, y),
+                (w, ids, *(z for d in range(view_count) for z in z_piece(w, *pieces[2 * d : 2 * d + 2]))),
+                2,
+            ))
             field = call(
                 ratio_kernel, "ratio", [f32(*field.shape)], (w, ids, field, inner, outer, obs), 2,
                 scratch=[sides(field)],
             )[0]
-        a2, b2, a1, b1, a3, b3, a0, b0 = split(w, ids, view_count, *y_blur(w, ids, field, True))
+            sent = split(w, ids, view_count, y_blur(w, ids, field, True, TRIM), (((0, 0, y_cells),),))
+        a0, b0, a1, b1, a2, b2, a3, b3 = sent
         pair = [f32(*a0.shape)] * 2
         ra, rb = turn(a2, 1, view_count), turn(b2, -1, view_count)
         near_b, near_a = turn(b1, 1, view_count), turn(a3, -1, view_count)
@@ -543,10 +658,7 @@
         prev_b, next_a = turn(own[1], 1, view_count), turn(own[0], -1, view_count)
         far_a, far_b = turn(prev_a, 1, view_count), turn(next_b, -1, view_count)
         pieces = (*own, next_a, next_b, far_a, far_b, prev_a, prev_b)
-    return call(
-        functools.partial(join_kernel, view_count), "join", [f32(x_cells, y_cells, z_cells)],
-        (ids, *pieces),
-    )[0]
+    return join(view_count, estimate.shape, ids, pieces)
 
 
 def solution(mesh):

time: 201 us -> 227 us (1.13)
  Pallas kernels: 38.1 us -> 70.6 us
  waiting for transfers between devices: 86.9 us -> 82.8 us
    pallas_call x1, Pallas kernels: 7.25 us -> 33.6 us  [join(): pl.pallas_call(functools.partial(join_kernel, views), out_shape=f32(*shap...]
    all_to_all x1, waiting for transfers between devices: 42.7 us -> 29.6 us  [per_device(): lax.all_to_all(outgoing.reshape(peer_count, capacity + 1, 1, BRICK), ('bl...]
    ppermute x12 -> x14, waiting for transfers between devices: 22.9 us -> 35.6 us  [the longest x5 29.8 us: swap_layers(): outer = lax.ppermute(outer, 'rows', links + [(j, i) for i, j in links])]
    pallas_call x17 -> x21, Pallas kernels: 24.9 us -> 31.1 us  [call(): pl.pallas_call(kernel, out_shape=outs, in_specs=[smem()] * scalars + [vme...]
    ppermute x24, waiting for transfers between devices: 21.3 us -> 17.6 us  [turn(): lax.ppermute(value, 'views', [(i, (i + step) % count) for i in range(coun...]
    ppermute x12 -> x14, starting transfers between devices: 22.1 us -> 19.4 us  [the longest x5 10.7 us: swap_layers(): outer = lax.ppermute(outer, 'rows', links + [(j, i) for i, j in links])]
  transfers between devices with their start and end apart: 37 -> 39, of which waited for: 20 -> 20; matrix products, arithmetic and copies ran while one was open for 1% -> 1% of each run, Pallas kernels for 10% -> 8%
where the time goes in v5:
time: 227 us
  waiting for transfers between devices  82.8 us (36%)
  Pallas kernels  70.6 us (31%)
  starting transfers between devices  67.8 us (30%)
  local copies, waits for them, and re-layouts  3.23 us (1%)
    ppermute x24, starting transfers between devices, turn(): lax.ppermute(value, 'views', [(i, (i + step) % count) for i in range(coun...  36.8 us
    pallas_call x1, Pallas kernels, join(): pl.pallas_call(functools.partial(join_kernel, views), out_shape=f32(*shap...  33.6 us
    pallas_call x21, Pallas kernels, call(): pl.pallas_call(kernel, out_shape=outs, in_specs=[smem()] * scalars + [vme...  31.1 us
    ppermute x5, waiting for transfers between devices, swap_layers(): outer = lax.ppermute(outer, 'rows', links + [(j, i) for i, j in links])  29.8 us
    all_to_all x1, waiting for transfers between devices, per_device(): lax.all_to_all(outgoing.reshape(peer_count, capacity + 1, 1, BRICK), ('bl...  29.6 us
    ppermute x24, waiting for transfers between devices, turn(): lax.ppermute(value, 'views', [(i, (i + step) % count) for i in range(coun...  17.6 us
    all_to_all x1, starting transfers between devices, per_device(): lax.all_to_all(outgoing.reshape(peer_count, capacity + 1, 1, BRICK), ('bl...  11.7 us
    ppermute x5, starting transfers between devices, swap_layers(): outer = lax.ppermute(outer, 'rows', links + [(j, i) for i, j in links])  10.7 us
  transfers between devices with their start and end apart: 39, of which 20 were waited for; matrix products, arithmetic and copies ran while one was open for 1% of the time, Pallas kernels for 8%

profile of v5, /device:TPU:34, one launch (start us, length us, event | category | flops | bytes accessed | tf_op | source)
XLA Modules:
  0.0 226.9 jit_solution(12961357612978493425)
XLA Ops:
  1.0 3.8 %collective-permute-start.1 = (f32[8,16,256]{2,1,0:T(8,128)S(1)}, f32[8,16,256]{2,1,0:T(8,128)S(1)}, u32[]{:S(2)}, u32[]{:S(2)}) collective-permute-start(f32[8,16,256]{2,1,0:T(8,128)S(1)} %get-tuple-element.117), channel_id=1, source_target_pairs={{32,64},{96,128},{160,192},{64,32},{128,96},{192,160},{33,65},{97,... | collective-permute-start | bytes 393224 | tf_op jit(solution)/shard_map/ppermute | solution.py:294
  5.6 5.9 %pack.1 = f32[4160,1,128]{2,1,0:T(1,128)} custom-call(s32[1]{0:T(128)S(6)} %copy.6.shift_ref, s32[8,2,128]{2,1,0:T(2,128)} %bitcast.14, f32[8,128,256]{2,1,0:T(8,128)} %bitcast.13), custom_call_target="tpu_custom_call" | custom-call | tf_op jit(solution)/shard_map/pack/pallas_call | solution.py:89
  12.2 11.7 %all-to-all-start = ((f32[64,65,1,128]{3,2,1,0:T(1,128)}), f32[64,65,1,128]{3,2,1,0:T(1,128)S(1)}, u32[]{:S(2)}, u32[]{:S(2)}) async-start(f32[64,65,1,128]{3,2,1,0:T(1,128)} %bitcast.12), calls=%async_computation | async-start | bytes 4259840 | tf_op jit(solution)/shard_map/all_to_all | solution.py:595
  25.3 3.1 %z_blur.1.in_ref = f32[2,8,160,128]{3,2,1,0:T(8,128)S(1)} custom-call(f32[21]{0:T(128)S(1)} %div.13.w_ref, f32[8,128,256]{2,1,0:T(8,128)S(1)} %copy-done, f32[8,16,256]{2,1,0:T(8,128)S(1)} %get-tuple-element.120.lo, f32[8,16,256]{2,1,0:T(8,128)S(1)} %get-tuple-element.119.hi), custom_call_target="tpu_custom_call" | custom-call | flops 1000 | bytes 1000 | tf_op jit(solution)/shard_map/z_blur/pallas_call | solution.py:167
  29.9 2.4 %collective-permute-start.3 = (f32[2,3,152,128]{3,2,1,0:T(8,128)S(1)}, f32[2,3,152,128]{3,2,1,0:T(8,128)S(1)}, u32[]{:S(2)}, u32[]{:S(2)}) collective-permute-start(f32[2,3,152,128]{3,2,1,0:T(8,128)S(1)} %get-tuple-element.65), channel_id=1, source_target_pairs={{1,2},{3,4},{5,6},{2,1},{4,3},{6,5},{9,10},{11,12},{13,14},{10,9},... | collective-permute-start | bytes 1400840 | tf_op jit(solution)/shard_map/ppermute | solution.py:286
  32.3 11.9 %collective-permute-done.3.outer = f32[2,3,152,128]{3,2,1,0:T(8,128)S(1)} collective-permute-done((f32[2,3,152,128]{3,2,1,0:T(8,128)S(1)}, f32[2,3,152,128]{3,2,1,0:T(8,128)S(1)}, u32[]{:S(2)}, u32[]{:S(2)}) %collective-permute-start.3) | collective-permute-done | bytes 466976 | tf_op jit(solution)/shard_map/ppermute | solution.py:286
  45.4 29.6 %all-to-all-done = f32[64,65,1,128]{3,2,1,0:T(1,128)S(1)} async-done(((f32[64,65,1,128]{3,2,1,0:T(1,128)}), f32[64,65,1,128]{3,2,1,0:T(1,128)S(1)}, u32[]{:S(2)}, u32[]{:S(2)}) %all-to-all-start) | async-done | bytes 2129952 | tf_op jit(solution)/shard_map/all_to_all | solution.py:595
  75.0 5.2 %unpack.1 = (f32[2056,128]{1,0:T(8,128)S(1)}, f32[2,8,16,128]{3,2,1,0:T(8,128)S(1)}, f32[2,8,16,128]{3,2,1,0:T(8,128)S(1)}) custom-call(s32[5]{0:T(128)S(1)} %stack.23.id_ref, f32[4160,1,128]{2,1,0:T(1,128)S(1)} %bitcast.11), custom_call_target="tpu_custom_call" | custom-call | flops 1000 | bytes 1000 | tf_op jit(solution)/shard_map/unpack/pallas_call | solution.py:167
  80.3 2.8 %ratio_own.1.in_ref.own_ref = f32[2,8,128,128]{3,2,1,0:T(8,128)S(1)} custom-call(f32[21]{0:T(128)S(1)} %div.13.w_ref, f32[2,8,152,128]{3,2,1,0:T(8,128)S(1)} %x_blur.1.below, f32[2056,128]{1,0:T(8,128)S(1)} %get-tuple-element.68.moved), custom_call_target="tpu_custom_call" | custom-call | flops 1000 | bytes 1000 | tf_op jit(solution)/shard_map/ratio_own/pallas_call | solution.py:167
  84.2 2.5 %collective-permute-start.5 = (f32[2,3,112,128]{3,2,1,0:T(8,128)S(1)}, f32[2,3,112,128]{3,2,1,0:T(8,128)S(1)}, u32[]{:S(2)}, u32[]{:S(2)}) collective-permute-start(f32[2,3,112,128]{3,2,1,0:T(8,128)S(1)} %get-tuple-element.71), channel_id=1, source_target_pairs={{1,2},{3,4},{5,6},{2,1},{4,3},{6,5},{9,10},{11,12},{13,14},{10,9},... | collective-permute-start | bytes 1032200 | tf_op jit(solution)/shard_map/ppermute | solution.py:286
  88.2 2.2 collective-permute-start.7
  90.4 2.8 %collective-permute-done.6.inner = f32[2,8,16,128]{3,2,1,0:T(8,128)S(1)} collective-permute-done((f32[2,8,16,128]{3,2,1,0:T(8,128)S(1)}, f32[2,8,16,128]{3,2,1,0:T(8,128)S(1)}, u32[]{:S(2)}, u32[]{:S(2)}) %collective-permute-start.6) | collective-permute-done | bytes 131104 | tf_op jit(solution)/shard_map/ppermute | solution.py:295
  93.2 3.0 %collective-permute-done.7.outer = f32[2,8,16,128]{3,2,1,0:T(8,128)S(1)} collective-permute-done((f32[2,8,16,128]{3,2,1,0:T(8,128)S(1)}, f32[2,8,16,128]{3,2,1,0:T(8,128)S(1)}, u32[]{:S(2)}, u32[]{:S(2)}) %collective-permute-start.7) | collective-permute-done | bytes 131104 | tf_op jit(solution)/shard_map/ppermute | solution.py:294
  98.0 1.9 collective-permute-start.9
  100.0 4.0 %collective-permute-done.9.refs_5_ = f32[2,3,32,128]{3,2,1,0:T(8,128)S(1)} collective-permute-done((f32[2,3,32,128]{3,2,1,0:T(8,128)S(1)}, f32[2,3,32,128]{3,2,1,0:T(8,128)S(1)}, u32[]{:S(2)}, u32[]{:S(2)}) %collective-permute-start.9) | collective-permute-done | bytes 98336 | tf_op jit(solution)/shard_map/ppermute | solution.py:286
  110.8 2.2 collective-permute-done.11.ra
  117.6 2.8 %collective-permute-done.13.a2 = f32[2,144,128]{2,1,0:T(8,128)S(1)} collective-permute-done((f32[2,144,128]{2,1,0:T(8,128)S(1)}, f32[2,144,128]{2,1,0:T(8,128)S(1)}, u32[]{:S(2)}, u32[]{:S(2)}) %collective-permute-start.13) | collective-permute-done | bytes 147488 | tf_op jit(solution)/shard_map/ppermute | solution.py:571
  122.8 2.0 collective-permute-start.17
  124.8 3.2 %collective-permute-start.16 = (f32[2,144,128]{2,1,0:T(8,128)S(1)}, f32[2,144,128]{2,1,0:T(8,128)S(1)}, u32[]{:S(2)}, u32[]{:S(2)}) collective-permute-start(f32[2,144,128]{2,1,0:T(8,128)S(1)} %get-tuple-element.87.in_a.est_a), channel_id=1, source_target_pairs={{0,24},{8,0},{16,8},{24,16},{1,25},{9,1},{17,9},{25,17},{2,26},{10... | collective-permute-start | bytes 442376 | tf_op jit(solution)/shard_map/ppermute | solution.py:571
  129.5 3.2 %collective-permute-start.20 = (f32[2,144,128]{2,1,0:T(8,128)S(1)}, f32[2,144,128]{2,1,0:T(8,128)S(1)}, u32[]{:S(2)}, u32[]{:S(2)}) collective-permute-start(f32[2,144,128]{2,1,0:T(8,128)S(1)} %collective-permute-done.17.in_b), channel_id=1, source_target_pairs={{0,24},{8,0},{16,8},{24,16},{1,25},{9,1},{17,9},{25,17},{2,26},{10... | collective-permute-start | bytes 442376 | tf_op jit(solution)/shard_map/ppermute | solution.py:571
  138.5 1.9 collective-permute-start.23
  141.1 6.8 %collective-permute-done.23.outer = f32[2,3,136,128]{3,2,1,0:T(8,128)S(1)} collective-permute-done((f32[2,3,136,128]{3,2,1,0:T(8,128)S(1)}, f32[2,3,136,128]{3,2,1,0:T(8,128)S(1)}, u32[]{:S(2)}, u32[]{:S(2)}) %collective-permute-start.23) | collective-permute-done | bytes 417824 | tf_op jit(solution)/shard_map/ppermute | solution.py:286
  147.9 3.8 %ratio.1.in_ref = f32[2,8,136,128]{3,2,1,0:T(8,128)S(1)} custom-call(f32[21]{0:T(128)S(1)} %div.13.w_ref, s32[5]{0:T(128)S(1)} %stack.23.id_ref, f32[2,8,136,128]{3,2,1,0:T(8,128)S(1)} %get-tuple-element.97.field, f32[2,3,136,128]{3,2,1,0:T(8,128)S(1)} %collective-permute-done.22.inner, f32[2,3,136,128]{3,2,1,0:T(8,128)S(1)} %collective-permute-done.23.outer, ...), custom_call_target="tpu_custom_call" | custom-call | flops 1000 | bytes 1000 | tf_op jit(solution)/shard_map/ratio/pallas_call | solution.py:167
  155.3 7.2 %collective-permute-done.25.refs_2_ = f32[2,3,128,128]{3,2,1,0:T(8,128)S(1)} collective-permute-done((f32[2,3,128,128]{3,2,1,0:T(8,128)S(1)}, f32[2,3,128,128]{3,2,1,0:T(8,128)S(1)}, u32[]{:S(2)}, u32[]{:S(2)}) %collective-permute-start.25) | collective-permute-done | bytes 393248 | tf_op jit(solution)/shard_map/ppermute | solution.py:286
  163.9 3.2 %collective-permute-start.28 = (f32[2,128,128]{2,1,0:T(8,128)S(1)}, f32[2,128,128]{2,1,0:T(8,128)S(1)}, u32[]{:S(2)}, u32[]{:S(2)}) collective-permute-start(f32[2,128,128]{2,1,0:T(8,128)S(1)} %get-tuple-element.108), channel_id=1, source_target_pairs={{0,24},{8,0},{16,8},{24,16},{1,25},{9,1},{17,9},{25,17},{2,26},{10... | collective-permute-start | bytes 393224 | tf_op jit(solution)/shard_map/ppermute | solution.py:571
  172.6 2.3 %collective-permute-start.31 = (f32[2,128,128]{2,1,0:T(8,128)S(1)}, f32[2,128,128]{2,1,0:T(8,128)S(1)}, u32[]{:S(2)}, u32[]{:S(2)}) collective-permute-start(f32[2,128,128]{2,1,0:T(8,128)S(1)} %get-tuple-element.112), channel_id=1, source_target_pairs={{0,24},{8,0},{16,8},{24,16},{1,25},{9,1},{17,9},{25,17},{2,26},{10... | collective-permute-start | bytes 393224 | tf_op jit(solution)/shard_map/ppermute | solution.py:571
  177.9 2.2 collective-permute-start.34
  181.6 1.9 collective-permute-start.32
  183.6 2.0 collective-permute-done.34.refs_6_
  186.4 2.5 %collective-permute-start.36 = (f32[2,128,128]{2,1,0:T(8,128)S(1)}, f32[2,128,128]{2,1,0:T(8,128)S(1)}, u32[]{:S(2)}, u32[]{:S(2)}) collective-permute-start(f32[2,128,128]{2,1,0:T(8,128)S(1)} %collective-permute-done.33.refs_3_), channel_id=1, source_target_pairs={{0,24},{8,0},{16,8},{24,16},{1,25},{9,1},{17,9},{25,17},{2,26},{10... | collective-permute-start | bytes 393224 | tf_op jit(solution)/shard_map/ppermute | solution.py:571
  189.7 2.1 collective-permute-done.35.refs_4_
  193.1 33.6 %join.1 = f32[8,128,256]{2,1,0:T(8,128)} custom-call(s32[5]{0:T(128)} %copy-done.6, f32[2,128,128]{2,1,0:T(8,128)} %copy-done.4, f32[2,128,128]{2,1,0:T(8,128)} %copy-done.5, f32[2,128,128]{2,1,0:T(8,128)} %copy-done.10, f32[2,128,128]{2,1,0:T(8,128)} %copy-done.9, f32[2,128,128]{2,1,0:T(8,128)} %copy-done.12, f32[2,128,128]{2,1,0:T(8,128)} %copy-done.13, ...), custom_call_target="tpu_custom_call" | custom-call | tf_op jit(solution)/shard_map/join/pallas_call | solution.py:560
  (107 shorter events, 49.9 us)
Async XLA Ops:
  1.0 10.5 %collective-permute-start.1 = (f32[8,16,256]{2,1,0:T(8,128)S(1)}, f32[8,16,256]{2,1,0:T(8,128)S(1)}, u32[]{:S(2)}, u32[]{:S(2)}) collective-permute-start(f32[8,16,256]{2,1,0:T(8,128)S(1)} %get-tuple-element.117), channel_id=1, source_target_pairs={{32,64},{96,128},{160,192},{64,32},{128,96},{192,160},{33,65},{97,... | collective-permute-start | bytes 393224 | tf_op jit(solution)/shard_map/ppermute | solution.py:294
  4.8 6.7 %collective-permute-start = (f32[8,16,256]{2,1,0:T(8,128)S(1)}, f32[8,16,256]{2,1,0:T(8,128)S(1)}, u32[]{:S(2)}, u32[]{:S(2)}) collective-permute-start(f32[8,16,256]{2,1,0:T(8,128)S(1)} %get-tuple-element.118), channel_id=1, source_target_pairs={{0,32},{32,0},{64,96},{96,64},{128,160},{160,128},{192,224},{224,1... | collective-permute-start | bytes 393224 | tf_op jit(solution)/shard_map/ppermute | solution.py:295
  12.2 62.8 %all-to-all-start = ((f32[64,65,1,128]{3,2,1,0:T(1,128)}), f32[64,65,1,128]{3,2,1,0:T(1,128)S(1)}, u32[]{:S(2)}, u32[]{:S(2)}) async-start(f32[64,65,1,128]{3,2,1,0:T(1,128)} %bitcast.12), calls=%async_computation | async-start | bytes 4259840 | tf_op jit(solution)/shard_map/all_to_all | solution.py:595
  29.9 14.3 %collective-permute-start.3 = (f32[2,3,152,128]{3,2,1,0:T(8,128)S(1)}, f32[2,3,152,128]{3,2,1,0:T(8,128)S(1)}, u32[]{:S(2)}, u32[]{:S(2)}) collective-permute-start(f32[2,3,152,128]{3,2,1,0:T(8,128)S(1)} %get-tuple-element.65), channel_id=1, source_target_pairs={{1,2},{3,4},{5,6},{2,1},{4,3},{6,5},{9,10},{11,12},{13,14},{10,9},... | collective-permute-start | bytes 1400840 | tf_op jit(solution)/shard_map/ppermute | solution.py:286
  84.1 19.9 %collective-permute-start.4 = (f32[2,3,112,128]{3,2,1,0:T(8,128)S(1)}, f32[2,3,112,128]{3,2,1,0:T(8,128)S(1)}, u32[]{:S(2)}, u32[]{:S(2)}) collective-permute-start(f32[2,3,112,128]{3,2,1,0:T(8,128)S(1)} %get-tuple-element.70), channel_id=1, source_target_pairs={{0,1},{1,0},{2,3},{3,2},{4,5},{5,4},{6,7},{7,6},{8,9},{9,8},{10,11... | collective-permute-start | bytes 1032200 | tf_op jit(solution)/shard_map/ppermute | solution.py:287
  84.2 19.8 %collective-permute-start.5 = (f32[2,3,112,128]{3,2,1,0:T(8,128)S(1)}, f32[2,3,112,128]{3,2,1,0:T(8,128)S(1)}, u32[]{:S(2)}, u32[]{:S(2)}) collective-permute-start(f32[2,3,112,128]{3,2,1,0:T(8,128)S(1)} %get-tuple-element.71), channel_id=1, source_target_pairs={{1,2},{3,4},{5,6},{2,1},{4,3},{6,5},{9,10},{11,12},{13,14},{10,9},... | collective-permute-start | bytes 1032200 | tf_op jit(solution)/shard_map/ppermute | solution.py:286
  86.7 6.4 %collective-permute-start.6 = (f32[2,8,16,128]{3,2,1,0:T(8,128)S(1)}, f32[2,8,16,128]{3,2,1,0:T(8,128)S(1)}, u32[]{:S(2)}, u32[]{:S(2)}) collective-permute-start(f32[2,8,16,128]{3,2,1,0:T(8,128)S(1)} %get-tuple-element.72), channel_id=1, source_target_pairs={{0,32},{32,0},{64,96},{96,64},{128,160},{160,128},{192,224},{224,1... | collective-permute-start | bytes 393224 | tf_op jit(solution)/shard_map/ppermute | solution.py:295
  88.2 8.0 %collective-permute-start.7 = (f32[2,8,16,128]{3,2,1,0:T(8,128)S(1)}, f32[2,8,16,128]{3,2,1,0:T(8,128)S(1)}, u32[]{:S(2)}, u32[]{:S(2)}) collective-permute-start(f32[2,8,16,128]{3,2,1,0:T(8,128)S(1)} %get-tuple-element.73), channel_id=1, source_target_pairs={{32,64},{96,128},{160,192},{64,32},{128,96},{192,160},{33,65},{97,... | collective-permute-start | bytes 393224 | tf_op jit(solution)/shard_map/ppermute | solution.py:294
  98.0 5.9 %collective-permute-start.9 = (f32[2,3,32,128]{3,2,1,0:T(8,128)S(1)}, f32[2,3,32,128]{3,2,1,0:T(8,128)S(1)}, u32[]{:S(2)}, u32[]{:S(2)}) collective-permute-start(f32[2,3,32,128]{3,2,1,0:T(8,128)S(1)} %get-tuple-element.76), channel_id=1, source_target_pairs={{1,2},{3,4},{5,6},{2,1},{4,3},{6,5},{9,10},{11,12},{13,14},{10,9},... | collective-permute-start | bytes 294920 | tf_op jit(solution)/shard_map/ppermute | solution.py:286
  105.5 7.6 %collective-permute-start.11 = (f32[2,144,128]{2,1,0:T(8,128)S(1)}, f32[2,144,128]{2,1,0:T(8,128)S(1)}, u32[]{:S(2)}, u32[]{:S(2)}) collective-permute-start(f32[2,144,128]{2,1,0:T(8,128)S(1)} %get-tuple-element.80), channel_id=1, source_target_pairs={{0,8},{8,16},{16,24},{24,0},{1,9},{9,17},{17,25},{25,1},{2,10},{10... | collective-permute-start | bytes 442376 | tf_op jit(solution)/shard_map/ppermute | solution.py:571
  107.1 6.7 %collective-permute-start.12 = (f32[2,144,128]{2,1,0:T(8,128)S(1)}, f32[2,144,128]{2,1,0:T(8,128)S(1)}, u32[]{:S(2)}, u32[]{:S(2)}) collective-permute-start(f32[2,144,128]{2,1,0:T(8,128)S(1)} %get-tuple-element.82), channel_id=1, source_target_pairs={{0,24},{8,0},{16,8},{24,16},{1,25},{9,1},{17,9},{25,17},{2,26},{10... | collective-permute-start | bytes 442376 | tf_op jit(solution)/shard_map/ppermute | solution.py:571
  108.8 8.4 %collective-permute-start.10 = (f32[2,144,128]{2,1,0:T(8,128)S(1)}, f32[2,144,128]{2,1,0:T(8,128)S(1)}, u32[]{:S(2)}, u32[]{:S(2)}) collective-permute-start(f32[2,144,128]{2,1,0:T(8,128)S(1)} %get-tuple-element.78), channel_id=1, source_target_pairs={{0,24},{8,0},{16,8},{24,16},{1,25},{9,1},{17,9},{25,17},{2,26},{10... | collective-permute-start | bytes 442376 | tf_op jit(solution)/shard_map/ppermute | solution.py:571
  110.6 7.0 %collective-permute-start.14 = (f32[2,144,128]{2,1,0:T(8,128)S(1)}, f32[2,144,128]{2,1,0:T(8,128)S(1)}, u32[]{:S(2)}, u32[]{:S(2)}) collective-permute-start(f32[2,144,128]{2,1,0:T(8,128)S(1)} %get-tuple-element.85), channel_id=1, source_target_pairs={{0,8},{8,16},{16,24},{24,0},{1,9},{9,17},{17,25},{25,1},{2,10},{10... | collective-permute-start | bytes 442376 | tf_op jit(solution)/shard_map/ppermute | solution.py:571
  113.8 6.5 %collective-permute-start.13 = (f32[2,144,128]{2,1,0:T(8,128)S(1)}, f32[2,144,128]{2,1,0:T(8,128)S(1)}, u32[]{:S(2)}, u32[]{:S(2)}) collective-permute-start(f32[2,144,128]{2,1,0:T(8,128)S(1)} %get-tuple-element.83), channel_id=1, source_target_pairs={{0,8},{8,16},{16,24},{24,0},{1,9},{9,17},{17,25},{25,1},{2,10},{10... | collective-permute-start | bytes 442376 | tf_op jit(solution)/shard_map/ppermute | solution.py:571
  121.3 8.2 %collective-permute-start.18 = (f32[2,144,128]{2,1,0:T(8,128)S(1)}, f32[2,144,128]{2,1,0:T(8,128)S(1)}, u32[]{:S(2)}, u32[]{:S(2)}) collective-permute-start(f32[2,144,128]{2,1,0:T(8,128)S(1)} %get-tuple-element.87.in_a.est_a), channel_id=1, source_target_pairs={{0,8},{8,16},{16,24},{24,0},{1,9},{9,17},{17,25},{25,1},{2,10},{10... | collective-permute-start | bytes 442376 | tf_op jit(solution)/shard_map/ppermute | solution.py:571
  122.8 6.7 %collective-permute-start.17 = (f32[2,144,128]{2,1,0:T(8,128)S(1)}, f32[2,144,128]{2,1,0:T(8,128)S(1)}, u32[]{:S(2)}, u32[]{:S(2)}) collective-permute-start(f32[2,144,128]{2,1,0:T(8,128)S(1)} %get-tuple-element.88.in_b.est_b), channel_id=1, source_target_pairs={{0,24},{8,0},{16,8},{24,16},{1,25},{9,1},{17,9},{25,17},{2,26},{10... | collective-permute-start | bytes 442376 | tf_op jit(solution)/shard_map/ppermute | solution.py:571
  124.8 9.1 %collective-permute-start.21 = (f32[2,144,128]{2,1,0:T(8,128)S(1)}, f32[2,144,128]{2,1,0:T(8,128)S(1)}, u32[]{:S(2)}, u32[]{:S(2)}) collective-permute-start(f32[2,144,128]{2,1,0:T(8,128)S(1)} %get-tuple-element.88.in_b.est_b), channel_id=1, source_target_pairs={{0,8},{8,16},{16,24},{24,0},{1,9},{9,17},{17,25},{25,1},{2,10},{10... | collective-permute-start | bytes 442376 | tf_op jit(solution)/shard_map/ppermute | solution.py:571
  124.8 10.2 %collective-permute-start.16 = (f32[2,144,128]{2,1,0:T(8,128)S(1)}, f32[2,144,128]{2,1,0:T(8,128)S(1)}, u32[]{:S(2)}, u32[]{:S(2)}) collective-permute-start(f32[2,144,128]{2,1,0:T(8,128)S(1)} %get-tuple-element.87.in_a.est_a), channel_id=1, source_target_pairs={{0,24},{8,0},{16,8},{24,16},{1,25},{9,1},{17,9},{25,17},{2,26},{10... | collective-permute-start | bytes 442376 | tf_op jit(solution)/shard_map/ppermute | solution.py:571
  129.5 6.7 %collective-permute-start.19 = (f32[2,144,128]{2,1,0:T(8,128)S(1)}, f32[2,144,128]{2,1,0:T(8,128)S(1)}, u32[]{:S(2)}, u32[]{:S(2)}) collective-permute-start(f32[2,144,128]{2,1,0:T(8,128)S(1)} %collective-permute-done.18.in_a), channel_id=1, source_target_pairs={{0,8},{8,16},{16,24},{24,0},{1,9},{9,17},{17,25},{25,1},{2,10},{10... | collective-permute-start | bytes 442376 | tf_op jit(solution)/shard_map/ppermute | solution.py:571
  129.5 6.7 %collective-permute-start.20 = (f32[2,144,128]{2,1,0:T(8,128)S(1)}, f32[2,144,128]{2,1,0:T(8,128)S(1)}, u32[]{:S(2)}, u32[]{:S(2)}) collective-permute-start(f32[2,144,128]{2,1,0:T(8,128)S(1)} %collective-permute-done.17.in_b), channel_id=1, source_target_pairs={{0,24},{8,0},{16,8},{24,16},{1,25},{9,1},{17,9},{25,17},{2,26},{10... | collective-permute-start | bytes 442376 | tf_op jit(solution)/shard_map/ppermute | solution.py:571
  138.5 9.4 %collective-permute-start.23 = (f32[2,3,136,128]{3,2,1,0:T(8,128)S(1)}, f32[2,3,136,128]{3,2,1,0:T(8,128)S(1)}, u32[]{:S(2)}, u32[]{:S(2)}) collective-permute-start(f32[2,3,136,128]{3,2,1,0:T(8,128)S(1)} %get-tuple-element.99), channel_id=1, source_target_pairs={{1,2},{3,4},{5,6},{2,1},{4,3},{6,5},{9,10},{11,12},{13,14},{10,9},... | collective-permute-start | bytes 1253384 | tf_op jit(solution)/shard_map/ppermute | solution.py:286
  153.4 9.1 %collective-permute-start.25 = (f32[2,3,128,128]{3,2,1,0:T(8,128)S(1)}, f32[2,3,128,128]{3,2,1,0:T(8,128)S(1)}, u32[]{:S(2)}, u32[]{:S(2)}) collective-permute-start(f32[2,3,128,128]{3,2,1,0:T(8,128)S(1)} %get-tuple-element.102), channel_id=1, source_target_pairs={{1,2},{3,4},{5,6},{2,1},{4,3},{6,5},{9,10},{11,12},{13,14},{10,9},... | collective-permute-start | bytes 1179656 | tf_op jit(solution)/shard_map/ppermute | solution.py:286
  163.8 6.8 %collective-permute-start.27 = (f32[2,128,128]{2,1,0:T(8,128)S(1)}, f32[2,128,128]{2,1,0:T(8,128)S(1)}, u32[]{:S(2)}, u32[]{:S(2)}) collective-permute-start(f32[2,128,128]{2,1,0:T(8,128)S(1)} %get-tuple-element.106), channel_id=1, source_target_pairs={{0,8},{8,16},{16,24},{24,0},{1,9},{9,17},{17,25},{25,1},{2,10},{10... | collective-permute-start | bytes 393224 | tf_op jit(solution)/shard_map/ppermute | solution.py:571
  163.9 7.1 %collective-permute-start.28 = (f32[2,128,128]{2,1,0:T(8,128)S(1)}, f32[2,128,128]{2,1,0:T(8,128)S(1)}, u32[]{:S(2)}, u32[]{:S(2)}) collective-permute-start(f32[2,128,128]{2,1,0:T(8,128)S(1)} %get-tuple-element.108), channel_id=1, source_target_pairs={{0,24},{8,0},{16,8},{24,16},{1,25},{9,1},{17,9},{25,17},{2,26},{10... | collective-permute-start | bytes 393224 | tf_op jit(solution)/shard_map/ppermute | solution.py:571
  167.2 7.8 %collective-permute-start.26 = (f32[2,128,128]{2,1,0:T(8,128)S(1)}, f32[2,128,128]{2,1,0:T(8,128)S(1)}, u32[]{:S(2)}, u32[]{:S(2)}) collective-permute-start(f32[2,128,128]{2,1,0:T(8,128)S(1)} %get-tuple-element.104), channel_id=1, source_target_pairs={{0,24},{8,0},{16,8},{24,16},{1,25},{9,1},{17,9},{25,17},{2,26},{10... | collective-permute-start | bytes 393224 | tf_op jit(solution)/shard_map/ppermute | solution.py:571
  168.8 7.3 %collective-permute-start.30 = (f32[2,128,128]{2,1,0:T(8,128)S(1)}, f32[2,128,128]{2,1,0:T(8,128)S(1)}, u32[]{:S(2)}, u32[]{:S(2)}) collective-permute-start(f32[2,128,128]{2,1,0:T(8,128)S(1)} %get-tuple-element.111), channel_id=1, source_target_pairs={{0,8},{8,16},{16,24},{24,0},{1,9},{9,17},{17,25},{25,1},{2,10},{10... | collective-permute-start | bytes 393224 | tf_op jit(solution)/shard_map/ppermute | solution.py:571
  171.1 6.7 %collective-permute-start.29 = (f32[2,128,128]{2,1,0:T(8,128)S(1)}, f32[2,128,128]{2,1,0:T(8,128)S(1)}, u32[]{:S(2)}, u32[]{:S(2)}) collective-permute-start(f32[2,128,128]{2,1,0:T(8,128)S(1)} %get-tuple-element.109), channel_id=1, source_target_pairs={{0,8},{8,16},{16,24},{24,0},{1,9},{9,17},{17,25},{25,1},{2,10},{10... | collective-permute-start | bytes 393224 | tf_op jit(solution)/shard_map/ppermute | solution.py:571
  177.9 7.7 %collective-permute-start.34 = (f32[2,128,128]{2,1,0:T(8,128)S(1)}, f32[2,128,128]{2,1,0:T(8,128)S(1)}, u32[]{:S(2)}, u32[]{:S(2)}) collective-permute-start(f32[2,128,128]{2,1,0:T(8,128)S(1)} %get-tuple-element.113.refs_0_), channel_id=1, source_target_pairs={{0,8},{8,16},{16,24},{24,0},{1,9},{9,17},{17,25},{25,1},{2,10},{10... | collective-permute-start | bytes 393224 | tf_op jit(solution)/shard_map/ppermute | solution.py:571
  180.1 6.3 %collective-permute-start.33 = (f32[2,128,128]{2,1,0:T(8,128)S(1)}, f32[2,128,128]{2,1,0:T(8,128)S(1)}, u32[]{:S(2)}, u32[]{:S(2)}) collective-permute-start(f32[2,128,128]{2,1,0:T(8,128)S(1)} %get-tuple-element.114.refs_1_), channel_id=1, source_target_pairs={{0,24},{8,0},{16,8},{24,16},{1,25},{9,1},{17,9},{25,17},{2,26},{10... | collective-permute-start | bytes 393224 | tf_op jit(solution)/shard_map/ppermute | solution.py:571
  181.6 7.3 %collective-permute-start.32 = (f32[2,128,128]{2,1,0:T(8,128)S(1)}, f32[2,128,128]{2,1,0:T(8,128)S(1)}, u32[]{:S(2)}, u32[]{:S(2)}) collective-permute-start(f32[2,128,128]{2,1,0:T(8,128)S(1)} %get-tuple-element.113.refs_0_), channel_id=1, source_target_pairs={{0,24},{8,0},{16,8},{24,16},{1,25},{9,1},{17,9},{25,17},{2,26},{10... | collective-permute-start | bytes 393224 | tf_op jit(solution)/shard_map/ppermute | solution.py:571
  183.6 6.2 %collective-permute-start.37 = (f32[2,128,128]{2,1,0:T(8,128)S(1)}, f32[2,128,128]{2,1,0:T(8,128)S(1)}, u32[]{:S(2)}, u32[]{:S(2)}) collective-permute-start(f32[2,128,128]{2,1,0:T(8,128)S(1)} %get-tuple-element.114.refs_1_), channel_id=1, source_target_pairs={{0,8},{8,16},{16,24},{24,0},{1,9},{9,17},{17,25},{25,1},{2,10},{10... | collective-permute-start | bytes 393224 | tf_op jit(solution)/shard_map/ppermute | solution.py:571
  185.6 6.2 %collective-permute-start.35 = (f32[2,128,128]{2,1,0:T(8,128)S(1)}, f32[2,128,128]{2,1,0:T(8,128)S(1)}, u32[]{:S(2)}, u32[]{:S(2)}) collective-permute-start(f32[2,128,128]{2,1,0:T(8,128)S(1)} %collective-permute-done.34.refs_6_), channel_id=1, source_target_pairs={{0,8},{8,16},{16,24},{24,0},{1,9},{9,17},{17,25},{25,1},{2,10},{10... | collective-permute-start | bytes 393224 | tf_op jit(solution)/shard_map/ppermute | solution.py:571
  (22 other events, 272.8 us)

commit v6 on v5

--- a/solution.py
+++ b/solution.py
@@ -253,7 +253,7 @@
             outer[c, i] = field[c, odd * (x_cells - HALO) + i]
 
 
-def y_kernel(flip, trim, w_ref, id_ref, in_ref, out_ref, inner, outer):
+def y_kernel(flip, trim, w_ref, id_ref, in_ref, out_ref, *layers):
     _, x_cells, y_cells, _ = out_ref.shape
     w = taps_of(w_ref, 1, flip)
 
@@ -264,7 +264,8 @@
         return carry
 
     lax.fori_loop(0, x_cells, body, 0)
-    put_layers(id_ref, out_ref, inner, outer)
+    if layers:
+        put_layers(id_ref, out_ref, *layers)
 
 
 def y_pieces_kernel(views, w_ref, id_ref, *refs):
@@ -385,10 +386,12 @@
     lax.fori_loop(0, x_cells, body, 0)
 
 
-def rim_kernel(w_ref, id_ref, below, own_ref, inner, outer, out_ref, layers_in, layers_out, halo, strip):
+def rim_kernel(w_ref, id_ref, below, own_ref, middle, inner, outer, out_ref, *scratch):
     _, x_cells, own, _ = own_ref.shape
+    layers_in, layers_out, halo, strip = scratch
     u = taps_of(w_ref, 2, True)
     w = taps_of(w_ref, 1, True)
+    rows_out = out_ref.shape[2]
     skip = (below.shape[2] - own) // 2
     span = DEEP + 2 * TRIM
     odd = id_ref[4]
@@ -415,18 +418,22 @@
             for c, value in enumerate(blur_z(*rows, u)):
                 strip[c, here : here + skip, :] = value
                 strip[c, there : there + skip, :] = own_ref[c, x, rest : rest + skip, :]
-                out_ref[c, x, side * DEEP : (side + 1) * DEEP, :] = y_rows(strip, (c,), TRIM, w, 0, DEEP)
+                at = side * (rows_out - DEEP)
+                out_ref[c, x, at : at + DEEP, :] = y_rows(strip, (c,), TRIM, w, 0, DEEP)
+        for c in range(2):
+            out_ref[c, x, DEEP : rows_out - DEEP, :] = middle[c, x]
         return carry
 
     lax.fori_loop(0, x_cells, body, 0)
     put_layers(id_ref, out_ref, layers_in, layers_out)
 
 
-def rim(w, ids, below, own, inner, outer):
+def rim(w, ids, below, own, middle, inner, outer):
     _, x, y, _ = own.shape
     skip = (below.shape[2] - y) // 2
     return swap_layers(*call(
-        rim_kernel, "rim", field_and_layers(x, 2 * DEEP), (w, ids, below, own, inner, outer), 2,
+        rim_kernel, "rim", field_and_layers(x, middle.shape[2] + 2 * DEEP),
+        (w, ids, below, own, middle, inner, outer), 2,
         scratch=[
             pltpu.VMEM((2, 2, x, DEEP, BRICK), jnp.float32),
             pltpu.VMEM((2, 2 * skip, BRICK), jnp.float32),
@@ -473,22 +480,18 @@
     lax.fori_loop(0, y_cells // TILE, body, 0)
 
 
-def split_kernel(views, parts, w_ref, id_ref, *refs):
-    fields, outs, wide = refs[: 3 * len(parts)], refs[3 * len(parts) : -1], refs[-1]
-    x_cells = fields[0].shape[1]
-    y_cells = wide.shape[2]
+def split_kernel(views, w_ref, id_ref, field, inner, outer, *refs):
+    outs, wide = refs[:-1], refs[-1]
+    _, x_cells, y_cells, _ = field.shape
     depth = x_cells // views
     w = taps_of(w_ref, 0, True)
     odd = id_ref[1]
-    for p, spans in enumerate(parts):
-        field, inner, outer = fields[3 * p : 3 * p + 3]
-        for y, to, n in spans:
-            for c in range(2):
-                for i in range(HALO):
-                    wide[c, (1 - odd) * (HALO + x_cells) + i, to : to + n, :] = inner[c, i, y : y + n, :]
-                    wide[c, odd * (HALO + x_cells) + i, to : to + n, :] = outer[c, i, y : y + n, :]
-                for i in range(x_cells):
-                    wide[c, HALO + i, to : to + n, :] = field[c, i, y : y + n, :]
+    for c in range(2):
+        for i in range(HALO):
+            wide[c, (1 - odd) * (HALO + x_cells) + i] = inner[c, i]
+            wide[c, odd * (HALO + x_cells) + i] = outer[c, i]
+        for i in range(x_cells):
+            wide[c, HALO + i] = field[c, i]
     for r in range(views):
         base = lax.rem(id_ref[0] + r, views) * depth
 
@@ -503,12 +506,12 @@
         lax.fori_loop(0, y_cells // TILE, body, 0, unroll=2)
 
 
-def split(w, ids, views, fields, parts):
-    x = fields[0].shape[1]
-    y = sum(n for spans in parts for _, _, n in spans)
+def split(w, ids, views, field, inner, outer):
+    _, x, y, _ = field.shape
     outs = [f32(x // views, y, BRICK)] * (2 * views)
     return call(
-        functools.partial(split_kernel, views, parts), "x_blur_split", outs, (w, ids, *fields), 2,
+        functools.partial(split_kernel, views), "x_blur_split", outs,
+        (w, ids, field, inner, outer), 2,
         scratch=[pltpu.VMEM((2, x + 2 * HALO, y, BRICK), jnp.float32)],
     )
 
@@ -542,29 +545,13 @@
 
 
 def join_kernel(views, id_ref, *refs):
-    pieces, out_ref, sems = refs[: 2 * views], refs[2 * views], refs[2 * views + 1]
+    pieces, out_ref = refs[: 2 * views], refs[2 * views]
     depth = pieces[0].shape[0]
-    copies = []
     for d in range(views):
         base = lax.rem(id_ref[0] + d, views) * depth
-        for c in range(2):
-            part = out_ref.at[pl.ds(base, depth), :, pl.ds(c * BRICK, BRICK)]
-            copies.append(pltpu.make_async_copy(pieces[2 * d + c], part, sems.at[2 * d + c]))
-    for copy in copies:
-        copy.start()
-    for copy in copies:
-        copy.wait()
-
-
-def join(views, shape, ids, pieces):
-    return pl.pallas_call(
-        functools.partial(join_kernel, views),
-        out_shape=f32(*shape),
-        in_specs=[smem()] + [pl.BlockSpec(memory_space=pl.ANY)] * len(pieces),
-        out_specs=pl.BlockSpec(memory_space=pl.ANY),
-        scratch_shapes=[pltpu.SemaphoreType.DMA((len(pieces),))],
-        name="join",
-    )(ids, *pieces)
+        for i in range(depth):
+            out_ref[base + i, :, 0:BRICK] = pieces[2 * d][i]
+            out_ref[base + i, :, BRICK : 2 * BRICK] = pieces[2 * d + 1][i]
 
 
 def turn(value, step, count):
@@ -615,15 +602,16 @@
             own = call(
                 ratio_own_kernel, "ratio_own", [f32(2, x_cells, y_cells, BRICK)], (w, below, moved)
             )[0]
-            middle = y_blur(w, ids, own, True, TILE)
-            ends = rim(w, ids, below, own, inner, outer)
+            middle = call(
+                functools.partial(y_kernel, True, TILE), "y_blur",
+                [f32(2, x_cells, y_cells - 2 * TILE, BRICK)], (w, ids, own), 2,
+            )[0]
+            fields = rim(w, ids, below, own, middle, inner, outer)
             obs = call(
                 widen_kernel, "widen", [f32(2, x_cells, y_cells + 2 * DEEP, BRICK)],
                 (ids, moved, inner, outer),
             )[0]
-            wider = y_cells + 2 * TILE
-            parts = (((0, DEEP, wider - 2 * DEEP),), ((0, 0, DEEP), (DEEP, wider - DEEP, DEEP)))
-            sent = split(w, ids, view_count, (*middle, *ends), parts)
+            sent = split(w, ids, view_count, *fields)
         else:
             y = pieces[0].shape[1] - 2 * TRIM
             field, inner, outer = swap_layers(*call(
@@ -636,7 +624,7 @@
                 ratio_kernel, "ratio", [f32(*field.shape)], (w, ids, field, inner, outer, obs), 2,
                 scratch=[sides(field)],
             )[0]
-            sent = split(w, ids, view_count, y_blur(w, ids, field, True, TRIM), (((0, 0, y_cells),),))
+            sent = split(w, ids, view_count, *y_blur(w, ids, field, True, TRIM))
         a0, b0, a1, b1, a2, b2, a3, b3 = sent
         pair = [f32(*a0.shape)] * 2
         ra, rb = turn(a2, 1, view_count), turn(b2, -1, view_count)
@@ -658,7 +646,10 @@
         prev_b, next_a = turn(own[1], 1, view_count), turn(own[0], -1, view_count)
         far_a, far_b = turn(prev_a, 1, view_count), turn(next_b, -1, view_count)
         pieces = (*own, next_a, next_b, far_a, far_b, prev_a, prev_b)
-    return join(view_count, estimate.shape, ids, pieces)
+    return call(
+        functools.partial(join_kernel, view_count), "join", [f32(x_cells, y_cells, z_cells)],
+        (ids, *pieces),
+    )[0]
 
 
 def solution(mesh):

time: 227 us -> 189 us (0.83)
  Pallas kernels: 70.6 us -> 38.6 us
  starting transfers between devices: 67.8 us -> 63.7 us
    pallas_call x1 -> x0, Pallas kernels: 33.6 us -> none  [join(): pl.pallas_call(functools.partial(join_kernel, views), out_shape=f32(*shap...]
    ppermute x5 -> x4, waiting for transfers between devices: 29.8 us -> 32.9 us  [swap_layers(): outer = lax.ppermute(outer, 'rows', links + [(j, i) for i, j in links])]
    ppermute x2, waiting for transfers between devices: 2.78 us -> 0.01 us  [swap_rows(): inner = lax.ppermute(inner, 'blocks', [(i, i ^ 1) for i in range(count)])]
    all_to_all x1, starting transfers between devices: 11.7 us -> 9.33 us  [per_device(): lax.all_to_all(outgoing.reshape(peer_count, capacity + 1, 1, BRICK), ('bl...]
    ppermute x5 -> x4, starting transfers between devices: 10.7 us -> 8.8 us  [swap_layers(): outer = lax.ppermute(outer, 'rows', links + [(j, i) for i, j in links])]
    pallas_call x21 -> x22, Pallas kernels: 31.1 us -> 32.7 us  [call(): pl.pallas_call(kernel, out_shape=outs, in_specs=[smem()] * scalars + [vme...]
  transfers between devices with their start and end apart: 39 -> 37, of which waited for: 20 -> 19; matrix products, arithmetic and copies ran while one was open for 1% -> 1% of each run, Pallas kernels for 8% -> 10%
where the time goes in v6:
time: 189 us; the launch traced here: 188 us
  waiting for transfers between devices  81.8 us (43%)
  starting transfers between devices  63.7 us (34%)
  Pallas kernels  38.6 us (20%)
  local copies, waits for them, and re-layouts  1.96 us (1%)
    ppermute x24, starting transfers between devices, turn(): lax.ppermute(value, 'views', [(i, (i + step) % count) for i in range(coun...  35.4 us
    ppermute x4, waiting for transfers between devices, swap_layers(): outer = lax.ppermute(outer, 'rows', links + [(j, i) for i, j in links])  32.9 us
    pallas_call x22, Pallas kernels, call(): pl.pallas_call(kernel, out_shape=outs, in_specs=[smem()] * scalars + [vme...  32.7 us
    all_to_all x1, waiting for transfers between devices, per_device(): lax.all_to_all(outgoing.reshape(peer_count, capacity + 1, 1, BRICK), ('bl...  29.6 us
    ppermute x24, waiting for transfers between devices, turn(): lax.ppermute(value, 'views', [(i, (i + step) % count) for i in range(coun...  18.2 us
    all_to_all x1, starting transfers between devices, per_device(): lax.all_to_all(outgoing.reshape(peer_count, capacity + 1, 1, BRICK), ('bl...  9.33 us
    ppermute x4, starting transfers between devices, swap_layers(): outer = lax.ppermute(outer, 'rows', links + [(j, i) for i, j in links])  8.8 us
    ppermute x2, starting transfers between devices, swap_rows(): outer = lax.ppermute(outer, 'blocks', links + [(j, i) for i, j in links])  7.53 us
  transfers between devices with their start and end apart: 37, of which 19 were waited for; matrix products, arithmetic and copies ran while one was open for 1% of the time, Pallas kernels for 10%

profile of v6, /device:TPU:34, one launch (start us, length us, event | category | flops | bytes accessed | tf_op | source)
XLA Modules:
  0.0 188.2 jit_solution(1404583186879600437)
XLA Ops:
  1.2 5.6 %collective-permute-start.1 = (f32[8,16,256]{2,1,0:T(8,128)S(1)}, f32[8,16,256]{2,1,0:T(8,128)S(1)}, u32[]{:S(2)}, u32[]{:S(2)}) collective-permute-start(f32[8,16,256]{2,1,0:T(8,128)S(1)} %get-tuple-element.111), channel_id=1, source_target_pairs={{32,64},{96,128},{160,192},{64,32},{128,96},{192,160},{33,65},{97,... | collective-permute-start | bytes 393224 | tf_op jit(solution)/shard_map/ppermute | solution.py:295
  7.5 5.9 %pack.1 = f32[4160,1,128]{2,1,0:T(1,128)} custom-call(s32[1]{0:T(128)S(6)} %copy.6.shift_ref, s32[8,2,128]{2,1,0:T(2,128)} %bitcast.14, f32[8,128,256]{2,1,0:T(8,128)} %bitcast.13), custom_call_target="tpu_custom_call" | custom-call | tf_op jit(solution)/shard_map/pack/pallas_call | solution.py:89
  14.1 9.3 %all-to-all-start = ((f32[64,65,1,128]{3,2,1,0:T(1,128)}), f32[64,65,1,128]{3,2,1,0:T(1,128)S(1)}, u32[]{:S(2)}, u32[]{:S(2)}) async-start(f32[64,65,1,128]{3,2,1,0:T(1,128)} %bitcast.12), calls=%async_computation | async-start | bytes 4259840 | tf_op jit(solution)/shard_map/all_to_all | solution.py:582
  24.9 3.1 %z_blur.1.in_ref = f32[2,8,160,128]{3,2,1,0:T(8,128)S(1)} custom-call(f32[21]{0:T(128)S(1)} %div.13.w_ref, f32[8,128,256]{2,1,0:T(8,128)S(1)} %copy-done, f32[8,16,256]{2,1,0:T(8,128)S(1)} %get-tuple-element.114.lo, f32[8,16,256]{2,1,0:T(8,128)S(1)} %get-tuple-element.113.hi), custom_call_target="tpu_custom_call" | custom-call | flops 1000 | bytes 1000 | tf_op jit(solution)/shard_map/z_blur/pallas_call | solution.py:167
  29.4 2.4 %collective-permute-start.3 = (f32[2,3,152,128]{3,2,1,0:T(8,128)S(1)}, f32[2,3,152,128]{3,2,1,0:T(8,128)S(1)}, u32[]{:S(2)}, u32[]{:S(2)}) collective-permute-start(f32[2,3,152,128]{3,2,1,0:T(8,128)S(1)} %get-tuple-element.62), channel_id=1, source_target_pairs={{1,2},{3,4},{5,6},{2,1},{4,3},{6,5},{9,10},{11,12},{13,14},{10,9},... | collective-permute-start | bytes 1400840 | tf_op jit(solution)/shard_map/ppermute | solution.py:287
  31.9 11.9 %collective-permute-done.3.outer = f32[2,3,152,128]{3,2,1,0:T(8,128)S(1)} collective-permute-done((f32[2,3,152,128]{3,2,1,0:T(8,128)S(1)}, f32[2,3,152,128]{3,2,1,0:T(8,128)S(1)}, u32[]{:S(2)}, u32[]{:S(2)}) %collective-permute-start.3) | collective-permute-done | bytes 466976 | tf_op jit(solution)/shard_map/ppermute | solution.py:287
  45.0 29.6 %all-to-all-done = f32[64,65,1,128]{3,2,1,0:T(1,128)S(1)} async-done(((f32[64,65,1,128]{3,2,1,0:T(1,128)}), f32[64,65,1,128]{3,2,1,0:T(1,128)S(1)}, u32[]{:S(2)}, u32[]{:S(2)}) %all-to-all-start) | async-done | bytes 2129952 | tf_op jit(solution)/shard_map/all_to_all | solution.py:582
  74.6 5.2 %unpack.1 = (f32[2056,128]{1,0:T(8,128)S(1)}, f32[2,8,16,128]{3,2,1,0:T(8,128)S(1)}, f32[2,8,16,128]{3,2,1,0:T(8,128)S(1)}) custom-call(s32[5]{0:T(128)S(1)} %stack.23.id_ref, f32[4160,1,128]{2,1,0:T(1,128)S(1)} %bitcast.11), custom_call_target="tpu_custom_call" | custom-call | flops 1000 | bytes 1000 | tf_op jit(solution)/shard_map/unpack/pallas_call | solution.py:167
  81.3 1.9 %collective-permute-start.5 = (f32[2,8,16,128]{3,2,1,0:T(8,128)S(1)}, f32[2,8,16,128]{3,2,1,0:T(8,128)S(1)}, u32[]{:S(2)}, u32[]{:S(2)}) collective-permute-start(f32[2,8,16,128]{3,2,1,0:T(8,128)S(1)} %get-tuple-element.67), channel_id=1, source_target_pairs={{32,64},{96,128},{160,192},{64,32},{128,96},{192,160},{33,65},{97,... | collective-permute-start | bytes 393224 | tf_op jit(solution)/shard_map/ppermute | solution.py:295
  83.2 2.8 %ratio_own.1.in_ref.own_ref = f32[2,8,128,128]{3,2,1,0:T(8,128)S(1)} custom-call(f32[21]{0:T(128)S(1)} %div.13.w_ref, f32[2,8,152,128]{3,2,1,0:T(8,128)S(1)} %x_blur.1.below, f32[2056,128]{1,0:T(8,128)S(1)} %get-tuple-element.65.moved), custom_call_target="tpu_custom_call" | custom-call | flops 1000 | bytes 1000 | tf_op jit(solution)/shard_map/ratio_own/pallas_call | solution.py:167
  88.1 1.8 rim.1
  90.1 2.5 %collective-permute-start.7 = (f32[2,3,144,128]{3,2,1,0:T(8,128)S(1)}, f32[2,3,144,128]{3,2,1,0:T(8,128)S(1)}, u32[]{:S(2)}, u32[]{:S(2)}) collective-permute-start(f32[2,3,144,128]{3,2,1,0:T(8,128)S(1)} %get-tuple-element.70), channel_id=1, source_target_pairs={{1,2},{3,4},{5,6},{2,1},{4,3},{6,5},{9,10},{11,12},{13,14},{10,9},... | collective-permute-start | bytes 1327112 | tf_op jit(solution)/shard_map/ppermute | solution.py:287
  92.6 7.1 %collective-permute-done.7.outer = f32[2,3,144,128]{3,2,1,0:T(8,128)S(1)} collective-permute-done((f32[2,3,144,128]{3,2,1,0:T(8,128)S(1)}, f32[2,3,144,128]{3,2,1,0:T(8,128)S(1)}, u32[]{:S(2)}, u32[]{:S(2)}) %collective-permute-start.7) | collective-permute-done | bytes 442400 | tf_op jit(solution)/shard_map/ppermute | solution.py:287
  104.4 1.8 collective-permute-start.8
  106.5 2.2 %collective-permute-done.9.ra = f32[2,144,128]{2,1,0:T(8,128)S(1)} collective-permute-done((f32[2,144,128]{2,1,0:T(8,128)S(1)}, f32[2,144,128]{2,1,0:T(8,128)S(1)}, u32[]{:S(2)}, u32[]{:S(2)}) %collective-permute-start.9) | collective-permute-done | bytes 147488 | tf_op jit(solution)/shard_map/ppermute | solution.py:558
  109.5 1.7 collective-permute-start.11
  113.3 2.8 %collective-permute-done.11.a2 = f32[2,144,128]{2,1,0:T(8,128)S(1)} collective-permute-done((f32[2,144,128]{2,1,0:T(8,128)S(1)}, f32[2,144,128]{2,1,0:T(8,128)S(1)}, u32[]{:S(2)}, u32[]{:S(2)}) %collective-permute-start.11) | collective-permute-done | bytes 147488 | tf_op jit(solution)/shard_map/ppermute | solution.py:558
  118.3 2.0 %collective-permute-start.15 = (f32[2,144,128]{2,1,0:T(8,128)S(1)}, f32[2,144,128]{2,1,0:T(8,128)S(1)}, u32[]{:S(2)}, u32[]{:S(2)}) collective-permute-start(f32[2,144,128]{2,1,0:T(8,128)S(1)} %get-tuple-element.82.in_b.est_b), channel_id=1, source_target_pairs={{0,24},{8,0},{16,8},{24,16},{1,25},{9,1},{17,9},{25,17},{2,26},{10... | collective-permute-start | bytes 442376 | tf_op jit(solution)/shard_map/ppermute | solution.py:558
  122.3 2.1 %collective-permute-done.16.in_a = f32[2,144,128]{2,1,0:T(8,128)S(1)} collective-permute-done((f32[2,144,128]{2,1,0:T(8,128)S(1)}, f32[2,144,128]{2,1,0:T(8,128)S(1)}, u32[]{:S(2)}, u32[]{:S(2)}) %collective-permute-start.16) | collective-permute-done | bytes 147488 | tf_op jit(solution)/shard_map/ppermute | solution.py:558
  124.6 2.9 %collective-permute-start.18 = (f32[2,144,128]{2,1,0:T(8,128)S(1)}, f32[2,144,128]{2,1,0:T(8,128)S(1)}, u32[]{:S(2)}, u32[]{:S(2)}) collective-permute-start(f32[2,144,128]{2,1,0:T(8,128)S(1)} %collective-permute-done.15.in_b), channel_id=1, source_target_pairs={{0,24},{8,0},{16,8},{24,16},{1,25},{9,1},{17,9},{25,17},{2,26},{10... | collective-permute-start | bytes 442376 | tf_op jit(solution)/shard_map/ppermute | solution.py:558
  133.4 1.9 %collective-permute-start.21 = (f32[2,3,136,128]{3,2,1,0:T(8,128)S(1)}, f32[2,3,136,128]{3,2,1,0:T(8,128)S(1)}, u32[]{:S(2)}, u32[]{:S(2)}) collective-permute-start(f32[2,3,136,128]{3,2,1,0:T(8,128)S(1)} %get-tuple-element.93), channel_id=1, source_target_pairs={{1,2},{3,4},{5,6},{2,1},{4,3},{6,5},{9,10},{11,12},{13,14},{10,9},... | collective-permute-start | bytes 1253384 | tf_op jit(solution)/shard_map/ppermute | solution.py:287
  136.0 6.8 %collective-permute-done.21.outer = f32[2,3,136,128]{3,2,1,0:T(8,128)S(1)} collective-permute-done((f32[2,3,136,128]{3,2,1,0:T(8,128)S(1)}, f32[2,3,136,128]{3,2,1,0:T(8,128)S(1)}, u32[]{:S(2)}, u32[]{:S(2)}) %collective-permute-start.21) | collective-permute-done | bytes 417824 | tf_op jit(solution)/shard_map/ppermute | solution.py:287
  142.8 3.8 %ratio.1.in_ref = f32[2,8,136,128]{3,2,1,0:T(8,128)S(1)} custom-call(f32[21]{0:T(128)S(1)} %div.13.w_ref, s32[5]{0:T(128)S(1)} %stack.23.id_ref, f32[2,8,136,128]{3,2,1,0:T(8,128)S(1)} %get-tuple-element.91.field, f32[2,3,136,128]{3,2,1,0:T(8,128)S(1)} %collective-permute-done.20.inner, f32[2,3,136,128]{3,2,1,0:T(8,128)S(1)} %collective-permute-done.21.outer, ...), custom_call_target="tpu_custom_call" | custom-call | flops 1000 | bytes 1000 | tf_op jit(solution)/shard_map/ratio/pallas_call | solution.py:167
  148.2 1.9 %collective-permute-start.23 = (f32[2,3,128,128]{3,2,1,0:T(8,128)S(1)}, f32[2,3,128,128]{3,2,1,0:T(8,128)S(1)}, u32[]{:S(2)}, u32[]{:S(2)}) collective-permute-start(f32[2,3,128,128]{3,2,1,0:T(8,128)S(1)} %get-tuple-element.96), channel_id=1, source_target_pairs={{1,2},{3,4},{5,6},{2,1},{4,3},{6,5},{9,10},{11,12},{13,14},{10,9},... | collective-permute-start | bytes 1179656 | tf_op jit(solution)/shard_map/ppermute | solution.py:287
  150.2 7.2 %collective-permute-done.23.outer = f32[2,3,128,128]{3,2,1,0:T(8,128)S(1)} collective-permute-done((f32[2,3,128,128]{3,2,1,0:T(8,128)S(1)}, f32[2,3,128,128]{3,2,1,0:T(8,128)S(1)}, u32[]{:S(2)}, u32[]{:S(2)}) %collective-permute-start.23) | collective-permute-done | bytes 393248 | tf_op jit(solution)/shard_map/ppermute | solution.py:287
  159.3 2.8 %collective-permute-start.26 = (f32[2,128,128]{2,1,0:T(8,128)S(1)}, f32[2,128,128]{2,1,0:T(8,128)S(1)}, u32[]{:S(2)}, u32[]{:S(2)}) collective-permute-start(f32[2,128,128]{2,1,0:T(8,128)S(1)} %get-tuple-element.102), channel_id=1, source_target_pairs={{0,24},{8,0},{16,8},{24,16},{1,25},{9,1},{17,9},{25,17},{2,26},{10... | collective-permute-start | bytes 393224 | tf_op jit(solution)/shard_map/ppermute | solution.py:558
  167.5 2.3 %collective-permute-start.29 = (f32[2,128,128]{2,1,0:T(8,128)S(1)}, f32[2,128,128]{2,1,0:T(8,128)S(1)}, u32[]{:S(2)}, u32[]{:S(2)}) collective-permute-start(f32[2,128,128]{2,1,0:T(8,128)S(1)} %get-tuple-element.106), channel_id=1, source_target_pairs={{0,24},{8,0},{16,8},{24,16},{1,25},{9,1},{17,9},{25,17},{2,26},{10... | collective-permute-start | bytes 393224 | tf_op jit(solution)/shard_map/ppermute | solution.py:558
  172.8 2.2 %collective-permute-start.32 = (f32[2,128,128]{2,1,0:T(8,128)S(1)}, f32[2,128,128]{2,1,0:T(8,128)S(1)}, u32[]{:S(2)}, u32[]{:S(2)}) collective-permute-start(f32[2,128,128]{2,1,0:T(8,128)S(1)} %get-tuple-element.107.refs_0_), channel_id=1, source_target_pairs={{0,8},{8,16},{16,24},{24,0},{1,9},{9,17},{17,25},{25,1},{2,10},{10... | collective-permute-start | bytes 393224 | tf_op jit(solution)/shard_map/ppermute | solution.py:558
  176.5 1.9 %collective-permute-start.30 = (f32[2,128,128]{2,1,0:T(8,128)S(1)}, f32[2,128,128]{2,1,0:T(8,128)S(1)}, u32[]{:S(2)}, u32[]{:S(2)}) collective-permute-start(f32[2,128,128]{2,1,0:T(8,128)S(1)} %get-tuple-element.107.refs_0_), channel_id=1, source_target_pairs={{0,24},{8,0},{16,8},{24,16},{1,25},{9,1},{17,9},{25,17},{2,26},{10... | collective-permute-start | bytes 393224 | tf_op jit(solution)/shard_map/ppermute | solution.py:558
  178.5 2.0 %collective-permute-done.32.refs_6_ = f32[2,128,128]{2,1,0:T(8,128)S(1)} collective-permute-done((f32[2,128,128]{2,1,0:T(8,128)S(1)}, f32[2,128,128]{2,1,0:T(8,128)S(1)}, u32[]{:S(2)}, u32[]{:S(2)}) %collective-permute-start.32) | collective-permute-done | bytes 131104 | tf_op jit(solution)/shard_map/ppermute | solution.py:558
  181.3 2.5 %collective-permute-start.34 = (f32[2,128,128]{2,1,0:T(8,128)S(1)}, f32[2,128,128]{2,1,0:T(8,128)S(1)}, u32[]{:S(2)}, u32[]{:S(2)}) collective-permute-start(f32[2,128,128]{2,1,0:T(8,128)S(1)} %collective-permute-done.31.refs_3_), channel_id=1, source_target_pairs={{0,24},{8,0},{16,8},{24,16},{1,25},{9,1},{17,9},{25,17},{2,26},{10... | collective-permute-start | bytes 393224 | tf_op jit(solution)/shard_map/ppermute | solution.py:558
  184.6 2.1 %collective-permute-done.33.refs_4_ = f32[2,128,128]{2,1,0:T(8,128)S(1)} collective-permute-done((f32[2,128,128]{2,1,0:T(8,128)S(1)}, f32[2,128,128]{2,1,0:T(8,128)S(1)}, u32[]{:S(2)}, u32[]{:S(2)}) %collective-permute-start.33) | collective-permute-done | bytes 131104 | tf_op jit(solution)/shard_map/ppermute | solution.py:558
  (85 shorter events, 45.3 us)
Async XLA Ops:
  1.0 12.4 %collective-permute-start = (f32[8,16,256]{2,1,0:T(8,128)S(1)}, f32[8,16,256]{2,1,0:T(8,128)S(1)}, u32[]{:S(2)}, u32[]{:S(2)}) collective-permute-start(f32[8,16,256]{2,1,0:T(8,128)S(1)} %get-tuple-element.112), channel_id=1, source_target_pairs={{0,32},{32,0},{64,96},{96,64},{128,160},{160,128},{192,224},{224,1... | collective-permute-start | bytes 393224 | tf_op jit(solution)/shard_map/ppermute | solution.py:296
  1.2 12.2 %collective-permute-start.1 = (f32[8,16,256]{2,1,0:T(8,128)S(1)}, f32[8,16,256]{2,1,0:T(8,128)S(1)}, u32[]{:S(2)}, u32[]{:S(2)}) collective-permute-start(f32[8,16,256]{2,1,0:T(8,128)S(1)} %get-tuple-element.111), channel_id=1, source_target_pairs={{32,64},{96,128},{160,192},{64,32},{128,96},{192,160},{33,65},{97,... | collective-permute-start | bytes 393224 | tf_op jit(solution)/shard_map/ppermute | solution.py:295
  14.1 60.5 %all-to-all-start = ((f32[64,65,1,128]{3,2,1,0:T(1,128)}), f32[64,65,1,128]{3,2,1,0:T(1,128)S(1)}, u32[]{:S(2)}, u32[]{:S(2)}) async-start(f32[64,65,1,128]{3,2,1,0:T(1,128)} %bitcast.12), calls=%async_computation | async-start | bytes 4259840 | tf_op jit(solution)/shard_map/all_to_all | solution.py:582
  29.4 14.3 %collective-permute-start.3 = (f32[2,3,152,128]{3,2,1,0:T(8,128)S(1)}, f32[2,3,152,128]{3,2,1,0:T(8,128)S(1)}, u32[]{:S(2)}, u32[]{:S(2)}) collective-permute-start(f32[2,3,152,128]{3,2,1,0:T(8,128)S(1)} %get-tuple-element.62), channel_id=1, source_target_pairs={{1,2},{3,4},{5,6},{2,1},{4,3},{6,5},{9,10},{11,12},{13,14},{10,9},... | collective-permute-start | bytes 1400840 | tf_op jit(solution)/shard_map/ppermute | solution.py:287
  79.8 7.2 %collective-permute-start.4 = (f32[2,8,16,128]{3,2,1,0:T(8,128)S(1)}, f32[2,8,16,128]{3,2,1,0:T(8,128)S(1)}, u32[]{:S(2)}, u32[]{:S(2)}) collective-permute-start(f32[2,8,16,128]{3,2,1,0:T(8,128)S(1)} %get-tuple-element.66), channel_id=1, source_target_pairs={{0,32},{32,0},{64,96},{96,64},{128,160},{160,128},{192,224},{224,1... | collective-permute-start | bytes 393224 | tf_op jit(solution)/shard_map/ppermute | solution.py:296
  81.3 6.8 %collective-permute-start.5 = (f32[2,8,16,128]{3,2,1,0:T(8,128)S(1)}, f32[2,8,16,128]{3,2,1,0:T(8,128)S(1)}, u32[]{:S(2)}, u32[]{:S(2)}) collective-permute-start(f32[2,8,16,128]{3,2,1,0:T(8,128)S(1)} %get-tuple-element.67), channel_id=1, source_target_pairs={{32,64},{96,128},{160,192},{64,32},{128,96},{192,160},{33,65},{97,... | collective-permute-start | bytes 393224 | tf_op jit(solution)/shard_map/ppermute | solution.py:295
  90.1 9.6 %collective-permute-start.7 = (f32[2,3,144,128]{3,2,1,0:T(8,128)S(1)}, f32[2,3,144,128]{3,2,1,0:T(8,128)S(1)}, u32[]{:S(2)}, u32[]{:S(2)}) collective-permute-start(f32[2,3,144,128]{3,2,1,0:T(8,128)S(1)} %get-tuple-element.70), channel_id=1, source_target_pairs={{1,2},{3,4},{5,6},{2,1},{4,3},{6,5},{9,10},{11,12},{13,14},{10,9},... | collective-permute-start | bytes 1327112 | tf_op jit(solution)/shard_map/ppermute | solution.py:287
  101.1 7.6 %collective-permute-start.9 = (f32[2,144,128]{2,1,0:T(8,128)S(1)}, f32[2,144,128]{2,1,0:T(8,128)S(1)}, u32[]{:S(2)}, u32[]{:S(2)}) collective-permute-start(f32[2,144,128]{2,1,0:T(8,128)S(1)} %get-tuple-element.74), channel_id=1, source_target_pairs={{0,8},{8,16},{16,24},{24,0},{1,9},{9,17},{17,25},{25,1},{2,10},{10... | collective-permute-start | bytes 442376 | tf_op jit(solution)/shard_map/ppermute | solution.py:558
  102.8 6.7 %collective-permute-start.10 = (f32[2,144,128]{2,1,0:T(8,128)S(1)}, f32[2,144,128]{2,1,0:T(8,128)S(1)}, u32[]{:S(2)}, u32[]{:S(2)}) collective-permute-start(f32[2,144,128]{2,1,0:T(8,128)S(1)} %get-tuple-element.76), channel_id=1, source_target_pairs={{0,24},{8,0},{16,8},{24,16},{1,25},{9,1},{17,9},{25,17},{2,26},{10... | collective-permute-start | bytes 442376 | tf_op jit(solution)/shard_map/ppermute | solution.py:558
  104.4 8.4 %collective-permute-start.8 = (f32[2,144,128]{2,1,0:T(8,128)S(1)}, f32[2,144,128]{2,1,0:T(8,128)S(1)}, u32[]{:S(2)}, u32[]{:S(2)}) collective-permute-start(f32[2,144,128]{2,1,0:T(8,128)S(1)} %get-tuple-element.72), channel_id=1, source_target_pairs={{0,24},{8,0},{16,8},{24,16},{1,25},{9,1},{17,9},{25,17},{2,26},{10... | collective-permute-start | bytes 442376 | tf_op jit(solution)/shard_map/ppermute | solution.py:558
  106.2 7.0 %collective-permute-start.12 = (f32[2,144,128]{2,1,0:T(8,128)S(1)}, f32[2,144,128]{2,1,0:T(8,128)S(1)}, u32[]{:S(2)}, u32[]{:S(2)}) collective-permute-start(f32[2,144,128]{2,1,0:T(8,128)S(1)} %get-tuple-element.79), channel_id=1, source_target_pairs={{0,8},{8,16},{16,24},{24,0},{1,9},{9,17},{17,25},{25,1},{2,10},{10... | collective-permute-start | bytes 442376 | tf_op jit(solution)/shard_map/ppermute | solution.py:558
  109.5 6.5 %collective-permute-start.11 = (f32[2,144,128]{2,1,0:T(8,128)S(1)}, f32[2,144,128]{2,1,0:T(8,128)S(1)}, u32[]{:S(2)}, u32[]{:S(2)}) collective-permute-start(f32[2,144,128]{2,1,0:T(8,128)S(1)} %get-tuple-element.77), channel_id=1, source_target_pairs={{0,8},{8,16},{16,24},{24,0},{1,9},{9,17},{17,25},{25,1},{2,10},{10... | collective-permute-start | bytes 442376 | tf_op jit(solution)/shard_map/ppermute | solution.py:558
  116.9 7.4 %collective-permute-start.16 = (f32[2,144,128]{2,1,0:T(8,128)S(1)}, f32[2,144,128]{2,1,0:T(8,128)S(1)}, u32[]{:S(2)}, u32[]{:S(2)}) collective-permute-start(f32[2,144,128]{2,1,0:T(8,128)S(1)} %get-tuple-element.81.in_a.est_a), channel_id=1, source_target_pairs={{0,8},{8,16},{16,24},{24,0},{1,9},{9,17},{17,25},{25,1},{2,10},{10... | collective-permute-start | bytes 442376 | tf_op jit(solution)/shard_map/ppermute | solution.py:558
  118.3 6.4 %collective-permute-start.15 = (f32[2,144,128]{2,1,0:T(8,128)S(1)}, f32[2,144,128]{2,1,0:T(8,128)S(1)}, u32[]{:S(2)}, u32[]{:S(2)}) collective-permute-start(f32[2,144,128]{2,1,0:T(8,128)S(1)} %get-tuple-element.82.in_b.est_b), channel_id=1, source_target_pairs={{0,24},{8,0},{16,8},{24,16},{1,25},{9,1},{17,9},{25,17},{2,26},{10... | collective-permute-start | bytes 442376 | tf_op jit(solution)/shard_map/ppermute | solution.py:558
  120.2 8.5 %collective-permute-start.14 = (f32[2,144,128]{2,1,0:T(8,128)S(1)}, f32[2,144,128]{2,1,0:T(8,128)S(1)}, u32[]{:S(2)}, u32[]{:S(2)}) collective-permute-start(f32[2,144,128]{2,1,0:T(8,128)S(1)} %get-tuple-element.81.in_a.est_a), channel_id=1, source_target_pairs={{0,24},{8,0},{16,8},{24,16},{1,25},{9,1},{17,9},{25,17},{2,26},{10... | collective-permute-start | bytes 442376 | tf_op jit(solution)/shard_map/ppermute | solution.py:558
  121.9 8.0 %collective-permute-start.19 = (f32[2,144,128]{2,1,0:T(8,128)S(1)}, f32[2,144,128]{2,1,0:T(8,128)S(1)}, u32[]{:S(2)}, u32[]{:S(2)}) collective-permute-start(f32[2,144,128]{2,1,0:T(8,128)S(1)} %get-tuple-element.82.in_b.est_b), channel_id=1, source_target_pairs={{0,8},{8,16},{16,24},{24,0},{1,9},{9,17},{17,25},{25,1},{2,10},{10... | collective-permute-start | bytes 442376 | tf_op jit(solution)/shard_map/ppermute | solution.py:558
  124.3 6.7 %collective-permute-start.17 = (f32[2,144,128]{2,1,0:T(8,128)S(1)}, f32[2,144,128]{2,1,0:T(8,128)S(1)}, u32[]{:S(2)}, u32[]{:S(2)}) collective-permute-start(f32[2,144,128]{2,1,0:T(8,128)S(1)} %collective-permute-done.16.in_a), channel_id=1, source_target_pairs={{0,8},{8,16},{16,24},{24,0},{1,9},{9,17},{17,25},{25,1},{2,10},{10... | collective-permute-start | bytes 442376 | tf_op jit(solution)/shard_map/ppermute | solution.py:558
  124.6 6.4 %collective-permute-start.18 = (f32[2,144,128]{2,1,0:T(8,128)S(1)}, f32[2,144,128]{2,1,0:T(8,128)S(1)}, u32[]{:S(2)}, u32[]{:S(2)}) collective-permute-start(f32[2,144,128]{2,1,0:T(8,128)S(1)} %collective-permute-done.15.in_b), channel_id=1, source_target_pairs={{0,24},{8,0},{16,8},{24,16},{1,25},{9,1},{17,9},{25,17},{2,26},{10... | collective-permute-start | bytes 442376 | tf_op jit(solution)/shard_map/ppermute | solution.py:558
  133.4 9.4 %collective-permute-start.21 = (f32[2,3,136,128]{3,2,1,0:T(8,128)S(1)}, f32[2,3,136,128]{3,2,1,0:T(8,128)S(1)}, u32[]{:S(2)}, u32[]{:S(2)}) collective-permute-start(f32[2,3,136,128]{3,2,1,0:T(8,128)S(1)} %get-tuple-element.93), channel_id=1, source_target_pairs={{1,2},{3,4},{5,6},{2,1},{4,3},{6,5},{9,10},{11,12},{13,14},{10,9},... | collective-permute-start | bytes 1253384 | tf_op jit(solution)/shard_map/ppermute | solution.py:287
  148.2 9.1 %collective-permute-start.23 = (f32[2,3,128,128]{3,2,1,0:T(8,128)S(1)}, f32[2,3,128,128]{3,2,1,0:T(8,128)S(1)}, u32[]{:S(2)}, u32[]{:S(2)}) collective-permute-start(f32[2,3,128,128]{3,2,1,0:T(8,128)S(1)} %get-tuple-element.96), channel_id=1, source_target_pairs={{1,2},{3,4},{5,6},{2,1},{4,3},{6,5},{9,10},{11,12},{13,14},{10,9},... | collective-permute-start | bytes 1179656 | tf_op jit(solution)/shard_map/ppermute | solution.py:287
  158.7 6.8 %collective-permute-start.25 = (f32[2,128,128]{2,1,0:T(8,128)S(1)}, f32[2,128,128]{2,1,0:T(8,128)S(1)}, u32[]{:S(2)}, u32[]{:S(2)}) collective-permute-start(f32[2,128,128]{2,1,0:T(8,128)S(1)} %get-tuple-element.100), channel_id=1, source_target_pairs={{0,8},{8,16},{16,24},{24,0},{1,9},{9,17},{17,25},{25,1},{2,10},{10... | collective-permute-start | bytes 393224 | tf_op jit(solution)/shard_map/ppermute | solution.py:558
  159.3 6.7 %collective-permute-start.26 = (f32[2,128,128]{2,1,0:T(8,128)S(1)}, f32[2,128,128]{2,1,0:T(8,128)S(1)}, u32[]{:S(2)}, u32[]{:S(2)}) collective-permute-start(f32[2,128,128]{2,1,0:T(8,128)S(1)} %get-tuple-element.102), channel_id=1, source_target_pairs={{0,24},{8,0},{16,8},{24,16},{1,25},{9,1},{17,9},{25,17},{2,26},{10... | collective-permute-start | bytes 393224 | tf_op jit(solution)/shard_map/ppermute | solution.py:558
  162.0 7.8 %collective-permute-start.24 = (f32[2,128,128]{2,1,0:T(8,128)S(1)}, f32[2,128,128]{2,1,0:T(8,128)S(1)}, u32[]{:S(2)}, u32[]{:S(2)}) collective-permute-start(f32[2,128,128]{2,1,0:T(8,128)S(1)} %get-tuple-element.98), channel_id=1, source_target_pairs={{0,24},{8,0},{16,8},{24,16},{1,25},{9,1},{17,9},{25,17},{2,26},{10... | collective-permute-start | bytes 393224 | tf_op jit(solution)/shard_map/ppermute | solution.py:558
  163.7 7.3 %collective-permute-start.28 = (f32[2,128,128]{2,1,0:T(8,128)S(1)}, f32[2,128,128]{2,1,0:T(8,128)S(1)}, u32[]{:S(2)}, u32[]{:S(2)}) collective-permute-start(f32[2,128,128]{2,1,0:T(8,128)S(1)} %get-tuple-element.105), channel_id=1, source_target_pairs={{0,8},{8,16},{16,24},{24,0},{1,9},{9,17},{17,25},{25,1},{2,10},{10... | collective-permute-start | bytes 393224 | tf_op jit(solution)/shard_map/ppermute | solution.py:558
  166.0 6.7 %collective-permute-start.27 = (f32[2,128,128]{2,1,0:T(8,128)S(1)}, f32[2,128,128]{2,1,0:T(8,128)S(1)}, u32[]{:S(2)}, u32[]{:S(2)}) collective-permute-start(f32[2,128,128]{2,1,0:T(8,128)S(1)} %get-tuple-element.103), channel_id=1, source_target_pairs={{0,8},{8,16},{16,24},{24,0},{1,9},{9,17},{17,25},{25,1},{2,10},{10... | collective-permute-start | bytes 393224 | tf_op jit(solution)/shard_map/ppermute | solution.py:558
  167.5 5.2 %collective-permute-start.29 = (f32[2,128,128]{2,1,0:T(8,128)S(1)}, f32[2,128,128]{2,1,0:T(8,128)S(1)}, u32[]{:S(2)}, u32[]{:S(2)}) collective-permute-start(f32[2,128,128]{2,1,0:T(8,128)S(1)} %get-tuple-element.106), channel_id=1, source_target_pairs={{0,24},{8,0},{16,8},{24,16},{1,25},{9,1},{17,9},{25,17},{2,26},{10... | collective-permute-start | bytes 393224 | tf_op jit(solution)/shard_map/ppermute | solution.py:558
  172.8 7.7 %collective-permute-start.32 = (f32[2,128,128]{2,1,0:T(8,128)S(1)}, f32[2,128,128]{2,1,0:T(8,128)S(1)}, u32[]{:S(2)}, u32[]{:S(2)}) collective-permute-start(f32[2,128,128]{2,1,0:T(8,128)S(1)} %get-tuple-element.107.refs_0_), channel_id=1, source_target_pairs={{0,8},{8,16},{16,24},{24,0},{1,9},{9,17},{17,25},{25,1},{2,10},{10... | collective-permute-start | bytes 393224 | tf_op jit(solution)/shard_map/ppermute | solution.py:558
  174.9 6.3 %collective-permute-start.31 = (f32[2,128,128]{2,1,0:T(8,128)S(1)}, f32[2,128,128]{2,1,0:T(8,128)S(1)}, u32[]{:S(2)}, u32[]{:S(2)}) collective-permute-start(f32[2,128,128]{2,1,0:T(8,128)S(1)} %get-tuple-element.108.refs_1_), channel_id=1, source_target_pairs={{0,24},{8,0},{16,8},{24,16},{1,25},{9,1},{17,9},{25,17},{2,26},{10... | collective-permute-start | bytes 393224 | tf_op jit(solution)/shard_map/ppermute | solution.py:558
  176.5 7.2 %collective-permute-start.30 = (f32[2,128,128]{2,1,0:T(8,128)S(1)}, f32[2,128,128]{2,1,0:T(8,128)S(1)}, u32[]{:S(2)}, u32[]{:S(2)}) collective-permute-start(f32[2,128,128]{2,1,0:T(8,128)S(1)} %get-tuple-element.107.refs_0_), channel_id=1, source_target_pairs={{0,24},{8,0},{16,8},{24,16},{1,25},{9,1},{17,9},{25,17},{2,26},{10... | collective-permute-start | bytes 393224 | tf_op jit(solution)/shard_map/ppermute | solution.py:558
  178.4 6.2 %collective-permute-start.35 = (f32[2,128,128]{2,1,0:T(8,128)S(1)}, f32[2,128,128]{2,1,0:T(8,128)S(1)}, u32[]{:S(2)}, u32[]{:S(2)}) collective-permute-start(f32[2,128,128]{2,1,0:T(8,128)S(1)} %get-tuple-element.108.refs_1_), channel_id=1, source_target_pairs={{0,8},{8,16},{16,24},{24,0},{1,9},{9,17},{17,25},{25,1},{2,10},{10... | collective-permute-start | bytes 393224 | tf_op jit(solution)/shard_map/ppermute | solution.py:558
  180.5 6.2 %collective-permute-start.33 = (f32[2,128,128]{2,1,0:T(8,128)S(1)}, f32[2,128,128]{2,1,0:T(8,128)S(1)}, u32[]{:S(2)}, u32[]{:S(2)}) collective-permute-start(f32[2,128,128]{2,1,0:T(8,128)S(1)} %collective-permute-done.32.refs_6_), channel_id=1, source_target_pairs={{0,8},{8,16},{16,24},{24,0},{1,9},{9,17},{17,25},{25,1},{2,10},{10... | collective-permute-start | bytes 393224 | tf_op jit(solution)/shard_map/ppermute | solution.py:558
  181.3 5.4 %collective-permute-start.34 = (f32[2,128,128]{2,1,0:T(8,128)S(1)}, f32[2,128,128]{2,1,0:T(8,128)S(1)}, u32[]{:S(2)}, u32[]{:S(2)}) collective-permute-start(f32[2,128,128]{2,1,0:T(8,128)S(1)} %collective-permute-done.31.refs_3_), channel_id=1, source_target_pairs={{0,24},{8,0},{16,8},{24,16},{1,25},{9,1},{17,9},{25,17},{2,26},{10... | collective-permute-start | bytes 393224 | tf_op jit(solution)/shard_map/ppermute | solution.py:558
  (11 other events, 74.1 us)

commit v7 on v6

--- a/solution.py
+++ b/solution.py
@@ -338,7 +338,7 @@
     return total
 
 
-def x_kernel(w_ref, id_ref, field, inner, outer, out_ref, side):
+def x_kernel(w_ref, id_ref, field, outer, inner, out_ref, side):
     _, x_cells, y_cells, _ = field.shape
     w = taps_of(w_ref, 0, False)
     set_sides(id_ref, inner, outer, side)
@@ -356,7 +356,7 @@
 
 def x_blur(w, ids, field, inner, outer):
     return call(
-        x_kernel, "x_blur", [f32(*field.shape)], (w, ids, field, inner, outer), 2,
+        x_kernel, "x_blur", [f32(*field.shape)], (w, ids, field, outer, inner), 2,
         scratch=[sides(field)],
     )[0]
 
@@ -455,7 +455,7 @@
             obs[c, x, pl.ds(high, DEEP), :] = outer[c, x]
 
 
-def ratio_kernel(w_ref, id_ref, field, inner, outer, obs, out_ref, side):
+def ratio_kernel(w_ref, id_ref, field, outer, inner, obs, out_ref, side):
     _, x_cells, y_cells, _ = field.shape
     skip = (obs.shape[2] - y_cells) // 2
     w = taps_of(w_ref, 0, False)
@@ -480,7 +480,7 @@
     lax.fori_loop(0, y_cells // TILE, body, 0)
 
 
-def split_kernel(views, w_ref, id_ref, field, inner, outer, *refs):
+def split_kernel(views, w_ref, id_ref, field, outer, inner, *refs):
     outs, wide = refs[:-1], refs[-1]
     _, x_cells, y_cells, _ = field.shape
     depth = x_cells // views
@@ -511,7 +511,7 @@
     outs = [f32(x // views, y, BRICK)] * (2 * views)
     return call(
         functools.partial(split_kernel, views), "x_blur_split", outs,
-        (w, ids, field, inner, outer), 2,
+        (w, ids, field, outer, inner), 2,
         scratch=[pltpu.VMEM((2, x + 2 * HALO, y, BRICK), jnp.float32)],
     )
 
@@ -544,14 +544,43 @@
     out_b[...] = est_b[:, at, :] * (b[...] + b1[...] + b2[...]) / views
 
 
-def join_kernel(views, id_ref, *refs):
-    pieces, out_ref = refs[: 2 * views], refs[2 * views]
+def join_kernel(count, id_ref, *refs):
+    pieces, out_ref = refs[: 2 * count], refs[-1]
+    step = pl.program_id(0)
+    for d in range(count):
+
+        @pl.when(step == d)
+        def _(d=d):
+            out_ref[:, :, 0:BRICK] = pieces[2 * d][...]
+            out_ref[:, :, BRICK : 2 * BRICK] = pieces[2 * d + 1][...]
+
+
+def join(ids, steps, pieces, shape, into=None):
+    count = len(steps)
+    views = shape[0] // pieces[0].shape[0]
     depth = pieces[0].shape[0]
-    for d in range(views):
-        base = lax.rem(id_ref[0] + d, views) * depth
-        for i in range(depth):
-            out_ref[base + i, :, 0:BRICK] = pieces[2 * d][i]
-            out_ref[base + i, :, BRICK : 2 * BRICK] = pieces[2 * d + 1][i]
+
+    def place(step, id_ref):
+        at = steps[0]
+        for d in range(1, count):
+            at = jnp.where(step == d, steps[d], at)
+        return (id_ref[0] + at) % views, 0, 0
+
+    whole = [pl.BlockSpec(p.shape, lambda step, id_ref: (0, 0, 0)) for p in pieces]
+    given = [] if into is None else [into]
+    return pl.pallas_call(
+        functools.partial(join_kernel, count),
+        out_shape=f32(*shape),
+        grid_spec=pltpu.PrefetchScalarGridSpec(
+            num_scalar_prefetch=1,
+            grid=(count,),
+            in_specs=whole + [pl.BlockSpec(memory_space=pl.ANY)] * len(given),
+            out_specs=pl.BlockSpec((depth, *shape[1:]), place),
+        ),
+        input_output_aliases={} if into is None else {1 + len(pieces): 0},
+        cost_estimate=pl.CostEstimate(flops=1000, bytes_accessed=1000, transcendentals=0),
+        name="join",
+    )(ids, *pieces, *given)
 
 
 def turn(value, step, count):
@@ -576,7 +605,9 @@
     est_in, est_out = swap_rows(*sent)
     targets = target[0].transpose(0, 2, 1)
     outgoing = pack(shifts, targets, views_data[0], geo)
-    outgoing, est_in, est_out = lax.optimization_barrier((outgoing, est_in, est_out))
+    outgoing, *first = lax.optimization_barrier((outgoing, est_in[:1, :1], est_out[:1, :1]))
+    est_in = lax.dynamic_update_slice(est_in, first[0], (0, 0, 0))
+    est_out = lax.dynamic_update_slice(est_out, first[1], (0, 0, 0))
     est_lo = jnp.where(odd == 1, est_in, est_out)
     est_hi = jnp.where(odd == 1, est_out, est_in)
     arrived = lax.all_to_all(
@@ -621,7 +652,7 @@
                 2,
             ))
             field = call(
-                ratio_kernel, "ratio", [f32(*field.shape)], (w, ids, field, inner, outer, obs), 2,
+                ratio_kernel, "ratio", [f32(*field.shape)], (w, ids, field, outer, inner, obs), 2,
                 scratch=[sides(field)],
             )[0]
             sent = split(w, ids, view_count, *y_blur(w, ids, field, True, TRIM))
@@ -646,10 +677,9 @@
         prev_b, next_a = turn(own[1], 1, view_count), turn(own[0], -1, view_count)
         far_a, far_b = turn(prev_a, 1, view_count), turn(next_b, -1, view_count)
         pieces = (*own, next_a, next_b, far_a, far_b, prev_a, prev_b)
-    return call(
-        functools.partial(join_kernel, view_count), "join", [f32(x_cells, y_cells, z_cells)],
-        (ids, *pieces),
-    )[0]
+    shape = (x_cells, y_cells, z_cells)
+    near = join(ids, (0, 1, 3), pieces[:4] + pieces[6:], shape)
+    return join(ids, (2,), pieces[4:6], shape, near)
 
 
 def solution(mesh):

time: 189 us -> 192 us (1.016)
  waiting for transfers between devices: 81.8 us -> 74.5 us
  starting transfers between devices: 63.7 us -> 68.3 us
  Pallas kernels: 38.6 us -> 42.8 us
  local copies, waits for them, and re-layouts: 1.96 us -> 4.01 us
    pallas_call x0 -> x2, Pallas kernels: none -> 5.72 us  [join(): pl.pallas_call(functools.partial(join_kernel, count), out_shape=f32(*shap...]
    ppermute x4, waiting for transfers between devices: 32.9 us -> 27.3 us  [swap_layers(): outer = lax.ppermute(outer, 'rows', links + [(j, i) for i, j in links])]
    ppermute x4, starting transfers between devices: 0.99 us -> 6.24 us  [swap_layers(): inner = lax.ppermute(inner, 'rows', [(i, i ^ 1) for i in range(count)])]
    unnamed x12 -> x30, local copies, waits for them, and re-layouts: 0.65 us -> 2.64 us
    pallas_call x22 -> x21, Pallas kernels: 32.7 us -> 31.1 us  [call(): pl.pallas_call(kernel, out_shape=outs, in_specs=[smem()] * scalars + [vme...]
  transfers between devices with their start and end apart: 37 -> 37, of which waited for: 19 -> 18; matrix products, arithmetic and copies ran while one was open for 1% -> 1% of each run, Pallas kernels for 10% -> 12%
where the time goes in v7:
time: 192 us
  waiting for transfers between devices  74.5 us (39%)
  starting transfers between devices  68.3 us (36%)
  Pallas kernels  42.8 us (22%)
  local copies, waits for them, and re-layouts  4.01 us (2%)
    ppermute x24, starting transfers between devices, turn(): lax.ppermute(value, 'views', [(i, (i + step) % count) for i in range(coun...  35.4 us
    pallas_call x21, Pallas kernels, call(): pl.pallas_call(kernel, out_shape=outs, in_specs=[smem()] * scalars + [vme...  31.1 us
    all_to_all x1, waiting for transfers between devices, per_device(): lax.all_to_all(outgoing.reshape(peer_count, capacity + 1, 1, BRICK), ('bl...  29.3 us
    ppermute x4, waiting for transfers between devices, swap_layers(): outer = lax.ppermute(outer, 'rows', links + [(j, i) for i, j in links])  27.3 us
    ppermute x24, waiting for transfers between devices, turn(): lax.ppermute(value, 'views', [(i, (i + step) % count) for i in range(coun...  16.8 us
    all_to_all x1, starting transfers between devices, per_device(): lax.all_to_all(outgoing.reshape(peer_count, capacity + 1, 1, BRICK), ('bl...  9.47 us
    ppermute x4, starting transfers between devices, swap_layers(): outer = lax.ppermute(outer, 'rows', links + [(j, i) for i, j in links])  7.99 us
    ppermute x2, starting transfers between devices, swap_rows(): outer = lax.ppermute(outer, 'blocks', links + [(j, i) for i, j in links])  7.53 us
  transfers between devices with their start and end apart: 37, of which 18 were waited for; matrix products, arithmetic and copies ran while one was open for 1% of the time, Pallas kernels for 12%

profile of v7, /device:TPU:34, one launch (start us, length us, event | category | flops | bytes accessed | tf_op | source)
XLA Modules:
  0.0 191.7 jit_solution(3252593201949937874)
XLA Ops:
  1.2 5.6 %collective-permute-start.1 = (f32[8,16,256]{2,1,0:T(8,128)S(1)}, f32[8,16,256]{2,1,0:T(8,128)S(1)}, u32[]{:S(2)}, u32[]{:S(2)}) collective-permute-start(f32[8,16,256]{2,1,0:T(8,128)S(1)} %get-tuple-element.111), channel_id=1, source_target_pairs={{32,64},{96,128},{160,192},{64,32},{128,96},{192,160},{33,65},{97,... | collective-permute-start | bytes 393224 | tf_op jit(solution)/shard_map/ppermute | solution.py:295
  7.5 5.9 %pack.1 = f32[4160,1,128]{2,1,0:T(1,128)} custom-call(s32[1]{0:T(128)S(6)} %copy.10.shift_ref, s32[8,2,128]{2,1,0:T(2,128)} %bitcast.14, f32[8,128,256]{2,1,0:T(8,128)} %bitcast.13), custom_call_target="tpu_custom_call" | custom-call | tf_op jit(solution)/shard_map/pack/pallas_call | solution.py:89
  13.5 9.5 %all-to-all-start = ((f32[64,65,1,128]{3,2,1,0:T(1,128)}), f32[64,65,1,128]{3,2,1,0:T(1,128)S(1)}, u32[]{:S(2)}, u32[]{:S(2)}) async-start(f32[64,65,1,128]{3,2,1,0:T(1,128)} %bitcast.12), calls=%async_computation | async-start | bytes 4259840 | tf_op jit(solution)/shard_map/all_to_all | solution.py:613
  25.1 3.1 %z_blur.1.in_ref = f32[2,8,160,128]{3,2,1,0:T(8,128)S(1)} custom-call(f32[21]{0:T(128)S(1)} %div.13.w_ref, f32[8,128,256]{2,1,0:T(8,128)S(1)} %copy-done, f32[8,16,256]{2,1,0:T(8,128)S(1)} %get-tuple-element.114.lo, f32[8,16,256]{2,1,0:T(8,128)S(1)} %get-tuple-element.113.hi), custom_call_target="tpu_custom_call" | custom-call | flops 1000 | bytes 1000 | tf_op jit(solution)/shard_map/z_blur/pallas_call | solution.py:167
  29.4 2.2 %collective-permute-start.2 = (f32[2,3,152,128]{3,2,1,0:T(8,128)S(1)}, f32[2,3,152,128]{3,2,1,0:T(8,128)S(1)}, u32[]{:S(2)}, u32[]{:S(2)}) collective-permute-start(f32[2,3,152,128]{3,2,1,0:T(8,128)S(1)} %get-tuple-element.61), channel_id=1, source_target_pairs={{1,2},{3,4},{5,6},{2,1},{4,3},{6,5},{9,10},{11,12},{13,14},{10,9},... | collective-permute-start | bytes 1400840 | tf_op jit(solution)/shard_map/ppermute | solution.py:287
  33.0 10.5 %collective-permute-done.2.outer = f32[2,3,152,128]{3,2,1,0:T(8,128)S(1)} collective-permute-done((f32[2,3,152,128]{3,2,1,0:T(8,128)S(1)}, f32[2,3,152,128]{3,2,1,0:T(8,128)S(1)}, u32[]{:S(2)}, u32[]{:S(2)}) %collective-permute-start.2) | collective-permute-done | bytes 466976 | tf_op jit(solution)/shard_map/ppermute | solution.py:287
  44.8 29.3 %all-to-all-done = f32[64,65,1,128]{3,2,1,0:T(1,128)S(1)} async-done(((f32[64,65,1,128]{3,2,1,0:T(1,128)}), f32[64,65,1,128]{3,2,1,0:T(1,128)S(1)}, u32[]{:S(2)}, u32[]{:S(2)}) %all-to-all-start) | async-done | bytes 2129952 | tf_op jit(solution)/shard_map/all_to_all | solution.py:613
  74.1 5.2 %unpack.1 = (f32[2056,128]{1,0:T(8,128)S(1)}, f32[2,8,16,128]{3,2,1,0:T(8,128)S(1)}, f32[2,8,16,128]{3,2,1,0:T(8,128)S(1)}) custom-call(s32[5]{0:T(128)S(1)} %stack.23.id_ref, f32[4160,1,128]{2,1,0:T(1,128)S(1)} %bitcast.11), custom_call_target="tpu_custom_call" | custom-call | flops 1000 | bytes 1000 | tf_op jit(solution)/shard_map/unpack/pallas_call | solution.py:167
  80.8 1.9 collective-permute-start.5
  82.7 2.8 %ratio_own.1.in_ref.own_ref = f32[2,8,128,128]{3,2,1,0:T(8,128)S(1)} custom-call(f32[21]{0:T(128)S(1)} %div.13.w_ref, f32[2,8,152,128]{3,2,1,0:T(8,128)S(1)} %x_blur.1.below, f32[2056,128]{1,0:T(8,128)S(1)} %get-tuple-element.65.moved), custom_call_target="tpu_custom_call" | custom-call | flops 1000 | bytes 1000 | tf_op jit(solution)/shard_map/ratio_own/pallas_call | solution.py:167
  87.7 1.8 rim.1
  89.5 1.9 %collective-permute-start.6 = (f32[2,3,144,128]{3,2,1,0:T(8,128)S(1)}, f32[2,3,144,128]{3,2,1,0:T(8,128)S(1)}, u32[]{:S(2)}, u32[]{:S(2)}) collective-permute-start(f32[2,3,144,128]{3,2,1,0:T(8,128)S(1)} %get-tuple-element.69), channel_id=1, source_target_pairs={{1,2},{3,4},{5,6},{2,1},{4,3},{6,5},{9,10},{11,12},{13,14},{10,9},... | collective-permute-start | bytes 1327112 | tf_op jit(solution)/shard_map/ppermute | solution.py:287
  93.1 6.0 %collective-permute-done.6.outer = f32[2,3,144,128]{3,2,1,0:T(8,128)S(1)} collective-permute-done((f32[2,3,144,128]{3,2,1,0:T(8,128)S(1)}, f32[2,3,144,128]{3,2,1,0:T(8,128)S(1)}, u32[]{:S(2)}, u32[]{:S(2)}) %collective-permute-start.6) | collective-permute-done | bytes 442400 | tf_op jit(solution)/shard_map/ppermute | solution.py:287
  103.9 1.8 collective-permute-start.8
  105.9 1.9 collective-permute-done.9.ra
  113.1 2.3 %collective-permute-done.11.a2 = f32[2,144,128]{2,1,0:T(8,128)S(1)} collective-permute-done((f32[2,144,128]{2,1,0:T(8,128)S(1)}, f32[2,144,128]{2,1,0:T(8,128)S(1)}, u32[]{:S(2)}, u32[]{:S(2)}) %collective-permute-start.11) | collective-permute-done | bytes 147488 | tf_op jit(solution)/shard_map/ppermute | solution.py:587
  117.8 2.0 %collective-permute-start.15 = (f32[2,144,128]{2,1,0:T(8,128)S(1)}, f32[2,144,128]{2,1,0:T(8,128)S(1)}, u32[]{:S(2)}, u32[]{:S(2)}) collective-permute-start(f32[2,144,128]{2,1,0:T(8,128)S(1)} %get-tuple-element.82.in_b.est_b), channel_id=1, source_target_pairs={{0,24},{8,0},{16,8},{24,16},{1,25},{9,1},{17,9},{25,17},{2,26},{10... | collective-permute-start | bytes 442376 | tf_op jit(solution)/shard_map/ppermute | solution.py:587
  121.7 2.7 %collective-permute-done.16.in_a = f32[2,144,128]{2,1,0:T(8,128)S(1)} collective-permute-done((f32[2,144,128]{2,1,0:T(8,128)S(1)}, f32[2,144,128]{2,1,0:T(8,128)S(1)}, u32[]{:S(2)}, u32[]{:S(2)}) %collective-permute-start.16) | collective-permute-done | bytes 147488 | tf_op jit(solution)/shard_map/ppermute | solution.py:587
  124.5 3.2 %collective-permute-start.18 = (f32[2,144,128]{2,1,0:T(8,128)S(1)}, f32[2,144,128]{2,1,0:T(8,128)S(1)}, u32[]{:S(2)}, u32[]{:S(2)}) collective-permute-start(f32[2,144,128]{2,1,0:T(8,128)S(1)} %collective-permute-done.15.in_b), channel_id=1, source_target_pairs={{0,24},{8,0},{16,8},{24,16},{1,25},{9,1},{17,9},{25,17},{2,26},{10... | collective-permute-start | bytes 442376 | tf_op jit(solution)/shard_map/ppermute | solution.py:587
  133.4 1.9 %collective-permute-start.20 = (f32[2,3,136,128]{3,2,1,0:T(8,128)S(1)}, f32[2,3,136,128]{3,2,1,0:T(8,128)S(1)}, u32[]{:S(2)}, u32[]{:S(2)}) collective-permute-start(f32[2,3,136,128]{3,2,1,0:T(8,128)S(1)} %get-tuple-element.92), channel_id=1, source_target_pairs={{1,2},{3,4},{5,6},{2,1},{4,3},{6,5},{9,10},{11,12},{13,14},{10,9},... | collective-permute-start | bytes 1253384 | tf_op jit(solution)/shard_map/ppermute | solution.py:287
  137.5 5.2 %collective-permute-done.20.outer = f32[2,3,136,128]{3,2,1,0:T(8,128)S(1)} collective-permute-done((f32[2,3,136,128]{3,2,1,0:T(8,128)S(1)}, f32[2,3,136,128]{3,2,1,0:T(8,128)S(1)}, u32[]{:S(2)}, u32[]{:S(2)}) %collective-permute-start.20) | collective-permute-done | bytes 417824 | tf_op jit(solution)/shard_map/ppermute | solution.py:287
  142.7 3.8 %ratio.1.in_ref = f32[2,8,136,128]{3,2,1,0:T(8,128)S(1)} custom-call(f32[21]{0:T(128)S(1)} %div.13.w_ref, s32[5]{0:T(128)S(1)} %stack.23.id_ref, f32[2,8,136,128]{3,2,1,0:T(8,128)S(1)} %get-tuple-element.91.field, f32[2,3,136,128]{3,2,1,0:T(8,128)S(1)} %collective-permute-done.20.outer, f32[2,3,136,128]{3,2,1,0:T(8,128)S(1)} %collective-permute-done.21.inner, ...), custom_call_target="tpu_custom_call" | custom-call | flops 1000 | bytes 1000 | tf_op jit(solution)/shard_map/ratio/pallas_call | solution.py:167
  147.7 1.9 %collective-permute-start.22 = (f32[2,3,128,128]{3,2,1,0:T(8,128)S(1)}, f32[2,3,128,128]{3,2,1,0:T(8,128)S(1)}, u32[]{:S(2)}, u32[]{:S(2)}) collective-permute-start(f32[2,3,128,128]{3,2,1,0:T(8,128)S(1)} %get-tuple-element.95), channel_id=1, source_target_pairs={{1,2},{3,4},{5,6},{2,1},{4,3},{6,5},{9,10},{11,12},{13,14},{10,9},... | collective-permute-start | bytes 1179656 | tf_op jit(solution)/shard_map/ppermute | solution.py:287
  151.2 5.6 %collective-permute-done.22.outer = f32[2,3,128,128]{3,2,1,0:T(8,128)S(1)} collective-permute-done((f32[2,3,128,128]{3,2,1,0:T(8,128)S(1)}, f32[2,3,128,128]{3,2,1,0:T(8,128)S(1)}, u32[]{:S(2)}, u32[]{:S(2)}) %collective-permute-start.22) | collective-permute-done | bytes 393248 | tf_op jit(solution)/shard_map/ppermute | solution.py:287
  158.2 3.2 %collective-permute-start.26 = (f32[2,128,128]{2,1,0:T(8,128)S(1)}, f32[2,128,128]{2,1,0:T(8,128)S(1)}, u32[]{:S(2)}, u32[]{:S(2)}) collective-permute-start(f32[2,128,128]{2,1,0:T(8,128)S(1)} %get-tuple-element.102), channel_id=1, source_target_pairs={{0,24},{8,0},{16,8},{24,16},{1,25},{9,1},{17,9},{25,17},{2,26},{10... | collective-permute-start | bytes 393224 | tf_op jit(solution)/shard_map/ppermute | solution.py:587
  166.9 2.3 %collective-permute-start.29 = (f32[2,128,128]{2,1,0:T(8,128)S(1)}, f32[2,128,128]{2,1,0:T(8,128)S(1)}, u32[]{:S(2)}, u32[]{:S(2)}) collective-permute-start(f32[2,128,128]{2,1,0:T(8,128)S(1)} %get-tuple-element.106), channel_id=1, source_target_pairs={{0,24},{8,0},{16,8},{24,16},{1,25},{9,1},{17,9},{25,17},{2,26},{10... | collective-permute-start | bytes 393224 | tf_op jit(solution)/shard_map/ppermute | solution.py:587
  172.2 2.2 %collective-permute-start.30 = (f32[2,128,128]{2,1,0:T(8,128)S(1)}, f32[2,128,128]{2,1,0:T(8,128)S(1)}, u32[]{:S(2)}, u32[]{:S(2)}) collective-permute-start(f32[2,128,128]{2,1,0:T(8,128)S(1)} %get-tuple-element.107.refs_0_), channel_id=1, source_target_pairs={{0,8},{8,16},{16,24},{24,0},{1,9},{9,17},{17,25},{25,1},{2,10},{10... | collective-permute-start | bytes 393224 | tf_op jit(solution)/shard_map/ppermute | solution.py:587
  175.9 1.9 %collective-permute-start.34 = (f32[2,128,128]{2,1,0:T(8,128)S(1)}, f32[2,128,128]{2,1,0:T(8,128)S(1)}, u32[]{:S(2)}, u32[]{:S(2)}) collective-permute-start(f32[2,128,128]{2,1,0:T(8,128)S(1)} %get-tuple-element.107.refs_0_), channel_id=1, source_target_pairs={{0,24},{8,0},{16,8},{24,16},{1,25},{9,1},{17,9},{25,17},{2,26},{10... | collective-permute-start | bytes 393224 | tf_op jit(solution)/shard_map/ppermute | solution.py:587
  177.9 2.0 %collective-permute-done.30.refs_4_ = f32[2,128,128]{2,1,0:T(8,128)S(1)} collective-permute-done((f32[2,128,128]{2,1,0:T(8,128)S(1)}, f32[2,128,128]{2,1,0:T(8,128)S(1)}, u32[]{:S(2)}, u32[]{:S(2)}) %collective-permute-start.30) | collective-permute-done | bytes 131104 | tf_op jit(solution)/shard_map/ppermute | solution.py:587
  180.7 2.5 %collective-permute-start.33 = (f32[2,128,128]{2,1,0:T(8,128)S(1)}, f32[2,128,128]{2,1,0:T(8,128)S(1)}, u32[]{:S(2)}, u32[]{:S(2)}) collective-permute-start(f32[2,128,128]{2,1,0:T(8,128)S(1)} %collective-permute-done.32.refs_3_), channel_id=1, source_target_pairs={{0,24},{8,0},{16,8},{24,16},{1,25},{9,1},{17,9},{25,17},{2,26},{10... | collective-permute-start | bytes 393224 | tf_op jit(solution)/shard_map/ppermute | solution.py:587
  184.7 3.4 %join.2.refs_2_ = f32[8,128,256]{2,1,0:T(8,128)} custom-call(s32[5]{0:T(128)} %copy-done.6, f32[2,128,128]{2,1,0:T(8,128)} %copy-done.4, f32[2,128,128]{2,1,0:T(8,128)} %copy-done.5, f32[2,128,128]{2,1,0:T(8,128)} %copy-done.12, f32[2,128,128]{2,1,0:T(8,128)} %copy-done.11, f32[2,128,128]{2,1,0:T(8,128)} %copy-done.10, f32[2,128,128]{2,1,0:T(8,128)} %copy-done.13), custom_call_target="tpu_custom_call" | custom-call | flops 1000 | bytes 1000 | tf_op jit(solution)/shard_map/join/pallas_call | solution.py:571
  189.4 2.3 %join.3 = f32[8,128,256]{2,1,0:T(8,128)} custom-call(s32[5]{0:T(128)} %copy-done.6, f32[2,128,128]{2,1,0:T(8,128)} %copy-done.8, f32[2,128,128]{2,1,0:T(8,128)} %copy-done.9, f32[8,128,256]{2,1,0:T(8,128)} %join.2.refs_2_), custom_call_target="tpu_custom_call", output_to_operand_aliasing={{}: (3, {})} | custom-call | flops 1000 | bytes 1000 | tf_op jit(solution)/shard_map/join/pallas_call | solution.py:571
  (108 shorter events, 52.8 us)
Async XLA Ops:
  1.0 12.4 %collective-permute-start = (f32[8,16,256]{2,1,0:T(8,128)S(1)}, f32[8,16,256]{2,1,0:T(8,128)S(1)}, u32[]{:S(2)}, u32[]{:S(2)}) collective-permute-start(f32[8,16,256]{2,1,0:T(8,128)S(1)} %get-tuple-element.112), channel_id=1, source_target_pairs={{0,32},{32,0},{64,96},{96,64},{128,160},{160,128},{192,224},{224,1... | collective-permute-start | bytes 393224 | tf_op jit(solution)/shard_map/ppermute | solution.py:296
  1.2 12.2 %collective-permute-start.1 = (f32[8,16,256]{2,1,0:T(8,128)S(1)}, f32[8,16,256]{2,1,0:T(8,128)S(1)}, u32[]{:S(2)}, u32[]{:S(2)}) collective-permute-start(f32[8,16,256]{2,1,0:T(8,128)S(1)} %get-tuple-element.111), channel_id=1, source_target_pairs={{32,64},{96,128},{160,192},{64,32},{128,96},{192,160},{33,65},{97,... | collective-permute-start | bytes 393224 | tf_op jit(solution)/shard_map/ppermute | solution.py:295
  13.5 60.6 %all-to-all-start = ((f32[64,65,1,128]{3,2,1,0:T(1,128)}), f32[64,65,1,128]{3,2,1,0:T(1,128)S(1)}, u32[]{:S(2)}, u32[]{:S(2)}) async-start(f32[64,65,1,128]{3,2,1,0:T(1,128)} %bitcast.12), calls=%async_computation | async-start | bytes 4259840 | tf_op jit(solution)/shard_map/all_to_all | solution.py:613
  29.4 14.1 %collective-permute-start.2 = (f32[2,3,152,128]{3,2,1,0:T(8,128)S(1)}, f32[2,3,152,128]{3,2,1,0:T(8,128)S(1)}, u32[]{:S(2)}, u32[]{:S(2)}) collective-permute-start(f32[2,3,152,128]{3,2,1,0:T(8,128)S(1)} %get-tuple-element.61), channel_id=1, source_target_pairs={{1,2},{3,4},{5,6},{2,1},{4,3},{6,5},{9,10},{11,12},{13,14},{10,9},... | collective-permute-start | bytes 1400840 | tf_op jit(solution)/shard_map/ppermute | solution.py:287
  31.7 11.8 %collective-permute-start.3 = (f32[2,3,152,128]{3,2,1,0:T(8,128)S(1)}, f32[2,3,152,128]{3,2,1,0:T(8,128)S(1)}, u32[]{:S(2)}, u32[]{:S(2)}) collective-permute-start(f32[2,3,152,128]{3,2,1,0:T(8,128)S(1)} %get-tuple-element.62), channel_id=1, source_target_pairs={{0,1},{1,0},{2,3},{3,2},{4,5},{5,4},{6,7},{7,6},{8,9},{9,8},{10,11... | collective-permute-start | bytes 1400840 | tf_op jit(solution)/shard_map/ppermute | solution.py:288
  79.3 7.2 %collective-permute-start.4 = (f32[2,8,16,128]{3,2,1,0:T(8,128)S(1)}, f32[2,8,16,128]{3,2,1,0:T(8,128)S(1)}, u32[]{:S(2)}, u32[]{:S(2)}) collective-permute-start(f32[2,8,16,128]{3,2,1,0:T(8,128)S(1)} %get-tuple-element.66), channel_id=1, source_target_pairs={{0,32},{32,0},{64,96},{96,64},{128,160},{160,128},{192,224},{224,1... | collective-permute-start | bytes 393224 | tf_op jit(solution)/shard_map/ppermute | solution.py:296
  80.8 6.8 %collective-permute-start.5 = (f32[2,8,16,128]{3,2,1,0:T(8,128)S(1)}, f32[2,8,16,128]{3,2,1,0:T(8,128)S(1)}, u32[]{:S(2)}, u32[]{:S(2)}) collective-permute-start(f32[2,8,16,128]{3,2,1,0:T(8,128)S(1)} %get-tuple-element.67), channel_id=1, source_target_pairs={{32,64},{96,128},{160,192},{64,32},{128,96},{192,160},{33,65},{97,... | collective-permute-start | bytes 393224 | tf_op jit(solution)/shard_map/ppermute | solution.py:295
  89.5 9.6 %collective-permute-start.6 = (f32[2,3,144,128]{3,2,1,0:T(8,128)S(1)}, f32[2,3,144,128]{3,2,1,0:T(8,128)S(1)}, u32[]{:S(2)}, u32[]{:S(2)}) collective-permute-start(f32[2,3,144,128]{3,2,1,0:T(8,128)S(1)} %get-tuple-element.69), channel_id=1, source_target_pairs={{1,2},{3,4},{5,6},{2,1},{4,3},{6,5},{9,10},{11,12},{13,14},{10,9},... | collective-permute-start | bytes 1327112 | tf_op jit(solution)/shard_map/ppermute | solution.py:287
  91.4 7.7 %collective-permute-start.7 = (f32[2,3,144,128]{3,2,1,0:T(8,128)S(1)}, f32[2,3,144,128]{3,2,1,0:T(8,128)S(1)}, u32[]{:S(2)}, u32[]{:S(2)}) collective-permute-start(f32[2,3,144,128]{3,2,1,0:T(8,128)S(1)} %get-tuple-element.70), channel_id=1, source_target_pairs={{0,1},{1,0},{2,3},{3,2},{4,5},{5,4},{6,7},{7,6},{8,9},{9,8},{10,11... | collective-permute-start | bytes 1327112 | tf_op jit(solution)/shard_map/ppermute | solution.py:288
  100.6 7.2 %collective-permute-start.9 = (f32[2,144,128]{2,1,0:T(8,128)S(1)}, f32[2,144,128]{2,1,0:T(8,128)S(1)}, u32[]{:S(2)}, u32[]{:S(2)}) collective-permute-start(f32[2,144,128]{2,1,0:T(8,128)S(1)} %get-tuple-element.74), channel_id=1, source_target_pairs={{0,8},{8,16},{16,24},{24,0},{1,9},{9,17},{17,25},{25,1},{2,10},{10... | collective-permute-start | bytes 442376 | tf_op jit(solution)/shard_map/ppermute | solution.py:587
  102.2 6.7 %collective-permute-start.10 = (f32[2,144,128]{2,1,0:T(8,128)S(1)}, f32[2,144,128]{2,1,0:T(8,128)S(1)}, u32[]{:S(2)}, u32[]{:S(2)}) collective-permute-start(f32[2,144,128]{2,1,0:T(8,128)S(1)} %get-tuple-element.76), channel_id=1, source_target_pairs={{0,24},{8,0},{16,8},{24,16},{1,25},{9,1},{17,9},{25,17},{2,26},{10... | collective-permute-start | bytes 442376 | tf_op jit(solution)/shard_map/ppermute | solution.py:587
  103.9 8.4 %collective-permute-start.8 = (f32[2,144,128]{2,1,0:T(8,128)S(1)}, f32[2,144,128]{2,1,0:T(8,128)S(1)}, u32[]{:S(2)}, u32[]{:S(2)}) collective-permute-start(f32[2,144,128]{2,1,0:T(8,128)S(1)} %get-tuple-element.72), channel_id=1, source_target_pairs={{0,24},{8,0},{16,8},{24,16},{1,25},{9,1},{17,9},{25,17},{2,26},{10... | collective-permute-start | bytes 442376 | tf_op jit(solution)/shard_map/ppermute | solution.py:587
  105.7 7.4 %collective-permute-start.12 = (f32[2,144,128]{2,1,0:T(8,128)S(1)}, f32[2,144,128]{2,1,0:T(8,128)S(1)}, u32[]{:S(2)}, u32[]{:S(2)}) collective-permute-start(f32[2,144,128]{2,1,0:T(8,128)S(1)} %get-tuple-element.79), channel_id=1, source_target_pairs={{0,8},{8,16},{16,24},{24,0},{1,9},{9,17},{17,25},{25,1},{2,10},{10... | collective-permute-start | bytes 442376 | tf_op jit(solution)/shard_map/ppermute | solution.py:587
  116.4 8.0 %collective-permute-start.16 = (f32[2,144,128]{2,1,0:T(8,128)S(1)}, f32[2,144,128]{2,1,0:T(8,128)S(1)}, u32[]{:S(2)}, u32[]{:S(2)}) collective-permute-start(f32[2,144,128]{2,1,0:T(8,128)S(1)} %get-tuple-element.81.in_a.est_a), channel_id=1, source_target_pairs={{0,8},{8,16},{16,24},{24,0},{1,9},{9,17},{17,25},{25,1},{2,10},{10... | collective-permute-start | bytes 442376 | tf_op jit(solution)/shard_map/ppermute | solution.py:587
  117.8 6.7 %collective-permute-start.15 = (f32[2,144,128]{2,1,0:T(8,128)S(1)}, f32[2,144,128]{2,1,0:T(8,128)S(1)}, u32[]{:S(2)}, u32[]{:S(2)}) collective-permute-start(f32[2,144,128]{2,1,0:T(8,128)S(1)} %get-tuple-element.82.in_b.est_b), channel_id=1, source_target_pairs={{0,24},{8,0},{16,8},{24,16},{1,25},{9,1},{17,9},{25,17},{2,26},{10... | collective-permute-start | bytes 442376 | tf_op jit(solution)/shard_map/ppermute | solution.py:587
  119.7 9.1 %collective-permute-start.14 = (f32[2,144,128]{2,1,0:T(8,128)S(1)}, f32[2,144,128]{2,1,0:T(8,128)S(1)}, u32[]{:S(2)}, u32[]{:S(2)}) collective-permute-start(f32[2,144,128]{2,1,0:T(8,128)S(1)} %get-tuple-element.81.in_a.est_a), channel_id=1, source_target_pairs={{0,24},{8,0},{16,8},{24,16},{1,25},{9,1},{17,9},{25,17},{2,26},{10... | collective-permute-start | bytes 442376 | tf_op jit(solution)/shard_map/ppermute | solution.py:587
  121.4 8.6 %collective-permute-start.19 = (f32[2,144,128]{2,1,0:T(8,128)S(1)}, f32[2,144,128]{2,1,0:T(8,128)S(1)}, u32[]{:S(2)}, u32[]{:S(2)}) collective-permute-start(f32[2,144,128]{2,1,0:T(8,128)S(1)} %get-tuple-element.82.in_b.est_b), channel_id=1, source_target_pairs={{0,8},{8,16},{16,24},{24,0},{1,9},{9,17},{17,25},{25,1},{2,10},{10... | collective-permute-start | bytes 442376 | tf_op jit(solution)/shard_map/ppermute | solution.py:587
  124.4 6.7 %collective-permute-start.17 = (f32[2,144,128]{2,1,0:T(8,128)S(1)}, f32[2,144,128]{2,1,0:T(8,128)S(1)}, u32[]{:S(2)}, u32[]{:S(2)}) collective-permute-start(f32[2,144,128]{2,1,0:T(8,128)S(1)} %collective-permute-done.16.in_a), channel_id=1, source_target_pairs={{0,8},{8,16},{16,24},{24,0},{1,9},{9,17},{17,25},{25,1},{2,10},{10... | collective-permute-start | bytes 442376 | tf_op jit(solution)/shard_map/ppermute | solution.py:587
  124.5 6.6 %collective-permute-start.18 = (f32[2,144,128]{2,1,0:T(8,128)S(1)}, f32[2,144,128]{2,1,0:T(8,128)S(1)}, u32[]{:S(2)}, u32[]{:S(2)}) collective-permute-start(f32[2,144,128]{2,1,0:T(8,128)S(1)} %collective-permute-done.15.in_b), channel_id=1, source_target_pairs={{0,24},{8,0},{16,8},{24,16},{1,25},{9,1},{17,9},{25,17},{2,26},{10... | collective-permute-start | bytes 442376 | tf_op jit(solution)/shard_map/ppermute | solution.py:587
  133.4 9.4 %collective-permute-start.20 = (f32[2,3,136,128]{3,2,1,0:T(8,128)S(1)}, f32[2,3,136,128]{3,2,1,0:T(8,128)S(1)}, u32[]{:S(2)}, u32[]{:S(2)}) collective-permute-start(f32[2,3,136,128]{3,2,1,0:T(8,128)S(1)} %get-tuple-element.92), channel_id=1, source_target_pairs={{1,2},{3,4},{5,6},{2,1},{4,3},{6,5},{9,10},{11,12},{13,14},{10,9},... | collective-permute-start | bytes 1253384 | tf_op jit(solution)/shard_map/ppermute | solution.py:287
  135.3 7.4 %collective-permute-start.21 = (f32[2,3,136,128]{3,2,1,0:T(8,128)S(1)}, f32[2,3,136,128]{3,2,1,0:T(8,128)S(1)}, u32[]{:S(2)}, u32[]{:S(2)}) collective-permute-start(f32[2,3,136,128]{3,2,1,0:T(8,128)S(1)} %get-tuple-element.93), channel_id=1, source_target_pairs={{0,1},{1,0},{2,3},{3,2},{4,5},{5,4},{6,7},{7,6},{8,9},{9,8},{10,11... | collective-permute-start | bytes 1253384 | tf_op jit(solution)/shard_map/ppermute | solution.py:288
  147.7 9.1 %collective-permute-start.22 = (f32[2,3,128,128]{3,2,1,0:T(8,128)S(1)}, f32[2,3,128,128]{3,2,1,0:T(8,128)S(1)}, u32[]{:S(2)}, u32[]{:S(2)}) collective-permute-start(f32[2,3,128,128]{3,2,1,0:T(8,128)S(1)} %get-tuple-element.95), channel_id=1, source_target_pairs={{1,2},{3,4},{5,6},{2,1},{4,3},{6,5},{9,10},{11,12},{13,14},{10,9},... | collective-permute-start | bytes 1179656 | tf_op jit(solution)/shard_map/ppermute | solution.py:287
  149.6 7.2 %collective-permute-start.23 = (f32[2,3,128,128]{3,2,1,0:T(8,128)S(1)}, f32[2,3,128,128]{3,2,1,0:T(8,128)S(1)}, u32[]{:S(2)}, u32[]{:S(2)}) collective-permute-start(f32[2,3,128,128]{3,2,1,0:T(8,128)S(1)} %get-tuple-element.96), channel_id=1, source_target_pairs={{0,1},{1,0},{2,3},{3,2},{4,5},{5,4},{6,7},{7,6},{8,9},{9,8},{10,11... | collective-permute-start | bytes 1179656 | tf_op jit(solution)/shard_map/ppermute | solution.py:288
  158.1 6.8 %collective-permute-start.25 = (f32[2,128,128]{2,1,0:T(8,128)S(1)}, f32[2,128,128]{2,1,0:T(8,128)S(1)}, u32[]{:S(2)}, u32[]{:S(2)}) collective-permute-start(f32[2,128,128]{2,1,0:T(8,128)S(1)} %get-tuple-element.100), channel_id=1, source_target_pairs={{0,8},{8,16},{16,24},{24,0},{1,9},{9,17},{17,25},{25,1},{2,10},{10... | collective-permute-start | bytes 393224 | tf_op jit(solution)/shard_map/ppermute | solution.py:587
  158.2 7.1 %collective-permute-start.26 = (f32[2,128,128]{2,1,0:T(8,128)S(1)}, f32[2,128,128]{2,1,0:T(8,128)S(1)}, u32[]{:S(2)}, u32[]{:S(2)}) collective-permute-start(f32[2,128,128]{2,1,0:T(8,128)S(1)} %get-tuple-element.102), channel_id=1, source_target_pairs={{0,24},{8,0},{16,8},{24,16},{1,25},{9,1},{17,9},{25,17},{2,26},{10... | collective-permute-start | bytes 393224 | tf_op jit(solution)/shard_map/ppermute | solution.py:587
  161.4 7.8 %collective-permute-start.24 = (f32[2,128,128]{2,1,0:T(8,128)S(1)}, f32[2,128,128]{2,1,0:T(8,128)S(1)}, u32[]{:S(2)}, u32[]{:S(2)}) collective-permute-start(f32[2,128,128]{2,1,0:T(8,128)S(1)} %get-tuple-element.98), channel_id=1, source_target_pairs={{0,24},{8,0},{16,8},{24,16},{1,25},{9,1},{17,9},{25,17},{2,26},{10... | collective-permute-start | bytes 393224 | tf_op jit(solution)/shard_map/ppermute | solution.py:587
  163.1 7.3 %collective-permute-start.28 = (f32[2,128,128]{2,1,0:T(8,128)S(1)}, f32[2,128,128]{2,1,0:T(8,128)S(1)}, u32[]{:S(2)}, u32[]{:S(2)}) collective-permute-start(f32[2,128,128]{2,1,0:T(8,128)S(1)} %get-tuple-element.105), channel_id=1, source_target_pairs={{0,8},{8,16},{16,24},{24,0},{1,9},{9,17},{17,25},{25,1},{2,10},{10... | collective-permute-start | bytes 393224 | tf_op jit(solution)/shard_map/ppermute | solution.py:587
  165.4 6.7 %collective-permute-start.27 = (f32[2,128,128]{2,1,0:T(8,128)S(1)}, f32[2,128,128]{2,1,0:T(8,128)S(1)}, u32[]{:S(2)}, u32[]{:S(2)}) collective-permute-start(f32[2,128,128]{2,1,0:T(8,128)S(1)} %get-tuple-element.103), channel_id=1, source_target_pairs={{0,8},{8,16},{16,24},{24,0},{1,9},{9,17},{17,25},{25,1},{2,10},{10... | collective-permute-start | bytes 393224 | tf_op jit(solution)/shard_map/ppermute | solution.py:587
  172.2 7.7 %collective-permute-start.30 = (f32[2,128,128]{2,1,0:T(8,128)S(1)}, f32[2,128,128]{2,1,0:T(8,128)S(1)}, u32[]{:S(2)}, u32[]{:S(2)}) collective-permute-start(f32[2,128,128]{2,1,0:T(8,128)S(1)} %get-tuple-element.107.refs_0_), channel_id=1, source_target_pairs={{0,8},{8,16},{16,24},{24,0},{1,9},{9,17},{17,25},{25,1},{2,10},{10... | collective-permute-start | bytes 393224 | tf_op jit(solution)/shard_map/ppermute | solution.py:587
  175.9 7.3 %collective-permute-start.34 = (f32[2,128,128]{2,1,0:T(8,128)S(1)}, f32[2,128,128]{2,1,0:T(8,128)S(1)}, u32[]{:S(2)}, u32[]{:S(2)}) collective-permute-start(f32[2,128,128]{2,1,0:T(8,128)S(1)} %get-tuple-element.107.refs_0_), channel_id=1, source_target_pairs={{0,24},{8,0},{16,8},{24,16},{1,25},{9,1},{17,9},{25,17},{2,26},{10... | collective-permute-start | bytes 393224 | tf_op jit(solution)/shard_map/ppermute | solution.py:587
  179.9 8.2 %collective-permute-start.31 = (f32[2,128,128]{2,1,0:T(8,128)S(1)}, f32[2,128,128]{2,1,0:T(8,128)S(1)}, u32[]{:S(2)}, u32[]{:S(2)}) collective-permute-start(f32[2,128,128]{2,1,0:T(8,128)S(1)} %collective-permute-done.30.refs_4_), channel_id=1, source_target_pairs={{0,8},{8,16},{16,24},{24,0},{1,9},{9,17},{17,25},{25,1},{2,10},{10... | collective-permute-start | bytes 393224 | tf_op jit(solution)/shard_map/ppermute | solution.py:587
  180.7 7.4 %collective-permute-start.33 = (f32[2,128,128]{2,1,0:T(8,128)S(1)}, f32[2,128,128]{2,1,0:T(8,128)S(1)}, u32[]{:S(2)}, u32[]{:S(2)}) collective-permute-start(f32[2,128,128]{2,1,0:T(8,128)S(1)} %collective-permute-done.32.refs_3_), channel_id=1, source_target_pairs={{0,24},{8,0},{16,8},{24,16},{1,25},{9,1},{17,9},{25,17},{2,26},{10... | collective-permute-start | bytes 393224 | tf_op jit(solution)/shard_map/ppermute | solution.py:587
  (20 other events, 254.9 us)

commit v8 on v2

v8 whole, which is shorter than its diff:
```python
import functools
import jax
import jax.numpy as jnp
from jax import lax
from jax.experimental import pallas as pl
from jax.experimental.pallas import tpu as pltpu
from jax.sharding import PartitionSpec as P

VMEM = pltpu.VMEM
BRICK = 128
HALO = 3
ITERS = 2
GROUP = 16
SPARE = 8
TAPS = 2 * HALO + 1
TILE = 8
TRIM = 4


def lane_sum(x):
    return jnp.sum(x, axis=1, keepdims=True)


def pack_kernel(geo, shift_ref, target_ref, views_ref, out_ref, rolled, pos_v, pos_s, sem):
    peers, cap, x_cells, y_cells, brick_cols, row_count, all_cols, view_count = geo
    groups = brick_cols * x_cells
    rows_per = cap + 1
    t = target_ref[...]
    bz = t % brick_cols
    column = t // brick_cols % all_cols
    line = t // (brick_cols * all_cols)
    dest = column // y_cells * row_count + line // x_cells
    part = y_cells // view_count
    y = column % y_cells
    slot = ((y // part * brick_cols + bz) * x_cells + line % x_cells) * part + y % part + 1
    high, low = slot // 64, slot % 64
    peer_id = lax.broadcasted_iota(jnp.int32, (peers, y_cells), 0)
    before = (
        lax.broadcasted_iota(jnp.int32, (y_cells, y_cells), 0)
        < lax.broadcasted_iota(jnp.int32, (y_cells, y_cells), 1)
    ).astype(jnp.bfloat16)
    kid = lax.broadcasted_iota(jnp.int32, (BRICK, y_cells), 0)
    carry = jnp.zeros((peers, 1), jnp.float32)
    listed = jnp.zeros((2 * peers, BRICK), jnp.float32)
    for g in range(groups):
        here = (g % x_cells, slice(g // x_cells, g // x_cells + 1))
        d = dest[here]
        hot = d == peer_id
        hot_f = hot.astype(jnp.float32)
        ahead = jnp.dot(hot_f.astype(jnp.bfloat16), before, preferred_element_type=jnp.float32)
        ranks = jnp.sum(hot_f * (ahead + carry), axis=0, keepdims=True)
        carry = carry + lane_sum(hot_f)
        rank_i = ranks.astype(jnp.int32)
        pos_v[g : g + 1, :] = d * rows_per + rank_i
        h = hot_f * high[here].astype(jnp.float32)
        l = hot_f * low[here].astype(jnp.float32)
        both = jnp.concatenate([h, l], axis=0).astype(jnp.bfloat16)
        at = (rank_i == kid).astype(jnp.float32).astype(jnp.bfloat16)
        listed = listed + lax.dot_general(
            both, at, (((1,), (1,)), ((), ())), preferred_element_type=jnp.float32
        )
    copy = pltpu.make_async_copy(pos_v, pos_s, sem)
    copy.start()
    entries = 64.0 * listed[:peers] + listed[peers:]
    for p in range(peers):
        out_ref[p * rows_per + cap] = entries[p : p + 1, :]
    shift = shift_ref[0]
    for bz_i in range(brick_cols):
        for x in range(x_cells):
            rolled[bz_i * x_cells + x] = pltpu.roll(
                views_ref[x, :, bz_i * BRICK : (bz_i + 1) * BRICK], shift, 1
            )
    copy.wait()

    def body(g, c):
        for base in range(0, y_cells, GROUP):
            places = [pos_s[g, base + i] for i in range(GROUP)]
            rows = [rolled[g, base + i : base + i + 1, :] for i in range(GROUP)]
            for place, row in zip(places, rows):
                out_ref[place] = row
        return c

    lax.fori_loop(0, groups, body, 0)


def pack(shift, target, views, geo):
    peers, cap, x_cells, y_cells, brick_cols, row_count, all_cols, view_count = geo
    groups = brick_cols * x_cells
    return pl.pallas_call(
        functools.partial(pack_kernel, geo),
        out_shape=jax.ShapeDtypeStruct((peers * (cap + 1), 1, BRICK), jnp.float32),
        in_specs=[
            pl.BlockSpec(memory_space=pltpu.SMEM),
            pl.BlockSpec(memory_space=pltpu.VMEM),
            pl.BlockSpec(memory_space=pltpu.VMEM),
        ],
        out_specs=pl.BlockSpec(memory_space=pltpu.VMEM),
        scratch_shapes=[
            pltpu.VMEM((groups, y_cells, BRICK), jnp.float32),
            pltpu.VMEM((groups, y_cells), jnp.int32),
            pltpu.SMEM((groups, y_cells), jnp.int32),
            pltpu.SemaphoreType.DMA,
        ],
        name="pack",
    )(shift, target, views)


def unpack_kernel(peers, cap, slots, in_ref, out_ref, placed, list_v, idx_v, idx_s, sem):
    rows_per = cap + 1
    for p in range(peers):
        list_v[p : p + 1, :] = in_ref[p * rows_per + cap]
    e = list_v[...].astype(jnp.int32)
    idx_v[...] = jnp.where(e > 0, e - 1, slots)
    copy = pltpu.make_async_copy(idx_v, idx_s, sem)
    copy.start()
    copy.wait()

    def per_peer(p, c):
        for base in range(0, cap, GROUP):
            places = [idx_s[p, base + i] for i in range(GROUP)]
            rows = [in_ref[p * rows_per + base + i] for i in range(GROUP)]
            for place, row in zip(places, rows):
                placed[pl.ds(place, 1), :] = row
        return c

    lax.fori_loop(0, peers, per_peer, 0)
    out_ref[...] = placed[0:slots, :]


def unpack(arrived, peers, cap, slots):
    return call(
        functools.partial(unpack_kernel, peers, cap, slots), "unpack", [f32(slots, BRICK)],
        (arrived,), 0,
        scratch=[
            pltpu.VMEM((slots + SPARE, BRICK), jnp.float32),
            pltpu.VMEM((peers, BRICK), jnp.float32),
            pltpu.VMEM((peers, BRICK), jnp.int32),
            pltpu.SMEM((peers, BRICK), jnp.int32),
            pltpu.SemaphoreType.DMA,
        ],
    )[0]


def vmem():
    return pl.BlockSpec(memory_space=pltpu.VMEM)


def smem():
    return pl.BlockSpec(memory_space=pltpu.SMEM)


def f32(*shape):
    return jax.ShapeDtypeStruct(shape, jnp.float32)


def call(kernel, name, outs, args, scalars=1, scratch=(), work=1000):
    return pl.pallas_call(
        kernel,
        out_shape=outs,
        in_specs=[smem()] * scalars + [vmem()] * (len(args) - scalars),
        out_specs=[vmem()] * len(outs),
        scratch_shapes=list(scratch),
        cost_estimate=pl.CostEstimate(flops=work, bytes_accessed=work, transcendentals=0),
        compiler_params=pltpu.CompilerParams(vmem_limit_bytes=32 * 1024 * 1024),
        name=name,
    )(*args)


def taps_of(w_ref, view, dim, flip):
    base = (view * 3 + dim) * TAPS
    return [w_ref[base + (TAPS - 1 - k if flip else k)] for k in range(TAPS)]


def blur_z(a, b, w):
    lane = lax.broadcasted_iota(jnp.int32, a.shape, 1)
    out_a, out_b = w[HALO] * a, w[HALO] * b
    for s in range(1, HALO + 1):
        keep = lane < BRICK - s
        ra, rb = pltpu.roll(a, BRICK - s, 1), pltpu.roll(b, BRICK - s, 1)
        out_a += w[HALO + s] * jnp.where(keep, ra, rb)
        out_b += w[HALO + s] * jnp.where(keep, rb, 0.0)
        fresh = lane < s
        la, lb = pltpu.roll(a, s, 1), pltpu.roll(b, s, 1)
        out_a += w[HALO - s] * jnp.where(fresh, 0.0, la)
        out_b += w[HALO - s] * jnp.where(fresh, la, lb)
    return out_a, out_b


def y_rows(ref, at, w, n):
    total = w[0] * ref[(*at, pl.ds(TRIM - HALO, n))]
    for k in range(1, TAPS):
        total += w[k] * ref[(*at, pl.ds(TRIM - HALO + k, n))]
    return total


def weigh(layers, w):
    total = w[0] * layers[0]
    for k in range(1, TAPS):
        total += w[k] * layers[k]
    return total


def spread(layers, w, x):
    total = None
    for k in range(TAPS):
        i = x + k - HALO
        if 0 <= i < len(layers):
            term = w[k] * layers[i]
            total = term if total is None else total + term
    return total


def part_kernel(id_ref, est, outer, inner, out_ref, send_in, send_out, wide):
    x_cells, y_cells, _ = est.shape
    part = out_ref.shape[2] - 2 * TILE
    odd = id_ref[2]
    start = pl.multiple_of(id_ref[0] * part, part)
    far = TILE + y_cells
    at_in = pl.ds(pl.multiple_of((1 - odd) * far, TILE), TILE)
    at_out = pl.ds(pl.multiple_of(odd * far, TILE), TILE)

    def body(x, carry):
        for c in range(2):
            lanes = slice(c * BRICK, (c + 1) * BRICK)
            wide[c, TILE:far, :] = est[x, :, lanes]
            wide[c, at_in, :] = inner[x, :, lanes]
            wide[c, at_out, :] = outer[x, :, lanes]
            out_ref[c, x] = wide[c, pl.ds(start, part + 2 * TILE), :]
        return carry

    lax.fori_loop(0, x_cells, body, 0)
    base = x_cells - HALO
    for c in range(2):
        for i in range(HALO):
            send_in[c, i] = out_ref[c, (1 - id_ref[1]) * base + i]
            send_out[c, i] = out_ref[c, id_ref[1] * base + i]


def extend_kernel(id_ref, own, outer, inner, out_ref):
    x_cells = own.shape[1]
    odd = id_ref[1]
    rows = slice(TRIM, own.shape[2] - TRIM)
    base = x_cells + HALO
    for c in range(2):
        for i in range(x_cells):
            out_ref[c, HALO + i] = own[c, i, rows, :]
        for i in range(HALO):
            out_ref[c, (1 - odd) * base + i] = inner[c, i, rows, :]
            out_ref[c, odd * base + i] = outer[c, i, rows, :]


def forward_kernel(w_ref, est, out_ref, partial):
    views, _, x_cells, part, _ = out_ref.shape

    def per_view(u, carry):
        wx, wy, wz = (taps_of(w_ref, u, dim, False) for dim in range(3))

        def per_tile(t, carry):
            at = pl.ds(pl.multiple_of(t * TILE, TILE), TILE)
            for c in range(2):
                layers = [est[c, i, at, :] for i in range(x_cells + 2 * HALO)]
                for x in range(x_cells):
                    partial[c, x, at, :] = weigh(layers[x : x + TAPS], wx)
            return carry

        lax.fori_loop(0, (part + 2 * TRIM) // TILE, per_tile, 0)

        def per_layer(x, carry):
            rows = [y_rows(partial, (c, x), wy, part) for c in range(2)]
            out_ref[u, 0, x], out_ref[u, 1, x] = blur_z(*rows, wz)
            return carry

        lax.fori_loop(0, x_cells, per_layer, 0)
        return carry

    lax.fori_loop(0, views, per_view, 0)


def forward(w, est, views, x_cells):
    rows = est.shape[2]
    return call(
        forward_kernel, "forward", [f32(views, 2, x_cells, rows - 2 * TRIM, BRICK)], (w, est),
        scratch=[pltpu.VMEM((2, x_cells, rows, BRICK), jnp.float32)],
    )[0]


def backward_kernel(w_ref, id_ref, below, obs, out_ref, send_in, send_out, wide, partial):
    views, _, x_cells, part, _ = obs.shape
    layers_out, count = out_ref.shape[1], send_in.shape[1]
    zeros = jnp.zeros((TILE, BRICK), jnp.float32)
    for c in range(2):
        for x in range(x_cells):
            wide[c, x, 0:TILE, :] = zeros
            wide[c, x, TILE + part : 2 * TILE + part, :] = zeros
    out_ref[...] = jnp.zeros_like(out_ref)

    def per_view(u, carry):
        wx, wy, wz = (taps_of(w_ref, u, dim, True) for dim in range(3))

        def per_layer(x, carry):
            rows = blur_z(*(obs[u, c, x] / below[u, c, x] for c in range(2)), wz)
            for c in range(2):
                wide[c, x, TILE : TILE + part, :] = rows[c]
                partial[c, x] = y_rows(wide, (c, x), wy, part + 2 * TRIM)
            return carry

        lax.fori_loop(0, x_cells, per_layer, 0)

        def per_tile(t, carry):
            at = pl.ds(pl.multiple_of(t * TILE, TILE), TILE)
            for c in range(2):
                layers = [partial[c, x, at, :] for x in range(x_cells)]
                for i in range(layers_out):
                    out_ref[c, i, at, :] += spread(layers, wx, i - HALO)
            return carry

        lax.fori_loop(0, (part + 2 * TRIM) // TILE, per_tile, 0)
        return carry

    lax.fori_loop(0, views, per_view, 0)
    odd = id_ref[1]
    base = layers_out - count
    for c in range(2):
        for i in range(count):
            send_in[c, i] = out_ref[c, (1 - odd) * base + i]
            send_out[c, i] = out_ref[c, odd * base + i]


def backward(w, ids, below, obs, count):
    _, _, x, part, _ = obs.shape
    rows = part + 2 * TRIM
    outs = [f32(2, x + 2 * HALO, rows, BRICK)] + [f32(2, count, rows, BRICK)] * 2
    return call(
        backward_kernel, "backward", outs, (w, ids, below, obs), 2,
        scratch=[
            pltpu.VMEM((2, x, part + 2 * TILE, BRICK), jnp.float32),
            pltpu.VMEM((2, x, rows, BRICK), jnp.float32),
        ],
    )


def merge_kernel(id_ref, total, outer, inner, out_ref, send_in, send_out):
    layers, rows = out_ref.shape[1:3]
    count = inner.shape[1]
    skip = (total.shape[1] - layers) // 2
    odd, odd_part = id_ref[1], lax.rem(id_ref[0], 2)
    base = layers - count
    at_in = pl.ds(pl.multiple_of((1 - odd_part) * (rows - TILE), TILE), TILE)
    at_out = pl.ds(pl.multiple_of(odd_part * (rows - TILE), TILE), TILE)
    for c in range(2):
        for i in range(layers):
            out_ref[c, i] = total[c, skip + i]
        for i in range(count):
            out_ref[c, (1 - odd) * base + i] += inner[c, i]
            out_ref[c, odd * base + i] += outer[c, i]
        for i in range(layers):
            send_in[c, i] = out_ref[c, i, at_in, :]
            send_out[c, i] = out_ref[c, i, at_out, :]


def merge(ids, total, outer, inner, layers):
    rows = total.shape[2]
    outs = [f32(2, layers, rows, BRICK)] + [f32(2, layers, TILE, BRICK)] * 2
    return call(merge_kernel, "merge", outs, (ids, total, outer, inner))


def update_kernel(views, id_ref, total, outer, inner, est, out_ref):
    layers, rows = out_ref.shape[1:3]
    odd = lax.rem(id_ref[0], 2)
    at_in = pl.ds(pl.multiple_of((1 - odd) * (rows - TILE), TILE), TILE)
    at_out = pl.ds(pl.multiple_of(odd * (rows - TILE), TILE), TILE)
    for c in range(2):
        for i in range(layers):
            out_ref[c, i] = est[c, i] * total[c, i] / views
            for at, more in ((at_in, inner), (at_out, outer)):
                out_ref[c, i, at, :] = est[c, i, at, :] * (total[c, i, at, :] + more[c, i]) / views


def finish_kernel(views, id_ref, total, outer, inner, est, out_a, out_b, wide):
    layers, rows = total.shape[1:3]
    odd = lax.rem(id_ref[0], 2)
    at_in = pl.ds(pl.multiple_of((1 - odd) * (rows - TILE), TILE), TILE)
    at_out = pl.ds(pl.multiple_of(odd * (rows - TILE), TILE), TILE)
    own = slice(TRIM, rows - TRIM)
    for c, out in ((0, out_a), (1, out_b)):
        for i in range(layers):
            wide[...] = total[c, i]
            wide[at_in, :] += inner[c, i]
            wide[at_out, :] += outer[c, i]
            out[i] = est[c, HALO + i, own, :] * wide[own, :] / views


def join_kernel(views, id_ref, *refs):
    pieces, out_ref = refs[: 2 * views], refs[2 * views]
    part = pieces[0].shape[1]
    for d in range(views):
        at = pl.ds(pl.multiple_of(lax.rem(id_ref[0] + d, views) * part, part), part)
        out_ref[:, at, 0:BRICK] = pieces[2 * d][...]
        out_ref[:, at, BRICK : 2 * BRICK] = pieces[2 * d + 1][...]


def swap(inner, outer, axes):
    count = lax.axis_size(axes)
    links = [(i, i + 1) for i in range(1, count - 1, 2)]
    outer = lax.ppermute(outer, axes, links + [(j, i) for i, j in links])
    inner = lax.ppermute(inner, axes, [(i, i ^ 1) for i in range(count)])
    return outer, inner


def turn(value, step, count):
    return lax.ppermute(value, "views", [(i, (i + step) % count) for i in range(count)])


def per_device(estimate, views_data, target, psf_taps, shifts):
    x_cells, y_cells, z_cells = estimate.shape
    row_count = lax.axis_size("rows")
    block_count = lax.axis_size("blocks")
    peer_count = block_count * row_count
    view_count = lax.axis_size("views")
    brick_cols = z_cells // BRICK
    brick_count = x_cells * y_cells * brick_cols
    capacity = 2 * brick_count // peer_count
    part = y_cells // view_count
    all_cols = y_cells * block_count
    geo = (peer_count, capacity, x_cells, y_cells, brick_cols, row_count, all_cols, view_count)
    block, row, place = (lax.axis_index(name) for name in ("blocks", "rows", "views"))
    odd = block % 2
    est_out, est_in = swap(*(
        lax.dynamic_slice_in_dim(estimate, at * (y_cells - TILE), TILE, 1) for at in (1 - odd, odd)
    ), "blocks")
    outgoing = pack(shifts, target[0].transpose(0, 2, 1), views_data[0], geo)
    outgoing, est_out, est_in = lax.optimization_barrier((outgoing, est_out, est_in))
    arrived = lax.all_to_all(
        outgoing.reshape(peer_count, capacity + 1, 1, BRICK),
        ("blocks", "rows"), split_axis=0, concat_axis=0, tiled=True,
    ).reshape(peer_count * (capacity + 1), 1, BRICK)
    taps = lax.all_gather(psf_taps, "views", axis=0, tiled=True)
    w = (taps / jnp.sum(taps, axis=2, keepdims=True)).reshape(-1)
    ids = jnp.stack([place, row % 2, odd]).astype(jnp.int32)
    halo = f32(2, HALO, part + 2 * TILE, BRICK)
    own, *sent = call(
        part_kernel, "part", [f32(2, x_cells, part + 2 * TILE, BRICK), halo, halo],
        (ids, estimate, est_out, est_in), scratch=[pltpu.VMEM((2, y_cells + 2 * TILE, BRICK), jnp.float32)],
    )
    wide = [f32(2, x_cells + 2 * HALO, part + 2 * TRIM, BRICK)]
    est = call(extend_kernel, "extend", wide, (ids, own, *swap(*sent, "rows")))[0]
    below = forward(w, est, view_count, x_cells)
    arrived, below = lax.optimization_barrier((arrived, below))
    moved = unpack(arrived, peer_count, capacity, brick_count)
    obs = lax.all_to_all(
        moved.reshape(view_count, brick_count // view_count, BRICK),
        "views", split_axis=0, concat_axis=0, tiled=True,
    ).reshape(view_count, brick_cols, x_cells, part, BRICK)
    for iteration in range(ITERS):
        if iteration > 0:
            below = forward(w, est, view_count, x_cells)
        more = iteration < ITERS - 1
        total, *sent = backward(w, ids, below, obs, (2 if more else 1) * HALO)
        layers = x_cells + (2 * HALO if more else 0)
        total, *sent = merge(ids, total, *swap(*sent, "rows"), layers)
        args = (ids, total, *swap(*sent, ("blocks", "views")), est)
        if more:
            est = call(functools.partial(update_kernel, view_count), "update", wide, args)[0]
    own = call(
        functools.partial(finish_kernel, view_count), "finish",
        [f32(x_cells, part, BRICK)] * 2, args,
        scratch=[pltpu.VMEM((part + 2 * TRIM, BRICK), jnp.float32)],
    )
    prev_a, next_b = turn(own[0], 1, view_count), turn(own[1], -1, view_count)
    prev_b, next_a = turn(own[1], 1, view_count), turn(own[0], -1, view_count)
    far_a, far_b = turn(prev_a, 1, view_count), turn(next_b, -1, view_count)
    pieces = (*own, next_a, next_b, far_a, far_b, prev_a, prev_b)
    return call(
        functools.partial(join_kernel, view_count), "join", [f32(x_cells, y_cells, z_cells)],
        (ids, *pieces),
    )[0]


def solution(mesh):
    placed = (
        P("rows", "blocks", None),
        P("views", "rows", "blocks", None),
        P("views", "rows", "blocks", None),
        P("views", None, None),
        P("views"),
    )
    return jax.shard_map(
        per_device, mesh=mesh, in_specs=placed, out_specs=P("rows", "blocks", None), check_vma=False
    )
```

time: 336 us -> 166 us (0.49)
  waiting for transfers between devices: 157 us -> 48.2 us
  other arithmetic: 72.4 us -> 0.16 us
  blocking collectives: 0 us -> 30.6 us
  Pallas kernels: 22.3 us -> 41 us
  starting transfers between devices: 57.9 us -> 40.9 us
  between operations: 15 us -> 0.88 us
  local copies, waits for them, and re-layouts: 9.94 us -> 3.69 us
    psum x2 -> x0, waiting for transfers between devices: 101 us -> none  [per_device(): combined = lax.psum(projected, 'views')]
    add x10 -> x0, other arithmetic: 56.4 us -> none  [axis_blur(): result + weights[offset] * lax.slice_in_dim(volume, offset, offset + leng...]
    ppermute x16 -> x18, waiting for transfers between devices: 55.3 us -> 25.8 us  [the longest x6 21 us: swap(): outer = lax.ppermute(outer, axes, links + [(j, i) for i, j in links])]
    pallas_call x1 -> x12, Pallas kernels: 11 us -> 35 us  [call(): pl.pallas_call(kernel, out_shape=outs, in_specs=[smem()] * scalars + [vme...]
    all_to_all x1, waiting for transfers between devices: 0.01 us -> 22.4 us  [per_device(): lax.all_to_all(outgoing.reshape(peer_count, capacity + 1, 1, BRICK), ('bl...]
    all_to_all x0 -> x1, blocking collectives: none -> 19.3 us  [per_device(): lax.all_to_all(moved.reshape(view_count, brick_count // view_count, BRICK...]
    div x5 -> x1, other arithmetic: 15.8 us -> 0.08 us  [per_device(): w = (taps / jnp.sum(taps, axis=2, keepdims=True)).reshape(-1)]
    ppermute x16 -> x18, starting transfers between devices: 46.1 us -> 31.5 us  [the longest x6 17.6 us: swap(): outer = lax.ppermute(outer, axes, links + [(j, i) for i, j in links])]
  transfers between devices with their start and end apart: 19 -> 19, of which waited for: 14 -> 8; matrix products, arithmetic and copies ran while one was open for 5% -> 0% of each run, Pallas kernels for 0% -> 8%
where the time goes in v8:
time: 166 us; the launch traced here: 165 us
  waiting for transfers between devices  48.2 us (29%)
  Pallas kernels  41 us (25%)
  starting transfers between devices  40.9 us (25%)
  blocking collectives  30.6 us (18%)
  local copies, waits for them, and re-layouts  3.69 us (2%)
    pallas_call x12, Pallas kernels, call(): pl.pallas_call(kernel, out_shape=outs, in_specs=[smem()] * scalars + [vme...  35 us
    all_to_all x1, waiting for transfers between devices, per_device(): lax.all_to_all(outgoing.reshape(peer_count, capacity + 1, 1, BRICK), ('bl...  22.4 us
    ppermute x6, waiting for transfers between devices, swap(): outer = lax.ppermute(outer, axes, links + [(j, i) for i, j in links])  21 us
    all_to_all x1, blocking collectives, per_device(): lax.all_to_all(moved.reshape(view_count, brick_count // view_count, BRICK...  19.3 us
    ppermute x6, starting transfers between devices, swap(): outer = lax.ppermute(outer, axes, links + [(j, i) for i, j in links])  17.6 us
    all_gather x1, blocking collectives, per_device(): taps = lax.all_gather(psf_taps, 'views', axis=0, tiled=True)  11.2 us
    all_to_all x1, starting transfers between devices, per_device(): lax.all_to_all(outgoing.reshape(peer_count, capacity + 1, 1, BRICK), ('bl...  9.47 us
    ppermute x6, starting transfers between devices, turn(): lax.ppermute(value, 'views', [(i, (i + step) % count) for i in range(coun...  8.56 us
  transfers between devices with their start and end apart: 19, of which 8 were waited for; matrix products, arithmetic and copies ran while one was open for 0% of the time, Pallas kernels for 8%

profile of v8, /device:TPU:34, one launch (start us, length us, event | category | flops | bytes accessed | tf_op | source)
XLA Modules:
  0.0 165.5 jit_solution(1168080269339944434)
XLA Ops:
  1.1 5.6 %collective-permute-start = (f32[8,8,256]{2,1,0:T(8,128)S(1)}, f32[8,8,256]{2,1,0:T(8,128)S(1)}, u32[]{:S(2)}, u32[]{:S(2)}) collective-permute-start(f32[8,8,256]{2,1,0:T(8,128)S(1)} %get-tuple-element.50), channel_id=1, source_target_pairs={{32,64},{96,128},{160,192},{64,32},{128,96},{192,160},{33,65},{97,... | collective-permute-start | bytes 196616 | tf_op jit(solution)/shard_map/ppermute | solution.py:405
  7.4 6.0 %pack.1 = f32[4160,1,128]{2,1,0:T(1,128)} custom-call(s32[1]{0:T(128)S(6)} %copy.9.shift_ref, s32[8,2,128]{2,1,0:T(2,128)} %bitcast.18, f32[8,128,256]{2,1,0:T(8,128)} %bitcast.17), custom_call_target="tpu_custom_call" | custom-call | tf_op jit(solution)/shard_map/pack/pallas_call | solution.py:89
  13.4 9.5 %all-to-all-start = ((f32[64,65,1,128]{3,2,1,0:T(1,128)}), f32[64,65,1,128]{3,2,1,0:T(1,128)S(1)}, u32[]{:S(2)}, u32[]{:S(2)}) async-start(f32[64,65,1,128]{3,2,1,0:T(1,128)} %bitcast.16), calls=%async_computation | async-start | bytes 4259840 | tf_op jit(solution)/shard_map/all_to_all | solution.py:433
  22.9 11.2 %all_gather.3 = f32[4,3,7]{2,1,0:T(4,128)S(1)} all-gather(f32[1,3,7]{2,1,0:T(4,128)S(1)} %copy.8), channel_id=1, replica_groups=mesh['blocks'=8,'views'=4,'rows'=8] {'views'}, dimensions={0}, use_global_device_ids=true | all-gather | bytes 420 | tf_op jit(solution)/shard_map/all_gather | solution.py:437
  34.2 1.4 part.1
  36.4 1.9 %collective-permute-start.2 = (f32[2,3,48,128]{3,2,1,0:T(8,128)}, f32[2,3,48,128]{3,2,1,0:T(8,128)S(1)}, u32[]{:S(2)}, u32[]{:S(2)}) collective-permute-start(f32[2,3,48,128]{3,2,1,0:T(8,128)} %get-tuple-element.31), channel_id=1, source_target_pairs={{1,2},{3,4},{5,6},{2,1},{4,3},{6,5},{9,10},{11,12},{13,14},{10,9},... | collective-permute-start | bytes 442376 | tf_op jit(solution)/shard_map/ppermute | solution.py:405
  38.3 1.7 collective-permute-start.3
  40.1 3.4 %collective-permute-done.2.outer = f32[2,3,48,128]{3,2,1,0:T(8,128)S(1)} collective-permute-done((f32[2,3,48,128]{3,2,1,0:T(8,128)}, f32[2,3,48,128]{3,2,1,0:T(8,128)S(1)}, u32[]{:S(2)}, u32[]{:S(2)}) %collective-permute-start.2) | collective-permute-done | bytes 147488 | tf_op jit(solution)/shard_map/ppermute | solution.py:405
  43.5 1.0 copy-done.4
  45.1 5.5 %forward.2.below = f32[4,2,8,32,128]{4,3,2,1,0:T(8,128)S(1)} custom-call(f32[84]{0:T(128)S(1)} %reshape.16.w_ref, f32[2,14,40,128]{3,2,1,0:T(8,128)S(1)} %extend.1.est), custom_call_target="tpu_custom_call" | custom-call | flops 1000 | bytes 1000 | tf_op jit(solution)/shard_map/forward/pallas_call | solution.py:157
  51.6 22.4 %all-to-all-done = f32[64,65,1,128]{3,2,1,0:T(1,128)S(1)} async-done(((f32[64,65,1,128]{3,2,1,0:T(1,128)}), f32[64,65,1,128]{3,2,1,0:T(1,128)S(1)}, u32[]{:S(2)}, u32[]{:S(2)}) %all-to-all-start) | async-done | bytes 2129952 | tf_op jit(solution)/shard_map/all_to_all | solution.py:433
  74.0 4.7 %unpack.1 = f32[2048,128]{1,0:T(8,128)S(1)} custom-call(f32[4160,1,128]{2,1,0:T(1,128)S(1)} %bitcast.14), custom_call_target="tpu_custom_call" | custom-call | flops 1000 | bytes 1000 | tf_op jit(solution)/shard_map/unpack/pallas_call | solution.py:157
  78.7 19.3 %all_to_all.10 = f32[4,512,128]{2,1,0:T(8,128)S(1)} all-to-all(f32[4,512,128]{2,1,0:T(8,128)S(1)} %bitcast.15), channel_id=1, replica_groups=mesh['blocks'=8,'views'=4,'rows'=8] {'views'}, dimensions={0} | all-to-all | bytes 2097152 | tf_op jit(solution)/shard_map/all_to_all | solution.py:450
  98.1 6.4 %backward.2 = (f32[2,14,40,128]{3,2,1,0:T(8,128)S(1)}, f32[2,6,40,128]{3,2,1,0:T(8,128)S(1)}, f32[2,6,40,128]{3,2,1,0:T(8,128)S(1)}) custom-call(f32[84]{0:T(128)S(1)} %reshape.16.w_ref, s32[3]{0:T(128)S(1)} %pad_add_fusion.id_ref, f32[4,2,8,32,128]{4,3,2,1,0:T(8,128)S(1)} %copy-done.1, f32[4,2,8,32,128]{4,3,2,1,0:T(8,128)S(1)} %bitcast.12), custom_call_target="tpu_custom_call" | custom-call | flops 1000 | bytes 1000 | tf_op jit(solution)/shard_map/backward/pallas_call | solution.py:157
  104.5 1.9 %collective-permute-start.4 = (f32[2,6,40,128]{3,2,1,0:T(8,128)S(1)}, f32[2,6,40,128]{3,2,1,0:T(8,128)S(1)}, u32[]{:S(2)}, u32[]{:S(2)}) collective-permute-start(f32[2,6,40,128]{3,2,1,0:T(8,128)S(1)} %get-tuple-element.36), channel_id=1, source_target_pairs={{1,2},{3,4},{5,6},{2,1},{4,3},{6,5},{9,10},{11,12},{13,14},{10,9},... | collective-permute-start | bytes 737288 | tf_op jit(solution)/shard_map/ppermute | solution.py:405
  106.4 1.7 %collective-permute-start.5 = (f32[2,6,40,128]{3,2,1,0:T(8,128)S(1)}, f32[2,6,40,128]{3,2,1,0:T(8,128)S(1)}, u32[]{:S(2)}, u32[]{:S(2)}) collective-permute-start(f32[2,6,40,128]{3,2,1,0:T(8,128)S(1)} %get-tuple-element.37), channel_id=1, source_target_pairs={{0,1},{1,0},{2,3},{3,2},{4,5},{5,4},{6,7},{7,6},{8,9},{9,8},{10,11... | collective-permute-start | bytes 737288 | tf_op jit(solution)/shard_map/ppermute | solution.py:406
  108.1 3.9 %collective-permute-done.4.outer = f32[2,6,40,128]{3,2,1,0:T(8,128)S(1)} collective-permute-done((f32[2,6,40,128]{3,2,1,0:T(8,128)S(1)}, f32[2,6,40,128]{3,2,1,0:T(8,128)S(1)}, u32[]{:S(2)}, u32[]{:S(2)}) %collective-permute-start.4) | collective-permute-done | bytes 245792 | tf_op jit(solution)/shard_map/ppermute | solution.py:405
  112.7 2.5 %collective-permute-start.6 = (f32[2,14,8,128]{3,2,1,0:T(8,128)S(1)}, f32[2,14,8,128]{3,2,1,0:T(8,128)S(1)}, u32[]{:S(2)}, u32[]{:S(2)}) collective-permute-start(f32[2,14,8,128]{3,2,1,0:T(8,128)S(1)} %get-tuple-element.39), channel_id=1, source_target_pairs={{8,16},{24,32},{40,48},{56,64},{72,80},{88,96},{104,112},{120,128}... | collective-permute-start | bytes 344072 | tf_op jit(solution)/shard_map/ppermute | solution.py:405
  115.5 6.4 %collective-permute-done.6.outer = f32[2,14,8,128]{3,2,1,0:T(8,128)S(1)} collective-permute-done((f32[2,14,8,128]{3,2,1,0:T(8,128)S(1)}, f32[2,14,8,128]{3,2,1,0:T(8,128)S(1)}, u32[]{:S(2)}, u32[]{:S(2)}) %collective-permute-start.6) | collective-permute-done | bytes 114720 | tf_op jit(solution)/shard_map/ppermute | solution.py:405
  122.6 5.5 %forward.3.below = f32[4,2,8,32,128]{4,3,2,1,0:T(8,128)S(1)} custom-call(f32[84]{0:T(128)S(1)} %reshape.16.w_ref, f32[2,14,40,128]{3,2,1,0:T(8,128)S(1)} %update.1.est), custom_call_target="tpu_custom_call" | custom-call | flops 1000 | bytes 1000 | tf_op jit(solution)/shard_map/forward/pallas_call | solution.py:157
  128.1 6.4 %backward.3 = (f32[2,14,40,128]{3,2,1,0:T(8,128)S(1)}, f32[2,3,40,128]{3,2,1,0:T(8,128)S(1)}, f32[2,3,40,128]{3,2,1,0:T(8,128)S(1)}) custom-call(f32[84]{0:T(128)S(1)} %reshape.16.w_ref, s32[3]{0:T(128)S(1)} %pad_add_fusion.id_ref, f32[4,2,8,32,128]{4,3,2,1,0:T(8,128)S(1)} %forward.3.below, f32[4,2,8,32,128]{4,3,2,1,0:T(8,128)S(1)} %bitcast.13), custom_call_target="tpu_custom_call" | custom-call | flops 1000 | bytes 1000 | tf_op jit(solution)/shard_map/backward/pallas_call | solution.py:157
  134.5 1.9 %collective-permute-start.8 = (f32[2,3,40,128]{3,2,1,0:T(8,128)S(1)}, f32[2,3,40,128]{3,2,1,0:T(8,128)S(1)}, u32[]{:S(2)}, u32[]{:S(2)}) collective-permute-start(f32[2,3,40,128]{3,2,1,0:T(8,128)S(1)} %get-tuple-element.42), channel_id=1, source_target_pairs={{1,2},{3,4},{5,6},{2,1},{4,3},{6,5},{9,10},{11,12},{13,14},{10,9},... | collective-permute-start | bytes 368648 | tf_op jit(solution)/shard_map/ppermute | solution.py:405
  136.4 1.4 collective-permute-start.9
  137.8 2.9 %collective-permute-done.8.outer = f32[2,3,40,128]{3,2,1,0:T(8,128)S(1)} collective-permute-done((f32[2,3,40,128]{3,2,1,0:T(8,128)S(1)}, f32[2,3,40,128]{3,2,1,0:T(8,128)S(1)}, u32[]{:S(2)}, u32[]{:S(2)}) %collective-permute-start.8) | collective-permute-done | bytes 122912 | tf_op jit(solution)/shard_map/ppermute | solution.py:405
  141.3 3.8 %collective-permute-start.10 = (f32[2,8,8,128]{3,2,1,0:T(8,128)S(1)}, f32[2,8,8,128]{3,2,1,0:T(8,128)S(1)}, u32[]{:S(2)}, u32[]{:S(2)}) collective-permute-start(f32[2,8,8,128]{3,2,1,0:T(8,128)S(1)} %get-tuple-element.45), channel_id=1, source_target_pairs={{8,16},{24,32},{40,48},{56,64},{72,80},{88,96},{104,112},{120,128}... | collective-permute-start | bytes 196616 | tf_op jit(solution)/shard_map/ppermute | solution.py:405
  145.2 4.4 %collective-permute-done.10.outer = f32[2,8,8,128]{3,2,1,0:T(8,128)S(1)} collective-permute-done((f32[2,8,8,128]{3,2,1,0:T(8,128)S(1)}, f32[2,8,8,128]{3,2,1,0:T(8,128)S(1)}, u32[]{:S(2)}, u32[]{:S(2)}) %collective-permute-start.10) | collective-permute-done | bytes 65568 | tf_op jit(solution)/shard_map/ppermute | solution.py:405
  150.5 3.2 %collective-permute-start.13 = (f32[8,32,128]{2,1,0:T(8,128)S(1)}, f32[8,32,128]{2,1,0:T(8,128)S(1)}, u32[]{:S(2)}, u32[]{:S(2)}) collective-permute-start(f32[8,32,128]{2,1,0:T(8,128)S(1)} %get-tuple-element.48.refs_1_), channel_id=1, source_target_pairs={{0,24},{8,0},{16,8},{24,16},{1,25},{9,1},{17,9},{25,17},{2,26},{10... | collective-permute-start | bytes 393224 | tf_op jit(solution)/shard_map/ppermute | solution.py:411
  153.8 2.0 %collective-permute-start.17 = (f32[8,32,128]{2,1,0:T(8,128)S(1)}, f32[8,32,128]{2,1,0:T(8,128)S(1)}, u32[]{:S(2)}, u32[]{:S(2)}) collective-permute-start(f32[8,32,128]{2,1,0:T(8,128)S(1)} %get-tuple-element.48.refs_1_), channel_id=1, source_target_pairs={{0,8},{8,16},{16,24},{24,0},{1,9},{9,17},{17,25},{25,1},{2,10},{10... | collective-permute-start | bytes 393224 | tf_op jit(solution)/shard_map/ppermute | solution.py:411
  155.8 1.9 %collective-permute-done.14.refs_6_ = f32[8,32,128]{2,1,0:T(8,128)S(1)} collective-permute-done((f32[8,32,128]{2,1,0:T(8,128)S(1)}, f32[8,32,128]{2,1,0:T(8,128)S(1)}, u32[]{:S(2)}, u32[]{:S(2)}) %collective-permute-start.14) | collective-permute-done | bytes 131104 | tf_op jit(solution)/shard_map/ppermute | solution.py:411
  157.7 3.2 %collective-permute-start.16 = (f32[8,32,128]{2,1,0:T(8,128)S(1)}, f32[8,32,128]{2,1,0:T(8,128)S(1)}, u32[]{:S(2)}, u32[]{:S(2)}) collective-permute-start(f32[8,32,128]{2,1,0:T(8,128)S(1)} %collective-permute-done.13.refs_3_), channel_id=1, source_target_pairs={{0,24},{8,0},{16,8},{24,16},{1,25},{9,1},{17,9},{25,17},{2,26},{10... | collective-permute-start | bytes 393224 | tf_op jit(solution)/shard_map/ppermute | solution.py:411
  160.9 2.9 %collective-permute-done.15.refs_4_ = f32[8,32,128]{2,1,0:T(8,128)S(1)} collective-permute-done((f32[8,32,128]{2,1,0:T(8,128)S(1)}, f32[8,32,128]{2,1,0:T(8,128)S(1)}, u32[]{:S(2)}, u32[]{:S(2)}) %collective-permute-start.15) | collective-permute-done | bytes 131104 | tf_op jit(solution)/shard_map/ppermute | solution.py:411
  163.9 1.6 join.1
  (38 shorter events, 6.9 us)
Async XLA Ops:
  0.9 12.5 %collective-permute-start.1 = (f32[8,8,256]{2,1,0:T(8,128)S(1)}, f32[8,8,256]{2,1,0:T(8,128)S(1)}, u32[]{:S(2)}, u32[]{:S(2)}) collective-permute-start(f32[8,8,256]{2,1,0:T(8,128)S(1)} %get-tuple-element.49), channel_id=1, source_target_pairs={{0,32},{32,0},{64,96},{96,64},{128,160},{160,128},{192,224},{224,1... | collective-permute-start | bytes 196616 | tf_op jit(solution)/shard_map/ppermute | solution.py:406
  1.1 12.3 %collective-permute-start = (f32[8,8,256]{2,1,0:T(8,128)S(1)}, f32[8,8,256]{2,1,0:T(8,128)S(1)}, u32[]{:S(2)}, u32[]{:S(2)}) collective-permute-start(f32[8,8,256]{2,1,0:T(8,128)S(1)} %get-tuple-element.50), channel_id=1, source_target_pairs={{32,64},{96,128},{160,192},{64,32},{128,96},{192,160},{33,65},{97,... | collective-permute-start | bytes 196616 | tf_op jit(solution)/shard_map/ppermute | solution.py:405
  13.4 9.5 %copy-start.5 = (f32[1,3,7]{2,0,1:T(1,128)S(1)}, f32[1,3,7]{2,0,1:T(1,128)}, u32[]{:S(2)}) copy-start(f32[1,3,7]{2,0,1:T(1,128)} %param.8) | copy-start | bytes 256
  13.4 20.8 %copy-start.2 = (f32[8,128,256]{2,1,0:T(8,128)S(1)}, f32[8,128,256]{2,1,0:T(8,128)}, u32[]{:S(2)}) copy-start(f32[8,128,256]{2,1,0:T(8,128)} %est.1) | copy-start | bytes 3145732
  13.4 60.6 %all-to-all-start = ((f32[64,65,1,128]{3,2,1,0:T(1,128)}), f32[64,65,1,128]{3,2,1,0:T(1,128)S(1)}, u32[]{:S(2)}, u32[]{:S(2)}) async-start(f32[64,65,1,128]{3,2,1,0:T(1,128)} %bitcast.16), calls=%async_computation | async-start | bytes 4259840 | tf_op jit(solution)/shard_map/all_to_all | solution.py:433
  35.7 0.7 copy-start.3
  36.4 7.1 %collective-permute-start.2 = (f32[2,3,48,128]{3,2,1,0:T(8,128)}, f32[2,3,48,128]{3,2,1,0:T(8,128)S(1)}, u32[]{:S(2)}, u32[]{:S(2)}) collective-permute-start(f32[2,3,48,128]{3,2,1,0:T(8,128)} %get-tuple-element.31), channel_id=1, source_target_pairs={{1,2},{3,4},{5,6},{2,1},{4,3},{6,5},{9,10},{11,12},{13,14},{10,9},... | collective-permute-start | bytes 442376 | tf_op jit(solution)/shard_map/ppermute | solution.py:405
  38.3 5.2 %collective-permute-start.3 = (f32[2,3,48,128]{3,2,1,0:T(8,128)S(1)}, f32[2,3,48,128]{3,2,1,0:T(8,128)S(1)}, u32[]{:S(2)}, u32[]{:S(2)}) collective-permute-start(f32[2,3,48,128]{3,2,1,0:T(8,128)S(1)} %get-tuple-element.32), channel_id=1, source_target_pairs={{0,1},{1,0},{2,3},{3,2},{4,5},{5,4},{6,7},{7,6},{8,9},{9,8},{10,11... | collective-permute-start | bytes 442376 | tf_op jit(solution)/shard_map/ppermute | solution.py:406
  43.5 1.0 copy-start.4
  50.7 1.0 copy-start
  74.0 24.1 %copy-start.1 = (f32[4,2,8,32,128]{4,3,2,1,0:T(8,128)S(1)}, f32[4,2,8,32,128]{4,3,2,1,0:T(8,128)}, u32[]{:S(2)}) copy-start(f32[4,2,8,32,128]{4,3,2,1,0:T(8,128)} %copy-done) | copy-start | bytes 3145732
  104.5 7.5 %collective-permute-start.4 = (f32[2,6,40,128]{3,2,1,0:T(8,128)S(1)}, f32[2,6,40,128]{3,2,1,0:T(8,128)S(1)}, u32[]{:S(2)}, u32[]{:S(2)}) collective-permute-start(f32[2,6,40,128]{3,2,1,0:T(8,128)S(1)} %get-tuple-element.36), channel_id=1, source_target_pairs={{1,2},{3,4},{5,6},{2,1},{4,3},{6,5},{9,10},{11,12},{13,14},{10,9},... | collective-permute-start | bytes 737288 | tf_op jit(solution)/shard_map/ppermute | solution.py:405
  106.4 5.6 %collective-permute-start.5 = (f32[2,6,40,128]{3,2,1,0:T(8,128)S(1)}, f32[2,6,40,128]{3,2,1,0:T(8,128)S(1)}, u32[]{:S(2)}, u32[]{:S(2)}) collective-permute-start(f32[2,6,40,128]{3,2,1,0:T(8,128)S(1)} %get-tuple-element.37), channel_id=1, source_target_pairs={{0,1},{1,0},{2,3},{3,2},{4,5},{5,4},{6,7},{7,6},{8,9},{9,8},{10,11... | collective-permute-start | bytes 737288 | tf_op jit(solution)/shard_map/ppermute | solution.py:406
  112.7 9.2 %collective-permute-start.6 = (f32[2,14,8,128]{3,2,1,0:T(8,128)S(1)}, f32[2,14,8,128]{3,2,1,0:T(8,128)S(1)}, u32[]{:S(2)}, u32[]{:S(2)}) collective-permute-start(f32[2,14,8,128]{3,2,1,0:T(8,128)S(1)} %get-tuple-element.39), channel_id=1, source_target_pairs={{8,16},{24,32},{40,48},{56,64},{72,80},{88,96},{104,112},{120,128}... | collective-permute-start | bytes 344072 | tf_op jit(solution)/shard_map/ppermute | solution.py:405
  115.2 6.7 %collective-permute-start.7 = (f32[2,14,8,128]{3,2,1,0:T(8,128)S(1)}, f32[2,14,8,128]{3,2,1,0:T(8,128)S(1)}, u32[]{:S(2)}, u32[]{:S(2)}) collective-permute-start(f32[2,14,8,128]{3,2,1,0:T(8,128)S(1)} %get-tuple-element.40), channel_id=1, source_target_pairs={{0,8},{8,0},{16,24},{24,16},{32,40},{40,32},{48,56},{56,48},{64,72... | collective-permute-start | bytes 344072 | tf_op jit(solution)/shard_map/ppermute | solution.py:406
  134.5 6.2 %collective-permute-start.8 = (f32[2,3,40,128]{3,2,1,0:T(8,128)S(1)}, f32[2,3,40,128]{3,2,1,0:T(8,128)S(1)}, u32[]{:S(2)}, u32[]{:S(2)}) collective-permute-start(f32[2,3,40,128]{3,2,1,0:T(8,128)S(1)} %get-tuple-element.42), channel_id=1, source_target_pairs={{1,2},{3,4},{5,6},{2,1},{4,3},{6,5},{9,10},{11,12},{13,14},{10,9},... | collective-permute-start | bytes 368648 | tf_op jit(solution)/shard_map/ppermute | solution.py:405
  136.4 4.3 %collective-permute-start.9 = (f32[2,3,40,128]{3,2,1,0:T(8,128)S(1)}, f32[2,3,40,128]{3,2,1,0:T(8,128)S(1)}, u32[]{:S(2)}, u32[]{:S(2)}) collective-permute-start(f32[2,3,40,128]{3,2,1,0:T(8,128)S(1)} %get-tuple-element.43), channel_id=1, source_target_pairs={{0,1},{1,0},{2,3},{3,2},{4,5},{5,4},{6,7},{7,6},{8,9},{9,8},{10,11... | collective-permute-start | bytes 368648 | tf_op jit(solution)/shard_map/ppermute | solution.py:406
  141.3 8.3 %collective-permute-start.10 = (f32[2,8,8,128]{3,2,1,0:T(8,128)S(1)}, f32[2,8,8,128]{3,2,1,0:T(8,128)S(1)}, u32[]{:S(2)}, u32[]{:S(2)}) collective-permute-start(f32[2,8,8,128]{3,2,1,0:T(8,128)S(1)} %get-tuple-element.45), channel_id=1, source_target_pairs={{8,16},{24,32},{40,48},{56,64},{72,80},{88,96},{104,112},{120,128}... | collective-permute-start | bytes 196616 | tf_op jit(solution)/shard_map/ppermute | solution.py:405
  145.1 4.5 %collective-permute-start.11 = (f32[2,8,8,128]{3,2,1,0:T(8,128)S(1)}, f32[2,8,8,128]{3,2,1,0:T(8,128)S(1)}, u32[]{:S(2)}, u32[]{:S(2)}) collective-permute-start(f32[2,8,8,128]{3,2,1,0:T(8,128)S(1)} %get-tuple-element.46), channel_id=1, source_target_pairs={{0,8},{8,0},{16,24},{24,16},{32,40},{40,32},{48,56},{56,48},{64,72... | collective-permute-start | bytes 196616 | tf_op jit(solution)/shard_map/ppermute | solution.py:406
  150.4 7.3 %collective-permute-start.14 = (f32[8,32,128]{2,1,0:T(8,128)S(1)}, f32[8,32,128]{2,1,0:T(8,128)S(1)}, u32[]{:S(2)}, u32[]{:S(2)}) collective-permute-start(f32[8,32,128]{2,1,0:T(8,128)S(1)} %get-tuple-element.47.refs_0_), channel_id=1, source_target_pairs={{0,8},{8,16},{16,24},{24,0},{1,9},{9,17},{17,25},{25,1},{2,10},{10... | collective-permute-start | bytes 393224 | tf_op jit(solution)/shard_map/ppermute | solution.py:411
  150.5 7.2 %collective-permute-start.13 = (f32[8,32,128]{2,1,0:T(8,128)S(1)}, f32[8,32,128]{2,1,0:T(8,128)S(1)}, u32[]{:S(2)}, u32[]{:S(2)}) collective-permute-start(f32[8,32,128]{2,1,0:T(8,128)S(1)} %get-tuple-element.48.refs_1_), channel_id=1, source_target_pairs={{0,24},{8,0},{16,8},{24,16},{1,25},{9,1},{17,9},{25,17},{2,26},{10... | collective-permute-start | bytes 393224 | tf_op jit(solution)/shard_map/ppermute | solution.py:411
  153.7 7.2 %collective-permute-start.12 = (f32[8,32,128]{2,1,0:T(8,128)S(1)}, f32[8,32,128]{2,1,0:T(8,128)S(1)}, u32[]{:S(2)}, u32[]{:S(2)}) collective-permute-start(f32[8,32,128]{2,1,0:T(8,128)S(1)} %get-tuple-element.47.refs_0_), channel_id=1, source_target_pairs={{0,24},{8,0},{16,8},{24,16},{1,25},{9,1},{17,9},{25,17},{2,26},{10... | collective-permute-start | bytes 393224 | tf_op jit(solution)/shard_map/ppermute | solution.py:411
  153.8 7.2 %collective-permute-start.17 = (f32[8,32,128]{2,1,0:T(8,128)S(1)}, f32[8,32,128]{2,1,0:T(8,128)S(1)}, u32[]{:S(2)}, u32[]{:S(2)}) collective-permute-start(f32[8,32,128]{2,1,0:T(8,128)S(1)} %get-tuple-element.48.refs_1_), channel_id=1, source_target_pairs={{0,8},{8,16},{16,24},{24,0},{1,9},{9,17},{17,25},{25,1},{2,10},{10... | collective-permute-start | bytes 393224 | tf_op jit(solution)/shard_map/ppermute | solution.py:411
  157.7 6.2 %collective-permute-start.15 = (f32[8,32,128]{2,1,0:T(8,128)S(1)}, f32[8,32,128]{2,1,0:T(8,128)S(1)}, u32[]{:S(2)}, u32[]{:S(2)}) collective-permute-start(f32[8,32,128]{2,1,0:T(8,128)S(1)} %collective-permute-done.14.refs_6_), channel_id=1, source_target_pairs={{0,8},{8,16},{16,24},{24,0},{1,9},{9,17},{17,25},{25,1},{2,10},{10... | collective-permute-start | bytes 393224 | tf_op jit(solution)/shard_map/ppermute | solution.py:411
  157.7 6.2 %collective-permute-start.16 = (f32[8,32,128]{2,1,0:T(8,128)S(1)}, f32[8,32,128]{2,1,0:T(8,128)S(1)}, u32[]{:S(2)}, u32[]{:S(2)}) collective-permute-start(f32[8,32,128]{2,1,0:T(8,128)S(1)} %collective-permute-done.13.refs_3_), channel_id=1, source_target_pairs={{0,24},{8,0},{16,8},{24,16},{1,25},{9,1},{17,9},{25,17},{2,26},{10... | collective-permute-start | bytes 393224 | tf_op jit(solution)/shard_map/ppermute | solution.py:411

commit v9 on v8

--- a/solution.py
+++ b/solution.py
@@ -105,7 +105,8 @@
     )(shift, target, views)
 
 
-def unpack_kernel(peers, cap, slots, in_ref, out_ref, placed, list_v, idx_v, idx_s, sem):
+def unpack_kernel(peers, cap, slots, id_ref, in_ref, *refs):
+    outs, (placed, list_v, idx_v, idx_s, sem) = refs[:-5], refs[-5:]
     rows_per = cap + 1
     for p in range(peers):
         list_v[p : p + 1, :] = in_ref[p * rows_per + cap]
@@ -124,13 +125,16 @@
         return c
 
     lax.fori_loop(0, peers, per_peer, 0)
-    out_ref[...] = placed[0:slots, :]
-
-
-def unpack(arrived, peers, cap, slots):
+    views, size = len(outs), slots // len(outs)
+    for d, out in enumerate(outs):
+        base = pl.multiple_of(lax.rem(id_ref[0] + d, views) * size, size)
+        out[...] = placed[pl.ds(base, size), :]
+
+
+def unpack(ids, arrived, peers, cap, slots, views):
     return call(
-        functools.partial(unpack_kernel, peers, cap, slots), "unpack", [f32(slots, BRICK)],
-        (arrived,), 0,
+        functools.partial(unpack_kernel, peers, cap, slots), "unpack",
+        [f32(slots // views, BRICK)] * views, (ids, arrived),
         scratch=[
             pltpu.VMEM((slots + SPARE, BRICK), jnp.float32),
             pltpu.VMEM((peers, BRICK), jnp.float32),
@@ -138,7 +142,7 @@
             pltpu.SMEM((peers, BRICK), jnp.int32),
             pltpu.SemaphoreType.DMA,
         ],
-    )[0]
+    )
 
 
 def vmem():
@@ -210,21 +214,18 @@
     return total
 
 
-def part_kernel(id_ref, est, outer, inner, out_ref, send_in, send_out, wide):
+def part_kernel(id_ref, est, edge, out_ref, send_in, send_out, wide):
     x_cells, y_cells, _ = est.shape
     part = out_ref.shape[2] - 2 * TILE
-    odd = id_ref[2]
     start = pl.multiple_of(id_ref[0] * part, part)
     far = TILE + y_cells
-    at_in = pl.ds(pl.multiple_of((1 - odd) * far, TILE), TILE)
-    at_out = pl.ds(pl.multiple_of(odd * far, TILE), TILE)
 
     def body(x, carry):
         for c in range(2):
             lanes = slice(c * BRICK, (c + 1) * BRICK)
             wide[c, TILE:far, :] = est[x, :, lanes]
-            wide[c, at_in, :] = inner[x, :, lanes]
-            wide[c, at_out, :] = outer[x, :, lanes]
+            wide[c, 0:TILE, :] = edge[x, :, lanes]
+            wide[c, far : far + TILE, :] = edge[x, :, lanes]
             out_ref[c, x] = wide[c, pl.ds(start, part + 2 * TILE), :]
         return carry
 
@@ -284,21 +285,105 @@
     )[0]
 
 
-def backward_kernel(w_ref, id_ref, below, obs, out_ref, send_in, send_out, wide, partial):
-    views, _, x_cells, part, _ = obs.shape
-    layers_out, count = out_ref.shape[1], send_in.shape[1]
+def blur_x_tile(est, at, wx, out, c, x_cells, rows):
+    layers = [est[c, i, at, :] for i in range(x_cells + 2 * HALO)]
+    for x in range(x_cells):
+        out[c, x, rows, :] = weigh(layers[x : x + TAPS], wx)
+
+
+def middle_kernel(w_ref, est, total, out_ref, part_ref, fresh):
+    views, _, x_cells, part, _ = out_ref.shape
+    tall = part_ref.shape[3]
+    rows = slice(TILE, TILE + tall)
+    for c in range(2):
+        for i in range(x_cells + 2 * HALO):
+            fresh[c, i] = est[c, i, rows, :] * total[c, i, rows, :] / views
+
+    def per_view(u, carry):
+        wx, wy, wz = (taps_of(w_ref, u, dim, False) for dim in range(3))
+
+        def per_tile(t, carry):
+            at = pl.ds(pl.multiple_of(t * TILE, TILE), TILE)
+            for c in range(2):
+                blur_x_tile(fresh, at, wx, part_ref.at[u], c, x_cells, at)
+            return carry
+
+        lax.fori_loop(0, tall // TILE, per_tile, 0)
+
+        def per_layer(x, carry):
+            rows = [y_rows(part_ref, (u, c, x), wy, part) for c in range(2)]
+            out_ref[u, 0, x], out_ref[u, 1, x] = blur_z(*rows, wz)
+            return carry
+
+        lax.fori_loop(0, x_cells, per_layer, 0)
+        return carry
+
+    lax.fori_loop(0, views, per_view, 0)
+
+
+def middle(w, est, total, views, x_cells):
+    tall = est.shape[2] - 2 * TILE
+    return call(
+        middle_kernel, "middle",
+        [f32(views, 2, x_cells, tall - TILE, BRICK), f32(views, 2, x_cells, tall, BRICK)],
+        (w, est, total), scratch=[pltpu.VMEM((2, x_cells + 2 * HALO, tall, BRICK), jnp.float32)],
+    )
+
+
+def ends_kernel(w_ref, est, mid, part_ref, out_ref, strip):
+    views, _, x_cells, part, _ = out_ref.shape
+    tall = part_ref.shape[3]
+    sides = ((0, 0, 0, TILE, 0), (tall + TILE, TILE, tall - TILE, 0, part - TILE))
+
+    def per_view(u, carry):
+        wx, wy, wz = (taps_of(w_ref, u, dim, False) for dim in range(3))
+        for s, (at, here, kept, there, to) in enumerate(sides):
+            for c in range(2):
+                blur_x_tile(est, slice(at, at + TILE), wx, strip.at[s], c, x_cells, slice(here, here + TILE))
+
+        def per_layer(x, carry):
+            for s, (at, here, kept, there, to) in enumerate(sides):
+                for c in range(2):
+                    strip[s, c, x, there : there + TILE, :] = part_ref[u, c, x, kept : kept + TILE, :]
+                rows = blur_z(*(y_rows(strip, (s, c, x), wy, TILE) for c in range(2)), wz)
+                for c in range(2):
+                    out_ref[u, c, x, to : to + TILE, :] = rows[c]
+            for c in range(2):
+                out_ref[u, c, x, TILE : part - TILE, :] = mid[u, c, x]
+            return carry
+
+        lax.fori_loop(0, x_cells, per_layer, 0)
+        return carry
+
+    lax.fori_loop(0, views, per_view, 0)
+
+
+def ends(w, est, mid, partial):
+    views, _, x, tall, _ = partial.shape
+    return call(
+        ends_kernel, "ends", [f32(views, 2, x, tall + TILE, BRICK)], (w, est, mid, partial),
+        scratch=[pltpu.VMEM((2, 2, x, 2 * TILE, BRICK), jnp.float32)],
+    )[0]
+
+
+def backward_kernel(views, rels, add, w_ref, id_ref, below, *refs):
+    observed, refs = refs[: len(rels)], refs[len(rels) :]
+    before, refs = (refs[0], refs[1:]) if add else (None, refs)
+    out_ref, *sends = refs[:-2]
+    wide, partial = refs[-2:]
+    x_cells, part = below.shape[2:4]
+    layers_out = out_ref.shape[1]
     zeros = jnp.zeros((TILE, BRICK), jnp.float32)
     for c in range(2):
         for x in range(x_cells):
             wide[c, x, 0:TILE, :] = zeros
             wide[c, x, TILE + part : 2 * TILE + part, :] = zeros
-    out_ref[...] = jnp.zeros_like(out_ref)
-
-    def per_view(u, carry):
+    for d, obs in zip(rels, observed):
+        u = lax.rem(id_ref[0] + d, views)
         wx, wy, wz = (taps_of(w_ref, u, dim, True) for dim in range(3))
 
-        def per_layer(x, carry):
-            rows = blur_z(*(obs[u, c, x] / below[u, c, x] for c in range(2)), wz)
+        def per_layer(x, carry, u=u, obs=obs, wy=wy, wz=wz):
+            rows = blur_z(*(obs[c, x] / below[u, c, x] for c in range(2)), wz)
             for c in range(2):
                 wide[c, x, TILE : TILE + part, :] = rows[c]
                 partial[c, x] = y_rows(wide, (c, x), wy, part + 2 * TRIM)
@@ -306,32 +391,33 @@
 
         lax.fori_loop(0, x_cells, per_layer, 0)
 
-        def per_tile(t, carry):
+        def per_tile(t, carry, wx=wx, source=before):
             at = pl.ds(pl.multiple_of(t * TILE, TILE), TILE)
             for c in range(2):
                 layers = [partial[c, x, at, :] for x in range(x_cells)]
                 for i in range(layers_out):
-                    out_ref[c, i, at, :] += spread(layers, wx, i - HALO)
+                    value = spread(layers, wx, i - HALO)
+                    out_ref[c, i, at, :] = value if source is None else value + source[c, i, at, :]
             return carry
 
         lax.fori_loop(0, (part + 2 * TRIM) // TILE, per_tile, 0)
-        return carry
-
-    lax.fori_loop(0, views, per_view, 0)
+        before = out_ref
     odd = id_ref[1]
-    base = layers_out - count
-    for c in range(2):
-        for i in range(count):
-            send_in[c, i] = out_ref[c, (1 - odd) * base + i]
-            send_out[c, i] = out_ref[c, odd * base + i]
-
-
-def backward(w, ids, below, obs, count):
-    _, _, x, part, _ = obs.shape
+    for slot, send in enumerate(sends):
+        base = layers_out - send.shape[1]
+        for c in range(2):
+            for i in range(send.shape[1]):
+                send[c, i] = out_ref[c, (odd if slot else 1 - odd) * base + i]
+
+
+def backward(w, ids, below, rels, observed, before, count):
+    views, _, x, part, _ = below.shape
     rows = part + 2 * TRIM
-    outs = [f32(2, x + 2 * HALO, rows, BRICK)] + [f32(2, count, rows, BRICK)] * 2
+    outs = [f32(2, x + 2 * HALO, rows, BRICK)] + [f32(2, count, rows, BRICK)] * (2 if count else 0)
+    given = () if before is None else (before,)
     return call(
-        backward_kernel, "backward", outs, (w, ids, below, obs), 2,
+        functools.partial(backward_kernel, views, rels, before is not None), "backward", outs,
+        (w, ids, below, *observed, *given), 2,
         scratch=[
             pltpu.VMEM((2, x, part + 2 * TILE, BRICK), jnp.float32),
             pltpu.VMEM((2, x, rows, BRICK), jnp.float32),
@@ -423,44 +509,48 @@
     part = y_cells // view_count
     all_cols = y_cells * block_count
     geo = (peer_count, capacity, x_cells, y_cells, brick_cols, row_count, all_cols, view_count)
-    block, row, place = (lax.axis_index(name) for name in ("blocks", "rows", "views"))
-    odd = block % 2
-    est_out, est_in = swap(*(
-        lax.dynamic_slice_in_dim(estimate, at * (y_cells - TILE), TILE, 1) for at in (1 - odd, odd)
-    ), "blocks")
+    row, place = lax.axis_index("rows"), lax.axis_index("views")
+    chain = [(block * view_count - 1, block * view_count) for block in range(1, block_count)]
+    edge_at = jnp.where(place == 0, 0, y_cells - TILE)
+    edge = lax.ppermute(
+        lax.dynamic_slice_in_dim(estimate, edge_at, TILE, 1),
+        ("blocks", "views"), chain + [(j, i) for i, j in chain],
+    )
     outgoing = pack(shifts, target[0].transpose(0, 2, 1), views_data[0], geo)
-    outgoing, est_out, est_in = lax.optimization_barrier((outgoing, est_out, est_in))
+    outgoing, edge = lax.optimization_barrier((outgoing, edge))
     arrived = lax.all_to_all(
         outgoing.reshape(peer_count, capacity + 1, 1, BRICK),
         ("blocks", "rows"), split_axis=0, concat_axis=0, tiled=True,
     ).reshape(peer_count * (capacity + 1), 1, BRICK)
     taps = lax.all_gather(psf_taps, "views", axis=0, tiled=True)
     w = (taps / jnp.sum(taps, axis=2, keepdims=True)).reshape(-1)
-    ids = jnp.stack([place, row % 2, odd]).astype(jnp.int32)
+    ids = jnp.stack([place, row % 2]).astype(jnp.int32)
     halo = f32(2, HALO, part + 2 * TILE, BRICK)
     own, *sent = call(
         part_kernel, "part", [f32(2, x_cells, part + 2 * TILE, BRICK), halo, halo],
-        (ids, estimate, est_out, est_in), scratch=[pltpu.VMEM((2, y_cells + 2 * TILE, BRICK), jnp.float32)],
+        (ids, estimate, edge),
+        scratch=[pltpu.VMEM((2, y_cells + 2 * TILE, BRICK), jnp.float32)],
     )
     wide = [f32(2, x_cells + 2 * HALO, part + 2 * TRIM, BRICK)]
     est = call(extend_kernel, "extend", wide, (ids, own, *swap(*sent, "rows")))[0]
     below = forward(w, est, view_count, x_cells)
     arrived, below = lax.optimization_barrier((arrived, below))
-    moved = unpack(arrived, peer_count, capacity, brick_count)
-    obs = lax.all_to_all(
-        moved.reshape(view_count, brick_count // view_count, BRICK),
-        "views", split_axis=0, concat_axis=0, tiled=True,
-    ).reshape(view_count, brick_cols, x_cells, part, BRICK)
-    for iteration in range(ITERS):
-        if iteration > 0:
-            below = forward(w, est, view_count, x_cells)
-        more = iteration < ITERS - 1
-        total, *sent = backward(w, ids, below, obs, (2 if more else 1) * HALO)
-        layers = x_cells + (2 * HALO if more else 0)
-        total, *sent = merge(ids, total, *swap(*sent, "rows"), layers)
-        args = (ids, total, *swap(*sent, ("blocks", "views")), est)
-        if more:
-            est = call(functools.partial(update_kernel, view_count), "update", wide, args)[0]
+    moved = unpack(ids, arrived, peer_count, capacity, brick_count, view_count)
+    moved = [m.reshape(brick_cols, x_cells, part, BRICK) for m in moved]
+    behind, ahead = turn(moved[1], 1, view_count), turn(moved[3], -1, view_count)
+    across = turn(moved[2], 2, view_count)
+    total = backward(w, ids, below, (0,), moved[:1], None, 0)[0]
+    total = backward(w, ids, below, (3, 1), (behind, ahead), total, 0)[0]
+    total, *sent = backward(w, ids, below, (2,), (across,), total, 2 * HALO)
+    total, *sent = merge(ids, total, *swap(*sent, "rows"), x_cells + 2 * HALO)
+    mid, partial = middle(w, est, total, view_count, x_cells)
+    args = (ids, total, *swap(*sent, ("blocks", "views")), est)
+    est = call(functools.partial(update_kernel, view_count), "update", wide, args)[0]
+    below = ends(w, est, mid, partial)
+    observed = (moved[0], ahead, across, behind)
+    total, *sent = backward(w, ids, below, (0, 1, 2, 3), observed, None, HALO)
+    total, *sent = merge(ids, total, *swap(*sent, "rows"), x_cells)
+    args = (ids, total, *swap(*sent, ("blocks", "views")), est)
     own = call(
         functools.partial(finish_kernel, view_count), "finish",
         [f32(x_cells, part, BRICK)] * 2, args,

time: 166 us -> 163 us (0.982)
  blocking collectives: 30.6 us -> 10.4 us
  starting transfers between devices: 40.9 us -> 48.7 us
  waiting for transfers between devices: 48.2 us -> 54.2 us
  Pallas kernels: 41 us -> 46.3 us
  local copies, waits for them, and re-layouts: 3.69 us -> 0.95 us
    all_to_all x1 -> x0, blocking collectives: 19.3 us -> none  [per_device(): lax.all_to_all(moved.reshape(view_count, brick_count // view_count, BRICK...]
    ppermute x6 -> x9, waiting for transfers between devices: 4.86 us -> 13.1 us  [turn(): lax.ppermute(value, 'views', [(i, (i + step) % count) for i in range(coun...]
    ppermute x6 -> x5, waiting for transfers between devices: 21 us -> 15.4 us  [swap(): outer = lax.ppermute(outer, axes, links + [(j, i) for i, j in links])]
    pallas_call x12 -> x15, Pallas kernels: 35 us -> 40.3 us  [call(): pl.pallas_call(kernel, out_shape=outs, in_specs=[smem()] * scalars + [vme...]
    ppermute x0 -> x1, starting transfers between devices: none -> 4.46 us  [per_device(): lax.ppermute(lax.dynamic_slice_in_dim(estimate, edge_at, TILE, 1), ('bloc...]
    ppermute x6 -> x9, starting transfers between devices: 8.56 us -> 12.3 us  [turn(): lax.ppermute(value, 'views', [(i, (i + step) % count) for i in range(coun...]
    ppermute x6 -> x5, starting transfers between devices: 17.6 us -> 14.3 us  [swap(): outer = lax.ppermute(outer, axes, links + [(j, i) for i, j in links])]
    all_to_all x1, starting transfers between devices: 9.47 us -> 12.3 us  [per_device(): lax.all_to_all(outgoing.reshape(peer_count, capacity + 1, 1, BRICK), ('bl...]
  transfers between devices with their start and end apart: 19 -> 21, of which waited for: 8 -> 12; matrix products, arithmetic and copies ran while one was open for 0% -> 0% of each run, Pallas kernels for 8% -> 14%
where the time goes in v9:
time: 163 us; the launch traced here: 162 us
  waiting for transfers between devices  54.2 us (33%)
  starting transfers between devices  48.7 us (30%)
  Pallas kernels  46.3 us (28%)
  blocking collectives  10.4 us (6%)
    pallas_call x15, Pallas kernels, call(): pl.pallas_call(kernel, out_shape=outs, in_specs=[smem()] * scalars + [vme...  40.3 us
    all_to_all x1, waiting for transfers between devices, per_device(): lax.all_to_all(outgoing.reshape(peer_count, capacity + 1, 1, BRICK), ('bl...  25.1 us
    ppermute x5, waiting for transfers between devices, swap(): outer = lax.ppermute(outer, axes, links + [(j, i) for i, j in links])  15.4 us
    ppermute x5, starting transfers between devices, swap(): outer = lax.ppermute(outer, axes, links + [(j, i) for i, j in links])  14.3 us
    ppermute x9, waiting for transfers between devices, turn(): lax.ppermute(value, 'views', [(i, (i + step) % count) for i in range(coun...  13.1 us
    all_to_all x1, starting transfers between devices, per_device(): lax.all_to_all(outgoing.reshape(peer_count, capacity + 1, 1, BRICK), ('bl...  12.3 us
    ppermute x9, starting transfers between devices, turn(): lax.ppermute(value, 'views', [(i, (i + step) % count) for i in range(coun...  12.3 us
    all_gather x1, blocking collectives, per_device(): taps = lax.all_gather(psf_taps, 'views', axis=0, tiled=True)  10.4 us
  transfers between devices with their start and end apart: 21, of which 12 were waited for; matrix products, arithmetic and copies ran while one was open for 0% of the time, Pallas kernels for 14%

profile of v9, /device:TPU:34, one launch (start us, length us, event | category | flops | bytes accessed | tf_op | source)
XLA Modules:
  0.0 161.5 jit_solution(10952647408645300907)
XLA Ops:
  0.8 4.5 %collective-permute-start = (f32[8,8,256]{2,1,0:T(8,128)S(1)}, f32[8,8,256]{2,1,0:T(8,128)S(1)}, u32[]{:S(2)}, u32[]{:S(2)}) collective-permute-start(f32[8,8,256]{2,1,0:T(8,128)S(1)} %constant_dynamic-slice_fusion), channel_id=1, source_target_pairs={{24,32},{56,64},{88,96},{120,128},{152,160},{184,192},{216,224},{3... | collective-permute-start | bytes 196616 | tf_op jit(solution)/shard_map/ppermute | solution.py:515
  6.0 6.0 %pack.1 = f32[4160,1,128]{2,1,0:T(1,128)} custom-call(s32[1]{0:T(128)S(6)} %copy.9.shift_ref, s32[8,2,128]{2,1,0:T(2,128)} %bitcast.20, f32[8,128,256]{2,1,0:T(8,128)} %bitcast.19), custom_call_target="tpu_custom_call" | custom-call | tf_op jit(solution)/shard_map/pack/pallas_call | solution.py:89
  12.0 12.3 %all-to-all-start = ((f32[64,65,1,128]{3,2,1,0:T(1,128)}), f32[64,65,1,128]{3,2,1,0:T(1,128)}, u32[]{:S(2)}, u32[]{:S(2)}) async-start(f32[64,65,1,128]{3,2,1,0:T(1,128)} %bitcast.18), calls=%async_computation | async-start | bytes 4259840 | tf_op jit(solution)/shard_map/all_to_all | solution.py:521
  24.3 10.4 %all_gather.3 = f32[4,3,7]{2,1,0:T(4,128)S(1)} all-gather(f32[1,3,7]{2,1,0:T(4,128)S(1)} %copy.8), channel_id=1, replica_groups=mesh['blocks'=8,'views'=4,'rows'=8] {'views'}, dimensions={0}, use_global_device_ids=true | all-gather | bytes 420 | tf_op jit(solution)/shard_map/all_gather | solution.py:525
  35.6 1.9 %collective-permute-start.1 = (f32[2,3,48,128]{3,2,1,0:T(8,128)S(1)}, f32[2,3,48,128]{3,2,1,0:T(8,128)S(1)}, u32[]{:S(2)}, u32[]{:S(2)}) collective-permute-start(f32[2,3,48,128]{3,2,1,0:T(8,128)S(1)} %get-tuple-element.35), channel_id=1, source_target_pairs={{1,2},{3,4},{5,6},{2,1},{4,3},{6,5},{9,10},{11,12},{13,14},{10,9},... | collective-permute-start | bytes 442376 | tf_op jit(solution)/shard_map/ppermute | solution.py:491
  37.5 1.7 %collective-permute-start.2 = (f32[2,3,48,128]{3,2,1,0:T(8,128)S(1)}, f32[2,3,48,128]{3,2,1,0:T(8,128)S(1)}, u32[]{:S(2)}, u32[]{:S(2)}) collective-permute-start(f32[2,3,48,128]{3,2,1,0:T(8,128)S(1)} %get-tuple-element.36), channel_id=1, source_target_pairs={{0,1},{1,0},{2,3},{3,2},{4,5},{5,4},{6,7},{7,6},{8,9},{9,8},{10,11... | collective-permute-start | bytes 442376 | tf_op jit(solution)/shard_map/ppermute | solution.py:492
  39.3 4.8 %collective-permute-done.1.outer = f32[2,3,48,128]{3,2,1,0:T(8,128)S(1)} collective-permute-done((f32[2,3,48,128]{3,2,1,0:T(8,128)S(1)}, f32[2,3,48,128]{3,2,1,0:T(8,128)S(1)}, u32[]{:S(2)}, u32[]{:S(2)}) %collective-permute-start.1) | collective-permute-done | bytes 147488 | tf_op jit(solution)/shard_map/ppermute | solution.py:491
  44.7 5.5 %forward.1.below = f32[4,2,8,32,128]{4,3,2,1,0:T(8,128)S(1)} custom-call(f32[84]{0:T(128)S(1)} %reshape.22.w_ref, f32[2,14,40,128]{3,2,1,0:T(8,128)S(1)} %extend.1.est), custom_call_target="tpu_custom_call" | custom-call | flops 1000 | bytes 1000 | tf_op jit(solution)/shard_map/forward/pallas_call | solution.py:161
  50.2 25.1 %all-to-all-done = f32[64,65,1,128]{3,2,1,0:T(1,128)} async-done(((f32[64,65,1,128]{3,2,1,0:T(1,128)}), f32[64,65,1,128]{3,2,1,0:T(1,128)}, u32[]{:S(2)}, u32[]{:S(2)}) %all-to-all-start) | async-done | bytes 2129952 | tf_op jit(solution)/shard_map/all_to_all | solution.py:521
  75.3 6.4 %unpack.1 = (f32[512,128]{1,0:T(8,128)S(1)}, f32[512,128]{1,0:T(8,128)S(1)}, f32[512,128]{1,0:T(8,128)S(1)}, f32[512,128]{1,0:T(8,128)S(1)}) custom-call(s32[2]{0:T(128)S(1)} %pad_add_fusion.id_ref, f32[4160,1,128]{2,1,0:T(1,128)} %bitcast.6.in_ref), custom_call_target="tpu_custom_call" | custom-call | flops 1000 | bytes 1000 | tf_op jit(solution)/shard_map/unpack/pallas_call | solution.py:161
  81.8 3.2 %collective-permute-start.5 = (f32[2,8,32,128]{3,2,1,0:T(8,128)S(1)}, f32[2,8,32,128]{3,2,1,0:T(8,128)S(1)}, u32[]{:S(2)}, u32[]{:S(2)}) collective-permute-start(f32[2,8,32,128]{3,2,1,0:T(8,128)S(1)} %bitcast.16), channel_id=1, source_target_pairs={{0,24},{8,0},{16,8},{24,16},{1,25},{9,1},{17,9},{25,17},{2,26},{10... | collective-permute-start | bytes 786440 | tf_op jit(solution)/shard_map/ppermute | solution.py:497
  85.0 2.0 %backward.4.refs_2_ = f32[2,14,40,128]{3,2,1,0:T(8,128)S(1)} custom-call(f32[84]{0:T(128)S(1)} %reshape.22.w_ref, s32[2]{0:T(128)S(1)} %pad_add_fusion.id_ref, f32[4,2,8,32,128]{4,3,2,1,0:T(8,128)S(1)} %forward.1.below, f32[2,8,32,128]{3,2,1,0:T(8,128)S(1)} %bitcast.13), custom_call_target="tpu_custom_call" | custom-call | flops 1000 | bytes 1000 | tf_op jit(solution)/shard_map/backward/pallas_call | solution.py:161
  87.0 9.6 %collective-permute-done.4.refs_0_.refs_3_ = f32[2,8,32,128]{3,2,1,0:T(8,128)S(1)} collective-permute-done((f32[2,8,32,128]{3,2,1,0:T(8,128)S(1)}, f32[2,8,32,128]{3,2,1,0:T(8,128)S(1)}, u32[]{:S(2)}, u32[]{:S(2)}) %collective-permute-start.4) | collective-permute-done | bytes 262176 | tf_op jit(solution)/shard_map/ppermute | solution.py:497
  96.6 3.4 %backward.5.refs_1_ = f32[2,14,40,128]{3,2,1,0:T(8,128)S(1)} custom-call(f32[84]{0:T(128)S(1)} %reshape.22.w_ref, s32[2]{0:T(128)S(1)} %pad_add_fusion.id_ref, f32[4,2,8,32,128]{4,3,2,1,0:T(8,128)S(1)} %forward.1.below, f32[2,8,32,128]{3,2,1,0:T(8,128)S(1)} %collective-permute-done.4.refs_0_.refs_3_, f32[2,8,32,128]{3,2,1,0:T(8,128)S(1)} %collective-permute-done.5.refs_1_, ...), custom_call_target="tpu_custom_call" | custom-call | flops 1000 | bytes 1000 | tf_op jit(solution)/shard_map/backward/pallas_call | solution.py:161
  100.1 2.0 %backward.6 = (f32[2,14,40,128]{3,2,1,0:T(8,128)S(1)}, f32[2,6,40,128]{3,2,1,0:T(8,128)S(1)}, f32[2,6,40,128]{3,2,1,0:T(8,128)S(1)}) custom-call(f32[84]{0:T(128)S(1)} %reshape.22.w_ref, s32[2]{0:T(128)S(1)} %pad_add_fusion.id_ref, f32[4,2,8,32,128]{4,3,2,1,0:T(8,128)S(1)} %forward.1.below, f32[2,8,32,128]{3,2,1,0:T(8,128)S(1)} %collective-permute-done.3.refs_0_.refs_2_, ...), custom_call_target="tpu_custom_call" | custom-call | flops 1000 | bytes 1000 | tf_op jit(solution)/shard_map/backward/pallas_call | solution.py:161
  102.1 1.9 %collective-permute-start.6 = (f32[2,6,40,128]{3,2,1,0:T(8,128)S(1)}, f32[2,6,40,128]{3,2,1,0:T(8,128)S(1)}, u32[]{:S(2)}, u32[]{:S(2)}) collective-permute-start(f32[2,6,40,128]{3,2,1,0:T(8,128)S(1)} %get-tuple-element.44), channel_id=1, source_target_pairs={{1,2},{3,4},{5,6},{2,1},{4,3},{6,5},{9,10},{11,12},{13,14},{10,9},... | collective-permute-start | bytes 737288 | tf_op jit(solution)/shard_map/ppermute | solution.py:491
  104.1 1.7 %collective-permute-start.7 = (f32[2,6,40,128]{3,2,1,0:T(8,128)S(1)}, f32[2,6,40,128]{3,2,1,0:T(8,128)S(1)}, u32[]{:S(2)}, u32[]{:S(2)}) collective-permute-start(f32[2,6,40,128]{3,2,1,0:T(8,128)S(1)} %get-tuple-element.45), channel_id=1, source_target_pairs={{0,1},{1,0},{2,3},{3,2},{4,5},{5,4},{6,7},{7,6},{8,9},{9,8},{10,11... | collective-permute-start | bytes 737288 | tf_op jit(solution)/shard_map/ppermute | solution.py:492
  105.8 3.9 %collective-permute-done.6.outer = f32[2,6,40,128]{3,2,1,0:T(8,128)S(1)} collective-permute-done((f32[2,6,40,128]{3,2,1,0:T(8,128)S(1)}, f32[2,6,40,128]{3,2,1,0:T(8,128)S(1)}, u32[]{:S(2)}, u32[]{:S(2)}) %collective-permute-start.6) | collective-permute-done | bytes 245792 | tf_op jit(solution)/shard_map/ppermute | solution.py:491
  110.4 4.3 %collective-permute-start.8 = (f32[2,14,8,128]{3,2,1,0:T(8,128)S(1)}, f32[2,14,8,128]{3,2,1,0:T(8,128)S(1)}, u32[]{:S(2)}, u32[]{:S(2)}) collective-permute-start(f32[2,14,8,128]{3,2,1,0:T(8,128)S(1)} %get-tuple-element.47), channel_id=1, source_target_pairs={{8,16},{24,32},{40,48},{56,64},{72,80},{88,96},{104,112},{120,128}... | collective-permute-start | bytes 344072 | tf_op jit(solution)/shard_map/ppermute | solution.py:491
  114.8 4.4 %middle.1 = (f32[4,2,8,16,128]{4,3,2,1,0:T(8,128)S(1)}, f32[4,2,8,24,128]{4,3,2,1,0:T(8,128)S(1)}) custom-call(f32[84]{0:T(128)S(1)} %reshape.22.w_ref, f32[2,14,40,128]{3,2,1,0:T(8,128)S(1)} %extend.1.est, f32[2,14,40,128]{3,2,1,0:T(8,128)S(1)} %get-tuple-element.46.total), custom_call_target="tpu_custom_call" | custom-call | flops 1000 | bytes 1000 | tf_op jit(solution)/shard_map/middle/pallas_call | solution.py:161
  120.4 4.5 %ends.1.below = f32[4,2,8,32,128]{4,3,2,1,0:T(8,128)S(1)} custom-call(f32[84]{0:T(128)S(1)} %reshape.22.w_ref, f32[2,14,40,128]{3,2,1,0:T(8,128)S(1)} %update.1.est, f32[4,2,8,16,128]{4,3,2,1,0:T(8,128)S(1)} %get-tuple-element.49.mid, f32[4,2,8,24,128]{4,3,2,1,0:T(8,128)S(1)} %get-tuple-element.50.part_ref), custom_call_target="tpu_custom_call" | custom-call | flops 1000 | bytes 1000 | tf_op jit(solution)/shard_map/ends/pallas_call | solution.py:161
  125.0 6.3 %backward.7 = (f32[2,14,40,128]{3,2,1,0:T(8,128)S(1)}, f32[2,3,40,128]{3,2,1,0:T(8,128)S(1)}, f32[2,3,40,128]{3,2,1,0:T(8,128)S(1)}) custom-call(f32[84]{0:T(128)S(1)} %reshape.22.w_ref, s32[2]{0:T(128)S(1)} %pad_add_fusion.id_ref, f32[4,2,8,32,128]{4,3,2,1,0:T(8,128)S(1)} %ends.1.below, f32[2,8,32,128]{3,2,1,0:T(8,128)S(1)} %bitcast.14, ...), custom_call_target="tpu_custom_call" | custom-call | flops 1000 | bytes 1000 | tf_op jit(solution)/shard_map/backward/pallas_call | solution.py:161
  131.3 1.9 %collective-permute-start.10 = (f32[2,3,40,128]{3,2,1,0:T(8,128)S(1)}, f32[2,3,40,128]{3,2,1,0:T(8,128)S(1)}, u32[]{:S(2)}, u32[]{:S(2)}) collective-permute-start(f32[2,3,40,128]{3,2,1,0:T(8,128)S(1)} %get-tuple-element.52), channel_id=1, source_target_pairs={{1,2},{3,4},{5,6},{2,1},{4,3},{6,5},{9,10},{11,12},{13,14},{10,9},... | collective-permute-start | bytes 368648 | tf_op jit(solution)/shard_map/ppermute | solution.py:491
  133.2 1.8 %collective-permute-start.11 = (f32[2,3,40,128]{3,2,1,0:T(8,128)S(1)}, f32[2,3,40,128]{3,2,1,0:T(8,128)S(1)}, u32[]{:S(2)}, u32[]{:S(2)}) collective-permute-start(f32[2,3,40,128]{3,2,1,0:T(8,128)S(1)} %get-tuple-element.53), channel_id=1, source_target_pairs={{0,1},{1,0},{2,3},{3,2},{4,5},{5,4},{6,7},{7,6},{8,9},{9,8},{10,11... | collective-permute-start | bytes 368648 | tf_op jit(solution)/shard_map/ppermute | solution.py:492
  135.1 2.4 %collective-permute-done.10.outer = f32[2,3,40,128]{3,2,1,0:T(8,128)S(1)} collective-permute-done((f32[2,3,40,128]{3,2,1,0:T(8,128)S(1)}, f32[2,3,40,128]{3,2,1,0:T(8,128)S(1)}, u32[]{:S(2)}, u32[]{:S(2)}) %collective-permute-start.10) | collective-permute-done | bytes 122912 | tf_op jit(solution)/shard_map/ppermute | solution.py:491
  138.1 4.2 %collective-permute-start.12 = (f32[2,8,8,128]{3,2,1,0:T(8,128)S(1)}, f32[2,8,8,128]{3,2,1,0:T(8,128)S(1)}, u32[]{:S(2)}, u32[]{:S(2)}) collective-permute-start(f32[2,8,8,128]{3,2,1,0:T(8,128)S(1)} %get-tuple-element.55), channel_id=1, source_target_pairs={{8,16},{24,32},{40,48},{56,64},{72,80},{88,96},{104,112},{120,128}... | collective-permute-start | bytes 196616 | tf_op jit(solution)/shard_map/ppermute | solution.py:491
  142.4 4.0 %collective-permute-done.12.outer = f32[2,8,8,128]{3,2,1,0:T(8,128)S(1)} collective-permute-done((f32[2,8,8,128]{3,2,1,0:T(8,128)S(1)}, f32[2,8,8,128]{3,2,1,0:T(8,128)S(1)}, u32[]{:S(2)}, u32[]{:S(2)}) %collective-permute-start.12) | collective-permute-done | bytes 65568 | tf_op jit(solution)/shard_map/ppermute | solution.py:491
  147.6 3.2 %collective-permute-start.15 = (f32[8,32,128]{2,1,0:T(8,128)S(1)}, f32[8,32,128]{2,1,0:T(8,128)S(1)}, u32[]{:S(2)}, u32[]{:S(2)}) collective-permute-start(f32[8,32,128]{2,1,0:T(8,128)S(1)} %get-tuple-element.58.refs_1_), channel_id=1, source_target_pairs={{0,24},{8,0},{16,8},{24,16},{1,25},{9,1},{17,9},{25,17},{2,26},{10... | collective-permute-start | bytes 393224 | tf_op jit(solution)/shard_map/ppermute | solution.py:497
  150.8 1.2 collective-permute-start.14
  153.7 3.7 %collective-permute-start.18 = (f32[8,32,128]{2,1,0:T(8,128)S(1)}, f32[8,32,128]{2,1,0:T(8,128)S(1)}, u32[]{:S(2)}, u32[]{:S(2)}) collective-permute-start(f32[8,32,128]{2,1,0:T(8,128)S(1)} %collective-permute-done.15.refs_3_), channel_id=1, source_target_pairs={{0,24},{8,0},{16,8},{24,16},{1,25},{9,1},{17,9},{25,17},{2,26},{10... | collective-permute-start | bytes 393224 | tf_op jit(solution)/shard_map/ppermute | solution.py:497
  158.2 1.7 %collective-permute-done.17.refs_4_ = f32[8,32,128]{2,1,0:T(8,128)S(1)} collective-permute-done((f32[8,32,128]{2,1,0:T(8,128)S(1)}, f32[8,32,128]{2,1,0:T(8,128)S(1)}, u32[]{:S(2)}, u32[]{:S(2)}) %collective-permute-start.17) | collective-permute-done | bytes 131104 | tf_op jit(solution)/shard_map/ppermute | solution.py:497
  160.0 1.6 join.1
  (36 shorter events, 9.0 us)
Async XLA Ops:
  0.8 11.1 %collective-permute-start = (f32[8,8,256]{2,1,0:T(8,128)S(1)}, f32[8,8,256]{2,1,0:T(8,128)S(1)}, u32[]{:S(2)}, u32[]{:S(2)}) collective-permute-start(f32[8,8,256]{2,1,0:T(8,128)S(1)} %constant_dynamic-slice_fusion), channel_id=1, source_target_pairs={{24,32},{56,64},{88,96},{120,128},{152,160},{184,192},{216,224},{3... | collective-permute-start | bytes 196616 | tf_op jit(solution)/shard_map/ppermute | solution.py:515
  11.9 12.4 %copy-start.1 = (f32[1,3,7]{2,0,1:T(1,128)S(1)}, f32[1,3,7]{2,0,1:T(1,128)}, u32[]{:S(2)}) copy-start(f32[1,3,7]{2,0,1:T(1,128)} %param.8) | copy-start | bytes 256
  11.9 22.8 %copy-start = (f32[8,128,256]{2,1,0:T(8,128)S(1)}, f32[8,128,256]{2,1,0:T(8,128)}, u32[]{:S(2)}) copy-start(f32[8,128,256]{2,1,0:T(8,128)} %est.1) | copy-start | bytes 3145732
  12.0 63.4 %all-to-all-start = ((f32[64,65,1,128]{3,2,1,0:T(1,128)}), f32[64,65,1,128]{3,2,1,0:T(1,128)}, u32[]{:S(2)}, u32[]{:S(2)}) async-start(f32[64,65,1,128]{3,2,1,0:T(1,128)} %bitcast.18), calls=%async_computation | async-start | bytes 4259840 | tf_op jit(solution)/shard_map/all_to_all | solution.py:521
  35.6 8.5 %collective-permute-start.1 = (f32[2,3,48,128]{3,2,1,0:T(8,128)S(1)}, f32[2,3,48,128]{3,2,1,0:T(8,128)S(1)}, u32[]{:S(2)}, u32[]{:S(2)}) collective-permute-start(f32[2,3,48,128]{3,2,1,0:T(8,128)S(1)} %get-tuple-element.35), channel_id=1, source_target_pairs={{1,2},{3,4},{5,6},{2,1},{4,3},{6,5},{9,10},{11,12},{13,14},{10,9},... | collective-permute-start | bytes 442376 | tf_op jit(solution)/shard_map/ppermute | solution.py:491
  37.5 6.6 %collective-permute-start.2 = (f32[2,3,48,128]{3,2,1,0:T(8,128)S(1)}, f32[2,3,48,128]{3,2,1,0:T(8,128)S(1)}, u32[]{:S(2)}, u32[]{:S(2)}) collective-permute-start(f32[2,3,48,128]{3,2,1,0:T(8,128)S(1)} %get-tuple-element.36), channel_id=1, source_target_pairs={{0,1},{1,0},{2,3},{3,2},{4,5},{5,4},{6,7},{7,6},{8,9},{9,8},{10,11... | collective-permute-start | bytes 442376 | tf_op jit(solution)/shard_map/ppermute | solution.py:492
  81.7 14.9 %collective-permute-start.4 = (f32[2,8,32,128]{3,2,1,0:T(8,128)S(1)}, f32[2,8,32,128]{3,2,1,0:T(8,128)S(1)}, u32[]{:S(2)}, u32[]{:S(2)}) collective-permute-start(f32[2,8,32,128]{3,2,1,0:T(8,128)S(1)} %bitcast.17), channel_id=1, source_target_pairs={{0,8},{8,16},{16,24},{24,0},{1,9},{9,17},{17,25},{25,1},{2,10},{10... | collective-permute-start | bytes 786440 | tf_op jit(solution)/shard_map/ppermute | solution.py:497
  81.8 14.8 %collective-permute-start.5 = (f32[2,8,32,128]{3,2,1,0:T(8,128)S(1)}, f32[2,8,32,128]{3,2,1,0:T(8,128)S(1)}, u32[]{:S(2)}, u32[]{:S(2)}) collective-permute-start(f32[2,8,32,128]{3,2,1,0:T(8,128)S(1)} %bitcast.16), channel_id=1, source_target_pairs={{0,24},{8,0},{16,8},{24,16},{1,25},{9,1},{17,9},{25,17},{2,26},{10... | collective-permute-start | bytes 786440 | tf_op jit(solution)/shard_map/ppermute | solution.py:497
  85.0 15.1 %collective-permute-start.3 = (f32[2,8,32,128]{3,2,1,0:T(8,128)S(1)}, f32[2,8,32,128]{3,2,1,0:T(8,128)S(1)}, u32[]{:S(2)}, u32[]{:S(2)}) collective-permute-start(f32[2,8,32,128]{3,2,1,0:T(8,128)S(1)} %bitcast.15), channel_id=1, source_target_pairs={{0,16},{8,24},{16,0},{24,8},{1,17},{9,25},{17,1},{25,9},{2,18},{10... | collective-permute-start | bytes 786440 | tf_op jit(solution)/shard_map/ppermute | solution.py:497
  102.1 7.5 %collective-permute-start.6 = (f32[2,6,40,128]{3,2,1,0:T(8,128)S(1)}, f32[2,6,40,128]{3,2,1,0:T(8,128)S(1)}, u32[]{:S(2)}, u32[]{:S(2)}) collective-permute-start(f32[2,6,40,128]{3,2,1,0:T(8,128)S(1)} %get-tuple-element.44), channel_id=1, source_target_pairs={{1,2},{3,4},{5,6},{2,1},{4,3},{6,5},{9,10},{11,12},{13,14},{10,9},... | collective-permute-start | bytes 737288 | tf_op jit(solution)/shard_map/ppermute | solution.py:491
  104.1 5.6 %collective-permute-start.7 = (f32[2,6,40,128]{3,2,1,0:T(8,128)S(1)}, f32[2,6,40,128]{3,2,1,0:T(8,128)S(1)}, u32[]{:S(2)}, u32[]{:S(2)}) collective-permute-start(f32[2,6,40,128]{3,2,1,0:T(8,128)S(1)} %get-tuple-element.45), channel_id=1, source_target_pairs={{0,1},{1,0},{2,3},{3,2},{4,5},{5,4},{6,7},{7,6},{8,9},{9,8},{10,11... | collective-permute-start | bytes 737288 | tf_op jit(solution)/shard_map/ppermute | solution.py:492
  110.4 9.2 %collective-permute-start.8 = (f32[2,14,8,128]{3,2,1,0:T(8,128)S(1)}, f32[2,14,8,128]{3,2,1,0:T(8,128)S(1)}, u32[]{:S(2)}, u32[]{:S(2)}) collective-permute-start(f32[2,14,8,128]{3,2,1,0:T(8,128)S(1)} %get-tuple-element.47), channel_id=1, source_target_pairs={{8,16},{24,32},{40,48},{56,64},{72,80},{88,96},{104,112},{120,128}... | collective-permute-start | bytes 344072 | tf_op jit(solution)/shard_map/ppermute | solution.py:491
  114.7 5.1 %collective-permute-start.9 = (f32[2,14,8,128]{3,2,1,0:T(8,128)S(1)}, f32[2,14,8,128]{3,2,1,0:T(8,128)S(1)}, u32[]{:S(2)}, u32[]{:S(2)}) collective-permute-start(f32[2,14,8,128]{3,2,1,0:T(8,128)S(1)} %get-tuple-element.48), channel_id=1, source_target_pairs={{0,8},{8,0},{16,24},{24,16},{32,40},{40,32},{48,56},{56,48},{64,72... | collective-permute-start | bytes 344072 | tf_op jit(solution)/shard_map/ppermute | solution.py:492
  131.3 6.2 %collective-permute-start.10 = (f32[2,3,40,128]{3,2,1,0:T(8,128)S(1)}, f32[2,3,40,128]{3,2,1,0:T(8,128)S(1)}, u32[]{:S(2)}, u32[]{:S(2)}) collective-permute-start(f32[2,3,40,128]{3,2,1,0:T(8,128)S(1)} %get-tuple-element.52), channel_id=1, source_target_pairs={{1,2},{3,4},{5,6},{2,1},{4,3},{6,5},{9,10},{11,12},{13,14},{10,9},... | collective-permute-start | bytes 368648 | tf_op jit(solution)/shard_map/ppermute | solution.py:491
  133.2 4.3 %collective-permute-start.11 = (f32[2,3,40,128]{3,2,1,0:T(8,128)S(1)}, f32[2,3,40,128]{3,2,1,0:T(8,128)S(1)}, u32[]{:S(2)}, u32[]{:S(2)}) collective-permute-start(f32[2,3,40,128]{3,2,1,0:T(8,128)S(1)} %get-tuple-element.53), channel_id=1, source_target_pairs={{0,1},{1,0},{2,3},{3,2},{4,5},{5,4},{6,7},{7,6},{8,9},{9,8},{10,11... | collective-permute-start | bytes 368648 | tf_op jit(solution)/shard_map/ppermute | solution.py:492
  138.1 8.3 %collective-permute-start.12 = (f32[2,8,8,128]{3,2,1,0:T(8,128)S(1)}, f32[2,8,8,128]{3,2,1,0:T(8,128)S(1)}, u32[]{:S(2)}, u32[]{:S(2)}) collective-permute-start(f32[2,8,8,128]{3,2,1,0:T(8,128)S(1)} %get-tuple-element.55), channel_id=1, source_target_pairs={{8,16},{24,32},{40,48},{56,64},{72,80},{88,96},{104,112},{120,128}... | collective-permute-start | bytes 196616 | tf_op jit(solution)/shard_map/ppermute | solution.py:491
  142.3 4.4 %collective-permute-start.13 = (f32[2,8,8,128]{3,2,1,0:T(8,128)S(1)}, f32[2,8,8,128]{3,2,1,0:T(8,128)S(1)}, u32[]{:S(2)}, u32[]{:S(2)}) collective-permute-start(f32[2,8,8,128]{3,2,1,0:T(8,128)S(1)} %get-tuple-element.56), channel_id=1, source_target_pairs={{0,8},{8,0},{16,24},{24,16},{32,40},{40,32},{48,56},{56,48},{64,72... | collective-permute-start | bytes 196616 | tf_op jit(solution)/shard_map/ppermute | solution.py:492
  147.5 6.2 %collective-permute-start.16 = (f32[8,32,128]{2,1,0:T(8,128)S(1)}, f32[8,32,128]{2,1,0:T(8,128)S(1)}, u32[]{:S(2)}, u32[]{:S(2)}) collective-permute-start(f32[8,32,128]{2,1,0:T(8,128)S(1)} %get-tuple-element.57.refs_0_), channel_id=1, source_target_pairs={{0,8},{8,16},{16,24},{24,0},{1,9},{9,17},{17,25},{25,1},{2,10},{10... | collective-permute-start | bytes 393224 | tf_op jit(solution)/shard_map/ppermute | solution.py:497
  147.6 6.2 %collective-permute-start.15 = (f32[8,32,128]{2,1,0:T(8,128)S(1)}, f32[8,32,128]{2,1,0:T(8,128)S(1)}, u32[]{:S(2)}, u32[]{:S(2)}) collective-permute-start(f32[8,32,128]{2,1,0:T(8,128)S(1)} %get-tuple-element.58.refs_1_), channel_id=1, source_target_pairs={{0,24},{8,0},{16,8},{24,16},{1,25},{9,1},{17,9},{25,17},{2,26},{10... | collective-permute-start | bytes 393224 | tf_op jit(solution)/shard_map/ppermute | solution.py:497
  150.8 6.6 %collective-permute-start.14 = (f32[8,32,128]{2,1,0:T(8,128)S(1)}, f32[8,32,128]{2,1,0:T(8,128)S(1)}, u32[]{:S(2)}, u32[]{:S(2)}) collective-permute-start(f32[8,32,128]{2,1,0:T(8,128)S(1)} %get-tuple-element.57.refs_0_), channel_id=1, source_target_pairs={{0,24},{8,0},{16,8},{24,16},{1,25},{9,1},{17,9},{25,17},{2,26},{10... | collective-permute-start | bytes 393224 | tf_op jit(solution)/shard_map/ppermute | solution.py:497
  152.0 6.2 %collective-permute-start.19 = (f32[8,32,128]{2,1,0:T(8,128)S(1)}, f32[8,32,128]{2,1,0:T(8,128)S(1)}, u32[]{:S(2)}, u32[]{:S(2)}) collective-permute-start(f32[8,32,128]{2,1,0:T(8,128)S(1)} %get-tuple-element.58.refs_1_), channel_id=1, source_target_pairs={{0,8},{8,16},{16,24},{24,0},{1,9},{9,17},{17,25},{25,1},{2,10},{10... | collective-permute-start | bytes 393224 | tf_op jit(solution)/shard_map/ppermute | solution.py:497
  153.7 6.2 %collective-permute-start.17 = (f32[8,32,128]{2,1,0:T(8,128)S(1)}, f32[8,32,128]{2,1,0:T(8,128)S(1)}, u32[]{:S(2)}, u32[]{:S(2)}) collective-permute-start(f32[8,32,128]{2,1,0:T(8,128)S(1)} %collective-permute-done.16.refs_6_), channel_id=1, source_target_pairs={{0,8},{8,16},{16,24},{24,0},{1,9},{9,17},{17,25},{25,1},{2,10},{10... | collective-permute-start | bytes 393224 | tf_op jit(solution)/shard_map/ppermute | solution.py:497
  153.7 6.2 %collective-permute-start.18 = (f32[8,32,128]{2,1,0:T(8,128)S(1)}, f32[8,32,128]{2,1,0:T(8,128)S(1)}, u32[]{:S(2)}, u32[]{:S(2)}) collective-permute-start(f32[8,32,128]{2,1,0:T(8,128)S(1)} %collective-permute-done.15.refs_3_), channel_id=1, source_target_pairs={{0,24},{8,0},{16,8},{24,16},{1,25},{9,1},{17,9},{25,17},{2,26},{10... | collective-permute-start | bytes 393224 | tf_op jit(solution)/shard_map/ppermute | solution.py:497

commit v10 on v9

--- a/solution.py
+++ b/solution.py
@@ -21,7 +21,7 @@
     return jnp.sum(x, axis=1, keepdims=True)
 
 
-def pack_kernel(geo, shift_ref, target_ref, views_ref, out_ref, rolled, pos_v, pos_s, sem):
+def pack_kernel(geo, shift_ref, id_ref, target_ref, views_ref, out_ref, rolled, pos_v, pos_s, sem):
     peers, cap, x_cells, y_cells, brick_cols, row_count, all_cols, view_count = geo
     groups = brick_cols * x_cells
     rows_per = cap + 1
@@ -32,7 +32,8 @@
     dest = column // y_cells * row_count + line // x_cells
     part = y_cells // view_count
     y = column % y_cells
-    slot = ((y // part * brick_cols + bz) * x_cells + line % x_cells) * part + y % part + 1
+    turned = (y // part + view_count - id_ref[0]) % view_count
+    slot = ((turned * brick_cols + bz) * x_cells + line % x_cells) * part + y % part + 1
     high, low = slot // 64, slot % 64
     peer_id = lax.broadcasted_iota(jnp.int32, (peers, y_cells), 0)
     before = (
@@ -83,13 +84,14 @@
     lax.fori_loop(0, groups, body, 0)
 
 
-def pack(shift, target, views, geo):
+def pack(shift, ids, target, views, geo):
     peers, cap, x_cells, y_cells, brick_cols, row_count, all_cols, view_count = geo
     groups = brick_cols * x_cells
     return pl.pallas_call(
         functools.partial(pack_kernel, geo),
         out_shape=jax.ShapeDtypeStruct((peers * (cap + 1), 1, BRICK), jnp.float32),
         in_specs=[
+            pl.BlockSpec(memory_space=pltpu.SMEM),
             pl.BlockSpec(memory_space=pltpu.SMEM),
             pl.BlockSpec(memory_space=pltpu.VMEM),
             pl.BlockSpec(memory_space=pltpu.VMEM),
@@ -102,10 +104,10 @@
             pltpu.SemaphoreType.DMA,
         ],
         name="pack",
-    )(shift, target, views)
-
-
-def unpack_kernel(peers, cap, slots, id_ref, in_ref, *refs):
+    )(shift, ids, target, views)
+
+
+def unpack_kernel(peers, cap, slots, in_ref, *refs):
     outs, (placed, list_v, idx_v, idx_s, sem) = refs[:-5], refs[-5:]
     rows_per = cap + 1
     for p in range(peers):
@@ -127,14 +129,13 @@
     lax.fori_loop(0, peers, per_peer, 0)
     views, size = len(outs), slots // len(outs)
     for d, out in enumerate(outs):
-        base = pl.multiple_of(lax.rem(id_ref[0] + d, views) * size, size)
-        out[...] = placed[pl.ds(base, size), :]
-
-
-def unpack(ids, arrived, peers, cap, slots, views):
+        out[...] = placed[d * size : (d + 1) * size, :]
+
+
+def unpack(arrived, peers, cap, slots, views):
     return call(
         functools.partial(unpack_kernel, peers, cap, slots), "unpack",
-        [f32(slots // views, BRICK)] * views, (ids, arrived),
+        [f32(slots // views, BRICK)] * views, (arrived,), 0,
         scratch=[
             pltpu.VMEM((slots + SPARE, BRICK), jnp.float32),
             pltpu.VMEM((peers, BRICK), jnp.float32),
@@ -264,14 +265,14 @@
                     partial[c, x, at, :] = weigh(layers[x : x + TAPS], wx)
             return carry
 
-        lax.fori_loop(0, (part + 2 * TRIM) // TILE, per_tile, 0)
+        lax.fori_loop(0, (part + 2 * TRIM) // TILE, per_tile, 0, unroll=True)
 
         def per_layer(x, carry):
             rows = [y_rows(partial, (c, x), wy, part) for c in range(2)]
             out_ref[u, 0, x], out_ref[u, 1, x] = blur_z(*rows, wz)
             return carry
 
-        lax.fori_loop(0, x_cells, per_layer, 0)
+        lax.fori_loop(0, x_cells, per_layer, 0, unroll=True)
         return carry
 
     lax.fori_loop(0, views, per_view, 0)
@@ -282,87 +283,6 @@
     return call(
         forward_kernel, "forward", [f32(views, 2, x_cells, rows - 2 * TRIM, BRICK)], (w, est),
         scratch=[pltpu.VMEM((2, x_cells, rows, BRICK), jnp.float32)],
-    )[0]
-
-
-def blur_x_tile(est, at, wx, out, c, x_cells, rows):
-    layers = [est[c, i, at, :] for i in range(x_cells + 2 * HALO)]
-    for x in range(x_cells):
-        out[c, x, rows, :] = weigh(layers[x : x + TAPS], wx)
-
-
-def middle_kernel(w_ref, est, total, out_ref, part_ref, fresh):
-    views, _, x_cells, part, _ = out_ref.shape
-    tall = part_ref.shape[3]
-    rows = slice(TILE, TILE + tall)
-    for c in range(2):
-        for i in range(x_cells + 2 * HALO):
-            fresh[c, i] = est[c, i, rows, :] * total[c, i, rows, :] / views
-
-    def per_view(u, carry):
-        wx, wy, wz = (taps_of(w_ref, u, dim, False) for dim in range(3))
-
-        def per_tile(t, carry):
-            at = pl.ds(pl.multiple_of(t * TILE, TILE), TILE)
-            for c in range(2):
-                blur_x_tile(fresh, at, wx, part_ref.at[u], c, x_cells, at)
-            return carry
-
-        lax.fori_loop(0, tall // TILE, per_tile, 0)
-
-        def per_layer(x, carry):
-            rows = [y_rows(part_ref, (u, c, x), wy, part) for c in range(2)]
-            out_ref[u, 0, x], out_ref[u, 1, x] = blur_z(*rows, wz)
-            return carry
-
-        lax.fori_loop(0, x_cells, per_layer, 0)
-        return carry
-
-    lax.fori_loop(0, views, per_view, 0)
-
-
-def middle(w, est, total, views, x_cells):
-    tall = est.shape[2] - 2 * TILE
-    return call(
-        middle_kernel, "middle",
-        [f32(views, 2, x_cells, tall - TILE, BRICK), f32(views, 2, x_cells, tall, BRICK)],
-        (w, est, total), scratch=[pltpu.VMEM((2, x_cells + 2 * HALO, tall, BRICK), jnp.float32)],
-    )
-
-
-def ends_kernel(w_ref, est, mid, part_ref, out_ref, strip):
-    views, _, x_cells, part, _ = out_ref.shape
-    tall = part_ref.shape[3]
-    sides = ((0, 0, 0, TILE, 0), (tall + TILE, TILE, tall - TILE, 0, part - TILE))
-
-    def per_view(u, carry):
-        wx, wy, wz = (taps_of(w_ref, u, dim, False) for dim in range(3))
-        for s, (at, here, kept, there, to) in enumerate(sides):
-            for c in range(2):
-                blur_x_tile(est, slice(at, at + TILE), wx, strip.at[s], c, x_cells, slice(here, here + TILE))
-
-        def per_layer(x, carry):
-            for s, (at, here, kept, there, to) in enumerate(sides):
-                for c in range(2):
-                    strip[s, c, x, there : there + TILE, :] = part_ref[u, c, x, kept : kept + TILE, :]
-                rows = blur_z(*(y_rows(strip, (s, c, x), wy, TILE) for c in range(2)), wz)
-                for c in range(2):
-                    out_ref[u, c, x, to : to + TILE, :] = rows[c]
-            for c in range(2):
-                out_ref[u, c, x, TILE : part - TILE, :] = mid[u, c, x]
-            return carry
-
-        lax.fori_loop(0, x_cells, per_layer, 0)
-        return carry
-
-    lax.fori_loop(0, views, per_view, 0)
-
-
-def ends(w, est, mid, partial):
-    views, _, x, tall, _ = partial.shape
-    return call(
-        ends_kernel, "ends", [f32(views, 2, x, tall + TILE, BRICK)], (w, est, mid, partial),
-        scratch=[pltpu.VMEM((2, 2, x, 2 * TILE, BRICK), jnp.float32)],
     )[0]
 
 
@@ -389,7 +309,7 @@
                 partial[c, x] = y_rows(wide, (c, x), wy, part + 2 * TRIM)
             return carry
 
-        lax.fori_loop(0, x_cells, per_layer, 0)
+        lax.fori_loop(0, x_cells, per_layer, 0, unroll=True)
 
         def per_tile(t, carry, wx=wx, source=before):
             at = pl.ds(pl.multiple_of(t * TILE, TILE), TILE)
@@ -400,7 +320,7 @@
                     out_ref[c, i, at, :] = value if source is None else value + source[c, i, at, :]
             return carry
 
-        lax.fori_loop(0, (part + 2 * TRIM) // TILE, per_tile, 0)
+        lax.fori_loop(0, (part + 2 * TRIM) // TILE, per_tile, 0, unroll=True)
         before = out_ref
     odd = id_ref[1]
     for slot, send in enumerate(sends):
@@ -510,13 +430,14 @@
     all_cols = y_cells * block_count
     geo = (peer_count, capacity, x_cells, y_cells, brick_cols, row_count, all_cols, view_count)
     row, place = lax.axis_index("rows"), lax.axis_index("views")
+    ids = jnp.stack([place, row % 2]).astype(jnp.int32)
     chain = [(block * view_count - 1, block * view_count) for block in range(1, block_count)]
     edge_at = jnp.where(place == 0, 0, y_cells - TILE)
     edge = lax.ppermute(
         lax.dynamic_slice_in_dim(estimate, edge_at, TILE, 1),
         ("blocks", "views"), chain + [(j, i) for i, j in chain],
     )
-    outgoing = pack(shifts, target[0].transpose(0, 2, 1), views_data[0], geo)
+    outgoing = pack(shifts, ids, target[0].transpose(0, 2, 1), views_data[0], geo)
     outgoing, edge = lax.optimization_barrier((outgoing, edge))
     arrived = lax.all_to_all(
         outgoing.reshape(peer_count, capacity + 1, 1, BRICK),
@@ -524,7 +445,6 @@
     ).reshape(peer_count * (capacity + 1), 1, BRICK)
     taps = lax.all_gather(psf_taps, "views", axis=0, tiled=True)
     w = (taps / jnp.sum(taps, axis=2, keepdims=True)).reshape(-1)
-    ids = jnp.stack([place, row % 2]).astype(jnp.int32)
     halo = f32(2, HALO, part + 2 * TILE, BRICK)
     own, *sent = call(
         part_kernel, "part", [f32(2, x_cells, part + 2 * TILE, BRICK), halo, halo],
@@ -535,7 +455,7 @@
     est = call(extend_kernel, "extend", wide, (ids, own, *swap(*sent, "rows")))[0]
     below = forward(w, est, view_count, x_cells)
     arrived, below = lax.optimization_barrier((arrived, below))
-    moved = unpack(ids, arrived, peer_count, capacity, brick_count, view_count)
+    moved = unpack(arrived, peer_count, capacity, brick_count, view_count)
     moved = [m.reshape(brick_cols, x_cells, part, BRICK) for m in moved]
     behind, ahead = turn(moved[1], 1, view_count), turn(moved[3], -1, view_count)
     across = turn(moved[2], 2, view_count)
@@ -543,10 +463,9 @@
     total = backward(w, ids, below, (3, 1), (behind, ahead), total, 0)[0]
     total, *sent = backward(w, ids, below, (2,), (across,), total, 2 * HALO)
     total, *sent = merge(ids, total, *swap(*sent, "rows"), x_cells + 2 * HALO)
-    mid, partial = middle(w, est, total, view_count, x_cells)
     args = (ids, total, *swap(*sent, ("blocks", "views")), est)
     est = call(functools.partial(update_kernel, view_count), "update", wide, args)[0]
-    below = ends(w, est, mid, partial)
+    below = forward(w, est, view_count, x_cells)
     observed = (moved[0], ahead, across, behind)
     total, *sent = backward(w, ids, below, (0, 1, 2, 3), observed, None, HALO)
     total, *sent = merge(ids, total, *swap(*sent, "rows"), x_cells)

time: 163 us -> 155 us (0.951)
  Pallas kernels: 46.3 us -> 29.3 us
  waiting for transfers between devices: 54.2 us -> 59.6 us
  local copies, waits for them, and re-layouts: 0.95 us -> 3.5 us
    pallas_call x15 -> x14, Pallas kernels: 40.3 us -> 23.3 us  [call(): pl.pallas_call(kernel, out_shape=outs, in_specs=[smem()] * scalars + [vme...]
    ppermute x5, waiting for transfers between devices: 15.4 us -> 19.7 us  [swap(): outer = lax.ppermute(outer, axes, links + [(j, i) for i, j in links])]
    unnamed x5 -> x15, local copies, waits for them, and re-layouts: 0.02 us -> 2.57 us
  transfers between devices with their start and end apart: 21 -> 21, of which waited for: 12 -> 12; matrix products, arithmetic and copies ran while one was open for 0% -> 1% of each run, Pallas kernels for 14% -> 9%
where the time goes in v10:
time: 155 us; the launch traced here: 153 us
  waiting for transfers between devices  59.6 us (38%)
  starting transfers between devices  48.5 us (31%)
  Pallas kernels  29.3 us (19%)
  blocking collectives  10.4 us (7%)
  local copies, waits for them, and re-layouts  3.5 us (2%)
    all_to_all x1, waiting for transfers between devices, per_device(): lax.all_to_all(outgoing.reshape(peer_count, capacity + 1, 1, BRICK), ('bl...  25.5 us
    pallas_call x14, Pallas kernels, call(): pl.pallas_call(kernel, out_shape=outs, in_specs=[smem()] * scalars + [vme...  23.3 us
    ppermute x5, waiting for transfers between devices, swap(): outer = lax.ppermute(outer, axes, links + [(j, i) for i, j in links])  19.7 us
    ppermute x5, starting transfers between devices, swap(): outer = lax.ppermute(outer, axes, links + [(j, i) for i, j in links])  14.1 us
    ppermute x9, waiting for transfers between devices, turn(): lax.ppermute(value, 'views', [(i, (i + step) % count) for i in range(coun...  13.9 us
    ppermute x9, starting transfers between devices, turn(): lax.ppermute(value, 'views', [(i, (i + step) % count) for i in range(coun...  12.3 us
    all_to_all x1, starting transfers between devices, per_device(): lax.all_to_all(outgoing.reshape(peer_count, capacity + 1, 1, BRICK), ('bl...  12.2 us
    all_gather x1, blocking collectives, per_device(): taps = lax.all_gather(psf_taps, 'views', axis=0, tiled=True)  10.4 us
  transfers between devices with their start and end apart: 21, of which 12 were waited for; matrix products, arithmetic and copies ran while one was open for 1% of the time, Pallas kernels for 9%

profile of v10, /device:TPU:34, one launch (start us, length us, event | category | flops | bytes accessed | tf_op | source)
XLA Modules:
  0.0 153.0 jit_solution(17223058853349882796)
XLA Ops:
  0.8 4.5 %collective-permute-start = (f32[8,8,256]{2,1,0:T(8,128)S(1)}, f32[8,8,256]{2,1,0:T(8,128)S(1)}, u32[]{:S(2)}, u32[]{:S(2)}) collective-permute-start(f32[8,8,256]{2,1,0:T(8,128)S(1)} %constant_dynamic-slice_fusion), channel_id=1, source_target_pairs={{24,32},{56,64},{88,96},{120,128},{152,160},{184,192},{216,224},{3... | collective-permute-start | bytes 196616 | tf_op jit(solution)/shard_map/ppermute | solution.py:436
  6.6 6.0 %pack.1 = f32[4160,1,128]{2,1,0:T(1,128)} custom-call(s32[1]{0:T(128)S(6)} %copy.9.shift_ref, s32[2]{0:T(128)} %pad_add_fusion.id_ref, s32[8,2,128]{2,1,0:T(2,128)} %bitcast.21, f32[8,128,256]{2,1,0:T(8,128)} %bitcast.20), custom_call_target="tpu_custom_call" | custom-call | tf_op jit(solution)/shard_map/pack/pallas_call | solution.py:90
  12.7 12.2 %all-to-all-start = ((f32[64,65,1,128]{3,2,1,0:T(1,128)}), f32[64,65,1,128]{3,2,1,0:T(1,128)S(1)}, u32[]{:S(2)}, u32[]{:S(2)}) async-start(f32[64,65,1,128]{3,2,1,0:T(1,128)} %bitcast.19), calls=%async_computation | async-start | bytes 4259840 | tf_op jit(solution)/shard_map/all_to_all | solution.py:442
  24.9 10.4 %all_gather.3 = f32[4,3,7]{2,1,0:T(4,128)S(1)} all-gather(f32[1,3,7]{2,1,0:T(4,128)S(1)} %copy.8), channel_id=1, replica_groups=mesh['blocks'=8,'views'=4,'rows'=8] {'views'}, dimensions={0}, use_global_device_ids=true | all-gather | bytes 420 | tf_op jit(solution)/shard_map/all_gather | solution.py:446
  36.8 1.9 %collective-permute-start.1 = (f32[2,3,48,128]{3,2,1,0:T(8,128)S(1)}, f32[2,3,48,128]{3,2,1,0:T(8,128)S(1)}, u32[]{:S(2)}, u32[]{:S(2)}) collective-permute-start(f32[2,3,48,128]{3,2,1,0:T(8,128)S(1)} %get-tuple-element.33), channel_id=1, source_target_pairs={{1,2},{3,4},{5,6},{2,1},{4,3},{6,5},{9,10},{11,12},{13,14},{10,9},... | collective-permute-start | bytes 442376 | tf_op jit(solution)/shard_map/ppermute | solution.py:411
  38.7 1.7 %collective-permute-start.2 = (f32[2,3,48,128]{3,2,1,0:T(8,128)S(1)}, f32[2,3,48,128]{3,2,1,0:T(8,128)S(1)}, u32[]{:S(2)}, u32[]{:S(2)}) collective-permute-start(f32[2,3,48,128]{3,2,1,0:T(8,128)S(1)} %get-tuple-element.34), channel_id=1, source_target_pairs={{0,1},{1,0},{2,3},{3,2},{4,5},{5,4},{6,7},{7,6},{8,9},{9,8},{10,11... | collective-permute-start | bytes 442376 | tf_op jit(solution)/shard_map/ppermute | solution.py:412
  40.5 4.6 %collective-permute-done.1.outer = f32[2,3,48,128]{3,2,1,0:T(8,128)S(1)} collective-permute-done((f32[2,3,48,128]{3,2,1,0:T(8,128)S(1)}, f32[2,3,48,128]{3,2,1,0:T(8,128)S(1)}, u32[]{:S(2)}, u32[]{:S(2)}) %collective-permute-start.1) | collective-permute-done | bytes 147488 | tf_op jit(solution)/shard_map/ppermute | solution.py:411
  46.7 2.9 %forward.2.below = f32[4,2,8,32,128]{4,3,2,1,0:T(8,128)S(1)} custom-call(f32[84]{0:T(128)S(1)} %reshape.22.w_ref, f32[2,14,40,128]{3,2,1,0:T(8,128)S(1)} %extend.1.est), custom_call_target="tpu_custom_call" | custom-call | flops 1000 | bytes 1000 | tf_op jit(solution)/shard_map/forward/pallas_call | solution.py:162
  50.4 25.5 %all-to-all-done = f32[64,65,1,128]{3,2,1,0:T(1,128)S(1)} async-done(((f32[64,65,1,128]{3,2,1,0:T(1,128)}), f32[64,65,1,128]{3,2,1,0:T(1,128)S(1)}, u32[]{:S(2)}, u32[]{:S(2)}) %all-to-all-start) | async-done | bytes 2129952 | tf_op jit(solution)/shard_map/all_to_all | solution.py:442
  76.0 4.7 %unpack.1 = (f32[512,128]{1,0:T(8,128)S(1)}, f32[512,128]{1,0:T(8,128)S(1)}, f32[512,128]{1,0:T(8,128)S(1)}, f32[512,128]{1,0:T(8,128)S(1)}) custom-call(f32[4160,1,128]{2,1,0:T(1,128)S(1)} %bitcast.13), custom_call_target="tpu_custom_call" | custom-call | flops 1000 | bytes 1000 | tf_op jit(solution)/shard_map/unpack/pallas_call | solution.py:162
  80.8 3.2 %collective-permute-start.5 = (f32[2,8,32,128]{3,2,1,0:T(8,128)S(1)}, f32[2,8,32,128]{3,2,1,0:T(8,128)S(1)}, u32[]{:S(2)}, u32[]{:S(2)}) collective-permute-start(f32[2,8,32,128]{3,2,1,0:T(8,128)S(1)} %bitcast.17), channel_id=1, source_target_pairs={{0,24},{8,0},{16,8},{24,16},{1,25},{9,1},{17,9},{25,17},{2,26},{10... | collective-permute-start | bytes 786440 | tf_op jit(solution)/shard_map/ppermute | solution.py:417
  84.0 1.2 backward.4.refs_2_
  85.2 10.4 %collective-permute-done.4.refs_0_.refs_3_ = f32[2,8,32,128]{3,2,1,0:T(8,128)S(1)} collective-permute-done((f32[2,8,32,128]{3,2,1,0:T(8,128)S(1)}, f32[2,8,32,128]{3,2,1,0:T(8,128)S(1)}, u32[]{:S(2)}, u32[]{:S(2)}) %collective-permute-start.4) | collective-permute-done | bytes 262176 | tf_op jit(solution)/shard_map/ppermute | solution.py:417
  95.6 1.8 %backward.5.refs_1_ = f32[2,14,40,128]{3,2,1,0:T(8,128)S(1)} custom-call(f32[84]{0:T(128)S(1)} %reshape.22.w_ref, s32[2]{0:T(128)S(1)} %copy-done.5, f32[4,2,8,32,128]{4,3,2,1,0:T(8,128)S(1)} %forward.2.below, f32[2,8,32,128]{3,2,1,0:T(8,128)S(1)} %collective-permute-done.4.refs_0_.refs_3_, f32[2,8,32,128]{3,2,1,0:T(8,128)S(1)} %collective-permute-done.5.refs_1_, ...), custom_call_target="tpu_custom_call" | custom-call | flops 1000 | bytes 1000 | tf_op jit(solution)/shard_map/backward/pallas_call | solution.py:162
  97.4 1.3 backward.6
  98.7 1.9 %collective-permute-start.6 = (f32[2,6,40,128]{3,2,1,0:T(8,128)S(1)}, f32[2,6,40,128]{3,2,1,0:T(8,128)S(1)}, u32[]{:S(2)}, u32[]{:S(2)}) collective-permute-start(f32[2,6,40,128]{3,2,1,0:T(8,128)S(1)} %get-tuple-element.42), channel_id=1, source_target_pairs={{1,2},{3,4},{5,6},{2,1},{4,3},{6,5},{9,10},{11,12},{13,14},{10,9},... | collective-permute-start | bytes 737288 | tf_op jit(solution)/shard_map/ppermute | solution.py:411
  100.6 1.7 %collective-permute-start.7 = (f32[2,6,40,128]{3,2,1,0:T(8,128)S(1)}, f32[2,6,40,128]{3,2,1,0:T(8,128)S(1)}, u32[]{:S(2)}, u32[]{:S(2)}) collective-permute-start(f32[2,6,40,128]{3,2,1,0:T(8,128)S(1)} %get-tuple-element.43), channel_id=1, source_target_pairs={{0,1},{1,0},{2,3},{3,2},{4,5},{5,4},{6,7},{7,6},{8,9},{9,8},{10,11... | collective-permute-start | bytes 737288 | tf_op jit(solution)/shard_map/ppermute | solution.py:412
  102.3 3.9 %collective-permute-done.6.outer = f32[2,6,40,128]{3,2,1,0:T(8,128)S(1)} collective-permute-done((f32[2,6,40,128]{3,2,1,0:T(8,128)S(1)}, f32[2,6,40,128]{3,2,1,0:T(8,128)S(1)}, u32[]{:S(2)}, u32[]{:S(2)}) %collective-permute-start.6) | collective-permute-done | bytes 245792 | tf_op jit(solution)/shard_map/ppermute | solution.py:411
  106.9 4.3 %collective-permute-start.8 = (f32[2,14,8,128]{3,2,1,0:T(8,128)S(1)}, f32[2,14,8,128]{3,2,1,0:T(8,128)S(1)}, u32[]{:S(2)}, u32[]{:S(2)}) collective-permute-start(f32[2,14,8,128]{3,2,1,0:T(8,128)S(1)} %get-tuple-element.45), channel_id=1, source_target_pairs={{8,16},{24,32},{40,48},{56,64},{72,80},{88,96},{104,112},{120,128}... | collective-permute-start | bytes 344072 | tf_op jit(solution)/shard_map/ppermute | solution.py:411
  111.5 4.6 %collective-permute-done.8.outer = f32[2,14,8,128]{3,2,1,0:T(8,128)S(1)} collective-permute-done((f32[2,14,8,128]{3,2,1,0:T(8,128)S(1)}, f32[2,14,8,128]{3,2,1,0:T(8,128)S(1)}, u32[]{:S(2)}, u32[]{:S(2)}) %collective-permute-start.8) | collective-permute-done | bytes 114720 | tf_op jit(solution)/shard_map/ppermute | solution.py:411
  117.2 2.9 %forward.3.below = f32[4,2,8,32,128]{4,3,2,1,0:T(8,128)S(1)} custom-call(f32[84]{0:T(128)S(1)} %reshape.22.w_ref, f32[2,14,40,128]{3,2,1,0:T(8,128)S(1)} %update.1.est), custom_call_target="tpu_custom_call" | custom-call | flops 1000 | bytes 1000 | tf_op jit(solution)/shard_map/forward/pallas_call | solution.py:162
  120.1 2.9 %backward.7 = (f32[2,14,40,128]{3,2,1,0:T(8,128)S(1)}, f32[2,3,40,128]{3,2,1,0:T(8,128)S(1)}, f32[2,3,40,128]{3,2,1,0:T(8,128)S(1)}) custom-call(f32[84]{0:T(128)S(1)} %reshape.22.w_ref, s32[2]{0:T(128)S(1)} %copy-done.5, f32[4,2,8,32,128]{4,3,2,1,0:T(8,128)S(1)} %forward.3.below, f32[2,8,32,128]{3,2,1,0:T(8,128)S(1)} %bitcast.15, ...), custom_call_target="tpu_custom_call" | custom-call | flops 1000 | bytes 1000 | tf_op jit(solution)/shard_map/backward/pallas_call | solution.py:162
  123.0 1.9 %collective-permute-start.10 = (f32[2,3,40,128]{3,2,1,0:T(8,128)S(1)}, f32[2,3,40,128]{3,2,1,0:T(8,128)S(1)}, u32[]{:S(2)}, u32[]{:S(2)}) collective-permute-start(f32[2,3,40,128]{3,2,1,0:T(8,128)S(1)} %get-tuple-element.48), channel_id=1, source_target_pairs={{1,2},{3,4},{5,6},{2,1},{4,3},{6,5},{9,10},{11,12},{13,14},{10,9},... | collective-permute-start | bytes 368648 | tf_op jit(solution)/shard_map/ppermute | solution.py:411
  124.9 1.8 %collective-permute-start.11 = (f32[2,3,40,128]{3,2,1,0:T(8,128)S(1)}, f32[2,3,40,128]{3,2,1,0:T(8,128)S(1)}, u32[]{:S(2)}, u32[]{:S(2)}) collective-permute-start(f32[2,3,40,128]{3,2,1,0:T(8,128)S(1)} %get-tuple-element.49), channel_id=1, source_target_pairs={{0,1},{1,0},{2,3},{3,2},{4,5},{5,4},{6,7},{7,6},{8,9},{9,8},{10,11... | collective-permute-start | bytes 368648 | tf_op jit(solution)/shard_map/ppermute | solution.py:412
  126.7 2.4 %collective-permute-done.10.outer = f32[2,3,40,128]{3,2,1,0:T(8,128)S(1)} collective-permute-done((f32[2,3,40,128]{3,2,1,0:T(8,128)S(1)}, f32[2,3,40,128]{3,2,1,0:T(8,128)S(1)}, u32[]{:S(2)}, u32[]{:S(2)}) %collective-permute-start.10) | collective-permute-done | bytes 122912 | tf_op jit(solution)/shard_map/ppermute | solution.py:411
  129.8 4.0 %collective-permute-start.12 = (f32[2,8,8,128]{3,2,1,0:T(8,128)S(1)}, f32[2,8,8,128]{3,2,1,0:T(8,128)S(1)}, u32[]{:S(2)}, u32[]{:S(2)}) collective-permute-start(f32[2,8,8,128]{3,2,1,0:T(8,128)S(1)} %get-tuple-element.51), channel_id=1, source_target_pairs={{8,16},{24,32},{40,48},{56,64},{72,80},{88,96},{104,112},{120,128}... | collective-permute-start | bytes 196616 | tf_op jit(solution)/shard_map/ppermute | solution.py:411
  133.9 4.1 %collective-permute-done.12.outer = f32[2,8,8,128]{3,2,1,0:T(8,128)S(1)} collective-permute-done((f32[2,8,8,128]{3,2,1,0:T(8,128)S(1)}, f32[2,8,8,128]{3,2,1,0:T(8,128)S(1)}, u32[]{:S(2)}, u32[]{:S(2)}) %collective-permute-start.12) | collective-permute-done | bytes 65568 | tf_op jit(solution)/shard_map/ppermute | solution.py:411
  139.1 3.2 %collective-permute-start.15 = (f32[8,32,128]{2,1,0:T(8,128)S(1)}, f32[8,32,128]{2,1,0:T(8,128)S(1)}, u32[]{:S(2)}, u32[]{:S(2)}) collective-permute-start(f32[8,32,128]{2,1,0:T(8,128)S(1)} %get-tuple-element.54.refs_1_), channel_id=1, source_target_pairs={{0,24},{8,0},{16,8},{24,16},{1,25},{9,1},{17,9},{25,17},{2,26},{10... | collective-permute-start | bytes 393224 | tf_op jit(solution)/shard_map/ppermute | solution.py:417
  142.3 1.2 collective-permute-start.14
  145.2 3.7 %collective-permute-start.18 = (f32[8,32,128]{2,1,0:T(8,128)S(1)}, f32[8,32,128]{2,1,0:T(8,128)S(1)}, u32[]{:S(2)}, u32[]{:S(2)}) collective-permute-start(f32[8,32,128]{2,1,0:T(8,128)S(1)} %collective-permute-done.15.refs_3_), channel_id=1, source_target_pairs={{0,24},{8,0},{16,8},{24,16},{1,25},{9,1},{17,9},{25,17},{2,26},{10... | collective-permute-start | bytes 393224 | tf_op jit(solution)/shard_map/ppermute | solution.py:417
  149.7 1.7 %collective-permute-done.17.refs_4_ = f32[8,32,128]{2,1,0:T(8,128)S(1)} collective-permute-done((f32[8,32,128]{2,1,0:T(8,128)S(1)}, f32[8,32,128]{2,1,0:T(8,128)S(1)}, u32[]{:S(2)}, u32[]{:S(2)}) %collective-permute-start.17) | collective-permute-done | bytes 131104 | tf_op jit(solution)/shard_map/ppermute | solution.py:417
  151.4 1.6 %join.1 = f32[8,128,256]{2,1,0:T(8,128)} custom-call(s32[2]{0:T(128)S(1)} %copy-done.5, f32[8,32,128]{2,1,0:T(8,128)S(1)} %get-tuple-element.53.refs_0_, f32[8,32,128]{2,1,0:T(8,128)S(1)} %get-tuple-element.54.refs_1_, f32[8,32,128]{2,1,0:T(8,128)S(1)} %collective-permute-done.14.refs_2_, f32[8,32,128]{2,1,0:T(8,128)S(1)} %collective-permute-done.15.refs_3_, ...), custom_call_target="tpu_custom_call" | custom-call | flops 1000 | bytes 1000 | tf_op jit(solution)/shard_map/join/pallas_call | solution.py:162
  (45 shorter events, 12.0 us)
Async XLA Ops:
  0.8 11.8 %collective-permute-start = (f32[8,8,256]{2,1,0:T(8,128)S(1)}, f32[8,8,256]{2,1,0:T(8,128)S(1)}, u32[]{:S(2)}, u32[]{:S(2)}) collective-permute-start(f32[8,8,256]{2,1,0:T(8,128)S(1)} %constant_dynamic-slice_fusion), channel_id=1, source_target_pairs={{24,32},{56,64},{88,96},{120,128},{152,160},{184,192},{216,224},{3... | collective-permute-start | bytes 196616 | tf_op jit(solution)/shard_map/ppermute | solution.py:436
  12.6 12.2 %copy-start.6 = (f32[1,3,7]{2,0,1:T(1,128)S(1)}, f32[1,3,7]{2,0,1:T(1,128)}, u32[]{:S(2)}) copy-start(f32[1,3,7]{2,0,1:T(1,128)} %param.8) | copy-start | bytes 256
  12.7 22.6 %copy-start.2 = (f32[8,128,256]{2,1,0:T(8,128)S(1)}, f32[8,128,256]{2,1,0:T(8,128)}, u32[]{:S(2)}) copy-start(f32[8,128,256]{2,1,0:T(8,128)} %est.1) | copy-start | bytes 3145732
  12.7 22.6 %copy-start.5 = (s32[2]{0:T(128)S(1)}, s32[2]{0:T(128)}, u32[]{:S(2)}) copy-start(s32[2]{0:T(128)} %pad_add_fusion.id_ref) | copy-start | bytes 28
  12.7 63.3 %all-to-all-start = ((f32[64,65,1,128]{3,2,1,0:T(1,128)}), f32[64,65,1,128]{3,2,1,0:T(1,128)S(1)}, u32[]{:S(2)}, u32[]{:S(2)}) async-start(f32[64,65,1,128]{3,2,1,0:T(1,128)} %bitcast.19), calls=%async_computation | async-start | bytes 4259840 | tf_op jit(solution)/shard_map/all_to_all | solution.py:442
  36.0 0.7 copy-start.3
  36.8 8.4 %collective-permute-start.1 = (f32[2,3,48,128]{3,2,1,0:T(8,128)S(1)}, f32[2,3,48,128]{3,2,1,0:T(8,128)S(1)}, u32[]{:S(2)}, u32[]{:S(2)}) collective-permute-start(f32[2,3,48,128]{3,2,1,0:T(8,128)S(1)} %get-tuple-element.33), channel_id=1, source_target_pairs={{1,2},{3,4},{5,6},{2,1},{4,3},{6,5},{9,10},{11,12},{13,14},{10,9},... | collective-permute-start | bytes 442376 | tf_op jit(solution)/shard_map/ppermute | solution.py:411
  38.7 6.4 %collective-permute-start.2 = (f32[2,3,48,128]{3,2,1,0:T(8,128)S(1)}, f32[2,3,48,128]{3,2,1,0:T(8,128)S(1)}, u32[]{:S(2)}, u32[]{:S(2)}) collective-permute-start(f32[2,3,48,128]{3,2,1,0:T(8,128)S(1)} %get-tuple-element.34), channel_id=1, source_target_pairs={{0,1},{1,0},{2,3},{3,2},{4,5},{5,4},{6,7},{7,6},{8,9},{9,8},{10,11... | collective-permute-start | bytes 442376 | tf_op jit(solution)/shard_map/ppermute | solution.py:412
  45.1 1.0 copy-start.4
  49.6 0.8 copy-start
  80.7 14.9 %collective-permute-start.4 = (f32[2,8,32,128]{3,2,1,0:T(8,128)S(1)}, f32[2,8,32,128]{3,2,1,0:T(8,128)S(1)}, u32[]{:S(2)}, u32[]{:S(2)}) collective-permute-start(f32[2,8,32,128]{3,2,1,0:T(8,128)S(1)} %bitcast.18), channel_id=1, source_target_pairs={{0,8},{8,16},{16,24},{24,0},{1,9},{9,17},{17,25},{25,1},{2,10},{10... | collective-permute-start | bytes 786440 | tf_op jit(solution)/shard_map/ppermute | solution.py:417
  80.8 14.8 %collective-permute-start.5 = (f32[2,8,32,128]{3,2,1,0:T(8,128)S(1)}, f32[2,8,32,128]{3,2,1,0:T(8,128)S(1)}, u32[]{:S(2)}, u32[]{:S(2)}) collective-permute-start(f32[2,8,32,128]{3,2,1,0:T(8,128)S(1)} %bitcast.17), channel_id=1, source_target_pairs={{0,24},{8,0},{16,8},{24,16},{1,25},{9,1},{17,9},{25,17},{2,26},{10... | collective-permute-start | bytes 786440 | tf_op jit(solution)/shard_map/ppermute | solution.py:417
  84.0 13.4 %collective-permute-start.3 = (f32[2,8,32,128]{3,2,1,0:T(8,128)S(1)}, f32[2,8,32,128]{3,2,1,0:T(8,128)S(1)}, u32[]{:S(2)}, u32[]{:S(2)}) collective-permute-start(f32[2,8,32,128]{3,2,1,0:T(8,128)S(1)} %bitcast.16), channel_id=1, source_target_pairs={{0,16},{8,24},{16,0},{24,8},{1,17},{9,25},{17,1},{25,9},{2,18},{10... | collective-permute-start | bytes 786440 | tf_op jit(solution)/shard_map/ppermute | solution.py:417
  97.4 19.1 %copy-start.1 = (f32[2,14,40,128]{3,2,1,0:T(8,128)S(1)}, f32[2,14,40,128]{3,2,1,0:T(8,128)}, u32[]{:S(2)}) copy-start(f32[2,14,40,128]{3,2,1,0:T(8,128)} %copy-done) | copy-start | bytes 1720324
  98.7 7.5 %collective-permute-start.6 = (f32[2,6,40,128]{3,2,1,0:T(8,128)S(1)}, f32[2,6,40,128]{3,2,1,0:T(8,128)S(1)}, u32[]{:S(2)}, u32[]{:S(2)}) collective-permute-start(f32[2,6,40,128]{3,2,1,0:T(8,128)S(1)} %get-tuple-element.42), channel_id=1, source_target_pairs={{1,2},{3,4},{5,6},{2,1},{4,3},{6,5},{9,10},{11,12},{13,14},{10,9},... | collective-permute-start | bytes 737288 | tf_op jit(solution)/shard_map/ppermute | solution.py:411
  100.6 5.6 %collective-permute-start.7 = (f32[2,6,40,128]{3,2,1,0:T(8,128)S(1)}, f32[2,6,40,128]{3,2,1,0:T(8,128)S(1)}, u32[]{:S(2)}, u32[]{:S(2)}) collective-permute-start(f32[2,6,40,128]{3,2,1,0:T(8,128)S(1)} %get-tuple-element.43), channel_id=1, source_target_pairs={{0,1},{1,0},{2,3},{3,2},{4,5},{5,4},{6,7},{7,6},{8,9},{9,8},{10,11... | collective-permute-start | bytes 737288 | tf_op jit(solution)/shard_map/ppermute | solution.py:412
  106.9 9.2 %collective-permute-start.8 = (f32[2,14,8,128]{3,2,1,0:T(8,128)S(1)}, f32[2,14,8,128]{3,2,1,0:T(8,128)S(1)}, u32[]{:S(2)}, u32[]{:S(2)}) collective-permute-start(f32[2,14,8,128]{3,2,1,0:T(8,128)S(1)} %get-tuple-element.45), channel_id=1, source_target_pairs={{8,16},{24,32},{40,48},{56,64},{72,80},{88,96},{104,112},{120,128}... | collective-permute-start | bytes 344072 | tf_op jit(solution)/shard_map/ppermute | solution.py:411
  111.2 5.3 %collective-permute-start.9 = (f32[2,14,8,128]{3,2,1,0:T(8,128)S(1)}, f32[2,14,8,128]{3,2,1,0:T(8,128)S(1)}, u32[]{:S(2)}, u32[]{:S(2)}) collective-permute-start(f32[2,14,8,128]{3,2,1,0:T(8,128)S(1)} %get-tuple-element.46), channel_id=1, source_target_pairs={{0,8},{8,0},{16,24},{24,16},{32,40},{40,32},{48,56},{56,48},{64,72... | collective-permute-start | bytes 344072 | tf_op jit(solution)/shard_map/ppermute | solution.py:412
  123.0 6.2 %collective-permute-start.10 = (f32[2,3,40,128]{3,2,1,0:T(8,128)S(1)}, f32[2,3,40,128]{3,2,1,0:T(8,128)S(1)}, u32[]{:S(2)}, u32[]{:S(2)}) collective-permute-start(f32[2,3,40,128]{3,2,1,0:T(8,128)S(1)} %get-tuple-element.48), channel_id=1, source_target_pairs={{1,2},{3,4},{5,6},{2,1},{4,3},{6,5},{9,10},{11,12},{13,14},{10,9},... | collective-permute-start | bytes 368648 | tf_op jit(solution)/shard_map/ppermute | solution.py:411
  124.9 4.3 %collective-permute-start.11 = (f32[2,3,40,128]{3,2,1,0:T(8,128)S(1)}, f32[2,3,40,128]{3,2,1,0:T(8,128)S(1)}, u32[]{:S(2)}, u32[]{:S(2)}) collective-permute-start(f32[2,3,40,128]{3,2,1,0:T(8,128)S(1)} %get-tuple-element.49), channel_id=1, source_target_pairs={{0,1},{1,0},{2,3},{3,2},{4,5},{5,4},{6,7},{7,6},{8,9},{9,8},{10,11... | collective-permute-start | bytes 368648 | tf_op jit(solution)/shard_map/ppermute | solution.py:412
  129.8 8.3 %collective-permute-start.12 = (f32[2,8,8,128]{3,2,1,0:T(8,128)S(1)}, f32[2,8,8,128]{3,2,1,0:T(8,128)S(1)}, u32[]{:S(2)}, u32[]{:S(2)}) collective-permute-start(f32[2,8,8,128]{3,2,1,0:T(8,128)S(1)} %get-tuple-element.51), channel_id=1, source_target_pairs={{8,16},{24,32},{40,48},{56,64},{72,80},{88,96},{104,112},{120,128}... | collective-permute-start | bytes 196616 | tf_op jit(solution)/shard_map/ppermute | solution.py:411
  133.8 4.4 %collective-permute-start.13 = (f32[2,8,8,128]{3,2,1,0:T(8,128)S(1)}, f32[2,8,8,128]{3,2,1,0:T(8,128)S(1)}, u32[]{:S(2)}, u32[]{:S(2)}) collective-permute-start(f32[2,8,8,128]{3,2,1,0:T(8,128)S(1)} %get-tuple-element.52), channel_id=1, source_target_pairs={{0,8},{8,0},{16,24},{24,16},{32,40},{40,32},{48,56},{56,48},{64,72... | collective-permute-start | bytes 196616 | tf_op jit(solution)/shard_map/ppermute | solution.py:412
  139.0 6.2 %collective-permute-start.16 = (f32[8,32,128]{2,1,0:T(8,128)S(1)}, f32[8,32,128]{2,1,0:T(8,128)S(1)}, u32[]{:S(2)}, u32[]{:S(2)}) collective-permute-start(f32[8,32,128]{2,1,0:T(8,128)S(1)} %get-tuple-element.53.refs_0_), channel_id=1, source_target_pairs={{0,8},{8,16},{16,24},{24,0},{1,9},{9,17},{17,25},{25,1},{2,10},{10... | collective-permute-start | bytes 393224 | tf_op jit(solution)/shard_map/ppermute | solution.py:417
  139.1 6.2 %collective-permute-start.15 = (f32[8,32,128]{2,1,0:T(8,128)S(1)}, f32[8,32,128]{2,1,0:T(8,128)S(1)}, u32[]{:S(2)}, u32[]{:S(2)}) collective-permute-start(f32[8,32,128]{2,1,0:T(8,128)S(1)} %get-tuple-element.54.refs_1_), channel_id=1, source_target_pairs={{0,24},{8,0},{16,8},{24,16},{1,25},{9,1},{17,9},{25,17},{2,26},{10... | collective-permute-start | bytes 393224 | tf_op jit(solution)/shard_map/ppermute | solution.py:417
  142.3 6.6 %collective-permute-start.14 = (f32[8,32,128]{2,1,0:T(8,128)S(1)}, f32[8,32,128]{2,1,0:T(8,128)S(1)}, u32[]{:S(2)}, u32[]{:S(2)}) collective-permute-start(f32[8,32,128]{2,1,0:T(8,128)S(1)} %get-tuple-element.53.refs_0_), channel_id=1, source_target_pairs={{0,24},{8,0},{16,8},{24,16},{1,25},{9,1},{17,9},{25,17},{2,26},{10... | collective-permute-start | bytes 393224 | tf_op jit(solution)/shard_map/ppermute | solution.py:417
  143.5 6.2 %collective-permute-start.19 = (f32[8,32,128]{2,1,0:T(8,128)S(1)}, f32[8,32,128]{2,1,0:T(8,128)S(1)}, u32[]{:S(2)}, u32[]{:S(2)}) collective-permute-start(f32[8,32,128]{2,1,0:T(8,128)S(1)} %get-tuple-element.54.refs_1_), channel_id=1, source_target_pairs={{0,8},{8,16},{16,24},{24,0},{1,9},{9,17},{17,25},{25,1},{2,10},{10... | collective-permute-start | bytes 393224 | tf_op jit(solution)/shard_map/ppermute | solution.py:417
  145.2 6.2 %collective-permute-start.17 = (f32[8,32,128]{2,1,0:T(8,128)S(1)}, f32[8,32,128]{2,1,0:T(8,128)S(1)}, u32[]{:S(2)}, u32[]{:S(2)}) collective-permute-start(f32[8,32,128]{2,1,0:T(8,128)S(1)} %collective-permute-done.16.refs_6_), channel_id=1, source_target_pairs={{0,8},{8,16},{16,24},{24,0},{1,9},{9,17},{17,25},{25,1},{2,10},{10... | collective-permute-start | bytes 393224 | tf_op jit(solution)/shard_map/ppermute | solution.py:417
  145.2 6.2 %collective-permute-start.18 = (f32[8,32,128]{2,1,0:T(8,128)S(1)}, f32[8,32,128]{2,1,0:T(8,128)S(1)}, u32[]{:S(2)}, u32[]{:S(2)}) collective-permute-start(f32[8,32,128]{2,1,0:T(8,128)S(1)} %collective-permute-done.15.refs_3_), channel_id=1, source_target_pairs={{0,24},{8,0},{16,8},{24,16},{1,25},{9,1},{17,9},{25,17},{2,26},{10... | collective-permute-start | bytes 393224 | tf_op jit(solution)/shard_map/ppermute | solution.py:417

commit v11 on v10

--- a/solution.py
+++ b/solution.py
@@ -17,24 +17,30 @@
 TRIM = 4
 
 
+def div_mod(x, n):
+    if n & (n - 1):
+        return x // n, x % n
+    return lax.shift_right_logical(x, n.bit_length() - 1), x & (n - 1)
+
+
 def lane_sum(x):
     return jnp.sum(x, axis=1, keepdims=True)
 
 
-def pack_kernel(geo, shift_ref, id_ref, target_ref, views_ref, out_ref, rolled, pos_v, pos_s, sem):
+def pack_kernel(geo, shift_ref, target_ref, views_ref, out_ref, rolled, pos_v, pos_s, sem):
     peers, cap, x_cells, y_cells, brick_cols, row_count, all_cols, view_count = geo
     groups = brick_cols * x_cells
     rows_per = cap + 1
     t = target_ref[...]
-    bz = t % brick_cols
-    column = t // brick_cols % all_cols
-    line = t // (brick_cols * all_cols)
-    dest = column // y_cells * row_count + line // x_cells
-    part = y_cells // view_count
-    y = column % y_cells
-    turned = (y // part + view_count - id_ref[0]) % view_count
-    slot = ((turned * brick_cols + bz) * x_cells + line % x_cells) * part + y % part + 1
-    high, low = slot // 64, slot % 64
+    t, bz = div_mod(t, brick_cols)
+    line, column = div_mod(t, all_cols)
+    block, y = div_mod(column, y_cells)
+    row, x = div_mod(line, x_cells)
+    dest = block * row_count + row
+    quarter, y = div_mod(y, y_cells // view_count)
+    quarter = jnp.where(block % 2 == 1, view_count - 1 - quarter, quarter)
+    slot = ((quarter * brick_cols + bz) * x_cells + x) * (y_cells // view_count) + y + 1
+    high, low = div_mod(slot, 64)
     peer_id = lax.broadcasted_iota(jnp.int32, (peers, y_cells), 0)
     before = (
         lax.broadcasted_iota(jnp.int32, (y_cells, y_cells), 0)
@@ -84,14 +90,13 @@
     lax.fori_loop(0, groups, body, 0)
 
 
-def pack(shift, ids, target, views, geo):
+def pack(shift, target, views, geo):
     peers, cap, x_cells, y_cells, brick_cols, row_count, all_cols, view_count = geo
     groups = brick_cols * x_cells
     return pl.pallas_call(
         functools.partial(pack_kernel, geo),
         out_shape=jax.ShapeDtypeStruct((peers * (cap + 1), 1, BRICK), jnp.float32),
         in_specs=[
-            pl.BlockSpec(memory_space=pltpu.SMEM),
             pl.BlockSpec(memory_space=pltpu.SMEM),
             pl.BlockSpec(memory_space=pltpu.VMEM),
             pl.BlockSpec(memory_space=pltpu.VMEM),
@@ -104,16 +109,20 @@
             pltpu.SemaphoreType.DMA,
         ],
         name="pack",
-    )(shift, ids, target, views)
-
-
-def unpack_kernel(peers, cap, slots, in_ref, *refs):
+    )(shift, target, views)
+
+
+def unpack_kernel(peers, cap, slots, id_ref, in_ref, *refs):
     outs, (placed, list_v, idx_v, idx_s, sem) = refs[:-5], refs[-5:]
     rows_per = cap + 1
     for p in range(peers):
         list_v[p : p + 1, :] = in_ref[p * rows_per + cap]
     e = list_v[...].astype(jnp.int32)
-    idx_v[...] = jnp.where(e > 0, e - 1, slots)
+    views, size = len(outs), slots // len(outs)
+    quarter, rest = div_mod(jnp.maximum(e - 1, 0), size)
+    turned = quarter - id_ref[0]
+    turned = jnp.where(turned < 0, turned + views, turned)
+    idx_v[...] = jnp.where(e > 0, turned * size + rest, slots)
     copy = pltpu.make_async_copy(idx_v, idx_s, sem)
     copy.start()
     copy.wait()
@@ -127,15 +136,14 @@
         return c
 
     lax.fori_loop(0, peers, per_peer, 0)
-    views, size = len(outs), slots // len(outs)
     for d, out in enumerate(outs):
         out[...] = placed[d * size : (d + 1) * size, :]
 
 
-def unpack(arrived, peers, cap, slots, views):
+def unpack(ids, arrived, peers, cap, slots, views):
     return call(
         functools.partial(unpack_kernel, peers, cap, slots), "unpack",
-        [f32(slots // views, BRICK)] * views, (arrived,), 0,
+        [f32(slots // views, BRICK)] * views, (ids, arrived),
         scratch=[
             pltpu.VMEM((slots + SPARE, BRICK), jnp.float32),
             pltpu.VMEM((peers, BRICK), jnp.float32),
@@ -218,7 +226,7 @@
 def part_kernel(id_ref, est, edge, out_ref, send_in, send_out, wide):
     x_cells, y_cells, _ = est.shape
     part = out_ref.shape[2] - 2 * TILE
-    start = pl.multiple_of(id_ref[0] * part, part)
+    start = pl.multiple_of(id_ref[2] * part, part)
     far = TILE + y_cells
 
     def body(x, carry):
@@ -349,7 +357,7 @@
     layers, rows = out_ref.shape[1:3]
     count = inner.shape[1]
     skip = (total.shape[1] - layers) // 2
-    odd, odd_part = id_ref[1], lax.rem(id_ref[0], 2)
+    odd, odd_part = id_ref[1], lax.rem(id_ref[2], 2)
     base = layers - count
     at_in = pl.ds(pl.multiple_of((1 - odd_part) * (rows - TILE), TILE), TILE)
     at_out = pl.ds(pl.multiple_of(odd_part * (rows - TILE), TILE), TILE)
@@ -372,7 +380,7 @@
 
 def update_kernel(views, id_ref, total, outer, inner, est, out_ref):
     layers, rows = out_ref.shape[1:3]
-    odd = lax.rem(id_ref[0], 2)
+    odd = lax.rem(id_ref[2], 2)
     at_in = pl.ds(pl.multiple_of((1 - odd) * (rows - TILE), TILE), TILE)
     at_out = pl.ds(pl.multiple_of(odd * (rows - TILE), TILE), TILE)
     for c in range(2):
@@ -384,7 +392,7 @@
 
 def finish_kernel(views, id_ref, total, outer, inner, est, out_a, out_b, wide):
     layers, rows = total.shape[1:3]
-    odd = lax.rem(id_ref[0], 2)
+    odd = lax.rem(id_ref[2], 2)
     at_in = pl.ds(pl.multiple_of((1 - odd) * (rows - TILE), TILE), TILE)
     at_out = pl.ds(pl.multiple_of(odd * (rows - TILE), TILE), TILE)
     own = slice(TRIM, rows - TRIM)
@@ -400,16 +408,34 @@
     pieces, out_ref = refs[: 2 * views], refs[2 * views]
     part = pieces[0].shape[1]
     for d in range(views):
-        at = pl.ds(pl.multiple_of(lax.rem(id_ref[0] + d, views) * part, part), part)
+        place = lax.rem(id_ref[0] + d, views)
+        place = jnp.where(id_ref[3] == 1, views - 1 - place, place)
+        at = pl.ds(pl.multiple_of(place * part, part), part)
         out_ref[:, at, 0:BRICK] = pieces[2 * d][...]
         out_ref[:, at, BRICK : 2 * BRICK] = pieces[2 * d + 1][...]
 
 
-def swap(inner, outer, axes):
-    count = lax.axis_size(axes)
-    links = [(i, i + 1) for i in range(1, count - 1, 2)]
-    outer = lax.ppermute(outer, axes, links + [(j, i) for i, j in links])
-    inner = lax.ppermute(inner, axes, [(i, i ^ 1) for i in range(count)])
+def snake(at, views):
+    block, quarter = divmod(at, views)
+    return block * views + (views - 1 - quarter if block % 2 else quarter)
+
+
+def both_ways(links):
+    return links + [(j, i) for i, j in links]
+
+
+def swap_layers(inner, outer):
+    count = lax.axis_size("rows")
+    outer = lax.ppermute(outer, "rows", both_ways([(i, i + 1) for i in range(1, count - 1, 2)]))
+    inner = lax.ppermute(inner, "rows", both_ways([(i, i + 1) for i in range(0, count, 2)]))
+    return outer, inner
+
+
+def swap_rows(inner, outer):
+    axes, views = ("blocks", "views"), lax.axis_size("views")
+    chain = [snake(i, views) for i in range(lax.axis_size(axes))]
+    outer = lax.ppermute(outer, axes, both_ways(list(zip(chain[1:-1:2], chain[2::2]))))
+    inner = lax.ppermute(inner, axes, both_ways(list(zip(chain[::2], chain[1::2]))))
     return outer, inner
 
 
@@ -430,19 +456,23 @@
     all_cols = y_cells * block_count
     geo = (peer_count, capacity, x_cells, y_cells, brick_cols, row_count, all_cols, view_count)
     row, place = lax.axis_index("rows"), lax.axis_index("views")
-    ids = jnp.stack([place, row % 2]).astype(jnp.int32)
-    chain = [(block * view_count - 1, block * view_count) for block in range(1, block_count)]
-    edge_at = jnp.where(place == 0, 0, y_cells - TILE)
+    turned = lax.axis_index("blocks") % 2
+    quarter = jnp.where(turned == 1, view_count - 1 - place, place)
+    borders = [
+        (snake(b * view_count - 1, view_count), snake(b * view_count, view_count))
+        for b in range(1, block_count)
+    ]
+    edge_at = jnp.where(quarter == 0, 0, y_cells - TILE)
     edge = lax.ppermute(
-        lax.dynamic_slice_in_dim(estimate, edge_at, TILE, 1),
-        ("blocks", "views"), chain + [(j, i) for i, j in chain],
-    )
-    outgoing = pack(shifts, ids, target[0].transpose(0, 2, 1), views_data[0], geo)
+        lax.dynamic_slice_in_dim(estimate, edge_at, TILE, 1), ("blocks", "views"), both_ways(borders)
+    )
+    outgoing = pack(shifts, target[0].transpose(0, 2, 1), views_data[0], geo)
     outgoing, edge = lax.optimization_barrier((outgoing, edge))
     arrived = lax.all_to_all(
         outgoing.reshape(peer_count, capacity + 1, 1, BRICK),
         ("blocks", "rows"), split_axis=0, concat_axis=0, tiled=True,
     ).reshape(peer_count * (capacity + 1), 1, BRICK)
+    ids = jnp.stack([place, row % 2, quarter, turned]).astype(jnp.int32)
     taps = lax.all_gather(psf_taps, "views", axis=0, tiled=True)
     w = (taps / jnp.sum(taps, axis=2, keepdims=True)).reshape(-1)
     halo = f32(2, HALO, part + 2 * TILE, BRICK)
@@ -452,24 +482,24 @@
         scratch=[pltpu.VMEM((2, y_cells + 2 * TILE, BRICK), jnp.float32)],
     )
     wide = [f32(2, x_cells + 2 * HALO, part + 2 * TRIM, BRICK)]
-    est = call(extend_kernel, "extend", wide, (ids, own, *swap(*sent, "rows")))[0]
+    est = call(extend_kernel, "extend", wide, (ids, own, *swap_layers(*sent)))[0]
     below = forward(w, est, view_count, x_cells)
     arrived, below = lax.optimization_barrier((arrived, below))
-    moved = unpack(arrived, peer_count, capacity, brick_count, view_count)
+    moved = unpack(ids, arrived, peer_count, capacity, brick_count, view_count)
     moved = [m.reshape(brick_cols, x_cells, part, BRICK) for m in moved]
     behind, ahead = turn(moved[1], 1, view_count), turn(moved[3], -1, view_count)
     across = turn(moved[2], 2, view_count)
     total = backward(w, ids, below, (0,), moved[:1], None, 0)[0]
     total = backward(w, ids, below, (3, 1), (behind, ahead), total, 0)[0]
     total, *sent = backward(w, ids, below, (2,), (across,), total, 2 * HALO)
-    total, *sent = merge(ids, total, *swap(*sent, "rows"), x_cells + 2 * HALO)
-    args = (ids, total, *swap(*sent, ("blocks", "views")), est)
+    total, *sent = merge(ids, total, *swap_layers(*sent), x_cells + 2 * HALO)
+    args = (ids, total, *swap_rows(*sent), est)
     est = call(functools.partial(update_kernel, view_count), "update", wide, args)[0]
     below = forward(w, est, view_count, x_cells)
     observed = (moved[0], ahead, across, behind)
     total, *sent = backward(w, ids, below, (0, 1, 2, 3), observed, None, HALO)
-    total, *sent = merge(ids, total, *swap(*sent, "rows"), x_cells)
-    args = (ids, total, *swap(*sent, ("blocks", "views")), est)
+    total, *sent = merge(ids, total, *swap_layers(*sent), x_cells)
+    args = (ids, total, *swap_rows(*sent), est)
     own = call(
         functools.partial(finish_kernel, view_count), "finish",
         [f32(x_cells, part, BRICK)] * 2, args,

time: 155 us -> 151 us (0.974)
  waiting for transfers between devices: 59.6 us -> 56.7 us
  starting transfers between devices: 48.5 us -> 46.9 us
    ppermute x10, waiting for transfers between devices: 20.2 us -> 17.8 us  [the longest x3 11.1 us: swap_layers(): lax.ppermute(outer, 'rows', both_ways([(i, i + 1) for i in range(1, count...]
    all_to_all x1, starting transfers between devices: 12.2 us -> 10.4 us  [per_device(): lax.all_to_all(outgoing.reshape(peer_count, capacity + 1, 1, BRICK), ('bl...]
  transfers between devices with their start and end apart: 21 -> 21, of which waited for: 12 -> 14; matrix products, arithmetic and copies ran while one was open for 1% -> 0% of each run, Pallas kernels for 9% -> 9%
where the time goes in v11:
time: 151 us; the launch traced here: 148 us
  waiting for transfers between devices  56.7 us (38%)
  starting transfers between devices  46.9 us (31%)
  Pallas kernels  29.7 us (20%)
  blocking collectives  10.7 us (7%)
  local copies, waits for them, and re-layouts  3.5 us (2%)
    all_to_all x1, waiting for transfers between devices, per_device(): lax.all_to_all(outgoing.reshape(peer_count, capacity + 1, 1, BRICK), ('bl...  25.4 us
    pallas_call x14, Pallas kernels, call(): pl.pallas_call(kernel, out_shape=outs, in_specs=[smem()] * scalars + [vme...  23.8 us
    ppermute x9, starting transfers between devices, turn(): lax.ppermute(value, 'views', [(i, (i + step) % count) for i in range(coun...  13.6 us
    ppermute x9, waiting for transfers between devices, turn(): lax.ppermute(value, 'views', [(i, (i + step) % count) for i in range(coun...  13.4 us
    ppermute x3, waiting for transfers between devices, swap_layers(): lax.ppermute(outer, 'rows', both_ways([(i, i + 1) for i in range(1, count...  11.1 us
    all_gather x1, blocking collectives, per_device(): taps = lax.all_gather(psf_taps, 'views', axis=0, tiled=True)  10.7 us
    all_to_all x1, starting transfers between devices, per_device(): lax.all_to_all(outgoing.reshape(peer_count, capacity + 1, 1, BRICK), ('bl...  10.4 us
    ppermute x2, starting transfers between devices, swap_rows(): lax.ppermute(outer, axes, both_ways(list(zip(chain[1:-1:2], chain[2::2]))))  5.94 us
  transfers between devices with their start and end apart: 21, of which 14 were waited for; matrix products, arithmetic and copies ran while one was open for 0% of the time, Pallas kernels for 9%

profile of v11, /device:TPU:34, one launch (start us, length us, event | category | flops | bytes accessed | tf_op | source)
XLA Modules:
  0.0 148.5 jit_solution(13165135944300404948)
XLA Ops:
  0.8 3.8 %collective-permute-start = (f32[8,8,256]{2,1,0:T(8,128)S(1)}, f32[8,8,256]{2,1,0:T(8,128)S(1)}, u32[]{:S(2)}, u32[]{:S(2)}) collective-permute-start(f32[8,8,256]{2,1,0:T(8,128)S(1)} %constant_dynamic-slice_fusion), channel_id=1, source_target_pairs={{24,56},{32,64},{88,120},{96,128},{152,184},{160,192},{216,248},{5... | collective-permute-start | bytes 196616 | tf_op jit(solution)/shard_map/ppermute | solution.py:466
  5.3 5.9 %pack.1 = f32[4160,1,128]{2,1,0:T(1,128)} custom-call(s32[1]{0:T(128)S(6)} %copy.9.shift_ref, s32[8,2,128]{2,1,0:T(2,128)} %bitcast.23, f32[8,128,256]{2,1,0:T(8,128)} %bitcast.22), custom_call_target="tpu_custom_call" | custom-call | tf_op jit(solution)/shard_map/pack/pallas_call | solution.py:96
  11.3 10.4 %all-to-all-start = ((f32[64,65,1,128]{3,2,1,0:T(1,128)}), f32[64,65,1,128]{3,2,1,0:T(1,128)S(1)}, u32[]{:S(2)}, u32[]{:S(2)}) async-start(f32[64,65,1,128]{3,2,1,0:T(1,128)} %bitcast.21), calls=%async_computation | async-start | bytes 4259840 | tf_op jit(solution)/shard_map/all_to_all | solution.py:471
  21.7 10.7 %all_gather.3 = f32[4,3,7]{2,1,0:T(4,128)S(1)} all-gather(f32[1,3,7]{2,1,0:T(4,128)S(1)} %copy.8), channel_id=1, replica_groups=mesh['blocks'=8,'views'=4,'rows'=8] {'views'}, dimensions={0}, use_global_device_ids=true | all-gather | bytes 420 | tf_op jit(solution)/shard_map/all_gather | solution.py:476
  34.0 1.9 %collective-permute-start.1 = (f32[2,3,48,128]{3,2,1,0:T(8,128)S(1)}, f32[2,3,48,128]{3,2,1,0:T(8,128)S(1)}, u32[]{:S(2)}, u32[]{:S(2)}) collective-permute-start(f32[2,3,48,128]{3,2,1,0:T(8,128)S(1)} %get-tuple-element.33), channel_id=1, source_target_pairs={{1,2},{3,4},{5,6},{2,1},{4,3},{6,5},{9,10},{11,12},{13,14},{10,9},... | collective-permute-start | bytes 442376 | tf_op jit(solution)/shard_map/ppermute | solution.py:429
  35.9 1.7 %collective-permute-start.2 = (f32[2,3,48,128]{3,2,1,0:T(8,128)S(1)}, f32[2,3,48,128]{3,2,1,0:T(8,128)S(1)}, u32[]{:S(2)}, u32[]{:S(2)}) collective-permute-start(f32[2,3,48,128]{3,2,1,0:T(8,128)S(1)} %get-tuple-element.34), channel_id=1, source_target_pairs={{0,1},{2,3},{4,5},{6,7},{1,0},{3,2},{5,4},{7,6},{8,9},{10,11},{12,... | collective-permute-start | bytes 442376 | tf_op jit(solution)/shard_map/ppermute | solution.py:430
  37.7 4.3 %collective-permute-done.1.outer = f32[2,3,48,128]{3,2,1,0:T(8,128)S(1)} collective-permute-done((f32[2,3,48,128]{3,2,1,0:T(8,128)S(1)}, f32[2,3,48,128]{3,2,1,0:T(8,128)S(1)}, u32[]{:S(2)}, u32[]{:S(2)}) %collective-permute-start.1) | collective-permute-done | bytes 147488 | tf_op jit(solution)/shard_map/ppermute | solution.py:429
  43.7 2.9 %forward.2.below = f32[4,2,8,32,128]{4,3,2,1,0:T(8,128)S(1)} custom-call(f32[84]{0:T(128)S(1)} %reshape.22.w_ref, f32[2,14,40,128]{3,2,1,0:T(8,128)S(1)} %extend.1.est), custom_call_target="tpu_custom_call" | custom-call | flops 1000 | bytes 1000 | tf_op jit(solution)/shard_map/forward/pallas_call | solution.py:170
  47.3 25.4 %all-to-all-done = f32[64,65,1,128]{3,2,1,0:T(1,128)S(1)} async-done(((f32[64,65,1,128]{3,2,1,0:T(1,128)}), f32[64,65,1,128]{3,2,1,0:T(1,128)S(1)}, u32[]{:S(2)}, u32[]{:S(2)}) %all-to-all-start) | async-done | bytes 2129952 | tf_op jit(solution)/shard_map/all_to_all | solution.py:471
  72.8 5.3 %unpack.1 = (f32[512,128]{1,0:T(8,128)S(1)}, f32[512,128]{1,0:T(8,128)S(1)}, f32[512,128]{1,0:T(8,128)S(1)}, f32[512,128]{1,0:T(8,128)S(1)}) custom-call(s32[4]{0:T(128)S(1)} %pad_add_fusion.id_ref, f32[4160,1,128]{2,1,0:T(1,128)S(1)} %bitcast.15), custom_call_target="tpu_custom_call" | custom-call | flops 1000 | bytes 1000 | tf_op jit(solution)/shard_map/unpack/pallas_call | solution.py:170
  78.1 3.5 %collective-permute-start.5 = (f32[2,8,32,128]{3,2,1,0:T(8,128)S(1)}, f32[2,8,32,128]{3,2,1,0:T(8,128)S(1)}, u32[]{:S(2)}, u32[]{:S(2)}) collective-permute-start(f32[2,8,32,128]{3,2,1,0:T(8,128)S(1)} %bitcast.19), channel_id=1, source_target_pairs={{0,24},{8,0},{16,8},{24,16},{1,25},{9,1},{17,9},{25,17},{2,26},{10... | collective-permute-start | bytes 786440 | tf_op jit(solution)/shard_map/ppermute | solution.py:443
  84.2 3.6 %collective-permute-done.4.refs_0_.refs_3_ = f32[2,8,32,128]{3,2,1,0:T(8,128)S(1)} collective-permute-done((f32[2,8,32,128]{3,2,1,0:T(8,128)S(1)}, f32[2,8,32,128]{3,2,1,0:T(8,128)S(1)}, u32[]{:S(2)}, u32[]{:S(2)}) %collective-permute-start.4) | collective-permute-done | bytes 262176 | tf_op jit(solution)/shard_map/ppermute | solution.py:443
  87.9 5.0 %collective-permute-done.5.refs_1_ = f32[2,8,32,128]{3,2,1,0:T(8,128)S(1)} collective-permute-done((f32[2,8,32,128]{3,2,1,0:T(8,128)S(1)}, f32[2,8,32,128]{3,2,1,0:T(8,128)S(1)}, u32[]{:S(2)}, u32[]{:S(2)}) %collective-permute-start.5) | collective-permute-done | bytes 262176 | tf_op jit(solution)/shard_map/ppermute | solution.py:443
  92.8 1.8 %backward.5.refs_1_ = f32[2,14,40,128]{3,2,1,0:T(8,128)S(1)} custom-call(f32[84]{0:T(128)S(1)} %reshape.22.w_ref, s32[4]{0:T(128)S(1)} %pad_add_fusion.id_ref, f32[4,2,8,32,128]{4,3,2,1,0:T(8,128)S(1)} %forward.2.below, f32[2,8,32,128]{3,2,1,0:T(8,128)S(1)} %collective-permute-done.4.refs_0_.refs_3_, f32[2,8,32,128]{3,2,1,0:T(8,128)S(1)} %collective-permute-done.5.refs_1_, ...), custom_call_target="tpu_custom_call" | custom-call | flops 1000 | bytes 1000 | tf_op jit(solution)/shard_map/backward/pallas_call | solution.py:170
  95.9 1.9 %collective-permute-start.6 = (f32[2,6,40,128]{3,2,1,0:T(8,128)S(1)}, f32[2,6,40,128]{3,2,1,0:T(8,128)S(1)}, u32[]{:S(2)}, u32[]{:S(2)}) collective-permute-start(f32[2,6,40,128]{3,2,1,0:T(8,128)S(1)} %get-tuple-element.42), channel_id=1, source_target_pairs={{1,2},{3,4},{5,6},{2,1},{4,3},{6,5},{9,10},{11,12},{13,14},{10,9},... | collective-permute-start | bytes 737288 | tf_op jit(solution)/shard_map/ppermute | solution.py:429
  97.9 1.7 %collective-permute-start.7 = (f32[2,6,40,128]{3,2,1,0:T(8,128)S(1)}, f32[2,6,40,128]{3,2,1,0:T(8,128)S(1)}, u32[]{:S(2)}, u32[]{:S(2)}) collective-permute-start(f32[2,6,40,128]{3,2,1,0:T(8,128)S(1)} %get-tuple-element.43), channel_id=1, source_target_pairs={{0,1},{2,3},{4,5},{6,7},{1,0},{3,2},{5,4},{7,6},{8,9},{10,11},{12,... | collective-permute-start | bytes 737288 | tf_op jit(solution)/shard_map/ppermute | solution.py:430
  99.5 3.9 %collective-permute-done.6.outer = f32[2,6,40,128]{3,2,1,0:T(8,128)S(1)} collective-permute-done((f32[2,6,40,128]{3,2,1,0:T(8,128)S(1)}, f32[2,6,40,128]{3,2,1,0:T(8,128)S(1)}, u32[]{:S(2)}, u32[]{:S(2)}) %collective-permute-start.6) | collective-permute-done | bytes 245792 | tf_op jit(solution)/shard_map/ppermute | solution.py:429
  104.1 2.3 %collective-permute-start.8 = (f32[2,14,8,128]{3,2,1,0:T(8,128)S(1)}, f32[2,14,8,128]{3,2,1,0:T(8,128)S(1)}, u32[]{:S(2)}, u32[]{:S(2)}) collective-permute-start(f32[2,14,8,128]{3,2,1,0:T(8,128)S(1)} %get-tuple-element.45), channel_id=1, source_target_pairs={{8,16},{24,56},{48,40},{32,64},{72,80},{88,120},{112,104},{96,128}... | collective-permute-start | bytes 344072 | tf_op jit(solution)/shard_map/ppermute | solution.py:437
  107.5 3.7 %collective-permute-done.8.outer = f32[2,14,8,128]{3,2,1,0:T(8,128)S(1)} collective-permute-done((f32[2,14,8,128]{3,2,1,0:T(8,128)S(1)}, f32[2,14,8,128]{3,2,1,0:T(8,128)S(1)}, u32[]{:S(2)}, u32[]{:S(2)}) %collective-permute-start.8) | collective-permute-done | bytes 114720 | tf_op jit(solution)/shard_map/ppermute | solution.py:437
  112.2 2.9 %forward.3.below = f32[4,2,8,32,128]{4,3,2,1,0:T(8,128)S(1)} custom-call(f32[84]{0:T(128)S(1)} %reshape.22.w_ref, f32[2,14,40,128]{3,2,1,0:T(8,128)S(1)} %update.1.est), custom_call_target="tpu_custom_call" | custom-call | flops 1000 | bytes 1000 | tf_op jit(solution)/shard_map/forward/pallas_call | solution.py:170
  115.0 2.8 %backward.7 = (f32[2,14,40,128]{3,2,1,0:T(8,128)S(1)}, f32[2,3,40,128]{3,2,1,0:T(8,128)S(1)}, f32[2,3,40,128]{3,2,1,0:T(8,128)S(1)}) custom-call(f32[84]{0:T(128)S(1)} %reshape.22.w_ref, s32[4]{0:T(128)S(1)} %pad_add_fusion.id_ref, f32[4,2,8,32,128]{4,3,2,1,0:T(8,128)S(1)} %forward.3.below, f32[2,8,32,128]{3,2,1,0:T(8,128)S(1)} %bitcast.17, ...), custom_call_target="tpu_custom_call" | custom-call | flops 1000 | bytes 1000 | tf_op jit(solution)/shard_map/backward/pallas_call | solution.py:170
  117.9 1.9 %collective-permute-start.10 = (f32[2,3,40,128]{3,2,1,0:T(8,128)S(1)}, f32[2,3,40,128]{3,2,1,0:T(8,128)S(1)}, u32[]{:S(2)}, u32[]{:S(2)}) collective-permute-start(f32[2,3,40,128]{3,2,1,0:T(8,128)S(1)} %get-tuple-element.48), channel_id=1, source_target_pairs={{1,2},{3,4},{5,6},{2,1},{4,3},{6,5},{9,10},{11,12},{13,14},{10,9},... | collective-permute-start | bytes 368648 | tf_op jit(solution)/shard_map/ppermute | solution.py:429
  121.2 2.9 %collective-permute-done.10.outer = f32[2,3,40,128]{3,2,1,0:T(8,128)S(1)} collective-permute-done((f32[2,3,40,128]{3,2,1,0:T(8,128)S(1)}, f32[2,3,40,128]{3,2,1,0:T(8,128)S(1)}, u32[]{:S(2)}, u32[]{:S(2)}) %collective-permute-start.10) | collective-permute-done | bytes 122912 | tf_op jit(solution)/shard_map/ppermute | solution.py:429
  124.7 3.6 %collective-permute-start.12 = (f32[2,8,8,128]{3,2,1,0:T(8,128)S(1)}, f32[2,8,8,128]{3,2,1,0:T(8,128)S(1)}, u32[]{:S(2)}, u32[]{:S(2)}) collective-permute-start(f32[2,8,8,128]{3,2,1,0:T(8,128)S(1)} %get-tuple-element.51), channel_id=1, source_target_pairs={{8,16},{24,56},{48,40},{32,64},{72,80},{88,120},{112,104},{96,128}... | collective-permute-start | bytes 196616 | tf_op jit(solution)/shard_map/ppermute | solution.py:437
  128.4 1.7 %collective-permute-start.13 = (f32[2,8,8,128]{3,2,1,0:T(8,128)S(1)}, f32[2,8,8,128]{3,2,1,0:T(8,128)S(1)}, u32[]{:S(2)}, u32[]{:S(2)}) collective-permute-start(f32[2,8,8,128]{3,2,1,0:T(8,128)S(1)} %get-tuple-element.52), channel_id=1, source_target_pairs={{0,8},{16,24},{56,48},{40,32},{64,72},{80,88},{120,112},{104,96},{... | collective-permute-start | bytes 196616 | tf_op jit(solution)/shard_map/ppermute | solution.py:438
  130.9 1.8 %collective-permute-done.13.inner = f32[2,8,8,128]{3,2,1,0:T(8,128)S(1)} collective-permute-done((f32[2,8,8,128]{3,2,1,0:T(8,128)S(1)}, f32[2,8,8,128]{3,2,1,0:T(8,128)S(1)}, u32[]{:S(2)}, u32[]{:S(2)}) %collective-permute-start.13) | collective-permute-done | bytes 65568 | tf_op jit(solution)/shard_map/ppermute | solution.py:438
  133.5 1.7 %collective-permute-start.16 = (f32[8,32,128]{2,1,0:T(8,128)S(1)}, f32[8,32,128]{2,1,0:T(8,128)S(1)}, u32[]{:S(2)}, u32[]{:S(2)}) collective-permute-start(f32[8,32,128]{2,1,0:T(8,128)S(1)} %get-tuple-element.53.refs_0_), channel_id=1, source_target_pairs={{0,8},{8,16},{16,24},{24,0},{1,9},{9,17},{17,25},{25,1},{2,10},{10... | collective-permute-start | bytes 393224 | tf_op jit(solution)/shard_map/ppermute | solution.py:443
  135.2 2.1 %collective-permute-start.15 = (f32[8,32,128]{2,1,0:T(8,128)S(1)}, f32[8,32,128]{2,1,0:T(8,128)S(1)}, u32[]{:S(2)}, u32[]{:S(2)}) collective-permute-start(f32[8,32,128]{2,1,0:T(8,128)S(1)} %get-tuple-element.54.refs_1_), channel_id=1, source_target_pairs={{0,24},{8,0},{16,8},{24,16},{1,25},{9,1},{17,9},{25,17},{2,26},{10... | collective-permute-start | bytes 393224 | tf_op jit(solution)/shard_map/ppermute | solution.py:443
  137.4 1.9 %collective-permute-start.14 = (f32[8,32,128]{2,1,0:T(8,128)S(1)}, f32[8,32,128]{2,1,0:T(8,128)S(1)}, u32[]{:S(2)}, u32[]{:S(2)}) collective-permute-start(f32[8,32,128]{2,1,0:T(8,128)S(1)} %get-tuple-element.53.refs_0_), channel_id=1, source_target_pairs={{0,24},{8,0},{16,8},{24,16},{1,25},{9,1},{17,9},{25,17},{2,26},{10... | collective-permute-start | bytes 393224 | tf_op jit(solution)/shard_map/ppermute | solution.py:443
  141.5 2.5 %collective-permute-start.18 = (f32[8,32,128]{2,1,0:T(8,128)S(1)}, f32[8,32,128]{2,1,0:T(8,128)S(1)}, u32[]{:S(2)}, u32[]{:S(2)}) collective-permute-start(f32[8,32,128]{2,1,0:T(8,128)S(1)} %collective-permute-done.15.refs_3_), channel_id=1, source_target_pairs={{0,24},{8,0},{16,8},{24,16},{1,25},{9,1},{17,9},{25,17},{2,26},{10... | collective-permute-start | bytes 393224 | tf_op jit(solution)/shard_map/ppermute | solution.py:443
  144.0 1.5 collective-permute-done.19.refs_7_
  146.9 1.6 %join.1 = f32[8,128,256]{2,1,0:T(8,128)} custom-call(s32[4]{0:T(128)S(1)} %pad_add_fusion.id_ref, f32[8,32,128]{2,1,0:T(8,128)S(1)} %get-tuple-element.53.refs_0_, f32[8,32,128]{2,1,0:T(8,128)S(1)} %get-tuple-element.54.refs_1_, f32[8,32,128]{2,1,0:T(8,128)S(1)} %collective-permute-done.14.refs_2_, f32[8,32,128]{2,1,0:T(8,128)S(1)} %collective-permute-done.15.refs_3_, ...), custom_call_target="tpu_custom_call" | custom-call | flops 1000 | bytes 1000 | tf_op jit(solution)/shard_map/join/pallas_call | solution.py:170
  (43 shorter events, 18.9 us)
Async XLA Ops:
  0.8 10.4 %collective-permute-start = (f32[8,8,256]{2,1,0:T(8,128)S(1)}, f32[8,8,256]{2,1,0:T(8,128)S(1)}, u32[]{:S(2)}, u32[]{:S(2)}) collective-permute-start(f32[8,8,256]{2,1,0:T(8,128)S(1)} %constant_dynamic-slice_fusion), channel_id=1, source_target_pairs={{24,56},{32,64},{88,120},{96,128},{152,184},{160,192},{216,248},{5... | collective-permute-start | bytes 196616 | tf_op jit(solution)/shard_map/ppermute | solution.py:466
  11.3 10.4 %copy-start.5 = (f32[1,3,7]{2,0,1:T(1,128)S(1)}, f32[1,3,7]{2,0,1:T(1,128)}, u32[]{:S(2)}) copy-start(f32[1,3,7]{2,0,1:T(1,128)} %param.8) | copy-start | bytes 256
  11.3 21.2 %copy-start.2 = (f32[8,128,256]{2,1,0:T(8,128)S(1)}, f32[8,128,256]{2,1,0:T(8,128)}, u32[]{:S(2)}) copy-start(f32[8,128,256]{2,1,0:T(8,128)} %est.1) | copy-start | bytes 3145732
  11.3 61.5 %all-to-all-start = ((f32[64,65,1,128]{3,2,1,0:T(1,128)}), f32[64,65,1,128]{3,2,1,0:T(1,128)S(1)}, u32[]{:S(2)}, u32[]{:S(2)}) async-start(f32[64,65,1,128]{3,2,1,0:T(1,128)} %bitcast.21), calls=%async_computation | async-start | bytes 4259840 | tf_op jit(solution)/shard_map/all_to_all | solution.py:471
  33.2 0.7 copy-start.3
  34.0 8.1 %collective-permute-start.1 = (f32[2,3,48,128]{3,2,1,0:T(8,128)S(1)}, f32[2,3,48,128]{3,2,1,0:T(8,128)S(1)}, u32[]{:S(2)}, u32[]{:S(2)}) collective-permute-start(f32[2,3,48,128]{3,2,1,0:T(8,128)S(1)} %get-tuple-element.33), channel_id=1, source_target_pairs={{1,2},{3,4},{5,6},{2,1},{4,3},{6,5},{9,10},{11,12},{13,14},{10,9},... | collective-permute-start | bytes 442376 | tf_op jit(solution)/shard_map/ppermute | solution.py:429
  35.9 6.2 %collective-permute-start.2 = (f32[2,3,48,128]{3,2,1,0:T(8,128)S(1)}, f32[2,3,48,128]{3,2,1,0:T(8,128)S(1)}, u32[]{:S(2)}, u32[]{:S(2)}) collective-permute-start(f32[2,3,48,128]{3,2,1,0:T(8,128)S(1)} %get-tuple-element.34), channel_id=1, source_target_pairs={{0,1},{2,3},{4,5},{6,7},{1,0},{3,2},{5,4},{7,6},{8,9},{10,11},{12,... | collective-permute-start | bytes 442376 | tf_op jit(solution)/shard_map/ppermute | solution.py:430
  42.1 1.0 copy-start.4
  46.5 0.8 copy-start
  78.1 9.8 %collective-permute-start.4 = (f32[2,8,32,128]{3,2,1,0:T(8,128)S(1)}, f32[2,8,32,128]{3,2,1,0:T(8,128)S(1)}, u32[]{:S(2)}, u32[]{:S(2)}) collective-permute-start(f32[2,8,32,128]{3,2,1,0:T(8,128)S(1)} %bitcast.20), channel_id=1, source_target_pairs={{0,8},{8,16},{16,24},{24,0},{1,9},{9,17},{17,25},{25,1},{2,10},{10... | collective-permute-start | bytes 786440 | tf_op jit(solution)/shard_map/ppermute | solution.py:443
  78.1 14.7 %collective-permute-start.5 = (f32[2,8,32,128]{3,2,1,0:T(8,128)S(1)}, f32[2,8,32,128]{3,2,1,0:T(8,128)S(1)}, u32[]{:S(2)}, u32[]{:S(2)}) collective-permute-start(f32[2,8,32,128]{3,2,1,0:T(8,128)S(1)} %bitcast.19), channel_id=1, source_target_pairs={{0,24},{8,0},{16,8},{24,16},{1,25},{9,1},{17,9},{25,17},{2,26},{10... | collective-permute-start | bytes 786440 | tf_op jit(solution)/shard_map/ppermute | solution.py:443
  81.7 13.0 %collective-permute-start.3 = (f32[2,8,32,128]{3,2,1,0:T(8,128)S(1)}, f32[2,8,32,128]{3,2,1,0:T(8,128)S(1)}, u32[]{:S(2)}, u32[]{:S(2)}) collective-permute-start(f32[2,8,32,128]{3,2,1,0:T(8,128)S(1)} %bitcast.18), channel_id=1, source_target_pairs={{0,16},{8,24},{16,0},{24,8},{1,17},{9,25},{17,1},{25,9},{2,18},{10... | collective-permute-start | bytes 786440 | tf_op jit(solution)/shard_map/ppermute | solution.py:443
  94.6 16.9 %copy-start.1 = (f32[2,14,40,128]{3,2,1,0:T(8,128)S(1)}, f32[2,14,40,128]{3,2,1,0:T(8,128)}, u32[]{:S(2)}) copy-start(f32[2,14,40,128]{3,2,1,0:T(8,128)} %copy-done) | copy-start | bytes 1720324
  95.9 7.5 %collective-permute-start.6 = (f32[2,6,40,128]{3,2,1,0:T(8,128)S(1)}, f32[2,6,40,128]{3,2,1,0:T(8,128)S(1)}, u32[]{:S(2)}, u32[]{:S(2)}) collective-permute-start(f32[2,6,40,128]{3,2,1,0:T(8,128)S(1)} %get-tuple-element.42), channel_id=1, source_target_pairs={{1,2},{3,4},{5,6},{2,1},{4,3},{6,5},{9,10},{11,12},{13,14},{10,9},... | collective-permute-start | bytes 737288 | tf_op jit(solution)/shard_map/ppermute | solution.py:429
  97.9 5.6 %collective-permute-start.7 = (f32[2,6,40,128]{3,2,1,0:T(8,128)S(1)}, f32[2,6,40,128]{3,2,1,0:T(8,128)S(1)}, u32[]{:S(2)}, u32[]{:S(2)}) collective-permute-start(f32[2,6,40,128]{3,2,1,0:T(8,128)S(1)} %get-tuple-element.43), channel_id=1, source_target_pairs={{0,1},{2,3},{4,5},{6,7},{1,0},{3,2},{5,4},{7,6},{8,9},{10,11},{12,... | collective-permute-start | bytes 737288 | tf_op jit(solution)/shard_map/ppermute | solution.py:430
  104.1 7.1 %collective-permute-start.8 = (f32[2,14,8,128]{3,2,1,0:T(8,128)S(1)}, f32[2,14,8,128]{3,2,1,0:T(8,128)S(1)}, u32[]{:S(2)}, u32[]{:S(2)}) collective-permute-start(f32[2,14,8,128]{3,2,1,0:T(8,128)S(1)} %get-tuple-element.45), channel_id=1, source_target_pairs={{8,16},{24,56},{48,40},{32,64},{72,80},{88,120},{112,104},{96,128}... | collective-permute-start | bytes 344072 | tf_op jit(solution)/shard_map/ppermute | solution.py:437
  106.4 5.1 %collective-permute-start.9 = (f32[2,14,8,128]{3,2,1,0:T(8,128)S(1)}, f32[2,14,8,128]{3,2,1,0:T(8,128)S(1)}, u32[]{:S(2)}, u32[]{:S(2)}) collective-permute-start(f32[2,14,8,128]{3,2,1,0:T(8,128)S(1)} %get-tuple-element.46), channel_id=1, source_target_pairs={{0,8},{16,24},{56,48},{40,32},{64,72},{80,88},{120,112},{104,96},{... | collective-permute-start | bytes 344072 | tf_op jit(solution)/shard_map/ppermute | solution.py:438
  117.9 6.2 %collective-permute-start.10 = (f32[2,3,40,128]{3,2,1,0:T(8,128)S(1)}, f32[2,3,40,128]{3,2,1,0:T(8,128)S(1)}, u32[]{:S(2)}, u32[]{:S(2)}) collective-permute-start(f32[2,3,40,128]{3,2,1,0:T(8,128)S(1)} %get-tuple-element.48), channel_id=1, source_target_pairs={{1,2},{3,4},{5,6},{2,1},{4,3},{6,5},{9,10},{11,12},{13,14},{10,9},... | collective-permute-start | bytes 368648 | tf_op jit(solution)/shard_map/ppermute | solution.py:429
  119.8 4.3 %collective-permute-start.11 = (f32[2,3,40,128]{3,2,1,0:T(8,128)S(1)}, f32[2,3,40,128]{3,2,1,0:T(8,128)S(1)}, u32[]{:S(2)}, u32[]{:S(2)}) collective-permute-start(f32[2,3,40,128]{3,2,1,0:T(8,128)S(1)} %get-tuple-element.49), channel_id=1, source_target_pairs={{0,1},{2,3},{4,5},{6,7},{1,0},{3,2},{5,4},{7,6},{8,9},{10,11},{12,... | collective-permute-start | bytes 368648 | tf_op jit(solution)/shard_map/ppermute | solution.py:430
  124.7 6.2 %collective-permute-start.12 = (f32[2,8,8,128]{3,2,1,0:T(8,128)S(1)}, f32[2,8,8,128]{3,2,1,0:T(8,128)S(1)}, u32[]{:S(2)}, u32[]{:S(2)}) collective-permute-start(f32[2,8,8,128]{3,2,1,0:T(8,128)S(1)} %get-tuple-element.51), channel_id=1, source_target_pairs={{8,16},{24,56},{48,40},{32,64},{72,80},{88,120},{112,104},{96,128}... | collective-permute-start | bytes 196616 | tf_op jit(solution)/shard_map/ppermute | solution.py:437
  128.4 4.4 %collective-permute-start.13 = (f32[2,8,8,128]{3,2,1,0:T(8,128)S(1)}, f32[2,8,8,128]{3,2,1,0:T(8,128)S(1)}, u32[]{:S(2)}, u32[]{:S(2)}) collective-permute-start(f32[2,8,8,128]{3,2,1,0:T(8,128)S(1)} %get-tuple-element.52), channel_id=1, source_target_pairs={{0,8},{16,24},{56,48},{40,32},{64,72},{80,88},{120,112},{104,96},{... | collective-permute-start | bytes 196616 | tf_op jit(solution)/shard_map/ppermute | solution.py:438
  133.5 6.7 %collective-permute-start.16 = (f32[8,32,128]{2,1,0:T(8,128)S(1)}, f32[8,32,128]{2,1,0:T(8,128)S(1)}, u32[]{:S(2)}, u32[]{:S(2)}) collective-permute-start(f32[8,32,128]{2,1,0:T(8,128)S(1)} %get-tuple-element.53.refs_0_), channel_id=1, source_target_pairs={{0,8},{8,16},{16,24},{24,0},{1,9},{9,17},{17,25},{25,1},{2,10},{10... | collective-permute-start | bytes 393224 | tf_op jit(solution)/shard_map/ppermute | solution.py:443
  135.2 6.3 %collective-permute-start.15 = (f32[8,32,128]{2,1,0:T(8,128)S(1)}, f32[8,32,128]{2,1,0:T(8,128)S(1)}, u32[]{:S(2)}, u32[]{:S(2)}) collective-permute-start(f32[8,32,128]{2,1,0:T(8,128)S(1)} %get-tuple-element.54.refs_1_), channel_id=1, source_target_pairs={{0,24},{8,0},{16,8},{24,16},{1,25},{9,1},{17,9},{25,17},{2,26},{10... | collective-permute-start | bytes 393224 | tf_op jit(solution)/shard_map/ppermute | solution.py:443
  137.4 6.7 %collective-permute-start.14 = (f32[8,32,128]{2,1,0:T(8,128)S(1)}, f32[8,32,128]{2,1,0:T(8,128)S(1)}, u32[]{:S(2)}, u32[]{:S(2)}) collective-permute-start(f32[8,32,128]{2,1,0:T(8,128)S(1)} %get-tuple-element.53.refs_0_), channel_id=1, source_target_pairs={{0,24},{8,0},{16,8},{24,16},{1,25},{9,1},{17,9},{25,17},{2,26},{10... | collective-permute-start | bytes 393224 | tf_op jit(solution)/shard_map/ppermute | solution.py:443
  139.3 6.2 %collective-permute-start.19 = (f32[8,32,128]{2,1,0:T(8,128)S(1)}, f32[8,32,128]{2,1,0:T(8,128)S(1)}, u32[]{:S(2)}, u32[]{:S(2)}) collective-permute-start(f32[8,32,128]{2,1,0:T(8,128)S(1)} %get-tuple-element.54.refs_1_), channel_id=1, source_target_pairs={{0,8},{8,16},{16,24},{24,0},{1,9},{9,17},{17,25},{25,1},{2,10},{10... | collective-permute-start | bytes 393224 | tf_op jit(solution)/shard_map/ppermute | solution.py:443
  140.2 6.7 %collective-permute-start.17 = (f32[8,32,128]{2,1,0:T(8,128)S(1)}, f32[8,32,128]{2,1,0:T(8,128)S(1)}, u32[]{:S(2)}, u32[]{:S(2)}) collective-permute-start(f32[8,32,128]{2,1,0:T(8,128)S(1)} %collective-permute-done.16.refs_6_), channel_id=1, source_target_pairs={{0,8},{8,16},{16,24},{24,0},{1,9},{9,17},{17,25},{25,1},{2,10},{10... | collective-permute-start | bytes 393224 | tf_op jit(solution)/shard_map/ppermute | solution.py:443
  141.5 5.4 %collective-permute-start.18 = (f32[8,32,128]{2,1,0:T(8,128)S(1)}, f32[8,32,128]{2,1,0:T(8,128)S(1)}, u32[]{:S(2)}, u32[]{:S(2)}) collective-permute-start(f32[8,32,128]{2,1,0:T(8,128)S(1)} %collective-permute-done.15.refs_3_), channel_id=1, source_target_pairs={{0,24},{8,0},{16,8},{24,16},{1,25},{9,1},{17,9},{25,17},{2,26},{10... | collective-permute-start | bytes 393224 | tf_op jit(solution)/shard_map/ppermute | solution.py:443

commit v12 on v11

--- a/solution.py
+++ b/solution.py
@@ -118,7 +118,8 @@
     for p in range(peers):
         list_v[p : p + 1, :] = in_ref[p * rows_per + cap]
     e = list_v[...].astype(jnp.int32)
-    views, size = len(outs), slots // len(outs)
+    views = len(outs) - 1
+    size = slots // views
     quarter, rest = div_mod(jnp.maximum(e - 1, 0), size)
     turned = quarter - id_ref[0]
     turned = jnp.where(turned < 0, turned + views, turned)
@@ -136,14 +137,17 @@
         return c
 
     lax.fori_loop(0, peers, per_peer, 0)
-    for d, out in enumerate(outs):
-        out[...] = placed[d * size : (d + 1) * size, :]
+    at = 0
+    for out in outs:
+        out[...] = placed[at : at + out.shape[0], :]
+        at += out.shape[0]
 
 
 def unpack(ids, arrived, peers, cap, slots, views):
+    size = slots // views
     return call(
         functools.partial(unpack_kernel, peers, cap, slots), "unpack",
-        [f32(slots // views, BRICK)] * views, (ids, arrived),
+        [f32(n, BRICK) for n in (size, size, size // 2, size // 2, size)], (ids, arrived),
         scratch=[
             pltpu.VMEM((slots + SPARE, BRICK), jnp.float32),
             pltpu.VMEM((peers, BRICK), jnp.float32),
@@ -295,7 +299,11 @@
 
 
 def backward_kernel(views, rels, add, w_ref, id_ref, below, *refs):
-    observed, refs = refs[: len(rels)], refs[len(rels) :]
+    observed = []
+    for d in rels:
+        count = 2 if 2 * d == views else 1
+        observed.append(refs[:count])
+        refs = refs[count:]
     before, refs = (refs[0], refs[1:]) if add else (None, refs)
     out_ref, *sends = refs[:-2]
     wide, partial = refs[-2:]
@@ -311,7 +319,8 @@
         wx, wy, wz = (taps_of(w_ref, u, dim, True) for dim in range(3))
 
         def per_layer(x, carry, u=u, obs=obs, wy=wy, wz=wz):
-            rows = blur_z(*(obs[c, x] / below[u, c, x] for c in range(2)), wz)
+            seen = (obs[0][0, x], obs[-1][obs[-1].shape[0] - 1, x])
+            rows = blur_z(*(seen[c] / below[u, c, x] for c in range(2)), wz)
             for c in range(2):
                 wide[c, x, TILE : TILE + part, :] = rows[c]
                 partial[c, x] = y_rows(wide, (c, x), wy, part + 2 * TRIM)
@@ -345,7 +354,7 @@
     given = () if before is None else (before,)
     return call(
         functools.partial(backward_kernel, views, rels, before is not None), "backward", outs,
-        (w, ids, below, *observed, *given), 2,
+        (w, ids, below, *(o for pair in observed for o in pair), *given), 2,
         scratch=[
             pltpu.VMEM((2, x, part + 2 * TILE, BRICK), jnp.float32),
             pltpu.VMEM((2, x, rows, BRICK), jnp.float32),
@@ -405,14 +414,34 @@
 
 
 def join_kernel(views, id_ref, *refs):
-    pieces, out_ref = refs[: 2 * views], refs[2 * views]
-    part = pieces[0].shape[1]
+    pieces, (out_ref, wide, sems) = refs[: 2 * views], refs[2 * views :]
+    layers, part, _ = pieces[0].shape
+    places = []
     for d in range(views):
         place = lax.rem(id_ref[0] + d, views)
         place = jnp.where(id_ref[3] == 1, views - 1 - place, place)
-        at = pl.ds(pl.multiple_of(place * part, part), part)
-        out_ref[:, at, 0:BRICK] = pieces[2 * d][...]
-        out_ref[:, at, BRICK : 2 * BRICK] = pieces[2 * d + 1][...]
+        places.append(pl.ds(pl.multiple_of(place * part, part), part))
+    copies = []
+    for i in range(layers):
+        for d, at in enumerate(places):
+            wide[i, at, 0:BRICK] = pieces[2 * d][i]
+            wide[i, at, BRICK : 2 * BRICK] = pieces[2 * d + 1][i]
+        copies.append(pltpu.make_async_copy(wide.at[i], out_ref.at[i], sems.at[i]))
+        copies[-1].start()
+    for copy in copies:
+        copy.wait()
+
+
+def join(ids, pieces, shape):
+    return pl.pallas_call(
+        functools.partial(join_kernel, len(pieces) // 2),
+        out_shape=f32(*shape),
+        in_specs=[smem()] + [vmem()] * len(pieces),
+        out_specs=pl.BlockSpec(memory_space=pl.ANY),
+        scratch_shapes=[pltpu.VMEM(shape, jnp.float32), pltpu.SemaphoreType.DMA((shape[0],))],
+        cost_estimate=pl.CostEstimate(flops=1000, bytes_accessed=1000, transcendentals=0),
+        name="join",
+    )(ids, *pieces)
 
 
 def snake(at, views):
@@ -486,17 +515,18 @@
     below = forward(w, est, view_count, x_cells)
     arrived, below = lax.optimization_barrier((arrived, below))
     moved = unpack(ids, arrived, peer_count, capacity, brick_count, view_count)
-    moved = [m.reshape(brick_cols, x_cells, part, BRICK) for m in moved]
-    behind, ahead = turn(moved[1], 1, view_count), turn(moved[3], -1, view_count)
-    across = turn(moved[2], 2, view_count)
-    total = backward(w, ids, below, (0,), moved[:1], None, 0)[0]
-    total = backward(w, ids, below, (3, 1), (behind, ahead), total, 0)[0]
-    total, *sent = backward(w, ids, below, (2,), (across,), total, 2 * HALO)
+    moved = [m.reshape(-1, x_cells, part, BRICK) for m in moved]
+    hop_a, hop_b = turn(moved[2], 1, view_count), turn(moved[3], -1, view_count)
+    behind, ahead = turn(moved[1], 1, view_count), turn(moved[4], -1, view_count)
+    across = (turn(hop_a, 1, view_count), turn(hop_b, -1, view_count))
+    total = backward(w, ids, below, (0,), [(moved[0],)], None, 0)[0]
+    total = backward(w, ids, below, (3, 1), [(behind,), (ahead,)], total, 0)[0]
+    total, *sent = backward(w, ids, below, (2,), [across], total, 2 * HALO)
     total, *sent = merge(ids, total, *swap_layers(*sent), x_cells + 2 * HALO)
     args = (ids, total, *swap_rows(*sent), est)
     est = call(functools.partial(update_kernel, view_count), "update", wide, args)[0]
     below = forward(w, est, view_count, x_cells)
-    observed = (moved[0], ahead, across, behind)
+    observed = [(moved[0],), (ahead,), across, (behind,)]
     total, *sent = backward(w, ids, below, (0, 1, 2, 3), observed, None, HALO)
     total, *sent = merge(ids, total, *swap_layers(*sent), x_cells)
     args = (ids, total, *swap_rows(*sent), est)
@@ -509,10 +539,7 @@
     prev_b, next_a = turn(own[1], 1, view_count), turn(own[0], -1, view_count)
     far_a, far_b = turn(prev_a, 1, view_count), turn(next_b, -1, view_count)
     pieces = (*own, next_a, next_b, far_a, far_b, prev_a, prev_b)
-    return call(
-        functools.partial(join_kernel, view_count), "join", [f32(x_cells, y_cells, z_cells)],
-        (ids, *pieces),
-    )[0]
+    return join(ids, pieces, (x_cells, y_cells, z_cells))
 
 
 def solution(mesh):

time: 151 us -> 156 us (1.033); the launches traced: 148 us -> 156 us
  starting transfers between devices: 46.9 us -> 49.5 us
  waiting for transfers between devices: 56.7 us -> 59.2 us
    ppermute x9 -> x12, starting transfers between devices: 13.6 us -> 18.6 us  [turn(): lax.ppermute(value, 'views', [(i, (i + step) % count) for i in range(coun...]
    ppermute x2, starting transfers between devices: 2.73 us -> 0.37 us  [swap_rows(): lax.ppermute(inner, axes, both_ways(list(zip(chain[::2], chain[1::2]))))]
    ppermute x2, waiting for transfers between devices: 4.54 us -> 6.89 us  [swap_rows(): lax.ppermute(outer, axes, both_ways(list(zip(chain[1:-1:2], chain[2::2]))))]
    pallas_call x0 -> x1, Pallas kernels: none -> 2.33 us  [join(): pl.pallas_call(functools.partial(join_kernel, len(pieces) // 2), out_shap...]
    pallas_call x14 -> x13, Pallas kernels: 23.8 us -> 21.7 us  [call(): pl.pallas_call(kernel, out_shape=outs, in_specs=[smem()] * scalars + [vme...]
    unnamed x13 -> x31, local copies, waits for them, and re-layouts: 2.56 us -> 3.83 us
    ppermute x9 -> x12, waiting for transfers between devices: 13.4 us -> 13.4 us  [turn(): lax.ppermute(value, 'views', [(i, (i + step) % count) for i in range(coun...]
  transfers between devices with their start and end apart: 21 -> 24, of which waited for: 14 -> 12; matrix products, arithmetic and copies ran while one was open for 0% -> 0% of each run, Pallas kernels for 9% -> 8%
where the time goes in v12:
time: 156 us
  waiting for transfers between devices  59.2 us (38%)
  starting transfers between devices  49.5 us (32%)
  Pallas kernels  30 us (19%)
  blocking collectives  10.7 us (7%)
  local copies, waits for them, and re-layouts  4.76 us (3%)
    all_to_all x1, waiting for transfers between devices, per_device(): lax.all_to_all(outgoing.reshape(peer_count, capacity + 1, 1, BRICK), ('bl...  25.7 us
    pallas_call x13, Pallas kernels, call(): pl.pallas_call(kernel, out_shape=outs, in_specs=[smem()] * scalars + [vme...  21.7 us
    ppermute x12, starting transfers between devices, turn(): lax.ppermute(value, 'views', [(i, (i + step) % count) for i in range(coun...  18.6 us
    ppermute x12, waiting for transfers between devices, turn(): lax.ppermute(value, 'views', [(i, (i + step) % count) for i in range(coun...  13.4 us
    ppermute x3, waiting for transfers between devices, swap_layers(): lax.ppermute(outer, 'rows', both_ways([(i, i + 1) for i in range(1, count...  11.1 us
    all_gather x1, blocking collectives, per_device(): taps = lax.all_gather(psf_taps, 'views', axis=0, tiled=True)  10.7 us
    all_to_all x1, starting transfers between devices, per_device(): lax.all_to_all(outgoing.reshape(peer_count, capacity + 1, 1, BRICK), ('bl...  10.4 us
    ppermute x2, waiting for transfers between devices, swap_rows(): lax.ppermute(outer, axes, both_ways(list(zip(chain[1:-1:2], chain[2::2]))))  6.89 us
  transfers between devices with their start and end apart: 24, of which 12 were waited for; matrix products, arithmetic and copies ran while one was open for 0% of the time, Pallas kernels for 8%

profile of v12, /device:TPU:34, one launch (start us, length us, event | category | flops | bytes accessed | tf_op | source)
XLA Modules:
  0.0 155.5 jit_solution(8238492286250163781)
XLA Ops:
  0.8 3.8 %collective-permute-start = (f32[8,8,256]{2,1,0:T(8,128)S(1)}, f32[8,8,256]{2,1,0:T(8,128)S(1)}, u32[]{:S(2)}, u32[]{:S(2)}) collective-permute-start(f32[8,8,256]{2,1,0:T(8,128)S(1)} %constant_dynamic-slice_fusion), channel_id=1, source_target_pairs={{24,56},{32,64},{88,120},{96,128},{152,184},{160,192},{216,248},{5... | collective-permute-start | bytes 196616 | tf_op jit(solution)/shard_map/ppermute | solution.py:495
  5.3 5.9 %pack.1 = f32[4160,1,128]{2,1,0:T(1,128)} custom-call(s32[1]{0:T(128)S(6)} %copy.9.shift_ref, s32[8,2,128]{2,1,0:T(2,128)} %bitcast.25, f32[8,128,256]{2,1,0:T(8,128)} %bitcast.24), custom_call_target="tpu_custom_call" | custom-call | tf_op jit(solution)/shard_map/pack/pallas_call | solution.py:96
  11.3 10.4 %all-to-all-start = ((f32[64,65,1,128]{3,2,1,0:T(1,128)}), f32[64,65,1,128]{3,2,1,0:T(1,128)S(1)}, u32[]{:S(2)}, u32[]{:S(2)}) async-start(f32[64,65,1,128]{3,2,1,0:T(1,128)} %bitcast.23), calls=%async_computation | async-start | bytes 4259840 | tf_op jit(solution)/shard_map/all_to_all | solution.py:500
  21.7 10.7 %all_gather.3 = f32[4,3,7]{2,1,0:T(4,128)S(1)} all-gather(f32[1,3,7]{2,1,0:T(4,128)S(1)} %copy.8), channel_id=1, replica_groups=mesh['blocks'=8,'views'=4,'rows'=8] {'views'}, dimensions={0}, use_global_device_ids=true | all-gather | bytes 420 | tf_op jit(solution)/shard_map/all_gather | solution.py:505
  34.0 1.9 %collective-permute-start.1 = (f32[2,3,48,128]{3,2,1,0:T(8,128)S(1)}, f32[2,3,48,128]{3,2,1,0:T(8,128)S(1)}, u32[]{:S(2)}, u32[]{:S(2)}) collective-permute-start(f32[2,3,48,128]{3,2,1,0:T(8,128)S(1)} %get-tuple-element.34), channel_id=1, source_target_pairs={{1,2},{3,4},{5,6},{2,1},{4,3},{6,5},{9,10},{11,12},{13,14},{10,9},... | collective-permute-start | bytes 442376 | tf_op jit(solution)/shard_map/ppermute | solution.py:458
  37.7 4.4 %collective-permute-done.1.outer = f32[2,3,48,128]{3,2,1,0:T(8,128)S(1)} collective-permute-done((f32[2,3,48,128]{3,2,1,0:T(8,128)S(1)}, f32[2,3,48,128]{3,2,1,0:T(8,128)S(1)}, u32[]{:S(2)}, u32[]{:S(2)}) %collective-permute-start.1) | collective-permute-done | bytes 147488 | tf_op jit(solution)/shard_map/ppermute | solution.py:458
  43.6 2.7 %forward.2.below = f32[4,2,8,32,128]{4,3,2,1,0:T(8,128)S(1)} custom-call(f32[84]{0:T(128)S(1)} %reshape.25.w_ref, f32[2,14,40,128]{3,2,1,0:T(8,128)S(1)} %extend.1.est), custom_call_target="tpu_custom_call" | custom-call | flops 1000 | bytes 1000 | tf_op jit(solution)/shard_map/forward/pallas_call | solution.py:174
  47.1 25.7 %all-to-all-done = f32[64,65,1,128]{3,2,1,0:T(1,128)S(1)} async-done(((f32[64,65,1,128]{3,2,1,0:T(1,128)}), f32[64,65,1,128]{3,2,1,0:T(1,128)S(1)}, u32[]{:S(2)}, u32[]{:S(2)}) %all-to-all-start) | async-done | bytes 2129952 | tf_op jit(solution)/shard_map/all_to_all | solution.py:500
  72.8 5.3 %unpack.1 = (f32[512,128]{1,0:T(8,128)S(1)}, f32[512,128]{1,0:T(8,128)S(1)}, f32[256,128]{1,0:T(8,128)S(1)}, f32[256,128]{1,0:T(8,128)S(1)}, f32[512,128]{1,0:T(8,128)S(1)}) custom-call(s32[4]{0:T(128)S(1)} %pad_add_fusion.id_ref, f32[4160,1,128]{2,1,0:T(1,128)S(1)} %bitcast.16), custom_call_target="tpu_custom_call" | custom-call | flops 1000 | bytes 1000 | tf_op jit(solution)/shard_map/unpack/pallas_call | solution.py:174
  78.1 3.5 %collective-permute-start.5 = (f32[1,8,32,128]{3,2,1,0:T(8,128)S(1)}, f32[1,8,32,128]{3,2,1,0:T(8,128)S(1)}, u32[]{:S(2)}, u32[]{:S(2)}) collective-permute-start(f32[1,8,32,128]{3,2,1,0:T(8,128)S(1)} %bitcast.22), channel_id=1, source_target_pairs={{0,24},{8,0},{16,8},{24,16},{1,25},{9,1},{17,9},{25,17},{2,26},{10... | collective-permute-start | bytes 393224 | tf_op jit(solution)/shard_map/ppermute | solution.py:472
  81.6 3.2 %collective-permute-start.8 = (f32[2,8,32,128]{3,2,1,0:T(8,128)S(1)}, f32[2,8,32,128]{3,2,1,0:T(8,128)S(1)}, u32[]{:S(2)}, u32[]{:S(2)}) collective-permute-start(f32[2,8,32,128]{3,2,1,0:T(8,128)S(1)} %bitcast.19), channel_id=1, source_target_pairs={{0,24},{8,0},{16,8},{24,16},{1,25},{9,1},{17,9},{25,17},{2,26},{10... | collective-permute-start | bytes 786440 | tf_op jit(solution)/shard_map/ppermute | solution.py:472
  84.8 3.2 %collective-permute-start.6 = (f32[1,8,32,128]{3,2,1,0:T(8,128)S(1)}, f32[1,8,32,128]{3,2,1,0:T(8,128)S(1)}, u32[]{:S(2)}, u32[]{:S(2)}) collective-permute-start(f32[1,8,32,128]{3,2,1,0:T(8,128)S(1)} %collective-permute-done.5), channel_id=1, source_target_pairs={{0,24},{8,0},{16,8},{24,16},{1,25},{9,1},{17,9},{25,17},{2,26},{10... | collective-permute-start | bytes 393224 | tf_op jit(solution)/shard_map/ppermute | solution.py:472
  88.1 5.3 %collective-permute-done.3 = f32[1,8,32,128]{3,2,1,0:T(8,128)S(1)} collective-permute-done((f32[1,8,32,128]{3,2,1,0:T(8,128)S(1)}, f32[1,8,32,128]{3,2,1,0:T(8,128)S(1)}, u32[]{:S(2)}, u32[]{:S(2)}) %collective-permute-start.3) | collective-permute-done | bytes 131104 | tf_op jit(solution)/shard_map/ppermute | solution.py:472
  94.6 1.8 %backward.5.refs_2_ = f32[2,14,40,128]{3,2,1,0:T(8,128)S(1)} custom-call(f32[84]{0:T(128)S(1)} %reshape.25.w_ref, s32[4]{0:T(128)S(1)} %pad_add_fusion.id_ref, f32[4,2,8,32,128]{4,3,2,1,0:T(8,128)S(1)} %forward.2.below, f32[2,8,32,128]{3,2,1,0:T(8,128)S(1)} %collective-permute-done.7.refs_0_.refs_4_, f32[2,8,32,128]{3,2,1,0:T(8,128)S(1)} %collective-permute-done.8.refs_1_, ...), custom_call_target="tpu_custom_call" | custom-call | flops 1000 | bytes 1000 | tf_op jit(solution)/shard_map/backward/pallas_call | solution.py:174
  96.4 3.2 %collective-permute-done.4.refs_0_.refs_2_ = f32[1,8,32,128]{3,2,1,0:T(8,128)S(1)} collective-permute-done((f32[1,8,32,128]{3,2,1,0:T(8,128)S(1)}, f32[1,8,32,128]{3,2,1,0:T(8,128)S(1)}, u32[]{:S(2)}, u32[]{:S(2)}) %collective-permute-start.4) | collective-permute-done | bytes 131104 | tf_op jit(solution)/shard_map/ppermute | solution.py:472
  100.8 1.9 %collective-permute-start.9 = (f32[2,6,40,128]{3,2,1,0:T(8,128)S(1)}, f32[2,6,40,128]{3,2,1,0:T(8,128)S(1)}, u32[]{:S(2)}, u32[]{:S(2)}) collective-permute-start(f32[2,6,40,128]{3,2,1,0:T(8,128)S(1)} %get-tuple-element.44), channel_id=1, source_target_pairs={{1,2},{3,4},{5,6},{2,1},{4,3},{6,5},{9,10},{11,12},{13,14},{10,9},... | collective-permute-start | bytes 737288 | tf_op jit(solution)/shard_map/ppermute | solution.py:458
  104.4 3.9 %collective-permute-done.9.outer = f32[2,6,40,128]{3,2,1,0:T(8,128)S(1)} collective-permute-done((f32[2,6,40,128]{3,2,1,0:T(8,128)S(1)}, f32[2,6,40,128]{3,2,1,0:T(8,128)S(1)}, u32[]{:S(2)}, u32[]{:S(2)}) %collective-permute-start.9) | collective-permute-done | bytes 245792 | tf_op jit(solution)/shard_map/ppermute | solution.py:458
  109.0 2.3 %collective-permute-start.11 = (f32[2,14,8,128]{3,2,1,0:T(8,128)S(1)}, f32[2,14,8,128]{3,2,1,0:T(8,128)S(1)}, u32[]{:S(2)}, u32[]{:S(2)}) collective-permute-start(f32[2,14,8,128]{3,2,1,0:T(8,128)S(1)} %get-tuple-element.47), channel_id=1, source_target_pairs={{8,16},{24,56},{48,40},{32,64},{72,80},{88,120},{112,104},{96,128}... | collective-permute-start | bytes 344072 | tf_op jit(solution)/shard_map/ppermute | solution.py:466
  111.6 4.5 %collective-permute-done.11.outer = f32[2,14,8,128]{3,2,1,0:T(8,128)S(1)} collective-permute-done((f32[2,14,8,128]{3,2,1,0:T(8,128)S(1)}, f32[2,14,8,128]{3,2,1,0:T(8,128)S(1)}, u32[]{:S(2)}, u32[]{:S(2)}) %collective-permute-start.11) | collective-permute-done | bytes 114720 | tf_op jit(solution)/shard_map/ppermute | solution.py:466
  117.0 2.7 %forward.3.below = f32[4,2,8,32,128]{4,3,2,1,0:T(8,128)S(1)} custom-call(f32[84]{0:T(128)S(1)} %reshape.25.w_ref, f32[2,14,40,128]{3,2,1,0:T(8,128)S(1)} %update.1.est), custom_call_target="tpu_custom_call" | custom-call | flops 1000 | bytes 1000 | tf_op jit(solution)/shard_map/forward/pallas_call | solution.py:174
  119.7 2.8 %backward.7 = (f32[2,14,40,128]{3,2,1,0:T(8,128)S(1)}, f32[2,3,40,128]{3,2,1,0:T(8,128)S(1)}, f32[2,3,40,128]{3,2,1,0:T(8,128)S(1)}) custom-call(f32[84]{0:T(128)S(1)} %reshape.25.w_ref, s32[4]{0:T(128)S(1)} %pad_add_fusion.id_ref, f32[4,2,8,32,128]{4,3,2,1,0:T(8,128)S(1)} %forward.3.below, f32[2,8,32,128]{3,2,1,0:T(8,128)S(1)} %bitcast.18, ...), custom_call_target="tpu_custom_call" | custom-call | flops 1000 | bytes 1000 | tf_op jit(solution)/shard_map/backward/pallas_call | solution.py:174
  122.5 1.9 %collective-permute-start.13 = (f32[2,3,40,128]{3,2,1,0:T(8,128)S(1)}, f32[2,3,40,128]{3,2,1,0:T(8,128)S(1)}, u32[]{:S(2)}, u32[]{:S(2)}) collective-permute-start(f32[2,3,40,128]{3,2,1,0:T(8,128)S(1)} %get-tuple-element.50), channel_id=1, source_target_pairs={{1,2},{3,4},{5,6},{2,1},{4,3},{6,5},{9,10},{11,12},{13,14},{10,9},... | collective-permute-start | bytes 368648 | tf_op jit(solution)/shard_map/ppermute | solution.py:458
  125.8 2.9 %collective-permute-done.13.outer = f32[2,3,40,128]{3,2,1,0:T(8,128)S(1)} collective-permute-done((f32[2,3,40,128]{3,2,1,0:T(8,128)S(1)}, f32[2,3,40,128]{3,2,1,0:T(8,128)S(1)}, u32[]{:S(2)}, u32[]{:S(2)}) %collective-permute-start.13) | collective-permute-done | bytes 122912 | tf_op jit(solution)/shard_map/ppermute | solution.py:458
  129.3 3.6 %collective-permute-start.15 = (f32[2,8,8,128]{3,2,1,0:T(8,128)S(1)}, f32[2,8,8,128]{3,2,1,0:T(8,128)S(1)}, u32[]{:S(2)}, u32[]{:S(2)}) collective-permute-start(f32[2,8,8,128]{3,2,1,0:T(8,128)S(1)} %get-tuple-element.53), channel_id=1, source_target_pairs={{8,16},{24,56},{48,40},{32,64},{72,80},{88,120},{112,104},{96,128}... | collective-permute-start | bytes 196616 | tf_op jit(solution)/shard_map/ppermute | solution.py:466
  133.1 2.4 %collective-permute-done.15.outer = f32[2,8,8,128]{3,2,1,0:T(8,128)S(1)} collective-permute-done((f32[2,8,8,128]{3,2,1,0:T(8,128)S(1)}, f32[2,8,8,128]{3,2,1,0:T(8,128)S(1)}, u32[]{:S(2)}, u32[]{:S(2)}) %collective-permute-start.15) | collective-permute-done | bytes 65568 | tf_op jit(solution)/shard_map/ppermute | solution.py:466
  135.5 1.8 %collective-permute-done.16.inner = f32[2,8,8,128]{3,2,1,0:T(8,128)S(1)} collective-permute-done((f32[2,8,8,128]{3,2,1,0:T(8,128)S(1)}, f32[2,8,8,128]{3,2,1,0:T(8,128)S(1)}, u32[]{:S(2)}, u32[]{:S(2)}) %collective-permute-start.16) | collective-permute-done | bytes 65568 | tf_op jit(solution)/shard_map/ppermute | solution.py:467
  138.3 3.2 %collective-permute-start.18 = (f32[8,32,128]{2,1,0:T(8,128)S(1)}, f32[8,32,128]{2,1,0:T(8,128)S(1)}, u32[]{:S(2)}, u32[]{:S(2)}) collective-permute-start(f32[8,32,128]{2,1,0:T(8,128)S(1)} %get-tuple-element.56.refs_1_), channel_id=1, source_target_pairs={{0,24},{8,0},{16,8},{24,16},{1,25},{9,1},{17,9},{25,17},{2,26},{10... | collective-permute-start | bytes 393224 | tf_op jit(solution)/shard_map/ppermute | solution.py:472
  141.5 2.0 %collective-permute-start.22 = (f32[8,32,128]{2,1,0:T(8,128)S(1)}, f32[8,32,128]{2,1,0:T(8,128)S(1)}, u32[]{:S(2)}, u32[]{:S(2)}) collective-permute-start(f32[8,32,128]{2,1,0:T(8,128)S(1)} %get-tuple-element.56.refs_1_), channel_id=1, source_target_pairs={{0,8},{8,16},{16,24},{24,0},{1,9},{9,17},{17,25},{25,1},{2,10},{10... | collective-permute-start | bytes 393224 | tf_op jit(solution)/shard_map/ppermute | solution.py:472
  143.5 2.0 %collective-permute-done.19.refs_6_ = f32[8,32,128]{2,1,0:T(8,128)S(1)} collective-permute-done((f32[8,32,128]{2,1,0:T(8,128)S(1)}, f32[8,32,128]{2,1,0:T(8,128)S(1)}, u32[]{:S(2)}, u32[]{:S(2)}) %collective-permute-start.19) | collective-permute-done | bytes 131104 | tf_op jit(solution)/shard_map/ppermute | solution.py:472
  145.5 3.2 %collective-permute-start.21 = (f32[8,32,128]{2,1,0:T(8,128)S(1)}, f32[8,32,128]{2,1,0:T(8,128)S(1)}, u32[]{:S(2)}, u32[]{:S(2)}) collective-permute-start(f32[8,32,128]{2,1,0:T(8,128)S(1)} %collective-permute-done.18.refs_3_), channel_id=1, source_target_pairs={{0,24},{8,0},{16,8},{24,16},{1,25},{9,1},{17,9},{25,17},{2,26},{10... | collective-permute-start | bytes 393224 | tf_op jit(solution)/shard_map/ppermute | solution.py:472
  148.8 2.9 %collective-permute-done.20.refs_4_ = f32[8,32,128]{2,1,0:T(8,128)S(1)} collective-permute-done((f32[8,32,128]{2,1,0:T(8,128)S(1)}, f32[8,32,128]{2,1,0:T(8,128)S(1)}, u32[]{:S(2)}, u32[]{:S(2)}) %collective-permute-start.20) | collective-permute-done | bytes 131104 | tf_op jit(solution)/shard_map/ppermute | solution.py:472
  153.0 2.3 %join.1 = f32[8,128,256]{2,1,0:T(8,128)} custom-call(s32[4]{0:T(128)} %copy-done.7, f32[8,32,128]{2,1,0:T(8,128)} %copy-done.5, f32[8,32,128]{2,1,0:T(8,128)} %copy-done.6, f32[8,32,128]{2,1,0:T(8,128)} %copy-done.10, f32[8,32,128]{2,1,0:T(8,128)} %copy-done.9, f32[8,32,128]{2,1,0:T(8,128)} %copy-done.12, f32[8,32,128]{2,1,0:T(8,128)} %copy-done.13, ...), custom_call_target="tpu_custom_call" | custom-call | flops 1000 | bytes 1000 | tf_op jit(solution)/shard_map/join/pallas_call | solution.py:436
  (67 shorter events, 17.0 us)
Async XLA Ops:
  0.8 10.4 %collective-permute-start = (f32[8,8,256]{2,1,0:T(8,128)S(1)}, f32[8,8,256]{2,1,0:T(8,128)S(1)}, u32[]{:S(2)}, u32[]{:S(2)}) collective-permute-start(f32[8,8,256]{2,1,0:T(8,128)S(1)} %constant_dynamic-slice_fusion), channel_id=1, source_target_pairs={{24,56},{32,64},{88,120},{96,128},{152,184},{160,192},{216,248},{5... | collective-permute-start | bytes 196616 | tf_op jit(solution)/shard_map/ppermute | solution.py:495
  11.3 10.4 %copy-start.14 = (f32[1,3,7]{2,0,1:T(1,128)S(1)}, f32[1,3,7]{2,0,1:T(1,128)}, u32[]{:S(2)}) copy-start(f32[1,3,7]{2,0,1:T(1,128)} %param.8) | copy-start | bytes 256
  11.3 21.2 %copy-start.2 = (f32[8,128,256]{2,1,0:T(8,128)S(1)}, f32[8,128,256]{2,1,0:T(8,128)}, u32[]{:S(2)}) copy-start(f32[8,128,256]{2,1,0:T(8,128)} %est.1) | copy-start | bytes 3145732
  11.3 61.5 %all-to-all-start = ((f32[64,65,1,128]{3,2,1,0:T(1,128)}), f32[64,65,1,128]{3,2,1,0:T(1,128)S(1)}, u32[]{:S(2)}, u32[]{:S(2)}) async-start(f32[64,65,1,128]{3,2,1,0:T(1,128)} %bitcast.23), calls=%async_computation | async-start | bytes 4259840 | tf_op jit(solution)/shard_map/all_to_all | solution.py:500
  32.4 104.9 %copy-start.7 = (s32[4]{0:T(128)}, s32[4]{0:T(128)S(1)}, u32[]{:S(2)}) copy-start(s32[4]{0:T(128)S(1)} %pad_add_fusion.id_ref) | copy-start | bytes 52
  34.0 8.1 %collective-permute-start.1 = (f32[2,3,48,128]{3,2,1,0:T(8,128)S(1)}, f32[2,3,48,128]{3,2,1,0:T(8,128)S(1)}, u32[]{:S(2)}, u32[]{:S(2)}) collective-permute-start(f32[2,3,48,128]{3,2,1,0:T(8,128)S(1)} %get-tuple-element.34), channel_id=1, source_target_pairs={{1,2},{3,4},{5,6},{2,1},{4,3},{6,5},{9,10},{11,12},{13,14},{10,9},... | collective-permute-start | bytes 442376 | tf_op jit(solution)/shard_map/ppermute | solution.py:458
  35.9 6.2 %collective-permute-start.2 = (f32[2,3,48,128]{3,2,1,0:T(8,128)S(1)}, f32[2,3,48,128]{3,2,1,0:T(8,128)S(1)}, u32[]{:S(2)}, u32[]{:S(2)}) collective-permute-start(f32[2,3,48,128]{3,2,1,0:T(8,128)S(1)} %get-tuple-element.35), channel_id=1, source_target_pairs={{0,1},{2,3},{4,5},{6,7},{1,0},{3,2},{5,4},{7,6},{8,9},{10,11},{12,... | collective-permute-start | bytes 442376 | tf_op jit(solution)/shard_map/ppermute | solution.py:459
  78.1 6.8 %collective-permute-start.5 = (f32[1,8,32,128]{3,2,1,0:T(8,128)S(1)}, f32[1,8,32,128]{3,2,1,0:T(8,128)S(1)}, u32[]{:S(2)}, u32[]{:S(2)}) collective-permute-start(f32[1,8,32,128]{3,2,1,0:T(8,128)S(1)} %bitcast.22), channel_id=1, source_target_pairs={{0,24},{8,0},{16,8},{24,16},{1,25},{9,1},{17,9},{25,17},{2,26},{10... | collective-permute-start | bytes 393224 | tf_op jit(solution)/shard_map/ppermute | solution.py:472
  81.6 13.0 %collective-permute-start.7 = (f32[2,8,32,128]{3,2,1,0:T(8,128)S(1)}, f32[2,8,32,128]{3,2,1,0:T(8,128)S(1)}, u32[]{:S(2)}, u32[]{:S(2)}) collective-permute-start(f32[2,8,32,128]{3,2,1,0:T(8,128)S(1)} %bitcast.20), channel_id=1, source_target_pairs={{0,8},{8,16},{16,24},{24,0},{1,9},{9,17},{17,25},{25,1},{2,10},{10... | collective-permute-start | bytes 786440 | tf_op jit(solution)/shard_map/ppermute | solution.py:472
  81.6 13.0 %collective-permute-start.8 = (f32[2,8,32,128]{3,2,1,0:T(8,128)S(1)}, f32[2,8,32,128]{3,2,1,0:T(8,128)S(1)}, u32[]{:S(2)}, u32[]{:S(2)}) collective-permute-start(f32[2,8,32,128]{3,2,1,0:T(8,128)S(1)} %bitcast.19), channel_id=1, source_target_pairs={{0,24},{8,0},{16,8},{24,16},{1,25},{9,1},{17,9},{25,17},{2,26},{10... | collective-permute-start | bytes 786440 | tf_op jit(solution)/shard_map/ppermute | solution.py:472
  84.8 8.5 %collective-permute-start.3 = (f32[1,8,32,128]{3,2,1,0:T(8,128)S(1)}, f32[1,8,32,128]{3,2,1,0:T(8,128)S(1)}, u32[]{:S(2)}, u32[]{:S(2)}) collective-permute-start(f32[1,8,32,128]{3,2,1,0:T(8,128)S(1)} %bitcast.21), channel_id=1, source_target_pairs={{0,8},{8,16},{16,24},{24,0},{1,9},{9,17},{17,25},{25,1},{2,10},{10... | collective-permute-start | bytes 393224 | tf_op jit(solution)/shard_map/ppermute | solution.py:472
  84.8 11.5 %collective-permute-start.6 = (f32[1,8,32,128]{3,2,1,0:T(8,128)S(1)}, f32[1,8,32,128]{3,2,1,0:T(8,128)S(1)}, u32[]{:S(2)}, u32[]{:S(2)}) collective-permute-start(f32[1,8,32,128]{3,2,1,0:T(8,128)S(1)} %collective-permute-done.5), channel_id=1, source_target_pairs={{0,24},{8,0},{16,8},{24,16},{1,25},{9,1},{17,9},{25,17},{2,26},{10... | collective-permute-start | bytes 393224 | tf_op jit(solution)/shard_map/ppermute | solution.py:472
  93.3 6.2 %collective-permute-start.4 = (f32[1,8,32,128]{3,2,1,0:T(8,128)S(1)}, f32[1,8,32,128]{3,2,1,0:T(8,128)S(1)}, u32[]{:S(2)}, u32[]{:S(2)}) collective-permute-start(f32[1,8,32,128]{3,2,1,0:T(8,128)S(1)} %collective-permute-done.3), channel_id=1, source_target_pairs={{0,8},{8,16},{16,24},{24,0},{1,9},{9,17},{17,25},{25,1},{2,10},{10... | collective-permute-start | bytes 393224 | tf_op jit(solution)/shard_map/ppermute | solution.py:472
  96.3 20.0 %copy-start.1 = (f32[2,14,40,128]{3,2,1,0:T(8,128)S(1)}, f32[2,14,40,128]{3,2,1,0:T(8,128)}, u32[]{:S(2)}) copy-start(f32[2,14,40,128]{3,2,1,0:T(8,128)} %copy-done) | copy-start | bytes 1720324
  100.8 7.5 %collective-permute-start.9 = (f32[2,6,40,128]{3,2,1,0:T(8,128)S(1)}, f32[2,6,40,128]{3,2,1,0:T(8,128)S(1)}, u32[]{:S(2)}, u32[]{:S(2)}) collective-permute-start(f32[2,6,40,128]{3,2,1,0:T(8,128)S(1)} %get-tuple-element.44), channel_id=1, source_target_pairs={{1,2},{3,4},{5,6},{2,1},{4,3},{6,5},{9,10},{11,12},{13,14},{10,9},... | collective-permute-start | bytes 737288 | tf_op jit(solution)/shard_map/ppermute | solution.py:458
  102.7 5.6 %collective-permute-start.10 = (f32[2,6,40,128]{3,2,1,0:T(8,128)S(1)}, f32[2,6,40,128]{3,2,1,0:T(8,128)S(1)}, u32[]{:S(2)}, u32[]{:S(2)}) collective-permute-start(f32[2,6,40,128]{3,2,1,0:T(8,128)S(1)} %get-tuple-element.45), channel_id=1, source_target_pairs={{0,1},{2,3},{4,5},{6,7},{1,0},{3,2},{5,4},{7,6},{8,9},{10,11},{12,... | collective-permute-start | bytes 737288 | tf_op jit(solution)/shard_map/ppermute | solution.py:459
  109.0 7.1 %collective-permute-start.11 = (f32[2,14,8,128]{3,2,1,0:T(8,128)S(1)}, f32[2,14,8,128]{3,2,1,0:T(8,128)S(1)}, u32[]{:S(2)}, u32[]{:S(2)}) collective-permute-start(f32[2,14,8,128]{3,2,1,0:T(8,128)S(1)} %get-tuple-element.47), channel_id=1, source_target_pairs={{8,16},{24,56},{48,40},{32,64},{72,80},{88,120},{112,104},{96,128}... | collective-permute-start | bytes 344072 | tf_op jit(solution)/shard_map/ppermute | solution.py:466
  111.3 5.1 %collective-permute-start.12 = (f32[2,14,8,128]{3,2,1,0:T(8,128)S(1)}, f32[2,14,8,128]{3,2,1,0:T(8,128)S(1)}, u32[]{:S(2)}, u32[]{:S(2)}) collective-permute-start(f32[2,14,8,128]{3,2,1,0:T(8,128)S(1)} %get-tuple-element.48), channel_id=1, source_target_pairs={{0,8},{16,24},{56,48},{40,32},{64,72},{80,88},{120,112},{104,96},{... | collective-permute-start | bytes 344072 | tf_op jit(solution)/shard_map/ppermute | solution.py:467
  122.5 6.2 %collective-permute-start.13 = (f32[2,3,40,128]{3,2,1,0:T(8,128)S(1)}, f32[2,3,40,128]{3,2,1,0:T(8,128)S(1)}, u32[]{:S(2)}, u32[]{:S(2)}) collective-permute-start(f32[2,3,40,128]{3,2,1,0:T(8,128)S(1)} %get-tuple-element.50), channel_id=1, source_target_pairs={{1,2},{3,4},{5,6},{2,1},{4,3},{6,5},{9,10},{11,12},{13,14},{10,9},... | collective-permute-start | bytes 368648 | tf_op jit(solution)/shard_map/ppermute | solution.py:458
  124.4 4.3 %collective-permute-start.14 = (f32[2,3,40,128]{3,2,1,0:T(8,128)S(1)}, f32[2,3,40,128]{3,2,1,0:T(8,128)S(1)}, u32[]{:S(2)}, u32[]{:S(2)}) collective-permute-start(f32[2,3,40,128]{3,2,1,0:T(8,128)S(1)} %get-tuple-element.51), channel_id=1, source_target_pairs={{0,1},{2,3},{4,5},{6,7},{1,0},{3,2},{5,4},{7,6},{8,9},{10,11},{12,... | collective-permute-start | bytes 368648 | tf_op jit(solution)/shard_map/ppermute | solution.py:459
  129.3 6.2 %collective-permute-start.15 = (f32[2,8,8,128]{3,2,1,0:T(8,128)S(1)}, f32[2,8,8,128]{3,2,1,0:T(8,128)S(1)}, u32[]{:S(2)}, u32[]{:S(2)}) collective-permute-start(f32[2,8,8,128]{3,2,1,0:T(8,128)S(1)} %get-tuple-element.53), channel_id=1, source_target_pairs={{8,16},{24,56},{48,40},{32,64},{72,80},{88,120},{112,104},{96,128}... | collective-permute-start | bytes 196616 | tf_op jit(solution)/shard_map/ppermute | solution.py:466
  133.0 4.4 %collective-permute-start.16 = (f32[2,8,8,128]{3,2,1,0:T(8,128)S(1)}, f32[2,8,8,128]{3,2,1,0:T(8,128)S(1)}, u32[]{:S(2)}, u32[]{:S(2)}) collective-permute-start(f32[2,8,8,128]{3,2,1,0:T(8,128)S(1)} %get-tuple-element.54), channel_id=1, source_target_pairs={{0,8},{16,24},{56,48},{40,32},{64,72},{80,88},{120,112},{104,96},{... | collective-permute-start | bytes 196616 | tf_op jit(solution)/shard_map/ppermute | solution.py:467
  138.1 13.6 %copy-start.5 = (f32[8,32,128]{2,1,0:T(8,128)}, f32[8,32,128]{2,1,0:T(8,128)S(1)}, u32[]{:S(2)}) copy-start(f32[8,32,128]{2,1,0:T(8,128)S(1)} %get-tuple-element.55.refs_0_) | copy-start | bytes 393220
  138.2 13.6 %copy-start.6 = (f32[8,32,128]{2,1,0:T(8,128)}, f32[8,32,128]{2,1,0:T(8,128)S(1)}, u32[]{:S(2)}) copy-start(f32[8,32,128]{2,1,0:T(8,128)S(1)} %get-tuple-element.56.refs_1_) | copy-start | bytes 393220
  138.2 7.4 %collective-permute-start.19 = (f32[8,32,128]{2,1,0:T(8,128)S(1)}, f32[8,32,128]{2,1,0:T(8,128)S(1)}, u32[]{:S(2)}, u32[]{:S(2)}) collective-permute-start(f32[8,32,128]{2,1,0:T(8,128)S(1)} %get-tuple-element.55.refs_0_), channel_id=1, source_target_pairs={{0,8},{8,16},{16,24},{24,0},{1,9},{9,17},{17,25},{25,1},{2,10},{10... | collective-permute-start | bytes 393224 | tf_op jit(solution)/shard_map/ppermute | solution.py:472
  138.3 7.3 %collective-permute-start.18 = (f32[8,32,128]{2,1,0:T(8,128)S(1)}, f32[8,32,128]{2,1,0:T(8,128)S(1)}, u32[]{:S(2)}, u32[]{:S(2)}) collective-permute-start(f32[8,32,128]{2,1,0:T(8,128)S(1)} %get-tuple-element.56.refs_1_), channel_id=1, source_target_pairs={{0,24},{8,0},{16,8},{24,16},{1,25},{9,1},{17,9},{25,17},{2,26},{10... | collective-permute-start | bytes 393224 | tf_op jit(solution)/shard_map/ppermute | solution.py:472
  141.5 7.3 %collective-permute-start.17 = (f32[8,32,128]{2,1,0:T(8,128)S(1)}, f32[8,32,128]{2,1,0:T(8,128)S(1)}, u32[]{:S(2)}, u32[]{:S(2)}) collective-permute-start(f32[8,32,128]{2,1,0:T(8,128)S(1)} %get-tuple-element.55.refs_0_), channel_id=1, source_target_pairs={{0,24},{8,0},{16,8},{24,16},{1,25},{9,1},{17,9},{25,17},{2,26},{10... | collective-permute-start | bytes 393224 | tf_op jit(solution)/shard_map/ppermute | solution.py:472
  141.5 7.3 %collective-permute-start.22 = (f32[8,32,128]{2,1,0:T(8,128)S(1)}, f32[8,32,128]{2,1,0:T(8,128)S(1)}, u32[]{:S(2)}, u32[]{:S(2)}) collective-permute-start(f32[8,32,128]{2,1,0:T(8,128)S(1)} %get-tuple-element.56.refs_1_), channel_id=1, source_target_pairs={{0,8},{8,16},{16,24},{24,0},{1,9},{9,17},{17,25},{25,1},{2,10},{10... | collective-permute-start | bytes 393224 | tf_op jit(solution)/shard_map/ppermute | solution.py:472
  145.5 6.2 %copy-start.8 = (f32[8,32,128]{2,1,0:T(8,128)}, f32[8,32,128]{2,1,0:T(8,128)S(1)}, u32[]{:S(2)}) copy-start(f32[8,32,128]{2,1,0:T(8,128)S(1)} %collective-permute-done.19.refs_6_) | copy-start | bytes 393220
  145.5 6.2 %collective-permute-start.20 = (f32[8,32,128]{2,1,0:T(8,128)S(1)}, f32[8,32,128]{2,1,0:T(8,128)S(1)}, u32[]{:S(2)}, u32[]{:S(2)}) collective-permute-start(f32[8,32,128]{2,1,0:T(8,128)S(1)} %collective-permute-done.19.refs_6_), channel_id=1, source_target_pairs={{0,8},{8,16},{16,24},{24,0},{1,9},{9,17},{17,25},{25,1},{2,10},{10... | collective-permute-start | bytes 393224 | tf_op jit(solution)/shard_map/ppermute | solution.py:472
  145.5 6.2 %copy-start.9 = (f32[8,32,128]{2,1,0:T(8,128)}, f32[8,32,128]{2,1,0:T(8,128)S(1)}, u32[]{:S(2)}) copy-start(f32[8,32,128]{2,1,0:T(8,128)S(1)} %collective-permute-done.18.refs_3_) | copy-start | bytes 393220
  145.5 6.2 %collective-permute-start.21 = (f32[8,32,128]{2,1,0:T(8,128)S(1)}, f32[8,32,128]{2,1,0:T(8,128)S(1)}, u32[]{:S(2)}, u32[]{:S(2)}) collective-permute-start(f32[8,32,128]{2,1,0:T(8,128)S(1)} %collective-permute-done.18.refs_3_), channel_id=1, source_target_pairs={{0,24},{8,0},{16,8},{24,16},{1,25},{9,1},{17,9},{25,17},{2,26},{10... | collective-permute-start | bytes 393224 | tf_op jit(solution)/shard_map/ppermute | solution.py:472
  (7 other events, 9.8 us)

commit v13 on v11

--- a/solution.py
+++ b/solution.py
@@ -294,6 +294,97 @@
     )[0]
 
 
+def blur_x_tile(est, at, wx, out, c, x_cells, rows):
+    layers = [est[c, i, at, :] for i in range(x_cells + 2 * HALO)]
+    for x in range(x_cells):
+        out[c, x, rows, :] = weigh(layers[x : x + TAPS], wx)
+
+
+def middle_kernel(w_ref, est, total, out_ref, part_ref, fresh):
+    views, _, x_cells, part, _ = out_ref.shape
+    tall = part_ref.shape[3]
+    rows = slice(TILE, TILE + tall)
+    for c in range(2):
+        for i in range(x_cells + 2 * HALO):
+            fresh[c, i] = est[c, i, rows, :] * total[c, i, rows, :] / views
+
+    def per_view(u, carry):
+        wx, wy, wz = (taps_of(w_ref, u, dim, False) for dim in range(3))
+
+        def per_tile(t, carry):
+            at = pl.ds(pl.multiple_of(t * TILE, TILE), TILE)
+            for c in range(2):
+                blur_x_tile(fresh, at, wx, part_ref.at[u], c, x_cells, at)
+            return carry
+
+        lax.fori_loop(0, tall // TILE, per_tile, 0, unroll=True)
+
+        def per_layer(x, carry):
+            rows = [y_rows(part_ref, (u, c, x), wy, part) for c in range(2)]
+            out_ref[u, 0, x], out_ref[u, 1, x] = blur_z(*rows, wz)
+            return carry
+
+        lax.fori_loop(0, x_cells, per_layer, 0, unroll=True)
+        return carry
+
+    lax.fori_loop(0, views, per_view, 0)
+
+
+def middle(w, est, total, views, x_cells):
+    tall = est.shape[2] - 2 * TILE
+    return call(
+        middle_kernel, "middle",
+        [f32(views, 2, x_cells, tall - TILE, BRICK), f32(views, 2, x_cells, tall, BRICK)],
+        (w, est, total), scratch=[pltpu.VMEM((2, x_cells + 2 * HALO, tall, BRICK), jnp.float32)],
+    )
+
+
+def renew(views, id_ref, total, outer, inner, est, out_ref):
+    layers, rows = out_ref.shape[1:3]
+    odd = lax.rem(id_ref[2], 2)
+    at_in = pl.ds(pl.multiple_of((1 - odd) * (rows - TILE), TILE), TILE)
+    at_out = pl.ds(pl.multiple_of(odd * (rows - TILE), TILE), TILE)
+    for c in range(2):
+        for i in range(layers):
+            out_ref[c, i] = est[c, i] * total[c, i] / views
+            for at, more in ((at_in, inner), (at_out, outer)):
+                out_ref[c, i, at, :] = est[c, i, at, :] * (total[c, i, at, :] + more[c, i]) / views
+
+
+def ends_kernel(w_ref, id_ref, total, outer, inner, est, mid, part_ref, new, out_ref, strip):
+    views, _, x_cells, part, _ = out_ref.shape
+    tall = part_ref.shape[3]
+    renew(views, id_ref, total, outer, inner, est, new)
+    sides = ((0, 0, 0, TILE, 0), (tall + TILE, TILE, tall - TILE, 0, part - TILE))
+
+    def per_view(u, carry):
+        wx, wy, wz = (taps_of(w_ref, u, dim, False) for dim in range(3))
+        for s, (at, here, kept, there, to) in enumerate(sides):
+            for c in range(2):
+                blur_x_tile(new, slice(at, at + TILE), wx, strip.at[s], c, x_cells, slice(here, here + TILE))
+        for x in range(x_cells):
+            for s, (at, here, kept, there, to) in enumerate(sides):
+                for c in range(2):
+                    strip[s, c, x, there : there + TILE, :] = part_ref[u, c, x, kept : kept + TILE, :]
+                rows = blur_z(*(y_rows(strip, (s, c, x), wy, TILE) for c in range(2)), wz)
+                for c in range(2):
+                    out_ref[u, c, x, to : to + TILE, :] = rows[c]
+            for c in range(2):
+                out_ref[u, c, x, TILE : part - TILE, :] = mid[u, c, x]
+        return carry
+
+    lax.fori_loop(0, views, per_view, 0)
+
+
+def ends(w, args, mid, partial):
+    views, _, x, tall, _ = partial.shape
+    rows = tall + 2 * TILE
+    return call(
+        ends_kernel, "ends", [f32(2, x + 2 * HALO, rows, BRICK), f32(views, 2, x, tall + TILE, BRICK)],
+        (w, *args, mid, partial), 2, scratch=[pltpu.VMEM((2, 2, x, 2 * TILE, BRICK), jnp.float32)],
+    )
+
+
 def backward_kernel(views, rels, add, w_ref, id_ref, below, *refs):
     observed, refs = refs[: len(rels)], refs[len(rels) :]
     before, refs = (refs[0], refs[1:]) if add else (None, refs)
@@ -376,18 +467,6 @@
     rows = total.shape[2]
     outs = [f32(2, layers, rows, BRICK)] + [f32(2, layers, TILE, BRICK)] * 2
     return call(merge_kernel, "merge", outs, (ids, total, outer, inner))
-
-
-def update_kernel(views, id_ref, total, outer, inner, est, out_ref):
-    layers, rows = out_ref.shape[1:3]
-    odd = lax.rem(id_ref[2], 2)
-    at_in = pl.ds(pl.multiple_of((1 - odd) * (rows - TILE), TILE), TILE)
-    at_out = pl.ds(pl.multiple_of(odd * (rows - TILE), TILE), TILE)
-    for c in range(2):
-        for i in range(layers):
-            out_ref[c, i] = est[c, i] * total[c, i] / views
-            for at, more in ((at_in, inner), (at_out, outer)):
-                out_ref[c, i, at, :] = est[c, i, at, :] * (total[c, i, at, :] + more[c, i]) / views
 
 
 def finish_kernel(views, id_ref, total, outer, inner, est, out_a, out_b, wide):
@@ -481,8 +560,8 @@
         (ids, estimate, edge),
         scratch=[pltpu.VMEM((2, y_cells + 2 * TILE, BRICK), jnp.float32)],
     )
-    wide = [f32(2, x_cells + 2 * HALO, part + 2 * TRIM, BRICK)]
-    est = call(extend_kernel, "extend", wide, (ids, own, *swap_layers(*sent)))[0]
+    wide = f32(2, x_cells + 2 * HALO, part + 2 * TRIM, BRICK)
+    est = call(extend_kernel, "extend", [wide], (ids, own, *swap_layers(*sent)))[0]
     below = forward(w, est, view_count, x_cells)
     arrived, below = lax.optimization_barrier((arrived, below))
     moved = unpack(ids, arrived, peer_count, capacity, brick_count, view_count)
@@ -493,9 +572,8 @@
     total = backward(w, ids, below, (3, 1), (behind, ahead), total, 0)[0]
     total, *sent = backward(w, ids, below, (2,), (across,), total, 2 * HALO)
     total, *sent = merge(ids, total, *swap_layers(*sent), x_cells + 2 * HALO)
-    args = (ids, total, *swap_rows(*sent), est)
-    est = call(functools.partial(update_kernel, view_count), "update", wide, args)[0]
-    below = forward(w, est, view_count, x_cells)
+    mid, partial = middle(w, est, total, view_count, x_cells)
+    est, below = ends(w, (ids, total, *swap_rows(*sent), est), mid, partial)
     observed = (moved[0], ahead, across, behind)
     total, *sent = backward(w, ids, below, (0, 1, 2, 3), observed, None, HALO)
     total, *sent = merge(ids, total, *swap_layers(*sent), x_cells)

time: 151 us -> 150 us (level)
  local copies, waits for them, and re-layouts: 3.5 us -> 0.95 us
    unnamed x13 -> x5, local copies, waits for them, and re-layouts: 2.56 us -> 0.02 us
    all_to_all x1, waiting for transfers between devices: 25.4 us -> 27.5 us  [per_device(): lax.all_to_all(outgoing.reshape(peer_count, capacity + 1, 1, BRICK), ('bl...]
    ppermute x2, waiting for transfers between devices: 4.54 us -> 2.73 us  [swap_rows(): lax.ppermute(outer, axes, both_ways(list(zip(chain[1:-1:2], chain[2::2]))))]
  transfers between devices with their start and end apart: 21 -> 21, of which waited for: 14 -> 15; matrix products, arithmetic and copies ran while one was open for 0% -> 0% of each run, Pallas kernels for 9% -> 10%
where the time goes in v13:
time: 150 us; the launch traced here: 148 us
  waiting for transfers between devices  57.3 us (38%)
  starting transfers between devices  47 us (31%)
  Pallas kernels  30.9 us (21%)
  blocking collectives  10.7 us (7%)
    all_to_all x1, waiting for transfers between devices, per_device(): lax.all_to_all(outgoing.reshape(peer_count, capacity + 1, 1, BRICK), ('bl...  27.5 us
    pallas_call x14, Pallas kernels, call(): pl.pallas_call(kernel, out_shape=outs, in_specs=[smem()] * scalars + [vme...  25 us
    ppermute x9, starting transfers between devices, turn(): lax.ppermute(value, 'views', [(i, (i + step) % count) for i in range(coun...  13.5 us
    ppermute x9, waiting for transfers between devices, turn(): lax.ppermute(value, 'views', [(i, (i + step) % count) for i in range(coun...  13.4 us
    ppermute x3, waiting for transfers between devices, swap_layers(): lax.ppermute(outer, 'rows', both_ways([(i, i + 1) for i in range(1, count...  11.5 us
    all_gather x1, blocking collectives, per_device(): taps = lax.all_gather(psf_taps, 'views', axis=0, tiled=True)  10.7 us
    all_to_all x1, starting transfers between devices, per_device(): lax.all_to_all(outgoing.reshape(peer_count, capacity + 1, 1, BRICK), ('bl...  10.5 us
    ppermute x2, starting transfers between devices, swap_rows(): lax.ppermute(outer, axes, both_ways(list(zip(chain[1:-1:2], chain[2::2]))))  5.94 us
  transfers between devices with their start and end apart: 21, of which 15 were waited for; matrix products, arithmetic and copies ran while one was open for 0% of the time, Pallas kernels for 10%

profile of v13, /device:TPU:34, one launch (start us, length us, event | category | flops | bytes accessed | tf_op | source)
XLA Modules:
  0.0 147.9 jit_solution(16723525703883716369)
XLA Ops:
  0.8 3.8 %collective-permute-start = (f32[8,8,256]{2,1,0:T(8,128)S(1)}, f32[8,8,256]{2,1,0:T(8,128)S(1)}, u32[]{:S(2)}, u32[]{:S(2)}) collective-permute-start(f32[8,8,256]{2,1,0:T(8,128)S(1)} %constant_dynamic-slice_fusion), channel_id=1, source_target_pairs={{24,56},{32,64},{88,120},{96,128},{152,184},{160,192},{216,248},{5... | collective-permute-start | bytes 196616 | tf_op jit(solution)/shard_map/ppermute | solution.py:545
  5.3 5.9 %pack.1 = f32[4160,1,128]{2,1,0:T(1,128)} custom-call(s32[1]{0:T(128)S(6)} %copy.9.shift_ref, s32[8,2,128]{2,1,0:T(2,128)} %bitcast.22, f32[8,128,256]{2,1,0:T(8,128)} %bitcast.21), custom_call_target="tpu_custom_call" | custom-call | tf_op jit(solution)/shard_map/pack/pallas_call | solution.py:96
  11.3 10.5 %all-to-all-start = ((f32[64,65,1,128]{3,2,1,0:T(1,128)}), f32[64,65,1,128]{3,2,1,0:T(1,128)}, u32[]{:S(2)}, u32[]{:S(2)}) async-start(f32[64,65,1,128]{3,2,1,0:T(1,128)} %bitcast.20), calls=%async_computation | async-start | bytes 4259840 | tf_op jit(solution)/shard_map/all_to_all | solution.py:550
  21.8 10.7 %all_gather.3 = f32[4,3,7]{2,1,0:T(4,128)S(1)} all-gather(f32[1,3,7]{2,1,0:T(4,128)S(1)} %copy.8), channel_id=1, replica_groups=mesh['blocks'=8,'views'=4,'rows'=8] {'views'}, dimensions={0}, use_global_device_ids=true | all-gather | bytes 420 | tf_op jit(solution)/shard_map/all_gather | solution.py:555
  33.4 1.9 %collective-permute-start.1 = (f32[2,3,48,128]{3,2,1,0:T(8,128)S(1)}, f32[2,3,48,128]{3,2,1,0:T(8,128)S(1)}, u32[]{:S(2)}, u32[]{:S(2)}) collective-permute-start(f32[2,3,48,128]{3,2,1,0:T(8,128)S(1)} %get-tuple-element.37), channel_id=1, source_target_pairs={{1,2},{3,4},{5,6},{2,1},{4,3},{6,5},{9,10},{11,12},{13,14},{10,9},... | collective-permute-start | bytes 442376 | tf_op jit(solution)/shard_map/ppermute | solution.py:508
  35.3 1.7 %collective-permute-start.2 = (f32[2,3,48,128]{3,2,1,0:T(8,128)S(1)}, f32[2,3,48,128]{3,2,1,0:T(8,128)S(1)}, u32[]{:S(2)}, u32[]{:S(2)}) collective-permute-start(f32[2,3,48,128]{3,2,1,0:T(8,128)S(1)} %get-tuple-element.38), channel_id=1, source_target_pairs={{0,1},{2,3},{4,5},{6,7},{1,0},{3,2},{5,4},{7,6},{8,9},{10,11},{12,... | collective-permute-start | bytes 442376 | tf_op jit(solution)/shard_map/ppermute | solution.py:509
  37.1 4.7 %collective-permute-done.1.outer = f32[2,3,48,128]{3,2,1,0:T(8,128)S(1)} collective-permute-done((f32[2,3,48,128]{3,2,1,0:T(8,128)S(1)}, f32[2,3,48,128]{3,2,1,0:T(8,128)S(1)}, u32[]{:S(2)}, u32[]{:S(2)}) %collective-permute-start.1) | collective-permute-done | bytes 147488 | tf_op jit(solution)/shard_map/ppermute | solution.py:508
  42.4 2.9 %forward.1.below = f32[4,2,8,32,128]{4,3,2,1,0:T(8,128)S(1)} custom-call(f32[84]{0:T(128)S(1)} %reshape.22.w_ref, f32[2,14,40,128]{3,2,1,0:T(8,128)S(1)} %extend.1.est), custom_call_target="tpu_custom_call" | custom-call | flops 1000 | bytes 1000 | tf_op jit(solution)/shard_map/forward/pallas_call | solution.py:170
  45.3 27.5 %all-to-all-done = f32[64,65,1,128]{3,2,1,0:T(1,128)} async-done(((f32[64,65,1,128]{3,2,1,0:T(1,128)}), f32[64,65,1,128]{3,2,1,0:T(1,128)}, u32[]{:S(2)}, u32[]{:S(2)}) %all-to-all-start) | async-done | bytes 2129952 | tf_op jit(solution)/shard_map/all_to_all | solution.py:550
  72.9 6.3 %unpack.1 = (f32[512,128]{1,0:T(8,128)S(1)}, f32[512,128]{1,0:T(8,128)S(1)}, f32[512,128]{1,0:T(8,128)S(1)}, f32[512,128]{1,0:T(8,128)S(1)}) custom-call(s32[4]{0:T(128)S(1)} %pad_add_fusion.id_ref, f32[4160,1,128]{2,1,0:T(1,128)} %bitcast.8.in_ref), custom_call_target="tpu_custom_call" | custom-call | flops 1000 | bytes 1000 | tf_op jit(solution)/shard_map/unpack/pallas_call | solution.py:170
  79.3 3.5 %collective-permute-start.5 = (f32[2,8,32,128]{3,2,1,0:T(8,128)S(1)}, f32[2,8,32,128]{3,2,1,0:T(8,128)S(1)}, u32[]{:S(2)}, u32[]{:S(2)}) collective-permute-start(f32[2,8,32,128]{3,2,1,0:T(8,128)S(1)} %bitcast.18), channel_id=1, source_target_pairs={{0,24},{8,0},{16,8},{24,16},{1,25},{9,1},{17,9},{25,17},{2,26},{10... | collective-permute-start | bytes 786440 | tf_op jit(solution)/shard_map/ppermute | solution.py:522
  85.4 3.6 %collective-permute-done.4.refs_0_.refs_3_ = f32[2,8,32,128]{3,2,1,0:T(8,128)S(1)} collective-permute-done((f32[2,8,32,128]{3,2,1,0:T(8,128)S(1)}, f32[2,8,32,128]{3,2,1,0:T(8,128)S(1)}, u32[]{:S(2)}, u32[]{:S(2)}) %collective-permute-start.4) | collective-permute-done | bytes 262176 | tf_op jit(solution)/shard_map/ppermute | solution.py:522
  89.0 5.0 %collective-permute-done.5.refs_1_ = f32[2,8,32,128]{3,2,1,0:T(8,128)S(1)} collective-permute-done((f32[2,8,32,128]{3,2,1,0:T(8,128)S(1)}, f32[2,8,32,128]{3,2,1,0:T(8,128)S(1)}, u32[]{:S(2)}, u32[]{:S(2)}) %collective-permute-start.5) | collective-permute-done | bytes 262176 | tf_op jit(solution)/shard_map/ppermute | solution.py:522
  94.0 1.7 %backward.5.refs_1_ = f32[2,14,40,128]{3,2,1,0:T(8,128)S(1)} custom-call(f32[84]{0:T(128)S(1)} %reshape.22.w_ref, s32[4]{0:T(128)S(1)} %pad_add_fusion.id_ref, f32[4,2,8,32,128]{4,3,2,1,0:T(8,128)S(1)} %forward.1.below, f32[2,8,32,128]{3,2,1,0:T(8,128)S(1)} %collective-permute-done.4.refs_0_.refs_3_, f32[2,8,32,128]{3,2,1,0:T(8,128)S(1)} %collective-permute-done.5.refs_1_, ...), custom_call_target="tpu_custom_call" | custom-call | flops 1000 | bytes 1000 | tf_op jit(solution)/shard_map/backward/pallas_call | solution.py:170
  97.1 1.9 %collective-permute-start.6 = (f32[2,6,40,128]{3,2,1,0:T(8,128)S(1)}, f32[2,6,40,128]{3,2,1,0:T(8,128)S(1)}, u32[]{:S(2)}, u32[]{:S(2)}) collective-permute-start(f32[2,6,40,128]{3,2,1,0:T(8,128)S(1)} %get-tuple-element.46), channel_id=1, source_target_pairs={{1,2},{3,4},{5,6},{2,1},{4,3},{6,5},{9,10},{11,12},{13,14},{10,9},... | collective-permute-start | bytes 737288 | tf_op jit(solution)/shard_map/ppermute | solution.py:508
  99.0 1.7 %collective-permute-start.7 = (f32[2,6,40,128]{3,2,1,0:T(8,128)S(1)}, f32[2,6,40,128]{3,2,1,0:T(8,128)S(1)}, u32[]{:S(2)}, u32[]{:S(2)}) collective-permute-start(f32[2,6,40,128]{3,2,1,0:T(8,128)S(1)} %get-tuple-element.47), channel_id=1, source_target_pairs={{0,1},{2,3},{4,5},{6,7},{1,0},{3,2},{5,4},{7,6},{8,9},{10,11},{12,... | collective-permute-start | bytes 737288 | tf_op jit(solution)/shard_map/ppermute | solution.py:509
  100.7 3.9 %collective-permute-done.6.outer = f32[2,6,40,128]{3,2,1,0:T(8,128)S(1)} collective-permute-done((f32[2,6,40,128]{3,2,1,0:T(8,128)S(1)}, f32[2,6,40,128]{3,2,1,0:T(8,128)S(1)}, u32[]{:S(2)}, u32[]{:S(2)}) %collective-permute-start.6) | collective-permute-done | bytes 245792 | tf_op jit(solution)/shard_map/ppermute | solution.py:508
  105.3 2.3 %collective-permute-start.8 = (f32[2,14,8,128]{3,2,1,0:T(8,128)S(1)}, f32[2,14,8,128]{3,2,1,0:T(8,128)S(1)}, u32[]{:S(2)}, u32[]{:S(2)}) collective-permute-start(f32[2,14,8,128]{3,2,1,0:T(8,128)S(1)} %get-tuple-element.49), channel_id=1, source_target_pairs={{8,16},{24,56},{48,40},{32,64},{72,80},{88,120},{112,104},{96,128}... | collective-permute-start | bytes 344072 | tf_op jit(solution)/shard_map/ppermute | solution.py:516
  108.6 1.8 %middle.1 = (f32[4,2,8,16,128]{4,3,2,1,0:T(8,128)S(1)}, f32[4,2,8,24,128]{4,3,2,1,0:T(8,128)S(1)}) custom-call(f32[84]{0:T(128)S(1)} %reshape.22.w_ref, f32[2,14,40,128]{3,2,1,0:T(8,128)S(1)} %extend.1.est, f32[2,14,40,128]{3,2,1,0:T(8,128)S(1)} %get-tuple-element.48.total), custom_call_target="tpu_custom_call" | custom-call | flops 1000 | bytes 1000 | tf_op jit(solution)/shard_map/middle/pallas_call | solution.py:170
  110.5 1.9 %collective-permute-done.8.outer = f32[2,14,8,128]{3,2,1,0:T(8,128)S(1)} collective-permute-done((f32[2,14,8,128]{3,2,1,0:T(8,128)S(1)}, f32[2,14,8,128]{3,2,1,0:T(8,128)S(1)}, u32[]{:S(2)}, u32[]{:S(2)}) %collective-permute-start.8) | collective-permute-done | bytes 114720 | tf_op jit(solution)/shard_map/ppermute | solution.py:516
  112.6 1.9 %ends.1 = (f32[2,14,40,128]{3,2,1,0:T(8,128)S(1)}, f32[4,2,8,32,128]{4,3,2,1,0:T(8,128)S(1)}) custom-call(f32[84]{0:T(128)S(1)} %reshape.22.w_ref, s32[4]{0:T(128)S(1)} %pad_add_fusion.id_ref, f32[2,14,40,128]{3,2,1,0:T(8,128)S(1)} %get-tuple-element.48.total, f32[2,14,8,128]{3,2,1,0:T(8,128)S(1)} %collective-permute-done.8.outer, ...), custom_call_target="tpu_custom_call" | custom-call | flops 1000 | bytes 1000 | tf_op jit(solution)/shard_map/ends/pallas_call | solution.py:170
  114.5 2.8 %backward.7 = (f32[2,14,40,128]{3,2,1,0:T(8,128)S(1)}, f32[2,3,40,128]{3,2,1,0:T(8,128)S(1)}, f32[2,3,40,128]{3,2,1,0:T(8,128)S(1)}) custom-call(f32[84]{0:T(128)S(1)} %reshape.22.w_ref, s32[4]{0:T(128)S(1)} %pad_add_fusion.id_ref, f32[4,2,8,32,128]{4,3,2,1,0:T(8,128)S(1)} %get-tuple-element.53.below, f32[2,8,32,128]{3,2,1,0:T(8,128)S(1)} %bitcast.16, ...), custom_call_target="tpu_custom_call" | custom-call | flops 1000 | bytes 1000 | tf_op jit(solution)/shard_map/backward/pallas_call | solution.py:170
  117.3 1.9 %collective-permute-start.10 = (f32[2,3,40,128]{3,2,1,0:T(8,128)S(1)}, f32[2,3,40,128]{3,2,1,0:T(8,128)S(1)}, u32[]{:S(2)}, u32[]{:S(2)}) collective-permute-start(f32[2,3,40,128]{3,2,1,0:T(8,128)S(1)} %get-tuple-element.55), channel_id=1, source_target_pairs={{1,2},{3,4},{5,6},{2,1},{4,3},{6,5},{9,10},{11,12},{13,14},{10,9},... | collective-permute-start | bytes 368648 | tf_op jit(solution)/shard_map/ppermute | solution.py:508
  120.7 2.9 %collective-permute-done.10.outer = f32[2,3,40,128]{3,2,1,0:T(8,128)S(1)} collective-permute-done((f32[2,3,40,128]{3,2,1,0:T(8,128)S(1)}, f32[2,3,40,128]{3,2,1,0:T(8,128)S(1)}, u32[]{:S(2)}, u32[]{:S(2)}) %collective-permute-start.10) | collective-permute-done | bytes 122912 | tf_op jit(solution)/shard_map/ppermute | solution.py:508
  124.2 3.6 %collective-permute-start.12 = (f32[2,8,8,128]{3,2,1,0:T(8,128)S(1)}, f32[2,8,8,128]{3,2,1,0:T(8,128)S(1)}, u32[]{:S(2)}, u32[]{:S(2)}) collective-permute-start(f32[2,8,8,128]{3,2,1,0:T(8,128)S(1)} %get-tuple-element.58), channel_id=1, source_target_pairs={{8,16},{24,56},{48,40},{32,64},{72,80},{88,120},{112,104},{96,128}... | collective-permute-start | bytes 196616 | tf_op jit(solution)/shard_map/ppermute | solution.py:516
  127.8 1.7 %collective-permute-start.13 = (f32[2,8,8,128]{3,2,1,0:T(8,128)S(1)}, f32[2,8,8,128]{3,2,1,0:T(8,128)S(1)}, u32[]{:S(2)}, u32[]{:S(2)}) collective-permute-start(f32[2,8,8,128]{3,2,1,0:T(8,128)S(1)} %get-tuple-element.59), channel_id=1, source_target_pairs={{0,8},{16,24},{56,48},{40,32},{64,72},{80,88},{120,112},{104,96},{... | collective-permute-start | bytes 196616 | tf_op jit(solution)/shard_map/ppermute | solution.py:517
  130.3 1.8 %collective-permute-done.13.inner = f32[2,8,8,128]{3,2,1,0:T(8,128)S(1)} collective-permute-done((f32[2,8,8,128]{3,2,1,0:T(8,128)S(1)}, f32[2,8,8,128]{3,2,1,0:T(8,128)S(1)}, u32[]{:S(2)}, u32[]{:S(2)}) %collective-permute-start.13) | collective-permute-done | bytes 65568 | tf_op jit(solution)/shard_map/ppermute | solution.py:517
  133.0 1.6 %collective-permute-start.16 = (f32[8,32,128]{2,1,0:T(8,128)S(1)}, f32[8,32,128]{2,1,0:T(8,128)S(1)}, u32[]{:S(2)}, u32[]{:S(2)}) collective-permute-start(f32[8,32,128]{2,1,0:T(8,128)S(1)} %get-tuple-element.61.refs_0_), channel_id=1, source_target_pairs={{0,8},{8,16},{16,24},{24,0},{1,9},{9,17},{17,25},{25,1},{2,10},{10... | collective-permute-start | bytes 393224 | tf_op jit(solution)/shard_map/ppermute | solution.py:522
  134.6 2.1 %collective-permute-start.15 = (f32[8,32,128]{2,1,0:T(8,128)S(1)}, f32[8,32,128]{2,1,0:T(8,128)S(1)}, u32[]{:S(2)}, u32[]{:S(2)}) collective-permute-start(f32[8,32,128]{2,1,0:T(8,128)S(1)} %get-tuple-element.62.refs_1_), channel_id=1, source_target_pairs={{0,24},{8,0},{16,8},{24,16},{1,25},{9,1},{17,9},{25,17},{2,26},{10... | collective-permute-start | bytes 393224 | tf_op jit(solution)/shard_map/ppermute | solution.py:522
  136.8 1.9 %collective-permute-start.14 = (f32[8,32,128]{2,1,0:T(8,128)S(1)}, f32[8,32,128]{2,1,0:T(8,128)S(1)}, u32[]{:S(2)}, u32[]{:S(2)}) collective-permute-start(f32[8,32,128]{2,1,0:T(8,128)S(1)} %get-tuple-element.61.refs_0_), channel_id=1, source_target_pairs={{0,24},{8,0},{16,8},{24,16},{1,25},{9,1},{17,9},{25,17},{2,26},{10... | collective-permute-start | bytes 393224 | tf_op jit(solution)/shard_map/ppermute | solution.py:522
  140.9 2.5 %collective-permute-start.18 = (f32[8,32,128]{2,1,0:T(8,128)S(1)}, f32[8,32,128]{2,1,0:T(8,128)S(1)}, u32[]{:S(2)}, u32[]{:S(2)}) collective-permute-start(f32[8,32,128]{2,1,0:T(8,128)S(1)} %collective-permute-done.15.refs_3_), channel_id=1, source_target_pairs={{0,24},{8,0},{16,8},{24,16},{1,25},{9,1},{17,9},{25,17},{2,26},{10... | collective-permute-start | bytes 393224 | tf_op jit(solution)/shard_map/ppermute | solution.py:522
  146.3 1.6 %join.1 = f32[8,128,256]{2,1,0:T(8,128)} custom-call(s32[4]{0:T(128)S(1)} %pad_add_fusion.id_ref, f32[8,32,128]{2,1,0:T(8,128)S(1)} %get-tuple-element.61.refs_0_, f32[8,32,128]{2,1,0:T(8,128)S(1)} %get-tuple-element.62.refs_1_, f32[8,32,128]{2,1,0:T(8,128)S(1)} %collective-permute-done.14.refs_2_, f32[8,32,128]{2,1,0:T(8,128)S(1)} %collective-permute-done.15.refs_3_, ...), custom_call_target="tpu_custom_call" | custom-call | flops 1000 | bytes 1000 | tf_op jit(solution)/shard_map/join/pallas_call | solution.py:170
  (35 shorter events, 17.2 us)
Async XLA Ops:
  0.8 10.4 %collective-permute-start = (f32[8,8,256]{2,1,0:T(8,128)S(1)}, f32[8,8,256]{2,1,0:T(8,128)S(1)}, u32[]{:S(2)}, u32[]{:S(2)}) collective-permute-start(f32[8,8,256]{2,1,0:T(8,128)S(1)} %constant_dynamic-slice_fusion), channel_id=1, source_target_pairs={{24,56},{32,64},{88,120},{96,128},{152,184},{160,192},{216,248},{5... | collective-permute-start | bytes 196616 | tf_op jit(solution)/shard_map/ppermute | solution.py:545
  11.2 10.6 %copy-start.1 = (f32[1,3,7]{2,0,1:T(1,128)S(1)}, f32[1,3,7]{2,0,1:T(1,128)}, u32[]{:S(2)}) copy-start(f32[1,3,7]{2,0,1:T(1,128)} %param.8) | copy-start | bytes 256
  11.3 21.3 %copy-start = (f32[8,128,256]{2,1,0:T(8,128)S(1)}, f32[8,128,256]{2,1,0:T(8,128)}, u32[]{:S(2)}) copy-start(f32[8,128,256]{2,1,0:T(8,128)} %est.1) | copy-start | bytes 3145732
  11.3 61.6 %all-to-all-start = ((f32[64,65,1,128]{3,2,1,0:T(1,128)}), f32[64,65,1,128]{3,2,1,0:T(1,128)}, u32[]{:S(2)}, u32[]{:S(2)}) async-start(f32[64,65,1,128]{3,2,1,0:T(1,128)} %bitcast.20), calls=%async_computation | async-start | bytes 4259840 | tf_op jit(solution)/shard_map/all_to_all | solution.py:550
  33.4 8.4 %collective-permute-start.1 = (f32[2,3,48,128]{3,2,1,0:T(8,128)S(1)}, f32[2,3,48,128]{3,2,1,0:T(8,128)S(1)}, u32[]{:S(2)}, u32[]{:S(2)}) collective-permute-start(f32[2,3,48,128]{3,2,1,0:T(8,128)S(1)} %get-tuple-element.37), channel_id=1, source_target_pairs={{1,2},{3,4},{5,6},{2,1},{4,3},{6,5},{9,10},{11,12},{13,14},{10,9},... | collective-permute-start | bytes 442376 | tf_op jit(solution)/shard_map/ppermute | solution.py:508
  35.3 6.5 %collective-permute-start.2 = (f32[2,3,48,128]{3,2,1,0:T(8,128)S(1)}, f32[2,3,48,128]{3,2,1,0:T(8,128)S(1)}, u32[]{:S(2)}, u32[]{:S(2)}) collective-permute-start(f32[2,3,48,128]{3,2,1,0:T(8,128)S(1)} %get-tuple-element.38), channel_id=1, source_target_pairs={{0,1},{2,3},{4,5},{6,7},{1,0},{3,2},{5,4},{7,6},{8,9},{10,11},{12,... | collective-permute-start | bytes 442376 | tf_op jit(solution)/shard_map/ppermute | solution.py:509
  79.2 9.8 %collective-permute-start.4 = (f32[2,8,32,128]{3,2,1,0:T(8,128)S(1)}, f32[2,8,32,128]{3,2,1,0:T(8,128)S(1)}, u32[]{:S(2)}, u32[]{:S(2)}) collective-permute-start(f32[2,8,32,128]{3,2,1,0:T(8,128)S(1)} %bitcast.19), channel_id=1, source_target_pairs={{0,8},{8,16},{16,24},{24,0},{1,9},{9,17},{17,25},{25,1},{2,10},{10... | collective-permute-start | bytes 786440 | tf_op jit(solution)/shard_map/ppermute | solution.py:522
  79.3 14.7 %collective-permute-start.5 = (f32[2,8,32,128]{3,2,1,0:T(8,128)S(1)}, f32[2,8,32,128]{3,2,1,0:T(8,128)S(1)}, u32[]{:S(2)}, u32[]{:S(2)}) collective-permute-start(f32[2,8,32,128]{3,2,1,0:T(8,128)S(1)} %bitcast.18), channel_id=1, source_target_pairs={{0,24},{8,0},{16,8},{24,16},{1,25},{9,1},{17,9},{25,17},{2,26},{10... | collective-permute-start | bytes 786440 | tf_op jit(solution)/shard_map/ppermute | solution.py:522
  82.8 13.0 %collective-permute-start.3 = (f32[2,8,32,128]{3,2,1,0:T(8,128)S(1)}, f32[2,8,32,128]{3,2,1,0:T(8,128)S(1)}, u32[]{:S(2)}, u32[]{:S(2)}) collective-permute-start(f32[2,8,32,128]{3,2,1,0:T(8,128)S(1)} %bitcast.17), channel_id=1, source_target_pairs={{0,16},{8,24},{16,0},{24,8},{1,17},{9,25},{17,1},{25,9},{2,18},{10... | collective-permute-start | bytes 786440 | tf_op jit(solution)/shard_map/ppermute | solution.py:522
  97.1 7.5 %collective-permute-start.6 = (f32[2,6,40,128]{3,2,1,0:T(8,128)S(1)}, f32[2,6,40,128]{3,2,1,0:T(8,128)S(1)}, u32[]{:S(2)}, u32[]{:S(2)}) collective-permute-start(f32[2,6,40,128]{3,2,1,0:T(8,128)S(1)} %get-tuple-element.46), channel_id=1, source_target_pairs={{1,2},{3,4},{5,6},{2,1},{4,3},{6,5},{9,10},{11,12},{13,14},{10,9},... | collective-permute-start | bytes 737288 | tf_op jit(solution)/shard_map/ppermute | solution.py:508
  99.0 5.6 %collective-permute-start.7 = (f32[2,6,40,128]{3,2,1,0:T(8,128)S(1)}, f32[2,6,40,128]{3,2,1,0:T(8,128)S(1)}, u32[]{:S(2)}, u32[]{:S(2)}) collective-permute-start(f32[2,6,40,128]{3,2,1,0:T(8,128)S(1)} %get-tuple-element.47), channel_id=1, source_target_pairs={{0,1},{2,3},{4,5},{6,7},{1,0},{3,2},{5,4},{7,6},{8,9},{10,11},{12,... | collective-permute-start | bytes 737288 | tf_op jit(solution)/shard_map/ppermute | solution.py:509
  105.3 7.1 %collective-permute-start.8 = (f32[2,14,8,128]{3,2,1,0:T(8,128)S(1)}, f32[2,14,8,128]{3,2,1,0:T(8,128)S(1)}, u32[]{:S(2)}, u32[]{:S(2)}) collective-permute-start(f32[2,14,8,128]{3,2,1,0:T(8,128)S(1)} %get-tuple-element.49), channel_id=1, source_target_pairs={{8,16},{24,56},{48,40},{32,64},{72,80},{88,120},{112,104},{96,128}... | collective-permute-start | bytes 344072 | tf_op jit(solution)/shard_map/ppermute | solution.py:516
  107.6 5.1 %collective-permute-start.9 = (f32[2,14,8,128]{3,2,1,0:T(8,128)S(1)}, f32[2,14,8,128]{3,2,1,0:T(8,128)S(1)}, u32[]{:S(2)}, u32[]{:S(2)}) collective-permute-start(f32[2,14,8,128]{3,2,1,0:T(8,128)S(1)} %get-tuple-element.50), channel_id=1, source_target_pairs={{0,8},{16,24},{56,48},{40,32},{64,72},{80,88},{120,112},{104,96},{... | collective-permute-start | bytes 344072 | tf_op jit(solution)/shard_map/ppermute | solution.py:517
  117.3 6.2 %collective-permute-start.10 = (f32[2,3,40,128]{3,2,1,0:T(8,128)S(1)}, f32[2,3,40,128]{3,2,1,0:T(8,128)S(1)}, u32[]{:S(2)}, u32[]{:S(2)}) collective-permute-start(f32[2,3,40,128]{3,2,1,0:T(8,128)S(1)} %get-tuple-element.55), channel_id=1, source_target_pairs={{1,2},{3,4},{5,6},{2,1},{4,3},{6,5},{9,10},{11,12},{13,14},{10,9},... | collective-permute-start | bytes 368648 | tf_op jit(solution)/shard_map/ppermute | solution.py:508
  119.3 4.3 %collective-permute-start.11 = (f32[2,3,40,128]{3,2,1,0:T(8,128)S(1)}, f32[2,3,40,128]{3,2,1,0:T(8,128)S(1)}, u32[]{:S(2)}, u32[]{:S(2)}) collective-permute-start(f32[2,3,40,128]{3,2,1,0:T(8,128)S(1)} %get-tuple-element.56), channel_id=1, source_target_pairs={{0,1},{2,3},{4,5},{6,7},{1,0},{3,2},{5,4},{7,6},{8,9},{10,11},{12,... | collective-permute-start | bytes 368648 | tf_op jit(solution)/shard_map/ppermute | solution.py:509
  124.2 6.2 %collective-permute-start.12 = (f32[2,8,8,128]{3,2,1,0:T(8,128)S(1)}, f32[2,8,8,128]{3,2,1,0:T(8,128)S(1)}, u32[]{:S(2)}, u32[]{:S(2)}) collective-permute-start(f32[2,8,8,128]{3,2,1,0:T(8,128)S(1)} %get-tuple-element.58), channel_id=1, source_target_pairs={{8,16},{24,56},{48,40},{32,64},{72,80},{88,120},{112,104},{96,128}... | collective-permute-start | bytes 196616 | tf_op jit(solution)/shard_map/ppermute | solution.py:516
  127.8 4.4 %collective-permute-start.13 = (f32[2,8,8,128]{3,2,1,0:T(8,128)S(1)}, f32[2,8,8,128]{3,2,1,0:T(8,128)S(1)}, u32[]{:S(2)}, u32[]{:S(2)}) collective-permute-start(f32[2,8,8,128]{3,2,1,0:T(8,128)S(1)} %get-tuple-element.59), channel_id=1, source_target_pairs={{0,8},{16,24},{56,48},{40,32},{64,72},{80,88},{120,112},{104,96},{... | collective-permute-start | bytes 196616 | tf_op jit(solution)/shard_map/ppermute | solution.py:517
  133.0 6.6 %collective-permute-start.16 = (f32[8,32,128]{2,1,0:T(8,128)S(1)}, f32[8,32,128]{2,1,0:T(8,128)S(1)}, u32[]{:S(2)}, u32[]{:S(2)}) collective-permute-start(f32[8,32,128]{2,1,0:T(8,128)S(1)} %get-tuple-element.61.refs_0_), channel_id=1, source_target_pairs={{0,8},{8,16},{16,24},{24,0},{1,9},{9,17},{17,25},{25,1},{2,10},{10... | collective-permute-start | bytes 393224 | tf_op jit(solution)/shard_map/ppermute | solution.py:522
  134.6 6.3 %collective-permute-start.15 = (f32[8,32,128]{2,1,0:T(8,128)S(1)}, f32[8,32,128]{2,1,0:T(8,128)S(1)}, u32[]{:S(2)}, u32[]{:S(2)}) collective-permute-start(f32[8,32,128]{2,1,0:T(8,128)S(1)} %get-tuple-element.62.refs_1_), channel_id=1, source_target_pairs={{0,24},{8,0},{16,8},{24,16},{1,25},{9,1},{17,9},{25,17},{2,26},{10... | collective-permute-start | bytes 393224 | tf_op jit(solution)/shard_map/ppermute | solution.py:522
  136.8 6.7 %collective-permute-start.14 = (f32[8,32,128]{2,1,0:T(8,128)S(1)}, f32[8,32,128]{2,1,0:T(8,128)S(1)}, u32[]{:S(2)}, u32[]{:S(2)}) collective-permute-start(f32[8,32,128]{2,1,0:T(8,128)S(1)} %get-tuple-element.61.refs_0_), channel_id=1, source_target_pairs={{0,24},{8,0},{16,8},{24,16},{1,25},{9,1},{17,9},{25,17},{2,26},{10... | collective-permute-start | bytes 393224 | tf_op jit(solution)/shard_map/ppermute | solution.py:522
  138.7 6.2 %collective-permute-start.19 = (f32[8,32,128]{2,1,0:T(8,128)S(1)}, f32[8,32,128]{2,1,0:T(8,128)S(1)}, u32[]{:S(2)}, u32[]{:S(2)}) collective-permute-start(f32[8,32,128]{2,1,0:T(8,128)S(1)} %get-tuple-element.62.refs_1_), channel_id=1, source_target_pairs={{0,8},{8,16},{16,24},{24,0},{1,9},{9,17},{17,25},{25,1},{2,10},{10... | collective-permute-start | bytes 393224 | tf_op jit(solution)/shard_map/ppermute | solution.py:522
  139.6 6.7 %collective-permute-start.17 = (f32[8,32,128]{2,1,0:T(8,128)S(1)}, f32[8,32,128]{2,1,0:T(8,128)S(1)}, u32[]{:S(2)}, u32[]{:S(2)}) collective-permute-start(f32[8,32,128]{2,1,0:T(8,128)S(1)} %collective-permute-done.16.refs_6_), channel_id=1, source_target_pairs={{0,8},{8,16},{16,24},{24,0},{1,9},{9,17},{17,25},{25,1},{2,10},{10... | collective-permute-start | bytes 393224 | tf_op jit(solution)/shard_map/ppermute | solution.py:522
  140.9 5.4 %collective-permute-start.18 = (f32[8,32,128]{2,1,0:T(8,128)S(1)}, f32[8,32,128]{2,1,0:T(8,128)S(1)}, u32[]{:S(2)}, u32[]{:S(2)}) collective-permute-start(f32[8,32,128]{2,1,0:T(8,128)S(1)} %collective-permute-done.15.refs_3_), channel_id=1, source_target_pairs={{0,24},{8,0},{16,8},{24,16},{1,25},{9,1},{17,9},{25,17},{2,26},{10... | collective-permute-start | bytes 393224 | tf_op jit(solution)/shard_map/ppermute | solution.py:522

commit v14 on v13

--- a/solution.py
+++ b/solution.py
@@ -87,7 +87,7 @@
                 out_ref[place] = row
         return c
 
-    lax.fori_loop(0, groups, body, 0)
+    lax.fori_loop(0, groups, body, 0, unroll=2)
 
 
 def pack(shift, target, views, geo):
@@ -135,7 +135,7 @@
                 placed[pl.ds(place, 1), :] = row
         return c
 
-    lax.fori_loop(0, peers, per_peer, 0)
+    lax.fori_loop(0, peers, per_peer, 0, unroll=2)
     for d, out in enumerate(outs):
         out[...] = placed[d * size : (d + 1) * size, :]
 
@@ -342,13 +342,15 @@
 def renew(views, id_ref, total, outer, inner, est, out_ref):
     layers, rows = out_ref.shape[1:3]
     odd = lax.rem(id_ref[2], 2)
-    at_in = pl.ds(pl.multiple_of((1 - odd) * (rows - TILE), TILE), TILE)
-    at_out = pl.ds(pl.multiple_of(odd * (rows - TILE), TILE), TILE)
+    spans = (slice(0, TILE), slice(TILE, rows - TILE), slice(rows - TILE, rows))
     for c in range(2):
         for i in range(layers):
-            out_ref[c, i] = est[c, i] * total[c, i] / views
-            for at, more in ((at_in, inner), (at_out, outer)):
-                out_ref[c, i, at, :] = est[c, i, at, :] * (total[c, i, at, :] + more[c, i]) / views
+            low, high = low_high(odd, inner[c, i], outer[c, i])
+            for at, more in zip(spans, (low, None, high)):
+                value = total[c, i, at, :]
+                if more is not None:
+                    value += more
+                out_ref[c, i, at, :] = est[c, i, at, :] * value / views
 
 
 def ends_kernel(w_ref, id_ref, total, outer, inner, est, mid, part_ref, new, out_ref, strip):
@@ -444,23 +446,25 @@
     )
 
 
+def low_high(odd, inner, outer):
+    return jnp.where(odd == 1, inner, outer), jnp.where(odd == 1, outer, inner)
+
+
 def merge_kernel(id_ref, total, outer, inner, out_ref, send_in, send_out):
     layers, rows = out_ref.shape[1:3]
     count = inner.shape[1]
     skip = (total.shape[1] - layers) // 2
     odd, odd_part = id_ref[1], lax.rem(id_ref[2], 2)
-    base = layers - count
-    at_in = pl.ds(pl.multiple_of((1 - odd_part) * (rows - TILE), TILE), TILE)
-    at_out = pl.ds(pl.multiple_of(odd_part * (rows - TILE), TILE), TILE)
     for c in range(2):
+        for i in range(count):
+            low, high = low_high(odd, inner[c, i], outer[c, i])
+            out_ref[c, i] = total[c, skip + i] + low
+            out_ref[c, layers - count + i] = total[c, skip + layers - count + i] + high
+        for i in range(count, layers - count):
+            out_ref[c, i] = total[c, skip + i]
         for i in range(layers):
-            out_ref[c, i] = total[c, skip + i]
-        for i in range(count):
-            out_ref[c, (1 - odd) * base + i] += inner[c, i]
-            out_ref[c, odd * base + i] += outer[c, i]
-        for i in range(layers):
-            send_in[c, i] = out_ref[c, i, at_in, :]
-            send_out[c, i] = out_ref[c, i, at_out, :]
+            top, bottom = out_ref[c, i, 0:TILE, :], out_ref[c, i, rows - TILE : rows, :]
+            send_in[c, i], send_out[c, i] = low_high(odd_part, top, bottom)
 
 
 def merge(ids, total, outer, inner, layers):
@@ -472,15 +476,16 @@
 def finish_kernel(views, id_ref, total, outer, inner, est, out_a, out_b, wide):
     layers, rows = total.shape[1:3]
     odd = lax.rem(id_ref[2], 2)
-    at_in = pl.ds(pl.multiple_of((1 - odd) * (rows - TILE), TILE), TILE)
-    at_out = pl.ds(pl.multiple_of(odd * (rows - TILE), TILE), TILE)
     own = slice(TRIM, rows - TRIM)
     for c, out in ((0, out_a), (1, out_b)):
         for i in range(layers):
-            wide[...] = total[c, i]
-            wide[at_in, :] += inner[c, i]
-            wide[at_out, :] += outer[c, i]
-            out[i] = est[c, HALO + i, own, :] * wide[own, :] / views
+            low, high = low_high(odd, inner[c, i], outer[c, i])
+            wide[c, i, 0:TILE, :] = total[c, i, 0:TILE, :] + low
+            wide[c, i, TILE : rows - TILE, :] = total[c, i, TILE : rows - TILE, :]
+            wide[c, i, rows - TILE : rows, :] = total[c, i, rows - TILE : rows, :] + high
+    for c, out in ((0, out_a), (1, out_b)):
+        for i in range(layers):
+            out[i] = est[c, HALO + i, own, :] * wide[c, i, own, :] / views
 
 
 def join_kernel(views, id_ref, *refs):
@@ -581,7 +586,7 @@
     own = call(
         functools.partial(finish_kernel, view_count), "finish",
         [f32(x_cells, part, BRICK)] * 2, args,
-        scratch=[pltpu.VMEM((part + 2 * TRIM, BRICK), jnp.float32)],
+        scratch=[pltpu.VMEM((2, x_cells, part + 2 * TRIM, BRICK), jnp.float32)],
     )
     prev_a, next_b = turn(own[0], 1, view_count), turn(own[1], -1, view_count)
     prev_b, next_a = turn(own[1], 1, view_count), turn(own[0], -1, view_count)

time: 150 us -> 150 us (level)
  no operation moved by 1% of the time
where the time goes in v14:
time: 150 us; the launch traced here: 147 us
  waiting for transfers between devices  57.3 us (38%)
  starting transfers between devices  47 us (31%)
  Pallas kernels  30.4 us (20%)
  blocking collectives  10.7 us (7%)
    all_to_all x1, waiting for transfers between devices, per_device(): lax.all_to_all(outgoing.reshape(peer_count, capacity + 1, 1, BRICK), ('bl...  27.5 us
    pallas_call x14, Pallas kernels, call(): pl.pallas_call(kernel, out_shape=outs, in_specs=[smem()] * scalars + [vme...  24.5 us
    ppermute x9, starting transfers between devices, turn(): lax.ppermute(value, 'views', [(i, (i + step) % count) for i in range(coun...  13.5 us
    ppermute x9, waiting for transfers between devices, turn(): lax.ppermute(value, 'views', [(i, (i + step) % count) for i in range(coun...  13.4 us
    ppermute x3, waiting for transfers between devices, swap_layers(): lax.ppermute(outer, 'rows', both_ways([(i, i + 1) for i in range(1, count...  11.5 us
    all_gather x1, blocking collectives, per_device(): taps = lax.all_gather(psf_taps, 'views', axis=0, tiled=True)  10.7 us
    all_to_all x1, starting transfers between devices, per_device(): lax.all_to_all(outgoing.reshape(peer_count, capacity + 1, 1, BRICK), ('bl...  10.5 us
    ppermute x2, starting transfers between devices, swap_rows(): lax.ppermute(outer, axes, both_ways(list(zip(chain[1:-1:2], chain[2::2]))))  5.94 us
  transfers between devices with their start and end apart: 21, of which 15 were waited for; matrix products, arithmetic and copies ran while one was open for 0% of the time, Pallas kernels for 10%

profile of v14, /device:TPU:34, one launch (start us, length us, event | category | flops | bytes accessed | tf_op | source)
XLA Modules:
  0.0 147.4 jit_solution(13156117716956655004)
XLA Ops:
  0.8 3.8 %collective-permute-start = (f32[8,8,256]{2,1,0:T(8,128)S(1)}, f32[8,8,256]{2,1,0:T(8,128)S(1)}, u32[]{:S(2)}, u32[]{:S(2)}) collective-permute-start(f32[8,8,256]{2,1,0:T(8,128)S(1)} %constant_dynamic-slice_fusion), channel_id=1, source_target_pairs={{24,56},{32,64},{88,120},{96,128},{152,184},{160,192},{216,248},{5... | collective-permute-start | bytes 196616 | tf_op jit(solution)/shard_map/ppermute | solution.py:550
  5.3 5.9 %pack.1 = f32[4160,1,128]{2,1,0:T(1,128)} custom-call(s32[1]{0:T(128)S(6)} %copy.9.shift_ref, s32[8,2,128]{2,1,0:T(2,128)} %bitcast.22, f32[8,128,256]{2,1,0:T(8,128)} %bitcast.21), custom_call_target="tpu_custom_call" | custom-call | tf_op jit(solution)/shard_map/pack/pallas_call | solution.py:96
  11.2 10.5 %all-to-all-start = ((f32[64,65,1,128]{3,2,1,0:T(1,128)}), f32[64,65,1,128]{3,2,1,0:T(1,128)}, u32[]{:S(2)}, u32[]{:S(2)}) async-start(f32[64,65,1,128]{3,2,1,0:T(1,128)} %bitcast.20), calls=%async_computation | async-start | bytes 4259840 | tf_op jit(solution)/shard_map/all_to_all | solution.py:555
  21.8 10.7 %all_gather.3 = f32[4,3,7]{2,1,0:T(4,128)S(1)} all-gather(f32[1,3,7]{2,1,0:T(4,128)S(1)} %copy.8), channel_id=1, replica_groups=mesh['blocks'=8,'views'=4,'rows'=8] {'views'}, dimensions={0}, use_global_device_ids=true | all-gather | bytes 420 | tf_op jit(solution)/shard_map/all_gather | solution.py:560
  33.3 1.9 %collective-permute-start.1 = (f32[2,3,48,128]{3,2,1,0:T(8,128)S(1)}, f32[2,3,48,128]{3,2,1,0:T(8,128)S(1)}, u32[]{:S(2)}, u32[]{:S(2)}) collective-permute-start(f32[2,3,48,128]{3,2,1,0:T(8,128)S(1)} %get-tuple-element.37), channel_id=1, source_target_pairs={{1,2},{3,4},{5,6},{2,1},{4,3},{6,5},{9,10},{11,12},{13,14},{10,9},... | collective-permute-start | bytes 442376 | tf_op jit(solution)/shard_map/ppermute | solution.py:513
  35.2 1.7 %collective-permute-start.2 = (f32[2,3,48,128]{3,2,1,0:T(8,128)S(1)}, f32[2,3,48,128]{3,2,1,0:T(8,128)S(1)}, u32[]{:S(2)}, u32[]{:S(2)}) collective-permute-start(f32[2,3,48,128]{3,2,1,0:T(8,128)S(1)} %get-tuple-element.38), channel_id=1, source_target_pairs={{0,1},{2,3},{4,5},{6,7},{1,0},{3,2},{5,4},{7,6},{8,9},{10,11},{12,... | collective-permute-start | bytes 442376 | tf_op jit(solution)/shard_map/ppermute | solution.py:514
  37.1 4.7 %collective-permute-done.1.outer = f32[2,3,48,128]{3,2,1,0:T(8,128)S(1)} collective-permute-done((f32[2,3,48,128]{3,2,1,0:T(8,128)S(1)}, f32[2,3,48,128]{3,2,1,0:T(8,128)S(1)}, u32[]{:S(2)}, u32[]{:S(2)}) %collective-permute-start.1) | collective-permute-done | bytes 147488 | tf_op jit(solution)/shard_map/ppermute | solution.py:513
  42.3 2.9 %forward.1.below = f32[4,2,8,32,128]{4,3,2,1,0:T(8,128)S(1)} custom-call(f32[84]{0:T(128)S(1)} %reshape.22.w_ref, f32[2,14,40,128]{3,2,1,0:T(8,128)S(1)} %extend.1.est), custom_call_target="tpu_custom_call" | custom-call | flops 1000 | bytes 1000 | tf_op jit(solution)/shard_map/forward/pallas_call | solution.py:170
  45.3 27.5 %all-to-all-done = f32[64,65,1,128]{3,2,1,0:T(1,128)} async-done(((f32[64,65,1,128]{3,2,1,0:T(1,128)}), f32[64,65,1,128]{3,2,1,0:T(1,128)}, u32[]{:S(2)}, u32[]{:S(2)}) %all-to-all-start) | async-done | bytes 2129952 | tf_op jit(solution)/shard_map/all_to_all | solution.py:555
  72.8 6.2 %unpack.1 = (f32[512,128]{1,0:T(8,128)S(1)}, f32[512,128]{1,0:T(8,128)S(1)}, f32[512,128]{1,0:T(8,128)S(1)}, f32[512,128]{1,0:T(8,128)S(1)}) custom-call(s32[4]{0:T(128)S(1)} %pad_add_fusion.id_ref, f32[4160,1,128]{2,1,0:T(1,128)} %bitcast.8.in_ref), custom_call_target="tpu_custom_call" | custom-call | flops 1000 | bytes 1000 | tf_op jit(solution)/shard_map/unpack/pallas_call | solution.py:170
  79.1 3.5 %collective-permute-start.5 = (f32[2,8,32,128]{3,2,1,0:T(8,128)S(1)}, f32[2,8,32,128]{3,2,1,0:T(8,128)S(1)}, u32[]{:S(2)}, u32[]{:S(2)}) collective-permute-start(f32[2,8,32,128]{3,2,1,0:T(8,128)S(1)} %bitcast.18), channel_id=1, source_target_pairs={{0,24},{8,0},{16,8},{24,16},{1,25},{9,1},{17,9},{25,17},{2,26},{10... | collective-permute-start | bytes 786440 | tf_op jit(solution)/shard_map/ppermute | solution.py:527
  85.2 3.6 %collective-permute-done.4.refs_0_.refs_3_ = f32[2,8,32,128]{3,2,1,0:T(8,128)S(1)} collective-permute-done((f32[2,8,32,128]{3,2,1,0:T(8,128)S(1)}, f32[2,8,32,128]{3,2,1,0:T(8,128)S(1)}, u32[]{:S(2)}, u32[]{:S(2)}) %collective-permute-start.4) | collective-permute-done | bytes 262176 | tf_op jit(solution)/shard_map/ppermute | solution.py:527
  88.8 5.0 %collective-permute-done.5.refs_1_ = f32[2,8,32,128]{3,2,1,0:T(8,128)S(1)} collective-permute-done((f32[2,8,32,128]{3,2,1,0:T(8,128)S(1)}, f32[2,8,32,128]{3,2,1,0:T(8,128)S(1)}, u32[]{:S(2)}, u32[]{:S(2)}) %collective-permute-start.5) | collective-permute-done | bytes 262176 | tf_op jit(solution)/shard_map/ppermute | solution.py:527
  93.8 1.7 %backward.5.refs_1_ = f32[2,14,40,128]{3,2,1,0:T(8,128)S(1)} custom-call(f32[84]{0:T(128)S(1)} %reshape.22.w_ref, s32[4]{0:T(128)S(1)} %pad_add_fusion.id_ref, f32[4,2,8,32,128]{4,3,2,1,0:T(8,128)S(1)} %forward.1.below, f32[2,8,32,128]{3,2,1,0:T(8,128)S(1)} %collective-permute-done.4.refs_0_.refs_3_, f32[2,8,32,128]{3,2,1,0:T(8,128)S(1)} %collective-permute-done.5.refs_1_, ...), custom_call_target="tpu_custom_call" | custom-call | flops 1000 | bytes 1000 | tf_op jit(solution)/shard_map/backward/pallas_call | solution.py:170
  96.9 1.9 %collective-permute-start.6 = (f32[2,6,40,128]{3,2,1,0:T(8,128)S(1)}, f32[2,6,40,128]{3,2,1,0:T(8,128)S(1)}, u32[]{:S(2)}, u32[]{:S(2)}) collective-permute-start(f32[2,6,40,128]{3,2,1,0:T(8,128)S(1)} %get-tuple-element.46), channel_id=1, source_target_pairs={{1,2},{3,4},{5,6},{2,1},{4,3},{6,5},{9,10},{11,12},{13,14},{10,9},... | collective-permute-start | bytes 737288 | tf_op jit(solution)/shard_map/ppermute | solution.py:513
  98.8 1.7 %collective-permute-start.7 = (f32[2,6,40,128]{3,2,1,0:T(8,128)S(1)}, f32[2,6,40,128]{3,2,1,0:T(8,128)S(1)}, u32[]{:S(2)}, u32[]{:S(2)}) collective-permute-start(f32[2,6,40,128]{3,2,1,0:T(8,128)S(1)} %get-tuple-element.47), channel_id=1, source_target_pairs={{0,1},{2,3},{4,5},{6,7},{1,0},{3,2},{5,4},{7,6},{8,9},{10,11},{12,... | collective-permute-start | bytes 737288 | tf_op jit(solution)/shard_map/ppermute | solution.py:514
  100.5 3.9 %collective-permute-done.6.outer = f32[2,6,40,128]{3,2,1,0:T(8,128)S(1)} collective-permute-done((f32[2,6,40,128]{3,2,1,0:T(8,128)S(1)}, f32[2,6,40,128]{3,2,1,0:T(8,128)S(1)}, u32[]{:S(2)}, u32[]{:S(2)}) %collective-permute-start.6) | collective-permute-done | bytes 245792 | tf_op jit(solution)/shard_map/ppermute | solution.py:513
  105.0 2.3 %collective-permute-start.8 = (f32[2,14,8,128]{3,2,1,0:T(8,128)S(1)}, f32[2,14,8,128]{3,2,1,0:T(8,128)S(1)}, u32[]{:S(2)}, u32[]{:S(2)}) collective-permute-start(f32[2,14,8,128]{3,2,1,0:T(8,128)S(1)} %get-tuple-element.49), channel_id=1, source_target_pairs={{8,16},{24,56},{48,40},{32,64},{72,80},{88,120},{112,104},{96,128}... | collective-permute-start | bytes 344072 | tf_op jit(solution)/shard_map/ppermute | solution.py:521
  108.3 1.8 %middle.1 = (f32[4,2,8,16,128]{4,3,2,1,0:T(8,128)S(1)}, f32[4,2,8,24,128]{4,3,2,1,0:T(8,128)S(1)}) custom-call(f32[84]{0:T(128)S(1)} %reshape.22.w_ref, f32[2,14,40,128]{3,2,1,0:T(8,128)S(1)} %extend.1.est, f32[2,14,40,128]{3,2,1,0:T(8,128)S(1)} %get-tuple-element.48.total), custom_call_target="tpu_custom_call" | custom-call | flops 1000 | bytes 1000 | tf_op jit(solution)/shard_map/middle/pallas_call | solution.py:170
  110.2 1.9 %collective-permute-done.8.outer = f32[2,14,8,128]{3,2,1,0:T(8,128)S(1)} collective-permute-done((f32[2,14,8,128]{3,2,1,0:T(8,128)S(1)}, f32[2,14,8,128]{3,2,1,0:T(8,128)S(1)}, u32[]{:S(2)}, u32[]{:S(2)}) %collective-permute-start.8) | collective-permute-done | bytes 114720 | tf_op jit(solution)/shard_map/ppermute | solution.py:521
  112.4 1.9 %ends.1 = (f32[2,14,40,128]{3,2,1,0:T(8,128)S(1)}, f32[4,2,8,32,128]{4,3,2,1,0:T(8,128)S(1)}) custom-call(f32[84]{0:T(128)S(1)} %reshape.22.w_ref, s32[4]{0:T(128)S(1)} %pad_add_fusion.id_ref, f32[2,14,40,128]{3,2,1,0:T(8,128)S(1)} %get-tuple-element.48.total, f32[2,14,8,128]{3,2,1,0:T(8,128)S(1)} %collective-permute-done.8.outer, ...), custom_call_target="tpu_custom_call" | custom-call | flops 1000 | bytes 1000 | tf_op jit(solution)/shard_map/ends/pallas_call | solution.py:170
  114.2 2.8 %backward.7 = (f32[2,14,40,128]{3,2,1,0:T(8,128)S(1)}, f32[2,3,40,128]{3,2,1,0:T(8,128)S(1)}, f32[2,3,40,128]{3,2,1,0:T(8,128)S(1)}) custom-call(f32[84]{0:T(128)S(1)} %reshape.22.w_ref, s32[4]{0:T(128)S(1)} %pad_add_fusion.id_ref, f32[4,2,8,32,128]{4,3,2,1,0:T(8,128)S(1)} %get-tuple-element.53.below, f32[2,8,32,128]{3,2,1,0:T(8,128)S(1)} %bitcast.16, ...), custom_call_target="tpu_custom_call" | custom-call | flops 1000 | bytes 1000 | tf_op jit(solution)/shard_map/backward/pallas_call | solution.py:170
  117.1 1.9 %collective-permute-start.10 = (f32[2,3,40,128]{3,2,1,0:T(8,128)S(1)}, f32[2,3,40,128]{3,2,1,0:T(8,128)S(1)}, u32[]{:S(2)}, u32[]{:S(2)}) collective-permute-start(f32[2,3,40,128]{3,2,1,0:T(8,128)S(1)} %get-tuple-element.55), channel_id=1, source_target_pairs={{1,2},{3,4},{5,6},{2,1},{4,3},{6,5},{9,10},{11,12},{13,14},{10,9},... | collective-permute-start | bytes 368648 | tf_op jit(solution)/shard_map/ppermute | solution.py:513
  120.4 2.9 %collective-permute-done.10.outer = f32[2,3,40,128]{3,2,1,0:T(8,128)S(1)} collective-permute-done((f32[2,3,40,128]{3,2,1,0:T(8,128)S(1)}, f32[2,3,40,128]{3,2,1,0:T(8,128)S(1)}, u32[]{:S(2)}, u32[]{:S(2)}) %collective-permute-start.10) | collective-permute-done | bytes 122912 | tf_op jit(solution)/shard_map/ppermute | solution.py:513
  123.8 3.6 %collective-permute-start.12 = (f32[2,8,8,128]{3,2,1,0:T(8,128)S(1)}, f32[2,8,8,128]{3,2,1,0:T(8,128)S(1)}, u32[]{:S(2)}, u32[]{:S(2)}) collective-permute-start(f32[2,8,8,128]{3,2,1,0:T(8,128)S(1)} %get-tuple-element.58), channel_id=1, source_target_pairs={{8,16},{24,56},{48,40},{32,64},{72,80},{88,120},{112,104},{96,128}... | collective-permute-start | bytes 196616 | tf_op jit(solution)/shard_map/ppermute | solution.py:521
  127.5 1.7 %collective-permute-start.13 = (f32[2,8,8,128]{3,2,1,0:T(8,128)S(1)}, f32[2,8,8,128]{3,2,1,0:T(8,128)S(1)}, u32[]{:S(2)}, u32[]{:S(2)}) collective-permute-start(f32[2,8,8,128]{3,2,1,0:T(8,128)S(1)} %get-tuple-element.59), channel_id=1, source_target_pairs={{0,8},{16,24},{56,48},{40,32},{64,72},{80,88},{120,112},{104,96},{... | collective-permute-start | bytes 196616 | tf_op jit(solution)/shard_map/ppermute | solution.py:522
  130.0 1.8 %collective-permute-done.13.inner = f32[2,8,8,128]{3,2,1,0:T(8,128)S(1)} collective-permute-done((f32[2,8,8,128]{3,2,1,0:T(8,128)S(1)}, f32[2,8,8,128]{3,2,1,0:T(8,128)S(1)}, u32[]{:S(2)}, u32[]{:S(2)}) %collective-permute-start.13) | collective-permute-done | bytes 65568 | tf_op jit(solution)/shard_map/ppermute | solution.py:522
  132.5 1.6 %collective-permute-start.16 = (f32[8,32,128]{2,1,0:T(8,128)S(1)}, f32[8,32,128]{2,1,0:T(8,128)S(1)}, u32[]{:S(2)}, u32[]{:S(2)}) collective-permute-start(f32[8,32,128]{2,1,0:T(8,128)S(1)} %get-tuple-element.61.refs_0_), channel_id=1, source_target_pairs={{0,8},{8,16},{16,24},{24,0},{1,9},{9,17},{17,25},{25,1},{2,10},{10... | collective-permute-start | bytes 393224 | tf_op jit(solution)/shard_map/ppermute | solution.py:527
  134.1 2.1 %collective-permute-start.15 = (f32[8,32,128]{2,1,0:T(8,128)S(1)}, f32[8,32,128]{2,1,0:T(8,128)S(1)}, u32[]{:S(2)}, u32[]{:S(2)}) collective-permute-start(f32[8,32,128]{2,1,0:T(8,128)S(1)} %get-tuple-element.62.refs_1_), channel_id=1, source_target_pairs={{0,24},{8,0},{16,8},{24,16},{1,25},{9,1},{17,9},{25,17},{2,26},{10... | collective-permute-start | bytes 393224 | tf_op jit(solution)/shard_map/ppermute | solution.py:527
  136.2 1.9 %collective-permute-start.14 = (f32[8,32,128]{2,1,0:T(8,128)S(1)}, f32[8,32,128]{2,1,0:T(8,128)S(1)}, u32[]{:S(2)}, u32[]{:S(2)}) collective-permute-start(f32[8,32,128]{2,1,0:T(8,128)S(1)} %get-tuple-element.61.refs_0_), channel_id=1, source_target_pairs={{0,24},{8,0},{16,8},{24,16},{1,25},{9,1},{17,9},{25,17},{2,26},{10... | collective-permute-start | bytes 393224 | tf_op jit(solution)/shard_map/ppermute | solution.py:527
  140.4 2.5 %collective-permute-start.18 = (f32[8,32,128]{2,1,0:T(8,128)S(1)}, f32[8,32,128]{2,1,0:T(8,128)S(1)}, u32[]{:S(2)}, u32[]{:S(2)}) collective-permute-start(f32[8,32,128]{2,1,0:T(8,128)S(1)} %collective-permute-done.15.refs_3_), channel_id=1, source_target_pairs={{0,24},{8,0},{16,8},{24,16},{1,25},{9,1},{17,9},{25,17},{2,26},{10... | collective-permute-start | bytes 393224 | tf_op jit(solution)/shard_map/ppermute | solution.py:527
  145.8 1.6 %join.1 = f32[8,128,256]{2,1,0:T(8,128)} custom-call(s32[4]{0:T(128)S(1)} %pad_add_fusion.id_ref, f32[8,32,128]{2,1,0:T(8,128)S(1)} %get-tuple-element.61.refs_0_, f32[8,32,128]{2,1,0:T(8,128)S(1)} %get-tuple-element.62.refs_1_, f32[8,32,128]{2,1,0:T(8,128)S(1)} %collective-permute-done.14.refs_2_, f32[8,32,128]{2,1,0:T(8,128)S(1)} %collective-permute-done.15.refs_3_, ...), custom_call_target="tpu_custom_call" | custom-call | flops 1000 | bytes 1000 | tf_op jit(solution)/shard_map/join/pallas_call | solution.py:170
  (35 shorter events, 16.9 us)
Async XLA Ops:
  0.8 10.4 %collective-permute-start = (f32[8,8,256]{2,1,0:T(8,128)S(1)}, f32[8,8,256]{2,1,0:T(8,128)S(1)}, u32[]{:S(2)}, u32[]{:S(2)}) collective-permute-start(f32[8,8,256]{2,1,0:T(8,128)S(1)} %constant_dynamic-slice_fusion), channel_id=1, source_target_pairs={{24,56},{32,64},{88,120},{96,128},{152,184},{160,192},{216,248},{5... | collective-permute-start | bytes 196616 | tf_op jit(solution)/shard_map/ppermute | solution.py:550
  11.2 10.6 %copy-start.1 = (f32[1,3,7]{2,0,1:T(1,128)S(1)}, f32[1,3,7]{2,0,1:T(1,128)}, u32[]{:S(2)}) copy-start(f32[1,3,7]{2,0,1:T(1,128)} %param.8) | copy-start | bytes 256
  11.2 21.3 %copy-start = (f32[8,128,256]{2,1,0:T(8,128)S(1)}, f32[8,128,256]{2,1,0:T(8,128)}, u32[]{:S(2)}) copy-start(f32[8,128,256]{2,1,0:T(8,128)} %est.1) | copy-start | bytes 3145732
  11.2 61.6 %all-to-all-start = ((f32[64,65,1,128]{3,2,1,0:T(1,128)}), f32[64,65,1,128]{3,2,1,0:T(1,128)}, u32[]{:S(2)}, u32[]{:S(2)}) async-start(f32[64,65,1,128]{3,2,1,0:T(1,128)} %bitcast.20), calls=%async_computation | async-start | bytes 4259840 | tf_op jit(solution)/shard_map/all_to_all | solution.py:555
  33.3 8.4 %collective-permute-start.1 = (f32[2,3,48,128]{3,2,1,0:T(8,128)S(1)}, f32[2,3,48,128]{3,2,1,0:T(8,128)S(1)}, u32[]{:S(2)}, u32[]{:S(2)}) collective-permute-start(f32[2,3,48,128]{3,2,1,0:T(8,128)S(1)} %get-tuple-element.37), channel_id=1, source_target_pairs={{1,2},{3,4},{5,6},{2,1},{4,3},{6,5},{9,10},{11,12},{13,14},{10,9},... | collective-permute-start | bytes 442376 | tf_op jit(solution)/shard_map/ppermute | solution.py:513
  35.2 6.5 %collective-permute-start.2 = (f32[2,3,48,128]{3,2,1,0:T(8,128)S(1)}, f32[2,3,48,128]{3,2,1,0:T(8,128)S(1)}, u32[]{:S(2)}, u32[]{:S(2)}) collective-permute-start(f32[2,3,48,128]{3,2,1,0:T(8,128)S(1)} %get-tuple-element.38), channel_id=1, source_target_pairs={{0,1},{2,3},{4,5},{6,7},{1,0},{3,2},{5,4},{7,6},{8,9},{10,11},{12,... | collective-permute-start | bytes 442376 | tf_op jit(solution)/shard_map/ppermute | solution.py:514
  79.0 9.8 %collective-permute-start.4 = (f32[2,8,32,128]{3,2,1,0:T(8,128)S(1)}, f32[2,8,32,128]{3,2,1,0:T(8,128)S(1)}, u32[]{:S(2)}, u32[]{:S(2)}) collective-permute-start(f32[2,8,32,128]{3,2,1,0:T(8,128)S(1)} %bitcast.19), channel_id=1, source_target_pairs={{0,8},{8,16},{16,24},{24,0},{1,9},{9,17},{17,25},{25,1},{2,10},{10... | collective-permute-start | bytes 786440 | tf_op jit(solution)/shard_map/ppermute | solution.py:527
  79.1 14.7 %collective-permute-start.5 = (f32[2,8,32,128]{3,2,1,0:T(8,128)S(1)}, f32[2,8,32,128]{3,2,1,0:T(8,128)S(1)}, u32[]{:S(2)}, u32[]{:S(2)}) collective-permute-start(f32[2,8,32,128]{3,2,1,0:T(8,128)S(1)} %bitcast.18), channel_id=1, source_target_pairs={{0,24},{8,0},{16,8},{24,16},{1,25},{9,1},{17,9},{25,17},{2,26},{10... | collective-permute-start | bytes 786440 | tf_op jit(solution)/shard_map/ppermute | solution.py:527
  82.6 13.0 %collective-permute-start.3 = (f32[2,8,32,128]{3,2,1,0:T(8,128)S(1)}, f32[2,8,32,128]{3,2,1,0:T(8,128)S(1)}, u32[]{:S(2)}, u32[]{:S(2)}) collective-permute-start(f32[2,8,32,128]{3,2,1,0:T(8,128)S(1)} %bitcast.17), channel_id=1, source_target_pairs={{0,16},{8,24},{16,0},{24,8},{1,17},{9,25},{17,1},{25,9},{2,18},{10... | collective-permute-start | bytes 786440 | tf_op jit(solution)/shard_map/ppermute | solution.py:527
  96.9 7.5 %collective-permute-start.6 = (f32[2,6,40,128]{3,2,1,0:T(8,128)S(1)}, f32[2,6,40,128]{3,2,1,0:T(8,128)S(1)}, u32[]{:S(2)}, u32[]{:S(2)}) collective-permute-start(f32[2,6,40,128]{3,2,1,0:T(8,128)S(1)} %get-tuple-element.46), channel_id=1, source_target_pairs={{1,2},{3,4},{5,6},{2,1},{4,3},{6,5},{9,10},{11,12},{13,14},{10,9},... | collective-permute-start | bytes 737288 | tf_op jit(solution)/shard_map/ppermute | solution.py:513
  98.8 5.6 %collective-permute-start.7 = (f32[2,6,40,128]{3,2,1,0:T(8,128)S(1)}, f32[2,6,40,128]{3,2,1,0:T(8,128)S(1)}, u32[]{:S(2)}, u32[]{:S(2)}) collective-permute-start(f32[2,6,40,128]{3,2,1,0:T(8,128)S(1)} %get-tuple-element.47), channel_id=1, source_target_pairs={{0,1},{2,3},{4,5},{6,7},{1,0},{3,2},{5,4},{7,6},{8,9},{10,11},{12,... | collective-permute-start | bytes 737288 | tf_op jit(solution)/shard_map/ppermute | solution.py:514
  105.0 7.1 %collective-permute-start.8 = (f32[2,14,8,128]{3,2,1,0:T(8,128)S(1)}, f32[2,14,8,128]{3,2,1,0:T(8,128)S(1)}, u32[]{:S(2)}, u32[]{:S(2)}) collective-permute-start(f32[2,14,8,128]{3,2,1,0:T(8,128)S(1)} %get-tuple-element.49), channel_id=1, source_target_pairs={{8,16},{24,56},{48,40},{32,64},{72,80},{88,120},{112,104},{96,128}... | collective-permute-start | bytes 344072 | tf_op jit(solution)/shard_map/ppermute | solution.py:521
  107.3 5.1 %collective-permute-start.9 = (f32[2,14,8,128]{3,2,1,0:T(8,128)S(1)}, f32[2,14,8,128]{3,2,1,0:T(8,128)S(1)}, u32[]{:S(2)}, u32[]{:S(2)}) collective-permute-start(f32[2,14,8,128]{3,2,1,0:T(8,128)S(1)} %get-tuple-element.50), channel_id=1, source_target_pairs={{0,8},{16,24},{56,48},{40,32},{64,72},{80,88},{120,112},{104,96},{... | collective-permute-start | bytes 344072 | tf_op jit(solution)/shard_map/ppermute | solution.py:522
  117.1 6.2 %collective-permute-start.10 = (f32[2,3,40,128]{3,2,1,0:T(8,128)S(1)}, f32[2,3,40,128]{3,2,1,0:T(8,128)S(1)}, u32[]{:S(2)}, u32[]{:S(2)}) collective-permute-start(f32[2,3,40,128]{3,2,1,0:T(8,128)S(1)} %get-tuple-element.55), channel_id=1, source_target_pairs={{1,2},{3,4},{5,6},{2,1},{4,3},{6,5},{9,10},{11,12},{13,14},{10,9},... | collective-permute-start | bytes 368648 | tf_op jit(solution)/shard_map/ppermute | solution.py:513
  119.0 4.3 %collective-permute-start.11 = (f32[2,3,40,128]{3,2,1,0:T(8,128)S(1)}, f32[2,3,40,128]{3,2,1,0:T(8,128)S(1)}, u32[]{:S(2)}, u32[]{:S(2)}) collective-permute-start(f32[2,3,40,128]{3,2,1,0:T(8,128)S(1)} %get-tuple-element.56), channel_id=1, source_target_pairs={{0,1},{2,3},{4,5},{6,7},{1,0},{3,2},{5,4},{7,6},{8,9},{10,11},{12,... | collective-permute-start | bytes 368648 | tf_op jit(solution)/shard_map/ppermute | solution.py:514
  123.8 6.2 %collective-permute-start.12 = (f32[2,8,8,128]{3,2,1,0:T(8,128)S(1)}, f32[2,8,8,128]{3,2,1,0:T(8,128)S(1)}, u32[]{:S(2)}, u32[]{:S(2)}) collective-permute-start(f32[2,8,8,128]{3,2,1,0:T(8,128)S(1)} %get-tuple-element.58), channel_id=1, source_target_pairs={{8,16},{24,56},{48,40},{32,64},{72,80},{88,120},{112,104},{96,128}... | collective-permute-start | bytes 196616 | tf_op jit(solution)/shard_map/ppermute | solution.py:521
  127.5 4.4 %collective-permute-start.13 = (f32[2,8,8,128]{3,2,1,0:T(8,128)S(1)}, f32[2,8,8,128]{3,2,1,0:T(8,128)S(1)}, u32[]{:S(2)}, u32[]{:S(2)}) collective-permute-start(f32[2,8,8,128]{3,2,1,0:T(8,128)S(1)} %get-tuple-element.59), channel_id=1, source_target_pairs={{0,8},{16,24},{56,48},{40,32},{64,72},{80,88},{120,112},{104,96},{... | collective-permute-start | bytes 196616 | tf_op jit(solution)/shard_map/ppermute | solution.py:522
  132.5 6.6 %collective-permute-start.16 = (f32[8,32,128]{2,1,0:T(8,128)S(1)}, f32[8,32,128]{2,1,0:T(8,128)S(1)}, u32[]{:S(2)}, u32[]{:S(2)}) collective-permute-start(f32[8,32,128]{2,1,0:T(8,128)S(1)} %get-tuple-element.61.refs_0_), channel_id=1, source_target_pairs={{0,8},{8,16},{16,24},{24,0},{1,9},{9,17},{17,25},{25,1},{2,10},{10... | collective-permute-start | bytes 393224 | tf_op jit(solution)/shard_map/ppermute | solution.py:527
  134.1 6.3 %collective-permute-start.15 = (f32[8,32,128]{2,1,0:T(8,128)S(1)}, f32[8,32,128]{2,1,0:T(8,128)S(1)}, u32[]{:S(2)}, u32[]{:S(2)}) collective-permute-start(f32[8,32,128]{2,1,0:T(8,128)S(1)} %get-tuple-element.62.refs_1_), channel_id=1, source_target_pairs={{0,24},{8,0},{16,8},{24,16},{1,25},{9,1},{17,9},{25,17},{2,26},{10... | collective-permute-start | bytes 393224 | tf_op jit(solution)/shard_map/ppermute | solution.py:527
  136.2 6.7 %collective-permute-start.14 = (f32[8,32,128]{2,1,0:T(8,128)S(1)}, f32[8,32,128]{2,1,0:T(8,128)S(1)}, u32[]{:S(2)}, u32[]{:S(2)}) collective-permute-start(f32[8,32,128]{2,1,0:T(8,128)S(1)} %get-tuple-element.61.refs_0_), channel_id=1, source_target_pairs={{0,24},{8,0},{16,8},{24,16},{1,25},{9,1},{17,9},{25,17},{2,26},{10... | collective-permute-start | bytes 393224 | tf_op jit(solution)/shard_map/ppermute | solution.py:527
  138.2 6.2 %collective-permute-start.19 = (f32[8,32,128]{2,1,0:T(8,128)S(1)}, f32[8,32,128]{2,1,0:T(8,128)S(1)}, u32[]{:S(2)}, u32[]{:S(2)}) collective-permute-start(f32[8,32,128]{2,1,0:T(8,128)S(1)} %get-tuple-element.62.refs_1_), channel_id=1, source_target_pairs={{0,8},{8,16},{16,24},{24,0},{1,9},{9,17},{17,25},{25,1},{2,10},{10... | collective-permute-start | bytes 393224 | tf_op jit(solution)/shard_map/ppermute | solution.py:527
  139.1 6.7 %collective-permute-start.17 = (f32[8,32,128]{2,1,0:T(8,128)S(1)}, f32[8,32,128]{2,1,0:T(8,128)S(1)}, u32[]{:S(2)}, u32[]{:S(2)}) collective-permute-start(f32[8,32,128]{2,1,0:T(8,128)S(1)} %collective-permute-done.16.refs_6_), channel_id=1, source_target_pairs={{0,8},{8,16},{16,24},{24,0},{1,9},{9,17},{17,25},{25,1},{2,10},{10... | collective-permute-start | bytes 393224 | tf_op jit(solution)/shard_map/ppermute | solution.py:527
  140.4 5.4 %collective-permute-start.18 = (f32[8,32,128]{2,1,0:T(8,128)S(1)}, f32[8,32,128]{2,1,0:T(8,128)S(1)}, u32[]{:S(2)}, u32[]{:S(2)}) collective-permute-start(f32[8,32,128]{2,1,0:T(8,128)S(1)} %collective-permute-done.15.refs_3_), channel_id=1, source_target_pairs={{0,24},{8,0},{16,8},{24,16},{1,25},{9,1},{17,9},{25,17},{2,26},{10... | collective-permute-start | bytes 393224 | tf_op jit(solution)/shard_map/ppermute | solution.py:527

commit v15 on v14

--- a/solution.py
+++ b/solution.py
@@ -135,7 +135,7 @@
                 placed[pl.ds(place, 1), :] = row
         return c
 
-    lax.fori_loop(0, peers, per_peer, 0, unroll=2)
+    lax.fori_loop(0, peers, per_peer, 0)
     for d, out in enumerate(outs):
         out[...] = placed[d * size : (d + 1) * size, :]
 

time: 150 us -> 150 us (level)
  no operation moved by 1% of the time
where the time goes in v15:
time: 150 us; the launch traced here: 148 us
  waiting for transfers between devices  57.3 us (38%)
  starting transfers between devices  47 us (31%)
  Pallas kernels  30.5 us (20%)
  blocking collectives  10.7 us (7%)
    all_to_all x1, waiting for transfers between devices, per_device(): lax.all_to_all(outgoing.reshape(peer_count, capacity + 1, 1, BRICK), ('bl...  27.5 us
    pallas_call x14, Pallas kernels, call(): pl.pallas_call(kernel, out_shape=outs, in_specs=[smem()] * scalars + [vme...  24.7 us
    ppermute x9, starting transfers between devices, turn(): lax.ppermute(value, 'views', [(i, (i + step) % count) for i in range(coun...  13.5 us
    ppermute x9, waiting for transfers between devices, turn(): lax.ppermute(value, 'views', [(i, (i + step) % count) for i in range(coun...  13.4 us
    ppermute x3, waiting for transfers between devices, swap_layers(): lax.ppermute(outer, 'rows', both_ways([(i, i + 1) for i in range(1, count...  11.5 us
    all_gather x1, blocking collectives, per_device(): taps = lax.all_gather(psf_taps, 'views', axis=0, tiled=True)  10.7 us
    all_to_all x1, starting transfers between devices, per_device(): lax.all_to_all(outgoing.reshape(peer_count, capacity + 1, 1, BRICK), ('bl...  10.5 us
    ppermute x2, starting transfers between devices, swap_rows(): lax.ppermute(outer, axes, both_ways(list(zip(chain[1:-1:2], chain[2::2]))))  5.94 us
  transfers between devices with their start and end apart: 21, of which 15 were waited for; matrix products, arithmetic and copies ran while one was open for 0% of the time, Pallas kernels for 10%

profile of v15, /device:TPU:34, one launch (start us, length us, event | category | flops | bytes accessed | tf_op | source)
XLA Modules:
  0.0 147.5 jit_solution(12813654528945393887)
XLA Ops:
  0.8 3.8 %collective-permute-start = (f32[8,8,256]{2,1,0:T(8,128)S(1)}, f32[8,8,256]{2,1,0:T(8,128)S(1)}, u32[]{:S(2)}, u32[]{:S(2)}) collective-permute-start(f32[8,8,256]{2,1,0:T(8,128)S(1)} %constant_dynamic-slice_fusion), channel_id=1, source_target_pairs={{24,56},{32,64},{88,120},{96,128},{152,184},{160,192},{216,248},{5... | collective-permute-start | bytes 196616 | tf_op jit(solution)/shard_map/ppermute | solution.py:550
  5.3 5.9 %pack.1 = f32[4160,1,128]{2,1,0:T(1,128)} custom-call(s32[1]{0:T(128)S(6)} %copy.9.shift_ref, s32[8,2,128]{2,1,0:T(2,128)} %bitcast.22, f32[8,128,256]{2,1,0:T(8,128)} %bitcast.21), custom_call_target="tpu_custom_call" | custom-call | tf_op jit(solution)/shard_map/pack/pallas_call | solution.py:96
  11.2 10.5 %all-to-all-start = ((f32[64,65,1,128]{3,2,1,0:T(1,128)}), f32[64,65,1,128]{3,2,1,0:T(1,128)}, u32[]{:S(2)}, u32[]{:S(2)}) async-start(f32[64,65,1,128]{3,2,1,0:T(1,128)} %bitcast.20), calls=%async_computation | async-start | bytes 4259840 | tf_op jit(solution)/shard_map/all_to_all | solution.py:555
  21.8 10.7 %all_gather.3 = f32[4,3,7]{2,1,0:T(4,128)S(1)} all-gather(f32[1,3,7]{2,1,0:T(4,128)S(1)} %copy.8), channel_id=1, replica_groups=mesh['blocks'=8,'views'=4,'rows'=8] {'views'}, dimensions={0}, use_global_device_ids=true | all-gather | bytes 420 | tf_op jit(solution)/shard_map/all_gather | solution.py:560
  33.3 1.9 %collective-permute-start.1 = (f32[2,3,48,128]{3,2,1,0:T(8,128)S(1)}, f32[2,3,48,128]{3,2,1,0:T(8,128)S(1)}, u32[]{:S(2)}, u32[]{:S(2)}) collective-permute-start(f32[2,3,48,128]{3,2,1,0:T(8,128)S(1)} %get-tuple-element.37), channel_id=1, source_target_pairs={{1,2},{3,4},{5,6},{2,1},{4,3},{6,5},{9,10},{11,12},{13,14},{10,9},... | collective-permute-start | bytes 442376 | tf_op jit(solution)/shard_map/ppermute | solution.py:513
  35.2 1.7 %collective-permute-start.2 = (f32[2,3,48,128]{3,2,1,0:T(8,128)S(1)}, f32[2,3,48,128]{3,2,1,0:T(8,128)S(1)}, u32[]{:S(2)}, u32[]{:S(2)}) collective-permute-start(f32[2,3,48,128]{3,2,1,0:T(8,128)S(1)} %get-tuple-element.38), channel_id=1, source_target_pairs={{0,1},{2,3},{4,5},{6,7},{1,0},{3,2},{5,4},{7,6},{8,9},{10,11},{12,... | collective-permute-start | bytes 442376 | tf_op jit(solution)/shard_map/ppermute | solution.py:514
  37.1 4.7 %collective-permute-done.1.outer = f32[2,3,48,128]{3,2,1,0:T(8,128)S(1)} collective-permute-done((f32[2,3,48,128]{3,2,1,0:T(8,128)S(1)}, f32[2,3,48,128]{3,2,1,0:T(8,128)S(1)}, u32[]{:S(2)}, u32[]{:S(2)}) %collective-permute-start.1) | collective-permute-done | bytes 147488 | tf_op jit(solution)/shard_map/ppermute | solution.py:513
  42.3 2.9 %forward.1.below = f32[4,2,8,32,128]{4,3,2,1,0:T(8,128)S(1)} custom-call(f32[84]{0:T(128)S(1)} %reshape.22.w_ref, f32[2,14,40,128]{3,2,1,0:T(8,128)S(1)} %extend.1.est), custom_call_target="tpu_custom_call" | custom-call | flops 1000 | bytes 1000 | tf_op jit(solution)/shard_map/forward/pallas_call | solution.py:170
  45.3 27.5 %all-to-all-done = f32[64,65,1,128]{3,2,1,0:T(1,128)} async-done(((f32[64,65,1,128]{3,2,1,0:T(1,128)}), f32[64,65,1,128]{3,2,1,0:T(1,128)}, u32[]{:S(2)}, u32[]{:S(2)}) %all-to-all-start) | async-done | bytes 2129952 | tf_op jit(solution)/shard_map/all_to_all | solution.py:555
  72.8 6.3 %unpack.1 = (f32[512,128]{1,0:T(8,128)S(1)}, f32[512,128]{1,0:T(8,128)S(1)}, f32[512,128]{1,0:T(8,128)S(1)}, f32[512,128]{1,0:T(8,128)S(1)}) custom-call(s32[4]{0:T(128)S(1)} %pad_add_fusion.id_ref, f32[4160,1,128]{2,1,0:T(1,128)} %bitcast.8.in_ref), custom_call_target="tpu_custom_call" | custom-call | flops 1000 | bytes 1000 | tf_op jit(solution)/shard_map/unpack/pallas_call | solution.py:170
  79.3 3.5 %collective-permute-start.5 = (f32[2,8,32,128]{3,2,1,0:T(8,128)S(1)}, f32[2,8,32,128]{3,2,1,0:T(8,128)S(1)}, u32[]{:S(2)}, u32[]{:S(2)}) collective-permute-start(f32[2,8,32,128]{3,2,1,0:T(8,128)S(1)} %bitcast.18), channel_id=1, source_target_pairs={{0,24},{8,0},{16,8},{24,16},{1,25},{9,1},{17,9},{25,17},{2,26},{10... | collective-permute-start | bytes 786440 | tf_op jit(solution)/shard_map/ppermute | solution.py:527
  85.4 3.6 %collective-permute-done.4.refs_0_.refs_3_ = f32[2,8,32,128]{3,2,1,0:T(8,128)S(1)} collective-permute-done((f32[2,8,32,128]{3,2,1,0:T(8,128)S(1)}, f32[2,8,32,128]{3,2,1,0:T(8,128)S(1)}, u32[]{:S(2)}, u32[]{:S(2)}) %collective-permute-start.4) | collective-permute-done | bytes 262176 | tf_op jit(solution)/shard_map/ppermute | solution.py:527
  89.0 5.0 %collective-permute-done.5.refs_1_ = f32[2,8,32,128]{3,2,1,0:T(8,128)S(1)} collective-permute-done((f32[2,8,32,128]{3,2,1,0:T(8,128)S(1)}, f32[2,8,32,128]{3,2,1,0:T(8,128)S(1)}, u32[]{:S(2)}, u32[]{:S(2)}) %collective-permute-start.5) | collective-permute-done | bytes 262176 | tf_op jit(solution)/shard_map/ppermute | solution.py:527
  93.9 1.7 %backward.5.refs_1_ = f32[2,14,40,128]{3,2,1,0:T(8,128)S(1)} custom-call(f32[84]{0:T(128)S(1)} %reshape.22.w_ref, s32[4]{0:T(128)S(1)} %pad_add_fusion.id_ref, f32[4,2,8,32,128]{4,3,2,1,0:T(8,128)S(1)} %forward.1.below, f32[2,8,32,128]{3,2,1,0:T(8,128)S(1)} %collective-permute-done.4.refs_0_.refs_3_, f32[2,8,32,128]{3,2,1,0:T(8,128)S(1)} %collective-permute-done.5.refs_1_, ...), custom_call_target="tpu_custom_call" | custom-call | flops 1000 | bytes 1000 | tf_op jit(solution)/shard_map/backward/pallas_call | solution.py:170
  97.0 1.9 %collective-permute-start.6 = (f32[2,6,40,128]{3,2,1,0:T(8,128)S(1)}, f32[2,6,40,128]{3,2,1,0:T(8,128)S(1)}, u32[]{:S(2)}, u32[]{:S(2)}) collective-permute-start(f32[2,6,40,128]{3,2,1,0:T(8,128)S(1)} %get-tuple-element.46), channel_id=1, source_target_pairs={{1,2},{3,4},{5,6},{2,1},{4,3},{6,5},{9,10},{11,12},{13,14},{10,9},... | collective-permute-start | bytes 737288 | tf_op jit(solution)/shard_map/ppermute | solution.py:513
  99.0 1.7 %collective-permute-start.7 = (f32[2,6,40,128]{3,2,1,0:T(8,128)S(1)}, f32[2,6,40,128]{3,2,1,0:T(8,128)S(1)}, u32[]{:S(2)}, u32[]{:S(2)}) collective-permute-start(f32[2,6,40,128]{3,2,1,0:T(8,128)S(1)} %get-tuple-element.47), channel_id=1, source_target_pairs={{0,1},{2,3},{4,5},{6,7},{1,0},{3,2},{5,4},{7,6},{8,9},{10,11},{12,... | collective-permute-start | bytes 737288 | tf_op jit(solution)/shard_map/ppermute | solution.py:514
  100.6 3.9 %collective-permute-done.6.outer = f32[2,6,40,128]{3,2,1,0:T(8,128)S(1)} collective-permute-done((f32[2,6,40,128]{3,2,1,0:T(8,128)S(1)}, f32[2,6,40,128]{3,2,1,0:T(8,128)S(1)}, u32[]{:S(2)}, u32[]{:S(2)}) %collective-permute-start.6) | collective-permute-done | bytes 245792 | tf_op jit(solution)/shard_map/ppermute | solution.py:513
  105.2 2.3 %collective-permute-start.8 = (f32[2,14,8,128]{3,2,1,0:T(8,128)S(1)}, f32[2,14,8,128]{3,2,1,0:T(8,128)S(1)}, u32[]{:S(2)}, u32[]{:S(2)}) collective-permute-start(f32[2,14,8,128]{3,2,1,0:T(8,128)S(1)} %get-tuple-element.49), channel_id=1, source_target_pairs={{8,16},{24,56},{48,40},{32,64},{72,80},{88,120},{112,104},{96,128}... | collective-permute-start | bytes 344072 | tf_op jit(solution)/shard_map/ppermute | solution.py:521
  108.5 1.8 %middle.1 = (f32[4,2,8,16,128]{4,3,2,1,0:T(8,128)S(1)}, f32[4,2,8,24,128]{4,3,2,1,0:T(8,128)S(1)}) custom-call(f32[84]{0:T(128)S(1)} %reshape.22.w_ref, f32[2,14,40,128]{3,2,1,0:T(8,128)S(1)} %extend.1.est, f32[2,14,40,128]{3,2,1,0:T(8,128)S(1)} %get-tuple-element.48.total), custom_call_target="tpu_custom_call" | custom-call | flops 1000 | bytes 1000 | tf_op jit(solution)/shard_map/middle/pallas_call | solution.py:170
  110.3 1.9 %collective-permute-done.8.outer = f32[2,14,8,128]{3,2,1,0:T(8,128)S(1)} collective-permute-done((f32[2,14,8,128]{3,2,1,0:T(8,128)S(1)}, f32[2,14,8,128]{3,2,1,0:T(8,128)S(1)}, u32[]{:S(2)}, u32[]{:S(2)}) %collective-permute-start.8) | collective-permute-done | bytes 114720 | tf_op jit(solution)/shard_map/ppermute | solution.py:521
  112.5 1.9 %ends.1 = (f32[2,14,40,128]{3,2,1,0:T(8,128)S(1)}, f32[4,2,8,32,128]{4,3,2,1,0:T(8,128)S(1)}) custom-call(f32[84]{0:T(128)S(1)} %reshape.22.w_ref, s32[4]{0:T(128)S(1)} %pad_add_fusion.id_ref, f32[2,14,40,128]{3,2,1,0:T(8,128)S(1)} %get-tuple-element.48.total, f32[2,14,8,128]{3,2,1,0:T(8,128)S(1)} %collective-permute-done.8.outer, ...), custom_call_target="tpu_custom_call" | custom-call | flops 1000 | bytes 1000 | tf_op jit(solution)/shard_map/ends/pallas_call | solution.py:170
  114.4 2.8 %backward.7 = (f32[2,14,40,128]{3,2,1,0:T(8,128)S(1)}, f32[2,3,40,128]{3,2,1,0:T(8,128)S(1)}, f32[2,3,40,128]{3,2,1,0:T(8,128)S(1)}) custom-call(f32[84]{0:T(128)S(1)} %reshape.22.w_ref, s32[4]{0:T(128)S(1)} %pad_add_fusion.id_ref, f32[4,2,8,32,128]{4,3,2,1,0:T(8,128)S(1)} %get-tuple-element.53.below, f32[2,8,32,128]{3,2,1,0:T(8,128)S(1)} %bitcast.16, ...), custom_call_target="tpu_custom_call" | custom-call | flops 1000 | bytes 1000 | tf_op jit(solution)/shard_map/backward/pallas_call | solution.py:170
  117.2 1.9 %collective-permute-start.10 = (f32[2,3,40,128]{3,2,1,0:T(8,128)S(1)}, f32[2,3,40,128]{3,2,1,0:T(8,128)S(1)}, u32[]{:S(2)}, u32[]{:S(2)}) collective-permute-start(f32[2,3,40,128]{3,2,1,0:T(8,128)S(1)} %get-tuple-element.55), channel_id=1, source_target_pairs={{1,2},{3,4},{5,6},{2,1},{4,3},{6,5},{9,10},{11,12},{13,14},{10,9},... | collective-permute-start | bytes 368648 | tf_op jit(solution)/shard_map/ppermute | solution.py:513
  120.5 2.9 %collective-permute-done.10.outer = f32[2,3,40,128]{3,2,1,0:T(8,128)S(1)} collective-permute-done((f32[2,3,40,128]{3,2,1,0:T(8,128)S(1)}, f32[2,3,40,128]{3,2,1,0:T(8,128)S(1)}, u32[]{:S(2)}, u32[]{:S(2)}) %collective-permute-start.10) | collective-permute-done | bytes 122912 | tf_op jit(solution)/shard_map/ppermute | solution.py:513
  124.0 3.6 %collective-permute-start.12 = (f32[2,8,8,128]{3,2,1,0:T(8,128)S(1)}, f32[2,8,8,128]{3,2,1,0:T(8,128)S(1)}, u32[]{:S(2)}, u32[]{:S(2)}) collective-permute-start(f32[2,8,8,128]{3,2,1,0:T(8,128)S(1)} %get-tuple-element.58), channel_id=1, source_target_pairs={{8,16},{24,56},{48,40},{32,64},{72,80},{88,120},{112,104},{96,128}... | collective-permute-start | bytes 196616 | tf_op jit(solution)/shard_map/ppermute | solution.py:521
  127.6 1.7 %collective-permute-start.13 = (f32[2,8,8,128]{3,2,1,0:T(8,128)S(1)}, f32[2,8,8,128]{3,2,1,0:T(8,128)S(1)}, u32[]{:S(2)}, u32[]{:S(2)}) collective-permute-start(f32[2,8,8,128]{3,2,1,0:T(8,128)S(1)} %get-tuple-element.59), channel_id=1, source_target_pairs={{0,8},{16,24},{56,48},{40,32},{64,72},{80,88},{120,112},{104,96},{... | collective-permute-start | bytes 196616 | tf_op jit(solution)/shard_map/ppermute | solution.py:522
  130.2 1.8 %collective-permute-done.13.inner = f32[2,8,8,128]{3,2,1,0:T(8,128)S(1)} collective-permute-done((f32[2,8,8,128]{3,2,1,0:T(8,128)S(1)}, f32[2,8,8,128]{3,2,1,0:T(8,128)S(1)}, u32[]{:S(2)}, u32[]{:S(2)}) %collective-permute-start.13) | collective-permute-done | bytes 65568 | tf_op jit(solution)/shard_map/ppermute | solution.py:522
  132.6 1.6 %collective-permute-start.16 = (f32[8,32,128]{2,1,0:T(8,128)S(1)}, f32[8,32,128]{2,1,0:T(8,128)S(1)}, u32[]{:S(2)}, u32[]{:S(2)}) collective-permute-start(f32[8,32,128]{2,1,0:T(8,128)S(1)} %get-tuple-element.61.refs_0_), channel_id=1, source_target_pairs={{0,8},{8,16},{16,24},{24,0},{1,9},{9,17},{17,25},{25,1},{2,10},{10... | collective-permute-start | bytes 393224 | tf_op jit(solution)/shard_map/ppermute | solution.py:527
  134.3 2.1 %collective-permute-start.15 = (f32[8,32,128]{2,1,0:T(8,128)S(1)}, f32[8,32,128]{2,1,0:T(8,128)S(1)}, u32[]{:S(2)}, u32[]{:S(2)}) collective-permute-start(f32[8,32,128]{2,1,0:T(8,128)S(1)} %get-tuple-element.62.refs_1_), channel_id=1, source_target_pairs={{0,24},{8,0},{16,8},{24,16},{1,25},{9,1},{17,9},{25,17},{2,26},{10... | collective-permute-start | bytes 393224 | tf_op jit(solution)/shard_map/ppermute | solution.py:527
  136.4 1.9 %collective-permute-start.14 = (f32[8,32,128]{2,1,0:T(8,128)S(1)}, f32[8,32,128]{2,1,0:T(8,128)S(1)}, u32[]{:S(2)}, u32[]{:S(2)}) collective-permute-start(f32[8,32,128]{2,1,0:T(8,128)S(1)} %get-tuple-element.61.refs_0_), channel_id=1, source_target_pairs={{0,24},{8,0},{16,8},{24,16},{1,25},{9,1},{17,9},{25,17},{2,26},{10... | collective-permute-start | bytes 393224 | tf_op jit(solution)/shard_map/ppermute | solution.py:527
  140.5 2.5 %collective-permute-start.18 = (f32[8,32,128]{2,1,0:T(8,128)S(1)}, f32[8,32,128]{2,1,0:T(8,128)S(1)}, u32[]{:S(2)}, u32[]{:S(2)}) collective-permute-start(f32[8,32,128]{2,1,0:T(8,128)S(1)} %collective-permute-done.15.refs_3_), channel_id=1, source_target_pairs={{0,24},{8,0},{16,8},{24,16},{1,25},{9,1},{17,9},{25,17},{2,26},{10... | collective-permute-start | bytes 393224 | tf_op jit(solution)/shard_map/ppermute | solution.py:527
  145.9 1.6 %join.1 = f32[8,128,256]{2,1,0:T(8,128)} custom-call(s32[4]{0:T(128)S(1)} %pad_add_fusion.id_ref, f32[8,32,128]{2,1,0:T(8,128)S(1)} %get-tuple-element.61.refs_0_, f32[8,32,128]{2,1,0:T(8,128)S(1)} %get-tuple-element.62.refs_1_, f32[8,32,128]{2,1,0:T(8,128)S(1)} %collective-permute-done.14.refs_2_, f32[8,32,128]{2,1,0:T(8,128)S(1)} %collective-permute-done.15.refs_3_, ...), custom_call_target="tpu_custom_call" | custom-call | flops 1000 | bytes 1000 | tf_op jit(solution)/shard_map/join/pallas_call | solution.py:170
  (35 shorter events, 16.9 us)
Async XLA Ops:
  0.8 10.4 %collective-permute-start = (f32[8,8,256]{2,1,0:T(8,128)S(1)}, f32[8,8,256]{2,1,0:T(8,128)S(1)}, u32[]{:S(2)}, u32[]{:S(2)}) collective-permute-start(f32[8,8,256]{2,1,0:T(8,128)S(1)} %constant_dynamic-slice_fusion), channel_id=1, source_target_pairs={{24,56},{32,64},{88,120},{96,128},{152,184},{160,192},{216,248},{5... | collective-permute-start | bytes 196616 | tf_op jit(solution)/shard_map/ppermute | solution.py:550
  11.2 10.6 %copy-start.1 = (f32[1,3,7]{2,0,1:T(1,128)S(1)}, f32[1,3,7]{2,0,1:T(1,128)}, u32[]{:S(2)}) copy-start(f32[1,3,7]{2,0,1:T(1,128)} %param.8) | copy-start | bytes 256
  11.2 21.3 %copy-start = (f32[8,128,256]{2,1,0:T(8,128)S(1)}, f32[8,128,256]{2,1,0:T(8,128)}, u32[]{:S(2)}) copy-start(f32[8,128,256]{2,1,0:T(8,128)} %est.1) | copy-start | bytes 3145732
  11.2 61.6 %all-to-all-start = ((f32[64,65,1,128]{3,2,1,0:T(1,128)}), f32[64,65,1,128]{3,2,1,0:T(1,128)}, u32[]{:S(2)}, u32[]{:S(2)}) async-start(f32[64,65,1,128]{3,2,1,0:T(1,128)} %bitcast.20), calls=%async_computation | async-start | bytes 4259840 | tf_op jit(solution)/shard_map/all_to_all | solution.py:555
  33.3 8.4 %collective-permute-start.1 = (f32[2,3,48,128]{3,2,1,0:T(8,128)S(1)}, f32[2,3,48,128]{3,2,1,0:T(8,128)S(1)}, u32[]{:S(2)}, u32[]{:S(2)}) collective-permute-start(f32[2,3,48,128]{3,2,1,0:T(8,128)S(1)} %get-tuple-element.37), channel_id=1, source_target_pairs={{1,2},{3,4},{5,6},{2,1},{4,3},{6,5},{9,10},{11,12},{13,14},{10,9},... | collective-permute-start | bytes 442376 | tf_op jit(solution)/shard_map/ppermute | solution.py:513
  35.2 6.5 %collective-permute-start.2 = (f32[2,3,48,128]{3,2,1,0:T(8,128)S(1)}, f32[2,3,48,128]{3,2,1,0:T(8,128)S(1)}, u32[]{:S(2)}, u32[]{:S(2)}) collective-permute-start(f32[2,3,48,128]{3,2,1,0:T(8,128)S(1)} %get-tuple-element.38), channel_id=1, source_target_pairs={{0,1},{2,3},{4,5},{6,7},{1,0},{3,2},{5,4},{7,6},{8,9},{10,11},{12,... | collective-permute-start | bytes 442376 | tf_op jit(solution)/shard_map/ppermute | solution.py:514
  79.2 9.8 %collective-permute-start.4 = (f32[2,8,32,128]{3,2,1,0:T(8,128)S(1)}, f32[2,8,32,128]{3,2,1,0:T(8,128)S(1)}, u32[]{:S(2)}, u32[]{:S(2)}) collective-permute-start(f32[2,8,32,128]{3,2,1,0:T(8,128)S(1)} %bitcast.19), channel_id=1, source_target_pairs={{0,8},{8,16},{16,24},{24,0},{1,9},{9,17},{17,25},{25,1},{2,10},{10... | collective-permute-start | bytes 786440 | tf_op jit(solution)/shard_map/ppermute | solution.py:527
  79.3 14.7 %collective-permute-start.5 = (f32[2,8,32,128]{3,2,1,0:T(8,128)S(1)}, f32[2,8,32,128]{3,2,1,0:T(8,128)S(1)}, u32[]{:S(2)}, u32[]{:S(2)}) collective-permute-start(f32[2,8,32,128]{3,2,1,0:T(8,128)S(1)} %bitcast.18), channel_id=1, source_target_pairs={{0,24},{8,0},{16,8},{24,16},{1,25},{9,1},{17,9},{25,17},{2,26},{10... | collective-permute-start | bytes 786440 | tf_op jit(solution)/shard_map/ppermute | solution.py:527
  82.8 13.0 %collective-permute-start.3 = (f32[2,8,32,128]{3,2,1,0:T(8,128)S(1)}, f32[2,8,32,128]{3,2,1,0:T(8,128)S(1)}, u32[]{:S(2)}, u32[]{:S(2)}) collective-permute-start(f32[2,8,32,128]{3,2,1,0:T(8,128)S(1)} %bitcast.17), channel_id=1, source_target_pairs={{0,16},{8,24},{16,0},{24,8},{1,17},{9,25},{17,1},{25,9},{2,18},{10... | collective-permute-start | bytes 786440 | tf_op jit(solution)/shard_map/ppermute | solution.py:527
  97.0 7.5 %collective-permute-start.6 = (f32[2,6,40,128]{3,2,1,0:T(8,128)S(1)}, f32[2,6,40,128]{3,2,1,0:T(8,128)S(1)}, u32[]{:S(2)}, u32[]{:S(2)}) collective-permute-start(f32[2,6,40,128]{3,2,1,0:T(8,128)S(1)} %get-tuple-element.46), channel_id=1, source_target_pairs={{1,2},{3,4},{5,6},{2,1},{4,3},{6,5},{9,10},{11,12},{13,14},{10,9},... | collective-permute-start | bytes 737288 | tf_op jit(solution)/shard_map/ppermute | solution.py:513
  99.0 5.6 %collective-permute-start.7 = (f32[2,6,40,128]{3,2,1,0:T(8,128)S(1)}, f32[2,6,40,128]{3,2,1,0:T(8,128)S(1)}, u32[]{:S(2)}, u32[]{:S(2)}) collective-permute-start(f32[2,6,40,128]{3,2,1,0:T(8,128)S(1)} %get-tuple-element.47), channel_id=1, source_target_pairs={{0,1},{2,3},{4,5},{6,7},{1,0},{3,2},{5,4},{7,6},{8,9},{10,11},{12,... | collective-permute-start | bytes 737288 | tf_op jit(solution)/shard_map/ppermute | solution.py:514
  105.2 7.1 %collective-permute-start.8 = (f32[2,14,8,128]{3,2,1,0:T(8,128)S(1)}, f32[2,14,8,128]{3,2,1,0:T(8,128)S(1)}, u32[]{:S(2)}, u32[]{:S(2)}) collective-permute-start(f32[2,14,8,128]{3,2,1,0:T(8,128)S(1)} %get-tuple-element.49), channel_id=1, source_target_pairs={{8,16},{24,56},{48,40},{32,64},{72,80},{88,120},{112,104},{96,128}... | collective-permute-start | bytes 344072 | tf_op jit(solution)/shard_map/ppermute | solution.py:521
  107.5 5.1 %collective-permute-start.9 = (f32[2,14,8,128]{3,2,1,0:T(8,128)S(1)}, f32[2,14,8,128]{3,2,1,0:T(8,128)S(1)}, u32[]{:S(2)}, u32[]{:S(2)}) collective-permute-start(f32[2,14,8,128]{3,2,1,0:T(8,128)S(1)} %get-tuple-element.50), channel_id=1, source_target_pairs={{0,8},{16,24},{56,48},{40,32},{64,72},{80,88},{120,112},{104,96},{... | collective-permute-start | bytes 344072 | tf_op jit(solution)/shard_map/ppermute | solution.py:522
  117.2 6.2 %collective-permute-start.10 = (f32[2,3,40,128]{3,2,1,0:T(8,128)S(1)}, f32[2,3,40,128]{3,2,1,0:T(8,128)S(1)}, u32[]{:S(2)}, u32[]{:S(2)}) collective-permute-start(f32[2,3,40,128]{3,2,1,0:T(8,128)S(1)} %get-tuple-element.55), channel_id=1, source_target_pairs={{1,2},{3,4},{5,6},{2,1},{4,3},{6,5},{9,10},{11,12},{13,14},{10,9},... | collective-permute-start | bytes 368648 | tf_op jit(solution)/shard_map/ppermute | solution.py:513
  119.1 4.3 %collective-permute-start.11 = (f32[2,3,40,128]{3,2,1,0:T(8,128)S(1)}, f32[2,3,40,128]{3,2,1,0:T(8,128)S(1)}, u32[]{:S(2)}, u32[]{:S(2)}) collective-permute-start(f32[2,3,40,128]{3,2,1,0:T(8,128)S(1)} %get-tuple-element.56), channel_id=1, source_target_pairs={{0,1},{2,3},{4,5},{6,7},{1,0},{3,2},{5,4},{7,6},{8,9},{10,11},{12,... | collective-permute-start | bytes 368648 | tf_op jit(solution)/shard_map/ppermute | solution.py:514
  124.0 6.2 %collective-permute-start.12 = (f32[2,8,8,128]{3,2,1,0:T(8,128)S(1)}, f32[2,8,8,128]{3,2,1,0:T(8,128)S(1)}, u32[]{:S(2)}, u32[]{:S(2)}) collective-permute-start(f32[2,8,8,128]{3,2,1,0:T(8,128)S(1)} %get-tuple-element.58), channel_id=1, source_target_pairs={{8,16},{24,56},{48,40},{32,64},{72,80},{88,120},{112,104},{96,128}... | collective-permute-start | bytes 196616 | tf_op jit(solution)/shard_map/ppermute | solution.py:521
  127.6 4.4 %collective-permute-start.13 = (f32[2,8,8,128]{3,2,1,0:T(8,128)S(1)}, f32[2,8,8,128]{3,2,1,0:T(8,128)S(1)}, u32[]{:S(2)}, u32[]{:S(2)}) collective-permute-start(f32[2,8,8,128]{3,2,1,0:T(8,128)S(1)} %get-tuple-element.59), channel_id=1, source_target_pairs={{0,8},{16,24},{56,48},{40,32},{64,72},{80,88},{120,112},{104,96},{... | collective-permute-start | bytes 196616 | tf_op jit(solution)/shard_map/ppermute | solution.py:522
  132.6 6.6 %collective-permute-start.16 = (f32[8,32,128]{2,1,0:T(8,128)S(1)}, f32[8,32,128]{2,1,0:T(8,128)S(1)}, u32[]{:S(2)}, u32[]{:S(2)}) collective-permute-start(f32[8,32,128]{2,1,0:T(8,128)S(1)} %get-tuple-element.61.refs_0_), channel_id=1, source_target_pairs={{0,8},{8,16},{16,24},{24,0},{1,9},{9,17},{17,25},{25,1},{2,10},{10... | collective-permute-start | bytes 393224 | tf_op jit(solution)/shard_map/ppermute | solution.py:527
  134.3 6.3 %collective-permute-start.15 = (f32[8,32,128]{2,1,0:T(8,128)S(1)}, f32[8,32,128]{2,1,0:T(8,128)S(1)}, u32[]{:S(2)}, u32[]{:S(2)}) collective-permute-start(f32[8,32,128]{2,1,0:T(8,128)S(1)} %get-tuple-element.62.refs_1_), channel_id=1, source_target_pairs={{0,24},{8,0},{16,8},{24,16},{1,25},{9,1},{17,9},{25,17},{2,26},{10... | collective-permute-start | bytes 393224 | tf_op jit(solution)/shard_map/ppermute | solution.py:527
  136.4 6.7 %collective-permute-start.14 = (f32[8,32,128]{2,1,0:T(8,128)S(1)}, f32[8,32,128]{2,1,0:T(8,128)S(1)}, u32[]{:S(2)}, u32[]{:S(2)}) collective-permute-start(f32[8,32,128]{2,1,0:T(8,128)S(1)} %get-tuple-element.61.refs_0_), channel_id=1, source_target_pairs={{0,24},{8,0},{16,8},{24,16},{1,25},{9,1},{17,9},{25,17},{2,26},{10... | collective-permute-start | bytes 393224 | tf_op jit(solution)/shard_map/ppermute | solution.py:527
  138.3 6.2 %collective-permute-start.19 = (f32[8,32,128]{2,1,0:T(8,128)S(1)}, f32[8,32,128]{2,1,0:T(8,128)S(1)}, u32[]{:S(2)}, u32[]{:S(2)}) collective-permute-start(f32[8,32,128]{2,1,0:T(8,128)S(1)} %get-tuple-element.62.refs_1_), channel_id=1, source_target_pairs={{0,8},{8,16},{16,24},{24,0},{1,9},{9,17},{17,25},{25,1},{2,10},{10... | collective-permute-start | bytes 393224 | tf_op jit(solution)/shard_map/ppermute | solution.py:527
  139.3 6.7 %collective-permute-start.17 = (f32[8,32,128]{2,1,0:T(8,128)S(1)}, f32[8,32,128]{2,1,0:T(8,128)S(1)}, u32[]{:S(2)}, u32[]{:S(2)}) collective-permute-start(f32[8,32,128]{2,1,0:T(8,128)S(1)} %collective-permute-done.16.refs_6_), channel_id=1, source_target_pairs={{0,8},{8,16},{16,24},{24,0},{1,9},{9,17},{17,25},{25,1},{2,10},{10... | collective-permute-start | bytes 393224 | tf_op jit(solution)/shard_map/ppermute | solution.py:527
  140.5 5.4 %collective-permute-start.18 = (f32[8,32,128]{2,1,0:T(8,128)S(1)}, f32[8,32,128]{2,1,0:T(8,128)S(1)}, u32[]{:S(2)}, u32[]{:S(2)}) collective-permute-start(f32[8,32,128]{2,1,0:T(8,128)S(1)} %collective-permute-done.15.refs_3_), channel_id=1, source_target_pairs={{0,24},{8,0},{16,8},{24,16},{1,25},{9,1},{17,9},{25,17},{2,26},{10... | collective-permute-start | bytes 393224 | tf_op jit(solution)/shard_map/ppermute | solution.py:527
